TPU v7x, 32 devices: a whole 2x2x4 slice. The times are simulated.
32 devices in a mesh: dp: 8 (over y, x, core), narrow: 4 (over z).
Axes of the slice: x: 2, y: 2, z: 4, core: 2. Of those that a mesh axis runs over, the one named last changes fastest.
Arguments:
- tokens: bfloat16 [16384, 2048], P(('dp', 'narrow')), may hold values from -6 to 6
- doc_lengths: int32 [8, 4], P('dp'), may hold values from 1 to 1792, as said below
- attn_gain: float32 [2048], replicated, may hold values from 0.5 to 1.5
- w_query: bfloat16 [2048, 2048], replicated, may hold values from -0.125 to 0.125
- w_key: bfloat16 [2048, 2048], replicated, may hold values from -0.125 to 0.125
- w_value: bfloat16 [2048, 2048], replicated, may hold values from -0.125 to 0.125
- w_beta: bfloat16 [2048, 16], replicated, may hold values from -0.125 to 0.125
- conv_weight: float32 [3, 4, 2048], replicated, may hold values from -3 to 3
- out_gain: float32 [128], replicated, may hold values from 0.25 to 1.75
- w_out: bfloat16 [2048, 2048], replicated, may hold values from -0.125 to 0.125
- mlp_gain: float32 [2048], replicated, may hold values from 0.5 to 1.5
- w_gate: bfloat16 [2048, 5632], P(None, 'narrow'), may hold values from -0.125 to 0.125
- w_up: bfloat16 [2048, 5632], P(None, 'narrow'), may hold values from -0.125 to 0.125
- w_down: bfloat16 [5632, 2048], P('narrow'), may hold values from -0.078125 to 0.078125
- grad_out: bfloat16 [16384, 2048], P(('dp', 'narrow')), may hold values from -6 to 6
Outputs:
- block_out: bfloat16 [16384, 2048], P(('dp', 'narrow'))
- grad_tokens: bfloat16 [16384, 2048], P(('dp', 'narrow'))
- grad_attn_gain: float32 [2048], P(('dp', 'narrow'))
- grad_query: float32 [2048, 2048], P(('dp', 'narrow'))
- grad_key: float32 [2048, 2048], P(('dp', 'narrow'))
- grad_value: float32 [2048, 2048], P(('dp', 'narrow'))
- grad_beta: float32 [2048, 16], P(('dp', 'narrow'))
- grad_conv: float32 [3, 4, 2048], P(None, None, ('dp', 'narrow'))
- grad_out_gain: float32 [128], P(('dp', 'narrow'))
- grad_w_out: float32 [2048, 2048], P(None, ('dp', 'narrow'))
- grad_mlp_gain: float32 [2048], P(('dp', 'narrow'))
- grad_gate: float32 [2048, 5632], P('dp', 'narrow')
- grad_up: float32 [2048, 5632], P('dp', 'narrow')
- grad_down: float32 [5632, 2048], P('narrow', 'dp')
Inputs may be any that keep to these rules, and one draw needn't show every extreme that they name: `doc_lengths`: each row holds the 4 document lengths of one packed sequence in order, summing to 2048; in every row the largest is exactly 1792.
All inputs are finite; a program needn't handle non-finite values.
Results may differ from a plain program's by a relative error of at most 0.017.
Values may be sent and summed in bfloat16 or wider, within the bound.
A program may use at most 512 MiB of HBM per device.

v0:
```python
import jax
import jax.numpy as jnp
from jax import lax
from jax.sharding import PartitionSpec as P

CONV = 4
SPAN = 64


EXACT_PRECISION = lax.Precision.HIGHEST


def shifted_2(value, axis, steps):
    count = lax.axis_size(axis)
    first, last = (max(0, -steps), min(count, count - steps))
    return lax.ppermute(value, axis, [(source, source + steps) for source in range(first, last)])


def carried_in(array, axis, combine, identity):
    length, index = (lax.axis_size(axis), lax.axis_index(axis))
    everything = jax.tree.map(
        lambda part, kind: lax.all_gather(part.astype(kind), axis),
        array,
        (jnp.bfloat16, jnp.bfloat16),
    )
    start = jax.tree.map(
        lambda part, zero: jnp.broadcast_to(jnp.asarray(zero, part.dtype), part.shape),
        array,
        identity,
    )

    def step(k, before):
        reached = k < index
        new = combine(
            before, jax.tree.map(lambda part, own: part[k].astype(own.dtype), everything, array)
        )
        return jax.tree.map(lambda a, b: jnp.where(reached, a, b), new, before)

    return lax.fori_loop(0, length, step, start)


def carried_in_2(array, axis, join, neutral):
    count = lax.axis_size(axis)
    place = lax.axis_index(axis)
    ahead = count - 1 - place
    gathered = jax.tree.map(
        lambda a, kind: lax.all_gather(a.astype(kind), axis),
        array,
        jax.tree.map(lambda a: jnp.bfloat16 if a.dtype == jnp.float32 else a.dtype, array),
    )
    state = jax.tree.map(lambda a, e: jnp.zeros_like(a) + jnp.asarray(e, a.dtype), array, neutral)

    def one(step, state):
        source = count - 1 - step
        return join(
            state,
            jax.tree.map(
                lambda a, own: lax.dynamic_index_in_dim(a, source, 0, False).astype(own.dtype),
                gathered,
                array,
            ),
        )

    return lax.fori_loop(0, ahead, one, state)


def shortened(array):

    def short(part):
        return part.astype(jnp.bfloat16) if part.dtype == jnp.float32 else part

    return jax.tree.map(short, array)


def matmul(left, right):
    return jnp.dot(left, right, preferred_element_type=jnp.float32)


def rms_scale(value_in, gain_vec, epsilon):
    return (
        value_in
        * lax.rsqrt(jnp.mean(value_in * value_in, axis=-1, keepdims=True) + epsilon)
        * gain_vec
    )


def norm_back(value_in, gain_vec, upstream, epsilon):
    inv_scale = lax.rsqrt(jnp.mean(value_in * value_in, axis=-1, keepdims=True) + epsilon)
    scaled_up = upstream * gain_vec
    gain_term = jnp.sum(upstream * value_in * inv_scale, axis=0)
    cubed = inv_scale * inv_scale * inv_scale
    back_value = inv_scale * scaled_up - value_in * cubed * jnp.mean(
        scaled_up * value_in, axis=-1, keepdims=True
    )
    return (back_value, gain_term)


def doc_positions(doc_lengths, seq_length):
    doc_ends = jnp.cumsum(doc_lengths, axis=1)
    position = jnp.arange(seq_length, dtype=jnp.int32)
    return jnp.sum((position[None, :, None] >= doc_ends[:, None, :]).astype(jnp.int32), axis=2)


def unit_lower_inverse(lower_terms):
    block_len = lower_terms.shape[-1]
    negated = -lower_terms
    inverse = negated + jnp.eye(block_len, dtype=jnp.float32)
    power = negated
    for level in range(max(1, (block_len - 1).bit_length() - 1)):
        power = jnp.matmul(power, power, precision=EXACT_PRECISION)
        inverse = inverse + jnp.matmul(inverse, power, precision=EXACT_PRECISION)
    return inverse


def block_products(query_vec, key_vec, value_vec, beta_gate, doc_block):
    block_len = doc_block.shape[-1]
    key_size = key_vec.shape[-1]
    position = jnp.arange(block_len, dtype=jnp.int32)
    same_doc = doc_block[..., :, None] == doc_block[..., None, :]
    strict = ((position[:, None] > position[None, :]) & same_doc)[:, :, None]
    causal = ((position[:, None] >= position[None, :]) & same_doc)[:, :, None]
    key_gram = jnp.einsum("abhid,abhjd->abhij", key_vec, key_vec, precision=EXACT_PRECISION)
    lower_terms = jnp.where(strict, key_gram * beta_gate[..., None], 0.0)
    inverse = unit_lower_inverse(lower_terms)
    right_side = jnp.concatenate(
        [key_vec * beta_gate[..., None], value_vec * beta_gate[..., None]], axis=-1
    )
    solved = jnp.einsum("abhij,abhjd->abhid", inverse, right_side, precision=EXACT_PRECISION)
    scores = jnp.where(
        causal, jnp.einsum("abhid,abhjd->abhij", query_vec, key_vec, precision=EXACT_PRECISION), 0.0
    )
    return (solved[..., :key_size], solved[..., key_size:], scores)


def state_step(carried, block_in):
    span_state, last_doc = carried
    query_vec, key_vec, w_rows, u_rows, scores, doc_block = block_in
    keep_state = (doc_block == last_doc[:, None]).astype(jnp.float32)[:, None, :, None]
    new_values = u_rows - keep_state * jnp.einsum(
        "bhed,bhcd->bhce", span_state, w_rows, precision=EXACT_PRECISION
    )
    span_out = keep_state * jnp.einsum(
        "bhed,bhcd->bhce", span_state, query_vec, precision=EXACT_PRECISION
    )
    span_out = span_out + jnp.einsum(
        "bhij,bhje->bhie", scores, new_values, precision=EXACT_PRECISION
    )
    last_mask = (doc_block == doc_block[:, -1:]).astype(jnp.float32)[:, None, :, None]
    state_add = jnp.einsum(
        "bhce,bhcd->bhed", new_values * last_mask, key_vec, precision=EXACT_PRECISION
    )
    span_state = keep_state[:, :, -1:, :] * span_state + state_add
    return ((span_state, doc_block[:, -1]), span_out)


def run_states(start_carry, blocks_in):
    query_blk, key_blk, value_blk, beta_blk, doc_blk = blocks_in
    w_rows, u_rows, scores = block_products(query_blk, key_blk, value_blk, beta_blk, doc_blk)
    return lax.scan(state_step, start_carry, (query_blk, key_blk, w_rows, u_rows, scores, doc_blk))


def mixer_blocks(proj_ext, beta_logit, conv_weight, doc_ext, edge):
    seq_count, ext_len = doc_ext.shape
    tok_rows = ext_len - edge
    model_width = proj_ext.shape[-1]
    head_count = beta_logit.shape[2]
    key_size = model_width // head_count
    doc_here = doc_ext[:, edge:]
    summed = proj_ext[:, edge:] * conv_weight[:, 0, :]
    for lag_steps in range(1, CONV):
        shifted = proj_ext[:, edge - lag_steps : edge - lag_steps + tok_rows]
        earlier = doc_ext[:, edge - lag_steps : edge - lag_steps + tok_rows]
        same_doc = (earlier == doc_here)[:, :, None, None]
        summed = summed + jnp.where(same_doc, shifted, 0.0) * conv_weight[:, lag_steps, :]
    mixer_in = jax.nn.silu(summed)
    query_vec = mixer_in[:, :, 0].reshape(seq_count, tok_rows, head_count, key_size)
    key_vec = mixer_in[:, :, 1].reshape(seq_count, tok_rows, head_count, key_size)
    value_vec = mixer_in[:, :, 2].reshape(seq_count, tok_rows, head_count, key_size)
    query_vec = (
        query_vec
        * lax.rsqrt(jnp.sum(query_vec * query_vec, axis=-1, keepdims=True) + 1e-06)
        * key_size ** (-0.5)
    )
    key_vec = key_vec * lax.rsqrt(jnp.sum(key_vec * key_vec, axis=-1, keepdims=True) + 1e-06)
    beta_gate = jax.nn.sigmoid(beta_logit)
    blocks = tok_rows // SPAN

    def to_blocks(array_in):
        return array_in.reshape(seq_count, blocks, SPAN, head_count, key_size).transpose(
            1, 0, 3, 2, 4
        )

    beta_blocks = beta_gate.reshape(seq_count, blocks, SPAN, head_count).transpose(1, 0, 3, 2)
    doc_blocks = doc_here.reshape(seq_count, blocks, SPAN).transpose(1, 0, 2)
    return (to_blocks(query_vec), to_blocks(key_vec), to_blocks(value_vec), beta_blocks, doc_blocks)


def mixer_local(proj_ext, beta_logit, conv_weight, out_gain, start_state, doc_ext):
    edge = CONV - 1
    seq_count, ext_len = doc_ext.shape
    tok_rows = ext_len - edge
    head_count = beta_logit.shape[2]
    key_size = out_gain.shape[0]
    blocks_in = mixer_blocks(proj_ext, beta_logit, conv_weight, doc_ext, edge)
    final_carry, span_outs = run_states((start_state, doc_ext[:, edge - 1]), blocks_in)
    core_out = span_outs.transpose(1, 0, 3, 2, 4).reshape(seq_count, tok_rows, head_count, key_size)
    core_out = (
        core_out
        * lax.rsqrt(jnp.mean(core_out * core_out, axis=-1, keepdims=True) + 1e-05)
        * out_gain
    )
    return (core_out.reshape(seq_count, tok_rows, head_count * key_size), final_carry[0])


def compose(earlier, later):
    early_map, early_add = earlier
    late_map, late_add = later
    joined_map = jnp.einsum("hij,hjk->hik", early_map, late_map, precision=EXACT_PRECISION)
    joined_add = (
        jnp.einsum("hei,hij->hej", early_add, late_map, precision=EXACT_PRECISION) + late_add
    )
    return (joined_map, joined_add)


def local(
    tokens,
    doc_lengths,
    attn_gain,
    w_query,
    w_key,
    w_value,
    w_beta,
    conv_weight,
    out_gain,
    w_out,
    mlp_gain,
    w_gate,
    w_up,
    w_down,
    grad_out,
):
    tok_rows, model_width = tokens.shape
    head_count = w_beta.shape[1]
    key_size = out_gain.shape[0]
    edge = CONV - 1
    seq_length = tok_rows * lax.axis_size("narrow")
    offset = lax.axis_index("narrow") * tok_rows
    doc_full = doc_positions(doc_lengths, seq_length)
    doc_padded = jnp.pad(doc_full, ((0, 0), (edge, 0)), constant_values=-1)
    doc_ext = lax.dynamic_slice_in_dim(doc_padded, offset, tok_rows + edge, 1)
    inputs = tokens.astype(jnp.float32)
    normed = rms_scale(inputs, attn_gain, 1e-06).astype(jnp.bfloat16)
    projected = jnp.stack(
        [matmul(normed, w_query), matmul(normed, w_key), matmul(normed, w_value)], axis=1
    )
    beta_logit = matmul(normed, w_beta)
    before = shifted_2(projected[tok_rows - edge :].astype(jnp.bfloat16), "narrow", 1).astype(
        jnp.float32
    )
    proj_ext = jnp.concatenate([before, projected], axis=0)[None]
    beta_in = beta_logit[None]
    query_blk, key_blk, value_blk, beta_blk, doc_blk = mixer_blocks(
        proj_ext, beta_in, conv_weight, doc_ext, edge
    )
    paired = (
        jnp.concatenate([query_blk, query_blk], axis=1),
        jnp.concatenate([key_blk, key_blk], axis=1),
        jnp.concatenate([value_blk, jnp.zeros_like(value_blk)], axis=1),
        jnp.concatenate([beta_blk, beta_blk], axis=1),
        jnp.concatenate([doc_blk, doc_blk], axis=1),
    )
    identity_map = jnp.broadcast_to(
        jnp.eye(key_size, dtype=jnp.float32), (head_count, key_size, key_size)
    )
    zero_state = jnp.zeros((head_count, key_size, key_size), jnp.float32)
    start_pair = jnp.stack([zero_state, identity_map])
    prior_doc = doc_ext[:, edge - 1]
    (end_pair, ignored), unused = run_states(
        (start_pair, jnp.concatenate([prior_doc, prior_doc])), paired
    )
    local_add = end_pair[0]
    transfer = end_pair[1]
    entry_map, entry_state = carried_in(
        (transfer, local_add), "narrow", compose, (identity_map, zero_state)
    )

    def mixer_fn(proj_in, beta_part, conv_in, gain_in, state_in):
        return mixer_local(proj_in, beta_part, conv_in, gain_in, state_in, doc_ext)

    (mixer_out, end_state), core_back = jax.vjp(
        mixer_fn, proj_ext, beta_in, conv_weight, out_gain, entry_state[None]
    )
    attn_mixed = mixer_out.reshape(tok_rows, model_width).astype(jnp.bfloat16)
    hidden = inputs + matmul(attn_mixed, w_out)
    normed_mlp = rms_scale(hidden, mlp_gain, 1e-06).astype(jnp.bfloat16)
    gathered = lax.all_gather(normed_mlp, "narrow", axis=0, tiled=True)
    gate_proj = matmul(gathered, w_gate)
    up_proj = matmul(gathered, w_up)
    gate_sigmoid = jax.nn.sigmoid(gate_proj)
    silu_gate = gate_proj * gate_sigmoid
    activation = (silu_gate * up_proj).astype(jnp.bfloat16)
    ffn_sum = lax.psum_scatter(
        matmul(activation, w_down).astype(jnp.bfloat16), "narrow", scatter_dimension=0, tiled=True
    ).astype(jnp.float32)
    block_out = (hidden + ffn_sum).astype(jnp.bfloat16)
    cot_rows = lax.all_gather(grad_out, "narrow", axis=0, tiled=True)
    d_act = jnp.einsum("rd,fd->rf", cot_rows, w_down, preferred_element_type=jnp.float32)
    down_term_grad = jnp.einsum(
        "rf,rd->fd", activation, cot_rows, preferred_element_type=jnp.float32
    )
    d_gate = (d_act * up_proj * gate_sigmoid * (1.0 + gate_proj * (1.0 - gate_sigmoid))).astype(
        jnp.bfloat16
    )
    d_up = (d_act * silu_gate).astype(jnp.bfloat16)
    gate_term_grad = jnp.einsum("rd,rf->df", gathered, d_gate, preferred_element_type=jnp.float32)
    up_term_grad = jnp.einsum("rd,rf->df", gathered, d_up, preferred_element_type=jnp.float32)
    from_gate = jnp.einsum("rf,df->rd", d_gate, w_gate, preferred_element_type=jnp.float32)
    d_normed_mlp = lax.psum_scatter(
        (
            from_gate + jnp.einsum("rf,df->rd", d_up, w_up, preferred_element_type=jnp.float32)
        ).astype(jnp.bfloat16),
        "narrow",
        scatter_dimension=0,
        tiled=True,
    ).astype(jnp.float32)
    grad_gate, grad_up, grad_down = (
        lax.psum_scatter(
            gate_term_grad.astype(jnp.bfloat16), "dp", scatter_dimension=0, tiled=True
        ).astype(jnp.float32),
        lax.psum_scatter(
            up_term_grad.astype(jnp.bfloat16), "dp", scatter_dimension=0, tiled=True
        ).astype(jnp.float32),
        lax.psum_scatter(
            down_term_grad.astype(jnp.bfloat16), "dp", scatter_dimension=1, tiled=True
        ).astype(jnp.float32),
    )
    d_hidden_norm, mlp_gain_term = norm_back(hidden, mlp_gain, d_normed_mlp, 1e-06)
    d_hidden = grad_out.astype(jnp.float32) + d_hidden_norm
    d_branch = d_hidden.astype(jnp.bfloat16)
    w_out_term = jnp.einsum("rd,re->de", attn_mixed, d_branch, preferred_element_type=jnp.float32)
    d_mixed = jnp.einsum("re,de->rd", d_branch, w_out, preferred_element_type=jnp.float32)
    d_core = d_mixed.reshape(1, tok_rows, model_width)
    start_grad = core_back((d_core, jnp.zeros_like(end_state)))[4][0]
    back_map, exit_grad = carried_in_2(
        (transfer.transpose(0, 2, 1), start_grad), "narrow", compose, (identity_map, zero_state)
    )
    d_proj_ext, d_beta_logit, conv_term, out_gain_term, unused_grad = core_back(
        (d_core, exit_grad[None])
    )
    after = shifted_2(shortened(d_proj_ext[0, :edge]), "narrow", -1)
    d_projected = d_proj_ext[0, edge:].at[tok_rows - edge :].add(after)
    d_proj_low = d_projected.astype(jnp.bfloat16)
    d_beta_low = d_beta_logit.reshape(tok_rows, head_count).astype(jnp.bfloat16)
    d_query = d_proj_low[:, 0]
    d_key = d_proj_low[:, 1]
    d_value = d_proj_low[:, 2]
    query_term = jnp.einsum("rd,re->de", normed, d_query, preferred_element_type=jnp.float32)
    key_term = jnp.einsum("rd,re->de", normed, d_key, preferred_element_type=jnp.float32)
    value_term = jnp.einsum("rd,re->de", normed, d_value, preferred_element_type=jnp.float32)
    beta_term = jnp.einsum("rd,rh->dh", normed, d_beta_low, preferred_element_type=jnp.float32)
    d_normed = jnp.einsum("re,de->rd", d_query, w_query, preferred_element_type=jnp.float32)
    d_normed = d_normed + jnp.einsum("re,de->rd", d_key, w_key, preferred_element_type=jnp.float32)
    d_normed = d_normed + jnp.einsum(
        "re,de->rd", d_value, w_value, preferred_element_type=jnp.float32
    )
    d_normed = d_normed + jnp.einsum(
        "rh,dh->rd", d_beta_low, w_beta, preferred_element_type=jnp.float32
    )
    d_input_norm, attn_gain_term = norm_back(inputs, attn_gain, d_normed, 1e-06)
    grad_tokens = (d_hidden + d_input_norm).astype(jnp.bfloat16)
    (
        grad_query,
        grad_key,
        grad_value,
        grad_beta,
        grad_w_out,
        grad_conv,
        grad_attn_gain,
        grad_out_gain,
        grad_mlp_gain,
    ) = (
        lax.psum_scatter(query_term, ("dp", "narrow"), scatter_dimension=0, tiled=True),
        lax.psum_scatter(key_term, ("dp", "narrow"), scatter_dimension=0, tiled=True),
        lax.psum_scatter(value_term, ("dp", "narrow"), scatter_dimension=0, tiled=True),
        lax.psum_scatter(beta_term, ("dp", "narrow"), scatter_dimension=0, tiled=True),
        lax.psum_scatter(w_out_term, ("dp", "narrow"), scatter_dimension=1, tiled=True),
        lax.psum_scatter(conv_term, ("dp", "narrow"), scatter_dimension=2, tiled=True),
        lax.psum_scatter(attn_gain_term, ("dp", "narrow"), scatter_dimension=0, tiled=True),
        lax.psum_scatter(out_gain_term, ("dp", "narrow"), scatter_dimension=0, tiled=True),
        lax.psum_scatter(mlp_gain_term, ("dp", "narrow"), scatter_dimension=0, tiled=True),
    )
    return (
        block_out,
        grad_tokens,
        grad_attn_gain,
        grad_query,
        grad_key,
        grad_value,
        grad_beta,
        grad_conv,
        grad_out_gain,
        grad_w_out,
        grad_mlp_gain,
        grad_gate,
        grad_up,
        grad_down,
    )


def solution(mesh):
    placed = (
        P(("dp", "narrow"), None),
        P("dp", None),
        P(),
        P(),
        P(),
        P(),
        P(),
        P(),
        P(),
        P(),
        P(),
        P(None, "narrow"),
        P(None, "narrow"),
        P("narrow", None),
        P(("dp", "narrow"), None),
    )
    return jax.shard_map(
        local,
        mesh=mesh,
        in_specs=placed,
        out_specs=(
            P(("dp", "narrow"), None),
            P(("dp", "narrow"), None),
            P(("dp", "narrow")),
            P(("dp", "narrow"), None),
            P(("dp", "narrow"), None),
            P(("dp", "narrow"), None),
            P(("dp", "narrow"), None),
            P(None, None, ("dp", "narrow")),
            P(("dp", "narrow")),
            P(None, ("dp", "narrow")),
            P(("dp", "narrow")),
            P("dp", "narrow"),
            P("dp", "narrow"),
            P("narrow", "dp"),
        ),
        check_vma=False,
    )
```

profile of v0, /device:TPU:0, one launch (start us, length us, event | category | flops | bytes accessed | tf_op | source)
XLA Modules:
  0.0 3920.8 jit_solution(4623187097081086975)
XLA Ops:
  51.9 13.3 fusion.134
  65.2 9.7 slice_bitcast_fusion.4
  92.3 15.9 fusion.242
  108.3 14.1 fusion.144
  122.4 11.6 fusion.297
  133.9 16.8 add_add_fusion
  150.7 10.3 fusion.186
  170.0 12.5 fusion.298
  182.4 11.1 fusion.300
  193.5 19.1 convolution_add_fusion.1
  212.6 12.0 fusion.299
  224.6 17.2 fusion.301
  241.9 14.9 convolution_add_fusion
  256.8 14.5 fusion.302
  271.3 24.3 fusion.128
  295.7 11.0 fusion.290
  306.7 102.4 %while.106 = (s32[]{:T(128)}, f32[2,16,128,128]{3,2,1,0:T(8,128)S(1)}, s32[2]{0:T(128)S(1)}, s32[8,2,64]{2,1,0:T(2,128)}, f32[8,2,16,64,128]{4,3,2,1,0:T(8,128)}...) while((s32[]{:T(128)}, f32[2,16,128,128]{3,2,1,0:T(8,128)S(1)}, ...), condition=%wide.region_5.6_spmd, body=%wide.region_4.5_spmd.sunk | while | flops 807142016 | bytes 11539747 | solution.py:159
  410.4 11.7 fusion.252
  473.7 11.6 convolution_add_fusion.7
  492.9 10.6 fusion.206
  513.1 10.2 select_bitcast_fusion
  523.3 13.7 while.110
  545.0 163.4 %while.107 = (s32[]{:T(128)}, f32[1,16,128,128]{3,2,1,0:T(8,128)S(1)}, s32[1]{0:T(128)}, f32[8,1,16,64,128]{4,3,2,1,0:T(8,128)}, f32[8,1,16,128,128]{4,3,2,1,0:T...) while((s32[]{:T(128)}, ...), condition=%wide.region_10.11_spmd, body=%wide.region_9.10_spmd.sunk | while | flops 705954304 | bytes 13114924 | solution.py:159
  732.7 149.4 %all-gather.12.cloned.1.call-done = bf16[2048,2048]{1,0:T(8,128)(2,1)} async-done(((bf16[512,2048]{1,0:T(8,128)(2,1)}), bf16[2048,2048]{1,0:T(8,128)(2,1)}) %all-gather.12.cloned.1.call-update) | async-done | bytes 8388624 | tf_op jit(solution)/shard_map/all_gather | solution.py:296
  882.1 18.7 fusion.307
  900.8 16.9 fusion.308
  917.7 113.6 %all-gather.14.cloned.1.call-done = bf16[2048,2048]{1,0:T(8,128)(2,1)} async-done(((bf16[512,2048]{1,0:T(8,128)(2,1)}), bf16[2048,2048]{1,0:T(8,128)(2,1)}) %all-gather.14.cloned.1.call-update) | async-done | bytes 8388624 | tf_op jit(solution)/shard_map/all_gather | solution.py:306
  1031.4 25.9 multiply_convert_fusion
  1057.3 19.4 fusion.309
  1076.7 21.5 add_convert_fusion
  1098.3 18.5 convolution_convert_fusion
  1119.3 121.8 %reduce-scatter.18.cloned.1.call-done = bf16[512,2048]{1,0:T(8,128)(2,1)} async-done(((bf16[2048,2048]{1,0:T(8,128)(2,1)}), bf16[512,2048]{1,0:T(8,128)(2,1)}) %reduce-scatter.18.cloned.1.call-update) | async-done | bytes 2097168 | tf_op jit(solution)/shard_map/reduce_scatter | solution.py:318
  1245.9 142.7 %reduce-scatter.16.cloned.1.call-done = bf16[512,2048]{1,0:T(8,128)(2,1)} async-done(((bf16[2048,2048]{1,0:T(8,128)(2,1)}), bf16[512,2048]{1,0:T(8,128)(2,1)}) %reduce-scatter.16.cloned.1.call-update) | async-done | bytes 2097168 | tf_op jit(solution)/shard_map/reduce_scatter | solution.py:302
  1393.9 14.6 multiply_reduce_fusion.4
  1417.4 103.9 %while.111 = (s32[]{:T(128)}, f32[1,16,128,128]{3,2,1,0:T(8,128)S(1)}, f32[8,1,1,1,1]{0,4,3,2,1:T(1,128)S(1)}, f32[8,1,1,64,1]{3,4,2,1,0:T(1,128)}, f32[8,1,16,6...) while((s32[]{:T(128)}, ...), condition=%wide.region_18.19_spmd.clone, body=%wide.region_17.18_spmd.clone.sunk | while | flops 706609152 | bytes 10490803 | solution.py:159
  1522.2 19.6 convolution_convert_fusion.3
  1541.9 19.3 convolution_convert_fusion.2
  1570.7 18.0 convolution_convert_fusion.1
  1588.9 10.1 while.108
  1612.2 210.0 %while.109 = (s32[]{:T(128)}, f32[1,16,128,128]{3,2,1,0:T(8,128)S(1)}, f32[8,1,16,64,128]{4,3,2,1,0:T(8,128)}, f32[8,1,16,64,128]{4,3,2,1,0:T(8,128)}, f32[8,1,1...) while((s32[]{:T(128)}, ...), condition=%wide.region_22.23_spmd, body=%wide.region_21.22_spmd.sunk | while | flops 1411121152 | bytes 18885596 | solution.py:159
  1822.2 13.1 fusion.136
  1864.8 9.9 add_add_fusion.8
  1928.6 11.2 add_add_fusion.6
  1960.8 10.7 add_add_fusion.5
  1980.3 9.4 fusion.251
  1989.8 16.3 fusion.207
  2014.3 12.9 multiply_reduce_fusion.5
  2027.3 11.0 fusion.181
  2047.8 10.2 fusion.171
  2082.4 13.1 broadcast_multiply_fusion.2
  2137.7 12.6 add_add_fusion.2
  2150.3 29.2 multiply_reduce_fusion.3
  2190.2 13.2 fusion.246
  2204.3 17.9 multiply_select_fusion.2
  2222.1 19.1 pad_add_fusion
  2255.3 9.9 fusion.235
  2265.2 9.9 fusion.237
  2275.4 9.9 fusion.239
  2317.7 41.5 %all-reduce.19 = (f32[2048]{0:T(1024)S(1)}, f32[128]{0:T(128)S(1)}, f32[2048]{0:T(1024)S(1)}) all-reduce(f32[2048]{0:T(1024)S(1)} %get-tuple-element.1272, f32[128]{0:T(128)S(1)} %bitcast_reduce_fusion, f32[2048]{0:T(1024)S(1)} %copy-done.104), channel_id=5, replica_groups=mesh['dp'=8,'narrow'=4] {'dp','narrow'}, use_global_device_ids=true, to_apply=%region_30.31.clone | all-reduce | flops 4224 | bytes 33792
  2368.5 86.9 %reduce-scatter.34.cloned.1.call-done = f32[64,16]{1,0:T(8,128)} async-done(((f32[2048,16]{1,0:T(8,128)}), f32[64,16]{1,0:T(8,128)}) %reduce-scatter.34.cloned.1.call-update) | async-done | bytes 4112
  2456.9 362.2 %reduce-scatter.26.cloned.1.call-done = f32[2048,64]{0,1:T(8,128)} async-done(((f32[2048,2048]{0,1:T(8,128)}), f32[2048,64]{0,1:T(8,128)}) %reduce-scatter.26.cloned.1.call-update) | async-done | bytes 524304 | tf_op jit(solution)/shard_map/reduce_scatter | solution.py:386
  2819.1 365.0 %reduce-scatter.20.cloned.1.call-done = f32[64,2048]{1,0:T(8,128)} async-done(((f32[2048,2048]{1,0:T(8,128)}), f32[64,2048]{1,0:T(8,128)}) %reduce-scatter.20.cloned.1.call-update) | async-done | bytes 524304 | tf_op jit(solution)/shard_map/reduce_scatter | solution.py:382
  3184.1 365.0 %reduce-scatter.22.cloned.1.call-done = f32[64,2048]{1,0:T(8,128)} async-done(((f32[2048,2048]{1,0:T(8,128)}), f32[64,2048]{1,0:T(8,128)}) %reduce-scatter.22.cloned.1.call-update) | async-done | bytes 524304 | tf_op jit(solution)/shard_map/reduce_scatter | solution.py:383
  3549.1 365.0 %reduce-scatter.24.cloned.1.call-done = f32[64,2048]{1,0:T(8,128)} async-done(((f32[2048,2048]{1,0:T(8,128)}), f32[64,2048]{1,0:T(8,128)}) %reduce-scatter.24.cloned.1.call-update) | async-done | bytes 524304 | tf_op jit(solution)/shard_map/reduce_scatter | solution.py:384
  (799 shorter events, 1073.8 us)
Async XLA Ops:
  7.2 31.9 copy-start
  7.2 516.1 %all-gather.8.cloned.1.call-start = ((), (), s32[]{:S(2)}) async-start(), calls=%async_computation.11 | async-start | bytes 2621440 | tf_op jit(solution)/shard_map/all_gather | solution.py:22
  7.2 11.5 slice-start.10
  10.1 29.0 copy-start.109
  10.1 13.3 slice-start.8
  30.2 15.3 collective-permute-start
  37.2 14.7 copy-start.114
  37.2 14.7 copy-start.116
  37.2 14.7 copy-start.118
  40.0 44.9 %copy-start.60 = (f32[1,8,64,16]{2,3,0,1:T(8,128)}, f32[1,8,64,16]{2,3,0,1:T(8,128)S(1)}, u32[]{:S(2)}) copy-start(f32[1,8,64,16]{2,3,0,1:T(8,128)S(1)} %copy.570) | copy-start | bytes 98308
  40.9 11.0 copy-start.78
  40.9 11.0 copy-start.80
  51.8 13.4 copy-start.1
  80.4 70.3 %copy-start.65 = (f32[8,64,16]{1,2,0:T(8,128)}, f32[8,64,16]{1,2,0:T(8,128)S(1)}, u32[]{:S(2)}) copy-start(f32[8,64,16]{1,2,0:T(8,128)S(1)} %copy.330) | copy-start | bytes 98308
  92.3 68.6 %copy-start.22 = (f32[8,1,16,64,128]{4,3,2,1,0:T(8,128)}, f32[8,1,16,64,128]{4,3,2,1,0:T(8,128)S(1)}, u32[]{:S(2)}) copy-start(f32[8,1,16,64,128]{4,3,2,1,0:T(8,128)S(1)} %get-tuple-element.2059) | copy-start | bytes 12582916
  212.6 29.3 slice-start
  224.6 17.2 slice-start.1
  295.7 11.0 copy-start.6
  295.7 11.0 copy-start.98
  306.7 103.7 %copy-start.61 = (f32[1,8,64,16]{2,3,0,1:T(8,128)S(1)}, f32[1,8,64,16]{2,3,0,1:T(8,128)}, u32[]{:S(2)}) copy-start(f32[1,8,64,16]{2,3,0,1:T(8,128)} %copy-done.60) | copy-start | bytes 98308
  306.7 103.6 %copy-start.63 = (pred[8,64,64]{1,2,0:T(8,128)(4,1)S(1)}, pred[8,64,64]{1,2,0:T(8,128)(4,1)}, u32[]{:S(2)}) copy-start(pred[8,64,64]{1,2,0:T(8,128)(4,1)} %get-tuple-element.1460) | copy-start | bytes 98308
  410.3 113.0 %all-gather.10.cloned.1.call-start = ((), (), s32[]{:S(2)}) async-start(), calls=%async_computation.12 | async-start | bytes 2621440 | tf_op jit(solution)/shard_map/all_gather | solution.py:22
  432.2 41.4 %copy-start.92 = (f32[512,16]{0,1:T(8,128)}, f32[512,16]{0,1:T(8,128)S(1)}, u32[]{:S(2)}) copy-start(f32[512,16]{0,1:T(8,128)S(1)} %copy.351) | copy-start | bytes 98308
  440.1 19.2 copy-start.9
  473.4 408.7 %all-gather.12.cloned.1.call-start = ((), (), s32[]{:S(2)}) async-start(), calls=%async_computation.13 | async-start | bytes 10485760 | tf_op jit(solution)/shard_map/all_gather | solution.py:296
  473.7 39.3 %copy-start.69 = (f32[8,64,16]{1,2,0:T(8,128)}, f32[8,64,16]{1,2,0:T(8,128)S(1)}, u32[]{:S(2)}) copy-start(f32[8,64,16]{1,2,0:T(8,128)S(1)} %copy.352) | copy-start | bytes 98308
  473.7 11.6 copy-start.34
  732.1 299.3 %all-gather.14.cloned.1.call-start = ((), (), s32[]{:S(2)}) async-start(), calls=%async_computation.15 | async-start | bytes 10485760 | tf_op jit(solution)/shard_map/all_gather | solution.py:306
  732.7 508.4 %reduce-scatter.18.cloned.1.call-start = ((), (), s32[]{:S(2)}) async-start(), calls=%async_computation.16 | async-start | bytes 10485760 | tf_op jit(solution)/shard_map/reduce_scatter | solution.py:318
  882.1 18.7 copy-start.122
  1098.2 290.3 %reduce-scatter.16.cloned.1.call-start = ((), (), s32[]{:S(2)}) async-start(), calls=%async_computation.14 | async-start | bytes 10485760 | tf_op jit(solution)/shard_map/reduce_scatter | solution.py:302
  1116.7 124.4 %copy-start.101 = (f32[2048]{0:T(1024)S(1)}, f32[2048]{0:T(1024)}, u32[]{:S(2)}) copy-start(f32[2048]{0:T(1024)} %param.39) | copy-start | bytes 24580
  1116.7 124.4 %copy-start.103 = (f32[512]{0:T(512)S(1)}, f32[512]{0:T(512)}, u32[]{:S(2)}) copy-start(f32[512]{0:T(512)} %copy-done.102) | copy-start | bytes 6148
  1116.8 271.8 %copy-start.59 = (bf16[512,2048]{1,0:T(8,128)(2,1)S(1)}, bf16[512,2048]{1,0:T(8,128)(2,1)}, u32[]{:S(2)}) copy-start(bf16[512,2048]{1,0:T(8,128)(2,1)} %param.43) | copy-start | bytes 6291460
  1116.8 271.8 %copy-start.111 = (f32[512]{0:T(512)S(1)}, f32[512]{0:T(512)}, u32[]{:S(2)}) copy-start(f32[512]{0:T(512)} %get-tuple-element.1463) | copy-start | bytes 6148
  1116.8 472.0 %all-gather.18.cloned.1.call-start = ((), (), s32[]{:S(2)}) async-start(), calls=%async_computation.25 | async-start | bytes 2621440 | tf_op jit(solution)/shard_map/all_gather | solution.py:47
  1119.1 469.8 %all-gather.16.cloned.1.call-start = ((), (), s32[]{:S(2)}) async-start(), calls=%async_computation.17 | async-start | bytes 2621440 | tf_op jit(solution)/shard_map/all_gather | solution.py:47
  1393.9 14.6 copy-start.50
  1522.2 763.2 %reduce-scatter.28.cloned.1.call-start = ((), (), s32[]{:S(2)}) async-start(), calls=%async_computation.22 | async-start | bytes 6488064 | tf_op jit(solution)/shard_map/reduce_scatter | solution.py:327
  1541.9 745.8 %reduce-scatter.30.cloned.1.call-start = ((), (), s32[]{:S(2)}) async-start(), calls=%async_computation.23 | async-start | bytes 6488064 | tf_op jit(solution)/shard_map/reduce_scatter | solution.py:330
  1561.2 728.8 %reduce-scatter.32.cloned.1.call-start = ((), (), s32[]{:S(2)}) async-start(), calls=%async_computation.24 | async-start | bytes 6488064 | tf_op jit(solution)/shard_map/reduce_scatter | solution.py:333
  1588.7 778.2 %reduce-scatter.36.cloned.1.call-start = ((), (), s32[]{:S(2)}) async-start(), calls=%async_computation.27 | async-start | bytes 1081344
  1822.2 13.1 copy-start.37
  1928.6 11.2 copy-start.38
  1928.6 11.2 copy-start.17
  1989.8 16.3 copy-start.23
  2014.3 12.9 copy-start.5
  2014.3 12.9 copy-start.67
  2027.3 11.1 copy-start.20
  2027.3 11.1 copy-start.40
  2027.3 11.1 copy-start.70
  2027.3 11.1 copy-start.71
  2027.3 20.4 slice-start.2
  2137.7 12.6 copy-start.115
  2137.7 12.6 copy-start.117
  2137.7 12.6 copy-start.119
  2187.9 267.5 %reduce-scatter.34.cloned.1.call-start = ((), (), s32[]{:S(2)}) async-start(), calls=%async_computation.26 | async-start | bytes 1081344
  2190.2 628.9 %reduce-scatter.26.cloned.1.call-start = ((), (), s32[]{:S(2)}) async-start(), calls=%async_computation.21 | async-start | bytes 17301504 | tf_op jit(solution)/shard_map/reduce_scatter | solution.py:386
  2203.5 980.6 %reduce-scatter.20.cloned.1.call-start = ((), (), s32[]{:S(2)}) async-start(), calls=%async_computation.18 | async-start | bytes 17301504 | tf_op jit(solution)/shard_map/reduce_scatter | solution.py:382
  2242.2 13.1 copy-start.49
  2242.2 10.5 collective-permute-start.1
  2265.2 1283.9 %reduce-scatter.22.cloned.1.call-start = ((), (), s32[]{:S(2)}) async-start(), calls=%async_computation.19 | async-start | bytes 17301504 | tf_op jit(solution)/shard_map/reduce_scatter | solution.py:383
  2275.2 1638.9 %reduce-scatter.24.cloned.1.call-start = ((), (), s32[]{:S(2)}) async-start(), calls=%async_computation.20 | async-start | bytes 17301504 | tf_op jit(solution)/shard_map/reduce_scatter | solution.py:384
  2314.2 46.8 %copy-start.113 = (f32[512]{0:T(512)S(1)}, f32[512]{0:T(512)}, u32[]{:S(2)}) copy-start(f32[512]{0:T(512)} %get-tuple-element.1461) | copy-start | bytes 6148
  (94 other events, 523.4 us)
Sparse Core Ops, SparseCore 0:
  410.4 46.1 all-gather.7
  473.5 46.1 all-gather.9
  732.2 149.8 all-gather.11
  883.5 147.8 all-gather.13
  1098.4 142.6 reduce-scatter.17
  1243.3 145.1 reduce-scatter.15
  1390.7 46.6 all-gather.17
  1522.3 46.6 all-gather.15
  1572.5 57.7 reduce-scatter.27
  1633.9 59.0 reduce-scatter.29
  1696.5 58.9 reduce-scatter.31
  2188.0 133.4 reduce-scatter.35
  2323.8 131.5 reduce-scatter.33
  2458.3 360.7 reduce-scatter.25
  2821.9 362.1 reduce-scatter.19
  3186.9 362.1 reduce-scatter.21
  3551.9 362.1 reduce-scatter.23
where the time goes:
time: 3940 us; the launch traced here: 3920 us
  waiting for transfers between devices  2070 us (53%)
  matrix products  1320 us (34%)
  local copies, waits for them, and re-layouts  234 us (6%)
  other arithmetic  216 us (5%)
  blocking collectives  41.5 us (1%)
    reduce_scatter x1, waiting for transfers between devices, local(): lax.psum_scatter(key_term, ('dp', 'narrow'), scatter_dimension=0, tiled=T...  365 us
    reduce_scatter x1, waiting for transfers between devices, local(): lax.psum_scatter(query_term, ('dp', 'narrow'), scatter_dimension=0, tiled...  365 us
    reduce_scatter x1, waiting for transfers between devices, local(): lax.psum_scatter(value_term, ('dp', 'narrow'), scatter_dimension=0, tiled...  365 us
    reduce_scatter x1, waiting for transfers between devices, local(): lax.psum_scatter(w_out_term, ('dp', 'narrow'), scatter_dimension=1, tiled...  362 us
    dot_general x20, matrix products, unit_lower_inverse(): inverse = inverse + jnp.matmul(inverse, power, precision=EXACT_PRECISION)  201 us
    dot_general x20, matrix products, unit_lower_inverse(): power = jnp.matmul(power, power, precision=EXACT_PRECISION)  187 us
    dot_general x40, matrix products, state_step(): jnp.einsum('bhed,bhcd->bhce', span_state, w_rows, precision=EXACT_PRECISION)  152 us
    all_gather x1, waiting for transfers between devices, local(): gathered = lax.all_gather(normed_mlp, 'narrow', axis=0, tiled=True)  149 us
  transfers between devices with their start and end apart: 19, of which 9 were waited for; matrix products, arithmetic and copies ran while one was open for 28% of the time, Pallas kernels for 0%

commit v1 on v0

v1 whole, which is shorter than its diff:
```python
import functools

import jax
import jax.numpy as jnp
from jax import lax
from jax.experimental import pallas as pl
from jax.experimental.pallas import tpu as pltpu
from jax.sharding import PartitionSpec as P

CONV = 4
BLOCK = 128
HEADS_STEP = 2
PAD = 8
MESH = pl.DeviceIdType.MESH
F32 = jnp.float32
BF16 = jnp.bfloat16
VMEM_LIMIT = 56 * 1024 * 1024


def mm(left, right, contract=(1, 0)):
    return lax.dot_general(
        left.astype(BF16),
        right.astype(BF16),
        (((contract[0],), (contract[1],)), ((), ())),
        preferred_element_type=F32,
    )


def mm_nt(left, right):
    return mm(left, right, (1, 1))


def mm_tn(left, right):
    return mm(left, right, (0, 0))


def iotas(size):
    row = lax.broadcasted_iota(jnp.int32, (size, size), 0)
    col = lax.broadcasted_iota(jnp.int32, (size, size), 1)
    return row, col


def block_masks(since):
    size = since.shape[0]
    row, col = iotas(size)
    back = row - col
    causal = (back >= 0) & (back <= since)
    strict = (back > 0) & (back <= since)
    keep = (since > row).astype(F32)
    last = since[size - 1 : size, :]
    last_mask = (row >= size - 1 - last).astype(F32)
    keep_last = (last > size - 1).astype(F32)
    return causal, strict, keep, last_mask, keep_last


def unit_lower_inverses(lowers):
    size = lowers[0].shape[0]
    row, col = iotas(size)
    width = 1
    inverses = None
    while width < size:
        join = (row // (2 * width) == col // (2 * width)) & (row // width != col // width)
        pieces = [jnp.where(join, low, 0.0) for low in lowers]
        if inverses is None:
            eye = (row == col).astype(F32)
            inverses = [eye - piece for piece in pieces]
        else:
            halves = [mm(piece, inv) for piece, inv in zip(pieces, inverses)]
            inverses = [inv - mm(inv, half) for inv, half in zip(inverses, halves)]
        width *= 2
    return inverses


def conv_front(ext, proj, halo, taps, since):
    rows = proj.shape[0]
    ext[0:PAD, :] = halo.astype(F32)
    ext[PAD : PAD + rows, :] = proj
    pre = proj * taps[0:1, :]
    for lag in range(1, CONV):
        moved = ext[PAD - lag : PAD - lag + rows, :]
        pre = pre + jnp.where(since >= lag, moved, 0.0) * taps[lag : lag + 1, :]
    gate = 1.0 / (1.0 + jnp.exp(-pre))
    return pre, gate, pre * gate


def unit_rows(value):
    inv = lax.rsqrt(jnp.sum(value * value, axis=-1, keepdims=True) + 1e-06)
    return value * inv, inv


def head_column(array, head):
    lane = lax.broadcasted_iota(jnp.int32, array.shape, 1)
    return jnp.sum(jnp.where(lane == head, array, 0.0), axis=1, keepdims=True)


def forward_kernel(
    since_ref, beta_ref, query_ref, key_ref, value_ref, halo_ref, taps_ref,
    out_add_ref, out_map_ref, new_add_ref, new_map_ref, inverse_ref, starts_ref, end_ref,
    ext,
):
    rows = since_ref.shape[0]
    blocks = rows // BLOCK
    since = since_ref[...]
    jobs = []
    for sub in range(HEADS_STEP):
        head = pl.program_id(0) * HEADS_STEP + sub
        lanes = slice(sub * BLOCK, (sub + 1) * BLOCK)
        mixed = []
        for part, ref in enumerate((query_ref, key_ref, value_ref)):
            _, _, act = conv_front(
                ext.at[sub * 3 + part], ref[:, lanes].astype(F32), halo_ref[part, :, lanes],
                taps_ref[part, :, lanes], since,
            )
            mixed.append(act)
        query = unit_rows(mixed[0])[0] * (BLOCK ** -0.5)
        key = unit_rows(mixed[1])[0]
        beta = 1.0 / (1.0 + jnp.exp(-head_column(beta_ref[...], head)))
        jobs.append((lanes, query, key, mixed[2], beta))
    lowers, scores = [], []
    for lanes, query, key, value, beta in jobs:
        for blk in range(blocks):
            span = slice(blk * BLOCK, (blk + 1) * BLOCK)
            causal, strict, _, _, _ = block_masks(since[span])
            both = mm_nt(jnp.concatenate([key[span], query[span]], axis=0), key[span])
            lowers.append(jnp.where(strict, both[:BLOCK] * beta[span], 0.0))
            scores.append(jnp.where(causal, both[BLOCK:], 0.0).astype(BF16))
    inverses = [inv.astype(BF16) for inv in unit_lower_inverses(lowers)]
    row, col = iotas(BLOCK)
    eye = (row == col).astype(F32)
    states = [jnp.concatenate([jnp.zeros((BLOCK, BLOCK), F32), eye], axis=1) for _ in jobs]
    for blk in range(blocks):
        span = slice(blk * BLOCK, (blk + 1) * BLOCK)
        _, _, keep, last_mask, keep_last = block_masks(since[span])
        for sub, (lanes, query, key, value, beta) in enumerate(jobs):
            at = sub * blocks + blk
            inverse_ref[sub, blk] = inverses[at]
            state = states[sub].astype(BF16)
            starts_ref[sub, blk] = state
            stacked = jnp.concatenate([key[span] * keep, query[span] * keep], axis=0)
            seen = mm(stacked, state)
            rest = jnp.concatenate([value[span], jnp.zeros((BLOCK, BLOCK), F32)], axis=1)
            right = (rest - seen[:BLOCK]) * beta[span]
            new = mm(inverses[at], right).astype(BF16)
            out = seen[BLOCK:] + mm(scores[at], new)
            out_add_ref[span, lanes] = out[:, :BLOCK].astype(BF16)
            out_map_ref[span, lanes] = out[:, BLOCK:].astype(BF16)
            new_add_ref[span, lanes] = new[:, :BLOCK]
            new_map_ref[span, lanes] = new[:, BLOCK:]
            keep_both = jnp.concatenate([keep_last, keep_last], axis=1)
            states[sub] = states[sub] * keep_both + mm_tn(key[span] * last_mask, new)
    for sub in range(len(jobs)):
        end_ref[sub] = states[sub]


def whole_spec(shape):
    return pl.BlockSpec(shape, lambda h: (0,) * len(shape))


def head_spec(rows):
    return pl.BlockSpec((rows, HEADS_STEP * BLOCK), lambda h: (0, h))


def per_head(*tail):
    return pl.BlockSpec((HEADS_STEP,) + tail, lambda h: (h,) + (0,) * len(tail))


def lanes_spec(first, second):
    return pl.BlockSpec((first, second, HEADS_STEP * BLOCK), lambda h: (0, 0, h))


def params():
    return pltpu.CompilerParams(vmem_limit_bytes=VMEM_LIMIT)


def mixer_forward(since, beta_logit, query, key, value, halo, taps):
    rows, width = query.shape
    heads = width // BLOCK
    blocks = rows // BLOCK
    wide = jax.ShapeDtypeStruct((rows, width), BF16)
    return pl.pallas_call(
        forward_kernel,
        grid=(heads // HEADS_STEP,),
        in_specs=[
            whole_spec(since.shape), whole_spec(beta_logit.shape),
            head_spec(rows), head_spec(rows), head_spec(rows),
            lanes_spec(3, PAD), lanes_spec(3, CONV),
        ],
        out_specs=[
            head_spec(rows), head_spec(rows), head_spec(rows), head_spec(rows),
            per_head(blocks, BLOCK, BLOCK), per_head(blocks, BLOCK, 2 * BLOCK),
            per_head(BLOCK, 2 * BLOCK),
        ],
        out_shape=[
            wide, wide, wide, wide,
            jax.ShapeDtypeStruct((heads, blocks, BLOCK, BLOCK), BF16),
            jax.ShapeDtypeStruct((heads, blocks, BLOCK, 2 * BLOCK), BF16),
            jax.ShapeDtypeStruct((heads, BLOCK, 2 * BLOCK), F32),
        ],
        scratch_shapes=[pltpu.VMEM((3 * HEADS_STEP, PAD + rows, BLOCK), F32)],
        compiler_params=params(),
        name="mixer_forward",
    )(since, beta_logit, query, key, value, halo, taps)


def join_kernel(out_add_ref, out_map_ref, entry_ref, gain_ref, mixed_ref):
    for sub in range(HEADS_STEP):
        lanes = slice(sub * BLOCK, (sub + 1) * BLOCK)
        core = out_add_ref[:, lanes].astype(F32) + mm(out_map_ref[:, lanes], entry_ref[sub])
        scale = lax.rsqrt(jnp.mean(core * core, axis=-1, keepdims=True) + 1e-05)
        mixed_ref[:, lanes] = (core * scale * gain_ref[...]).astype(BF16)


def mixer_join(out_add, out_map, entry, gain):
    rows, width = out_add.shape
    heads = width // BLOCK
    return pl.pallas_call(
        join_kernel,
        grid=(heads // HEADS_STEP,),
        in_specs=[head_spec(rows), head_spec(rows), per_head(BLOCK, BLOCK), whole_spec((1, BLOCK))],
        out_specs=head_spec(rows),
        out_shape=jax.ShapeDtypeStruct((rows, width), BF16),
        compiler_params=params(),
        name="mixer_join",
    )(out_add, out_map, entry, gain)


def core_back_kernel(out_add_ref, out_map_ref, entry_ref, gain_ref, up_ref, d_core_ref, start_ref, gain_out_ref):
    @pl.when(pl.program_id(0) == 0)
    def _():
        gain_out_ref[...] = jnp.zeros_like(gain_out_ref)

    for sub in range(HEADS_STEP):
        lanes = slice(sub * BLOCK, (sub + 1) * BLOCK)
        out_map = out_map_ref[:, lanes]
        core = out_add_ref[:, lanes].astype(F32) + mm(out_map, entry_ref[sub])
        scale = lax.rsqrt(jnp.mean(core * core, axis=-1, keepdims=True) + 1e-05)
        unit = core * scale
        up = up_ref[:, lanes].astype(F32)
        gain_out_ref[...] += jnp.sum(up * unit, axis=0, keepdims=True)
        scaled = up * gain_ref[...]
        d_core = scale * (scaled - unit * jnp.mean(scaled * unit, axis=-1, keepdims=True))
        d_core = d_core.astype(BF16)
        d_core_ref[:, lanes] = d_core
        start_ref[sub] = mm_tn(out_map, d_core)


def mixer_core_back(out_add, out_map, entry, gain, up):
    rows, width = out_add.shape
    heads = width // BLOCK
    return pl.pallas_call(
        core_back_kernel,
        grid=(heads // HEADS_STEP,),
        in_specs=[
            head_spec(rows), head_spec(rows), per_head(BLOCK, BLOCK), whole_spec((1, BLOCK)), head_spec(rows),
        ],
        out_specs=[head_spec(rows), per_head(BLOCK, BLOCK), whole_spec((1, BLOCK))],
        out_shape=[
            jax.ShapeDtypeStruct((rows, width), BF16),
            jax.ShapeDtypeStruct((heads, BLOCK, BLOCK), F32),
            jax.ShapeDtypeStruct((1, BLOCK), F32),
        ],
        compiler_params=params(),
        name="mixer_core_back",
    )(out_add, out_map, entry, gain, up)


def backward_kernel(
    since_ref, beta_ref, query_ref, key_ref, value_ref, halo_ref, taps_ref,
    new_add_ref, new_map_ref, inverse_ref, starts_ref, entry_ref, exit_ref, d_core_ref,
    d_query_ref, d_key_ref, d_value_ref, d_halo_ref, d_taps_ref, d_beta_ref,
    ext, back,
):
    rows = since_ref.shape[0]
    blocks = rows // BLOCK
    since = since_ref[...]
    jobs = []
    for sub in range(HEADS_STEP):
        head = pl.program_id(0) * HEADS_STEP + sub
        lanes = slice(sub * BLOCK, (sub + 1) * BLOCK)
        fronts = []
        for part, ref in enumerate((query_ref, key_ref, value_ref)):
            fronts.append(
                conv_front(
                    ext.at[sub * 3 + part], ref[:, lanes].astype(F32), halo_ref[part, :, lanes],
                    taps_ref[part, :, lanes], since,
                )
            )
        query_unit, query_inv = unit_rows(fronts[0][2])
        key, key_inv = unit_rows(fronts[1][2])
        query = query_unit * (BLOCK ** -0.5)
        beta = 1.0 / (1.0 + jnp.exp(-head_column(beta_ref[...], head)))
        jobs.append((head, lanes, fronts, query, query_unit, query_inv, key, key_inv, beta))

    saved = {}
    for sub, (head, lanes, fronts, query, query_unit, query_inv, key, key_inv, beta) in enumerate(jobs):
        entry = entry_ref[sub].astype(BF16)
        for blk in range(blocks):
            span = slice(blk * BLOCK, (blk + 1) * BLOCK)
            causal, _, keep, last_mask, _ = block_masks(since[span])
            start = starts_ref[sub, blk]
            state = (start[:, :BLOCK].astype(F32) + mm(start[:, BLOCK:], entry)).astype(BF16)
            new = (new_add_ref[span, lanes].astype(F32) + mm(new_map_ref[span, lanes], entry)).astype(BF16)
            scores = jnp.where(causal, mm_nt(query[span], key[span]), 0.0).astype(BF16)
            d_out = d_core_ref[span, lanes]
            d_new = mm_tn(scores, d_out)
            d_state = mm_tn(query[span] * keep, d_out)
            saved[sub, blk] = (state, new, d_out, d_new, d_state)

    carried = [exit_ref[sub].astype(F32) for sub in range(HEADS_STEP)]
    chain = {}
    for blk in reversed(range(blocks)):
        span = slice(blk * BLOCK, (blk + 1) * BLOCK)
        _, _, keep, last_mask, keep_last = block_masks(since[span])
        for sub, (head, lanes, fronts, query, query_unit, query_inv, key, key_inv, beta) in enumerate(jobs):
            state, new, d_out, d_new, d_state = saved[sub, blk]
            after = carried[sub].astype(BF16)
            d_new = d_new + mm(key[span] * last_mask, after)
            d_right = mm_tn(inverse_ref[sub, blk], d_new)
            d_rest = d_right * beta[span]
            carried[sub] = carried[sub] * keep_last + d_state - mm_tn(key[span] * keep, d_rest)
            chain[sub, blk] = (after, d_right, d_rest)

    lane = lax.broadcasted_iota(jnp.int32, (rows, beta_ref.shape[1]), 1)
    d_beta_all = jnp.zeros((rows, beta_ref.shape[1]), F32)
    for sub, (head, lanes, fronts, query, query_unit, query_inv, key, key_inv, beta) in enumerate(jobs):
        d_queries, d_keys, d_values, d_betas = [], [], [], []
        for blk in range(blocks):
            span = slice(blk * BLOCK, (blk + 1) * BLOCK)
            causal, strict, keep, last_mask, _ = block_masks(since[span])
            state, new, d_out, _, _ = saved[sub, blk]
            after, d_right, d_rest = chain[sub, blk]
            both = mm_nt(jnp.concatenate([d_out, d_right.astype(BF16)], axis=0), new)
            d_scores = jnp.where(causal, both[:BLOCK], 0.0).astype(BF16)
            d_gram = (jnp.where(strict, both[BLOCK:], 0.0) * (-beta[span])).astype(BF16)
            key_b = key[span].astype(BF16)
            from_state = mm_nt(jnp.concatenate([d_out, d_rest.astype(BF16)], axis=0), state)
            left = mm(jnp.concatenate([d_scores, d_gram], axis=0), key_b)
            d_queries.append(from_state[:BLOCK] * keep + left[:BLOCK])
            d_key = left[BLOCK:] + mm_tn(
                jnp.concatenate([d_scores, d_gram], axis=0),
                jnp.concatenate([query[span].astype(BF16), key_b], axis=0),
            )
            d_key = d_key + mm_nt(new, after) * last_mask - from_state[BLOCK:] * keep
            d_keys.append(d_key)
            d_values.append(d_rest)
            d_betas.append(
                jnp.sum(d_right * new.astype(F32), axis=1, keepdims=True) * (1.0 - beta[span])
            )
        d_query = jnp.concatenate(d_queries, axis=0) * (BLOCK ** -0.5)
        d_key = jnp.concatenate(d_keys, axis=0)
        d_query = query_inv * (
            d_query - query_unit * jnp.sum(d_query * query_unit, axis=-1, keepdims=True)
        )
        d_key = key_inv * (d_key - key * jnp.sum(d_key * key, axis=-1, keepdims=True))
        d_value = jnp.concatenate(d_values, axis=0)
        d_beta_all = d_beta_all + jnp.where(lane == head, jnp.concatenate(d_betas, axis=0), 0.0)
        outs = (d_query_ref, d_key_ref, d_value_ref)
        for part, d_act in enumerate((d_query, d_key, d_value)):
            pre, gate, _ = fronts[part]
            taps = taps_ref[part, :, lanes]
            source = ext.at[sub * 3 + part]
            d_pre = d_act * gate * (1.0 + pre * (1.0 - gate))
            room = back.at[sub * 3 + part]
            total = None
            d_taps = []
            for lag in range(CONV):
                masked = d_pre if lag == 0 else jnp.where(since >= lag, d_pre, 0.0)
                moved = source[PAD - lag : PAD - lag + rows, :]
                d_taps.append(jnp.sum(masked * moved, axis=0, keepdims=True))
                room[lag, 0:PAD, :] = jnp.zeros((PAD, BLOCK), F32)
                room[lag, PAD : PAD + rows, :] = masked * taps[lag : lag + 1, :]
                room[lag, PAD + rows : PAD + rows + PAD, :] = jnp.zeros((PAD, BLOCK), F32)
                term = room[lag, lag : lag + PAD + rows, :]
                total = term if total is None else total + term
            d_taps_ref[part, :, lanes] = jnp.concatenate(d_taps, axis=0)
            d_halo_ref[part, :, lanes] = total[:PAD].astype(d_halo_ref.dtype)
            outs[part][:, lanes] = total[PAD:].astype(BF16)

    @pl.when(pl.program_id(0) == 0)
    def _():
        d_beta_ref[...] = d_beta_all

    @pl.when(pl.program_id(0) > 0)
    def _():
        d_beta_ref[...] += d_beta_all


def mixer_backward(
    since, beta_logit, query, key, value, halo, taps, new_add, new_map, inverse, starts, entry, exit_grad, d_core
):
    rows, width = query.shape
    heads = width // BLOCK
    blocks = rows // BLOCK
    wide = jax.ShapeDtypeStruct((rows, width), BF16)
    return pl.pallas_call(
        backward_kernel,
        grid=(heads // HEADS_STEP,),
        in_specs=[
            whole_spec(since.shape), whole_spec(beta_logit.shape),
            head_spec(rows), head_spec(rows), head_spec(rows),
            lanes_spec(3, PAD), lanes_spec(3, CONV),
            head_spec(rows), head_spec(rows),
            per_head(blocks, BLOCK, BLOCK), per_head(blocks, BLOCK, 2 * BLOCK),
            per_head(BLOCK, BLOCK), per_head(BLOCK, BLOCK), head_spec(rows),
        ],
        out_specs=[
            head_spec(rows), head_spec(rows), head_spec(rows),
            lanes_spec(3, PAD), lanes_spec(3, CONV), whole_spec(beta_logit.shape),
        ],
        out_shape=[
            wide, wide, wide,
            jax.ShapeDtypeStruct((3, PAD, width), F32),
            jax.ShapeDtypeStruct((3, CONV, width), F32),
            jax.ShapeDtypeStruct(beta_logit.shape, F32),
        ],
        scratch_shapes=[
            pltpu.VMEM((3 * HEADS_STEP, PAD + rows, BLOCK), F32),
            pltpu.VMEM((3 * HEADS_STEP, CONV, PAD + rows + PAD, BLOCK), F32),
        ],
        compiler_params=params(),
        name="mixer_backward",
    )(
        since, beta_logit, query, key, value, halo, taps, new_add, new_map, inverse, starts, entry, exit_grad, d_core
    )


GROUPS = 4


def chain_kernel(axis, forward, map_ref, add_ref, out_ref, sent, landed, send_sem, recv_sem):
    count = lax.axis_size(axis)
    me = lax.axis_index(axis)
    heads = add_ref.shape[0]
    step = heads // GROUPS
    up, down = (me + 1, me - 1) if forward else (me - 1, me + 1)
    first, last = (0, count - 1) if forward else (count - 1, 0)
    barrier = pltpu.get_barrier_semaphore()

    @pl.when(me != first)
    def _():
        pl.semaphore_signal(barrier, inc=1, device_id={axis: down}, device_id_type=MESH)

    @pl.when(me != last)
    def _():
        pl.semaphore_wait(barrier, 1)

    def copy(group, target):
        return pltpu.make_async_remote_copy(
            src_ref=sent.at[group],
            dst_ref=landed.at[group],
            send_sem=send_sem.at[group],
            recv_sem=recv_sem.at[group],
            device_id={axis: target},
            device_id_type=MESH,
        )

    for group in range(GROUPS):
        @pl.when(me != first)
        def _():
            copy(group, up).wait_recv()
            for sub in range(step):
                head = group * step + sub
                out_ref[head] = landed[group, sub].astype(F32)

        @pl.when(me == first)
        def _():
            out_ref[group * step : (group + 1) * step] = jnp.zeros((step,) + out_ref.shape[1:], F32)

        @pl.when(me != last)
        def _():
            for sub in range(step):
                head = group * step + sub
                if forward:
                    moved = mm(map_ref[head], out_ref[head])
                else:
                    moved = mm_tn(map_ref[head], out_ref[head])
                sent[group, sub] = (moved + add_ref[head]).astype(BF16)
            copy(group, up).start()

    @pl.when(me != last)
    def _():
        for group in range(GROUPS):
            copy(group, up).wait_send()


def carry_chain(map_part, add_part, axis, forward):
    heads = add_part.shape[0]
    part = (GROUPS, heads // GROUPS, BLOCK, BLOCK)
    return pl.pallas_call(
        functools.partial(chain_kernel, axis, forward),
        in_specs=[pl.BlockSpec(memory_space=pltpu.VMEM)] * 2,
        out_specs=pl.BlockSpec(memory_space=pltpu.VMEM),
        out_shape=jax.ShapeDtypeStruct(add_part.shape, F32),
        scratch_shapes=[
            pltpu.VMEM(part, BF16),
            pltpu.VMEM(part, BF16),
            pltpu.SemaphoreType.DMA((GROUPS,)),
            pltpu.SemaphoreType.DMA((GROUPS,)),
        ],
        compiler_params=pltpu.CompilerParams(
            collective_id=1 if forward else 2, has_side_effects=True, vmem_limit_bytes=VMEM_LIMIT // 2
        ),
        name="carry_forward" if forward else "carry_backward",
    )(map_part, add_part)


def shifted(value, axis, steps):
    count = lax.axis_size(axis)
    first, last = (max(0, -steps), min(count, count - steps))
    return lax.ppermute(value, axis, [(source, source + steps) for source in range(first, last)])


def matmul(left, right):
    return jnp.dot(left, right, preferred_element_type=F32)


def dot_tn(left, right):
    return jnp.einsum("rd,re->de", left, right, preferred_element_type=F32)


def dot_nt(left, right):
    return jnp.einsum("re,de->rd", left, right, preferred_element_type=F32)


def rms_scale(value_in, gain_vec, epsilon):
    return value_in * lax.rsqrt(jnp.mean(value_in * value_in, axis=-1, keepdims=True) + epsilon) * gain_vec


def norm_back(value_in, gain_vec, upstream, epsilon):
    inv_scale = lax.rsqrt(jnp.mean(value_in * value_in, axis=-1, keepdims=True) + epsilon)
    scaled_up = upstream * gain_vec
    gain_term = jnp.sum(upstream * value_in * inv_scale, axis=0)
    cubed = inv_scale * inv_scale * inv_scale
    back_value = inv_scale * scaled_up - value_in * cubed * jnp.mean(
        scaled_up * value_in, axis=-1, keepdims=True
    )
    return (back_value, gain_term)


def since_start(doc_lengths, offset, rows):
    ends = jnp.cumsum(doc_lengths[0])
    position = offset + jnp.arange(rows, dtype=jnp.int32)
    starts = jnp.max(jnp.where(position[:, None] >= ends[None, :], ends[None, :], 0), axis=1)
    return jnp.broadcast_to((position - starts)[:, None], (rows, BLOCK)).astype(jnp.int32)


def scatter_all(value, dim):
    part = lax.psum_scatter(value, "dp", scatter_dimension=dim, tiled=True)
    return lax.psum_scatter(part, "narrow", scatter_dimension=dim, tiled=True)


def local(
    tokens,
    doc_lengths,
    attn_gain,
    w_query,
    w_key,
    w_value,
    w_beta,
    conv_weight,
    out_gain,
    w_out,
    mlp_gain,
    w_gate,
    w_up,
    w_down,
    grad_out,
):
    tok_rows, model_width = tokens.shape
    edge = CONV - 1
    offset = lax.axis_index("narrow") * tok_rows
    cot_rows = lax.all_gather(grad_out, "narrow", axis=0, tiled=True)
    since = since_start(doc_lengths, offset, tok_rows)
    inputs = tokens.astype(F32)
    normed = rms_scale(inputs, attn_gain, 1e-06).astype(BF16)
    query, key, value = (matmul(normed, w) for w in (w_query, w_key, w_value))
    beta_logit = matmul(normed, w_beta)
    halo = shifted(
        jnp.stack([part[tok_rows - PAD :].astype(BF16) for part in (query, key, value)]), "narrow", 1
    )
    out_add, out_map, new_add, new_map, inverse, starts, end = mixer_forward(
        since, beta_logit, query, key, value, halo, conv_weight
    )
    transfer = end[:, :, BLOCK:].astype(BF16)
    entry = carry_chain(transfer, end[:, :, :BLOCK], "narrow", True)
    gain_row = out_gain[None, :]
    attn_mixed = mixer_join(out_add, out_map, entry, gain_row)
    hidden = inputs + matmul(attn_mixed, w_out)
    normed_mlp = rms_scale(hidden, mlp_gain, 1e-06).astype(BF16)
    gathered = lax.all_gather(normed_mlp, "narrow", axis=0, tiled=True)
    gate_proj = matmul(gathered, w_gate)
    up_proj = matmul(gathered, w_up)
    gate_sigmoid = jax.nn.sigmoid(gate_proj)
    silu_gate = gate_proj * gate_sigmoid
    activation = (silu_gate * up_proj).astype(BF16)
    d_act = jnp.einsum("rd,fd->rf", cot_rows, w_down, preferred_element_type=F32)
    d_gate = (d_act * up_proj * gate_sigmoid * (1.0 + gate_proj * (1.0 - gate_sigmoid))).astype(BF16)
    d_up = (d_act * silu_gate).astype(BF16)
    from_gate = jnp.einsum("rf,df->rd", d_gate, w_gate, preferred_element_type=F32)
    d_normed_mlp = lax.psum_scatter(
        (from_gate + jnp.einsum("rf,df->rd", d_up, w_up, preferred_element_type=F32)).astype(BF16),
        "narrow",
        scatter_dimension=0,
        tiled=True,
    ).astype(F32)
    ffn_sum = lax.psum_scatter(
        matmul(activation, w_down).astype(BF16), "narrow", scatter_dimension=0, tiled=True
    ).astype(F32)
    block_out = (hidden + ffn_sum).astype(BF16)
    down_term_grad = dot_tn(activation, cot_rows)
    gate_term_grad = dot_tn(gathered, d_gate)
    up_term_grad = dot_tn(gathered, d_up)
    grad_gate, grad_up, grad_down = (
        lax.psum_scatter(gate_term_grad.astype(BF16), "dp", scatter_dimension=0, tiled=True).astype(F32),
        lax.psum_scatter(up_term_grad.astype(BF16), "dp", scatter_dimension=0, tiled=True).astype(F32),
        lax.psum_scatter(down_term_grad.astype(BF16), "dp", scatter_dimension=1, tiled=True).astype(F32),
    )
    d_hidden_norm, mlp_gain_term = norm_back(hidden, mlp_gain, d_normed_mlp, 1e-06)
    d_hidden = grad_out.astype(F32) + d_hidden_norm
    d_branch = d_hidden.astype(BF16)
    w_out_term = dot_tn(attn_mixed, d_branch)
    d_mixed = dot_nt(d_branch, w_out)
    d_core, start_grad, out_gain_term = mixer_core_back(out_add, out_map, entry, gain_row, d_mixed)
    exit_grad = carry_chain(transfer, start_grad, "narrow", False)
    d_query, d_key, d_value, d_halo, conv_term, d_beta = mixer_backward(
        since, beta_logit, query, key, value, halo, conv_weight,
        new_add, new_map, inverse, starts, entry, exit_grad, d_core,
    )
    after = shifted(d_halo.astype(BF16), "narrow", -1)
    d_query, d_key, d_value = (
        part.at[tok_rows - PAD :].add(after[place])
        for place, part in enumerate((d_query, d_key, d_value))
    )
    d_beta_low = d_beta.astype(BF16)
    query_term = dot_tn(normed, d_query)
    key_term = dot_tn(normed, d_key)
    value_term = dot_tn(normed, d_value)
    beta_term = jnp.einsum("rd,rh->dh", normed, d_beta_low, preferred_element_type=F32)
    d_normed = dot_nt(d_query, w_query) + dot_nt(d_key, w_key) + dot_nt(d_value, w_value)
    d_normed = d_normed + jnp.einsum("rh,dh->rd", d_beta_low, w_beta, preferred_element_type=F32)
    d_input_norm, attn_gain_term = norm_back(inputs, attn_gain, d_normed, 1e-06)
    grad_tokens = (d_hidden + d_input_norm).astype(BF16)
    both = ("dp", "narrow")
    grad_query, grad_key, grad_value = (
        scatter_all(term.astype(BF16), 0).astype(F32) for term in (query_term, key_term, value_term)
    )
    grad_w_out = scatter_all(w_out_term.astype(BF16), 1).astype(F32)
    grad_beta, grad_conv, grad_attn_gain, grad_out_gain, grad_mlp_gain = (
        lax.psum_scatter(beta_term, both, scatter_dimension=0, tiled=True),
        lax.psum_scatter(conv_term, both, scatter_dimension=2, tiled=True),
        lax.psum_scatter(attn_gain_term, both, scatter_dimension=0, tiled=True),
        lax.psum_scatter(out_gain_term[0], both, scatter_dimension=0, tiled=True),
        lax.psum_scatter(mlp_gain_term, both, scatter_dimension=0, tiled=True),
    )
    return (
        block_out,
        grad_tokens,
        grad_attn_gain,
        grad_query,
        grad_key,
        grad_value,
        grad_beta,
        grad_conv,
        grad_out_gain,
        grad_w_out,
        grad_mlp_gain,
        grad_gate,
        grad_up,
        grad_down,
    )


def solution(mesh):
    placed = (
        P(("dp", "narrow"), None),
        P("dp", None),
        P(),
        P(),
        P(),
        P(),
        P(),
        P(),
        P(),
        P(),
        P(),
        P(None, "narrow"),
        P(None, "narrow"),
        P("narrow", None),
        P(("dp", "narrow"), None),
    )
    return jax.shard_map(
        local,
        mesh=mesh,
        in_specs=placed,
        out_specs=(
            P(("dp", "narrow"), None),
            P(("dp", "narrow"), None),
            P(("dp", "narrow")),
            P(("dp", "narrow"), None),
            P(("dp", "narrow"), None),
            P(("dp", "narrow"), None),
            P(("dp", "narrow"), None),
            P(None, None, ("dp", "narrow")),
            P(("dp", "narrow")),
            P(None, ("dp", "narrow")),
            P(("dp", "narrow")),
            P("dp", "narrow"),
            P("dp", "narrow"),
            P("narrow", "dp"),
        ),
        check_vma=False,
    )
```

time: 3940 us -> 1730 us (0.44)
  matrix products: 1320 us -> 284 us
  waiting for transfers between devices: 2070 us -> 1150 us
  local copies, waits for them, and re-layouts: 234 us -> 31.1 us
  other arithmetic: 216 us -> 35.6 us
  Pallas kernels: 0 us -> 162 us
    reduce_scatter x8 -> x11, waiting for transfers between devices: 1600 us -> 510 us  [the longest x1 143 us: local(): lax.psum_scatter(matmul(activation, w_down).astype(BF16), 'narrow', scatt...]
    dot_general x225 -> x23, matrix products: 1320 us -> 282 us  [the longest x7 89.3 us: dot_tn(): return jnp.einsum('rd,re->de', left, right, preferred_element_type=F32)]
    pallas_call x0 -> x6, Pallas kernels: none -> 162 us  [the longest x1 55.5 us: mixer_backward(): pl.pallas_call(backward_kernel, grid=(heads // HEADS_STEP,), in_specs=[wh...]
    unnamed x19 -> x20, waiting for transfers between devices: 87.7 us -> 238 us
    reduce_sum x10 -> x0, other arithmetic: 50.4 us -> none  [the longest x1 29.2 us: mixer_blocks(): jnp.where(same_doc, shifted, 0.0) * conv_weight[:, lag_steps, :]]
  transfers between devices with their start and end apart: 19 -> 19, of which waited for: 9 -> 17; matrix products, arithmetic and copies ran while one was open for 28% -> 13% of each run, Pallas kernels for 0% -> 5%
where the time goes in v1:
time: 1730 us
  waiting for transfers between devices  1150 us (66%)
  matrix products  284 us (16%)
  Pallas kernels  162 us (9%)
  blocking collectives  40.1 us (2%)
  other arithmetic  35.6 us (2%)
  local copies, waits for them, and re-layouts  31.1 us (2%)
    unnamed x20, waiting for transfers between devices  238 us
    all_gather x1, waiting for transfers between devices, local(): gathered = lax.all_gather(normed_mlp, 'narrow', axis=0, tiled=True)  160 us
    reduce_scatter x1, waiting for transfers between devices, local(): lax.psum_scatter(matmul(activation, w_down).astype(BF16), 'narrow', scatt...  143 us
    reduce_scatter x4, waiting for transfers between devices, scatter_all(): part = lax.psum_scatter(value, 'dp', scatter_dimension=dim, tiled=True)  126 us
    reduce_scatter x1, waiting for transfers between devices, local(): lax.psum_scatter((from_gate + jnp.einsum('rf,df->rd', d_up, w_up, preferr...  124 us
    all_gather x1, waiting for transfers between devices, local(): cot_rows = lax.all_gather(grad_out, 'narrow', axis=0, tiled=True)  114 us
    dot_general x7, matrix products, dot_tn(): return jnp.einsum('rd,re->de', left, right, preferred_element_type=F32)  89.3 us
    dot_general x8, matrix products, matmul(): return jnp.dot(left, right, preferred_element_type=F32)  81.2 us
  transfers between devices with their start and end apart: 19, of which 17 were waited for; matrix products, arithmetic and copies ran while one was open for 13% of the time, Pallas kernels for 5%

profile of v1, /device:TPU:0, one launch (start us, length us, event | category | flops | bytes accessed | tf_op | source)
XLA Modules:
  0.0 1727.3 jit_solution(10286657911882565180)
XLA Ops:
  7.3 2.2 fusion.8
  10.1 8.6 fusion.45.query_ref
  18.8 4.6 fusion.43.key_ref
  23.4 4.6 fusion.41.value_ref
  28.1 2.0 copy-done.11
  30.2 5.2 collective-permute-start
  38.2 49.7 %mixer_forward.1 = (bf16[512,2048]{1,0:T(8,128)(2,1)}, bf16[512,2048]{1,0:T(8,128)(2,1)}, bf16[512,2048]{1,0:T(8,128)(2,1)}, bf16[512,2048]{1,0:T(8,128)(2,1)}, ...) custom-call(s32[512,128]{1,0:T(8,128)} %broadcast_in_dim.15.since_ref, ...), custom_call_target="tpu_custom_call" | custom-call | tf_op jit(solution)/shard_map/mixer_forward/pallas_call | solution.py:180
  89.2 1.5 slice.89.add_ref
  90.7 12.7 carry_forward.1.entry_ref
  104.4 7.6 mixer_join.1
  112.0 7.8 multiply_reduce_fusion
  121.8 1.7 multiply_convert_fusion.3
  124.8 159.8 %all-gather.3.cloned.1.call-done = bf16[2048,2048]{1,0:T(8,128)(2,1)} async-done(((bf16[512,2048]{1,0:T(8,128)(2,1)}), bf16[2048,2048]{1,0:T(8,128)(2,1)}) %all-gather.3.cloned.1.call-update) | async-done | bytes 8388624 | tf_op jit(solution)/shard_map/all_gather | solution.py:590
  284.7 18.7 %fusion.50 = f32[2048,1408]{1,0:T(8,128)} fusion(bf16[2048,2048]{1,0:T(8,128)(2,1)} %all-gather.3.cloned.1.call-done, bf16[2048,1408]{1,0:T(8,128)(2,1)} %param.33), kind=kOutput, calls=%fused_computation.81 | convolution fusion | flops 11811160064 | bytes 25690112 | tf_op jit(solution)/shard_map/dot_general | solution.py:514
  303.4 17.0 fusion.49
  320.4 113.8 %all-gather.5.cloned.1.call-done = bf16[2048,2048]{1,0:T(8,128)(2,1)} async-done(((bf16[512,2048]{1,0:T(8,128)(2,1)}), bf16[2048,2048]{1,0:T(8,128)(2,1)}) %all-gather.5.cloned.1.call-update) | async-done | bytes 8388624 | tf_op jit(solution)/shard_map/all_gather | solution.py:572
  434.1 25.9 %multiply_convert_fusion = (bf16[2048,1408]{1,0:T(8,128)(2,1)}, bf16[2048,1408]{1,0:T(8,128)(2,1)}, bf16[2048,1408]{1,0:T(8,128)(2,1)}) fusion(f32[2048,1408]{1,0:T(8,128)} %fusion.49, f32[2048,1408]{1,0:T(8,128)} %fusion.50, bf16[2048,2048]{1,0:T(8,128)(2,1)} %all-gather.5.cloned.1.call-done, bf16[1408,2048]{1,0:T(8,128)(2,1)} %param.34), kind=kOutput, calls=%fused_computation.1 | convolution fusion | flops 11854413824 | bytes 54525952 | tf_op jit(solution)/shard_map/rd,fd->rf/dot_general | solution.py:596
  460.0 19.5 %fusion.51 = f32[2048,2048]{1,0:T(8,128)} fusion(bf16[2048,1408]{1,0:T(8,128)(2,1)} %get-tuple-element.132, bf16[2048,1408]{1,0:T(8,128)(2,1)} %param.32), kind=kOutput, calls=%fused_computation.82 | convolution fusion | flops 11811160064 | bytes 28311552 | tf_op jit(solution)/shard_map/rf,df->rd/dot_general | solution.py:599
  479.5 21.4 %add_convert_fusion = bf16[2048,2048]{1,0:T(8,128)(2,1)} fusion(f32[2048,2048]{1,0:T(8,128)} %fusion.51, bf16[2048,1408]{1,0:T(8,128)(2,1)} %get-tuple-element.131, bf16[2048,1408]{1,0:T(8,128)(2,1)} %param.33), kind=kOutput, calls=%fused_computation | convolution fusion | flops 11819548672 | bytes 36700160 | tf_op jit(solution)/shard_map/rf,df->rd/dot_general | solution.py:601
  501.0 18.5 %convolution_convert_fusion.4 = bf16[2048,2048]{1,0:T(8,128)(2,1)} fusion(bf16[2048,1408]{1,0:T(8,128)(2,1)} %get-tuple-element.133, bf16[1408,2048]{1,0:T(8,128)(2,1)} %param.34), kind=kOutput, calls=%fused_computation.16 | convolution fusion | flops 11815354368 | bytes 19922944 | tf_op jit(solution)/shard_map/dot_general | solution.py:514
  519.8 124.0 %reduce-scatter.24.cloned.1.call-done = bf16[512,2048]{1,0:T(8,128)(2,1)} async-done(((bf16[2048,2048]{1,0:T(8,128)(2,1)}), bf16[512,2048]{1,0:T(8,128)(2,1)}) %reduce-scatter.24.cloned.1.call-update) | async-done | bytes 2097168 | tf_op jit(solution)/shard_map/reduce_scatter | solution.py:600
  643.8 4.2 fusion.7
  648.0 143.3 %reduce-scatter.22.cloned.1.call-done = bf16[512,2048]{1,0:T(8,128)(2,1)} async-done(((bf16[2048,2048]{1,0:T(8,128)(2,1)}), bf16[512,2048]{1,0:T(8,128)(2,1)}) %reduce-scatter.22.cloned.1.call-update) | async-done | bytes 2097168 | tf_op jit(solution)/shard_map/reduce_scatter | solution.py:606
  791.3 5.3 fusion.4
  796.6 2.0 copy-done.12
  798.6 6.9 convolution_convert_fusion
  805.6 11.6 fusion.19.up_ref
  817.1 10.4 mixer_core_back.1
  828.7 26.5 %carry_backward.1.exit_ref = f32[16,128,128]{2,1,0:T(8,128)S(1)} custom-call(bf16[16,128,128]{2,1,0:T(8,128)(2,1)S(1)} %copy-done.3, f32[16,128,128]{2,1,0:T(8,128)S(1)} %copy-done.5), custom_call_target="tpu_custom_call" | custom-call | tf_op jit(solution)/shard_map/carry_backward/pallas_call | solution.py:489
  856.2 55.5 %mixer_backward.1 = (bf16[512,2048]{1,0:T(8,128)(2,1)}, bf16[512,2048]{1,0:T(8,128)(2,1)}, bf16[512,2048]{1,0:T(8,128)(2,1)}, f32[3,8,2048]{2,1,0:T(8,128)}, f32[3,4,2048]{2,1,0:T(4,128)}, /*index=5*/f32[512,16]{1,0:T(8,128)}) custom-call(s32[512,128]{1,0:T(8,128)} %broadcast_in_dim.15.since_ref, f32[512,16]{1,0:T(8,128)} %fusion.47.beta_ref, ...), custom_call_target="tpu_custom_call" | custom-call | tf_op jit(solution)/shard_map/mixer_backward/pallas_call | solution.py:395
  913.9 5.2 collective-permute-done.1
  920.6 8.5 convolution_convert_fusion.3
  929.4 18.4 %convolution_convert_fusion.5 = bf16[1408,2048]{1,0:T(8,128)(2,1)} fusion(bf16[2048,1408]{1,0:T(8,128)(2,1)} %get-tuple-element.133, bf16[2048,2048]{1,0:T(8,128)(2,1)} %all-gather.5.cloned.1.call-done), kind=kOutput, calls=%fused_computation.17 | convolution fusion | flops 11814043648 | bytes 19922944 | tf_op jit(solution)/shard_map/rd,re->de/dot_general | solution.py:518
  947.8 19.0 %convolution_convert_fusion.6 = bf16[2048,1408]{1,0:T(8,128)(2,1)} fusion(bf16[2048,2048]{1,0:T(8,128)(2,1)} %all-gather.3.cloned.1.call-done, bf16[2048,1408]{1,0:T(8,128)(2,1)} %get-tuple-element.131), kind=kOutput, calls=%fused_computation.18 | convolution fusion | flops 11814043648 | bytes 19922944 | tf_op jit(solution)/shard_map/rd,re->de/dot_general | solution.py:518
  967.2 19.2 %convolution_convert_fusion.7 = bf16[2048,1408]{1,0:T(8,128)(2,1)} fusion(bf16[2048,2048]{1,0:T(8,128)(2,1)} %all-gather.3.cloned.1.call-done, bf16[2048,1408]{1,0:T(8,128)(2,1)} %get-tuple-element.132), kind=kOutput, calls=%fused_computation.19 | convolution fusion | flops 11814043648 | bytes 19922944 | tf_op jit(solution)/shard_map/rd,re->de/dot_general | solution.py:518
  986.5 8.6 convolution_convert_fusion.1
  995.1 8.7 convolution_convert_fusion.2
  1004.7 3.1 copy.41
  1007.8 5.6 reshape.184
  1013.9 2.0 fusion.21
  1015.9 2.3 copy.43
  1018.9 42.3 %reduce-scatter.44.cloned.1.call-done = bf16[1408,256]{1,0:T(8,128)(2,1)} async-done(((bf16[1408,2048]{1,0:T(8,128)(2,1)}), bf16[1408,256]{1,0:T(8,128)(2,1)}) %reduce-scatter.44.cloned.1.call-update) | async-done | bytes 720912 | tf_op jit(solution)/shard_map/reduce_scatter | solution.py:616
  1061.2 2.3 convert_element_type.123
  1063.5 60.6 %reduce-scatter.42.cloned.1.call-done = bf16[256,1408]{1,0:T(8,128)(2,1)} async-done(((bf16[2048,1408]{1,0:T(8,128)(2,1)}), bf16[256,1408]{1,0:T(8,128)(2,1)}) %reduce-scatter.42.cloned.1.call-update) | async-done | bytes 720912 | tf_op jit(solution)/shard_map/reduce_scatter | solution.py:615
  1124.1 2.3 convert_element_type.121
  1126.4 60.2 %reduce-scatter.40.cloned.1.call-done = bf16[256,1408]{1,0:T(8,128)(2,1)} async-done(((bf16[2048,1408]{1,0:T(8,128)(2,1)}), bf16[256,1408]{1,0:T(8,128)(2,1)}) %reduce-scatter.40.cloned.1.call-update) | async-done | bytes 720912 | tf_op jit(solution)/shard_map/reduce_scatter | solution.py:614
  1186.7 2.3 convert_element_type.119
  1189.0 72.7 %reduce-scatter.34.cloned.1.call-done = bf16[256,2048]{1,0:T(8,128)(2,1)} async-done(((bf16[2048,2048]{1,0:T(8,128)(2,1)}), bf16[256,2048]{1,0:T(8,128)(2,1)}) %reduce-scatter.34.cloned.1.call-update) | async-done | bytes 1048592 | tf_op jit(solution)/shard_map/reduce_scatter | solution.py:548
  1261.8 10.6 fusion.53
  1272.4 11.2 fusion.54
  1283.6 52.9 %reduce-scatter.30.cloned.1.call-done = bf16[256,2048]{1,0:T(8,128)(2,1)} async-done(((bf16[2048,2048]{1,0:T(8,128)(2,1)}), bf16[256,2048]{1,0:T(8,128)(2,1)}) %reduce-scatter.30.cloned.1.call-update) | async-done | bytes 1048592 | tf_op jit(solution)/shard_map/reduce_scatter | solution.py:548
  1336.5 7.8 fusion.52
  1344.3 3.4 fusion.17
  1347.8 40.1 %all-reduce.3 = (f32[2048]{0:T(1024)S(1)}, f32[128]{0:T(128)S(1)}, f32[2048]{0:T(1024)S(1)}) all-reduce(f32[2048]{0:T(1024)S(1)} %get-tuple-element.126, f32[128]{0:T(128)S(1)} %bitcast.75, f32[2048]{0:T(1024)S(1)} %get-tuple-element.124), channel_id=4, replica_groups=mesh['dp'=8,'narrow'=4] {'dp','narrow'}, use_global_device_ids=true, to_apply=%region_9.10.clone | all-reduce | flops 4224 | bytes 33792
  1389.6 5.9 fusion.14
  1395.5 78.5 %reduce-scatter.48.cloned.1.call-done = f32[64,12]{1,0:T(8,128)} async-done(((f32[2048,12]{1,0:T(8,128)}), f32[64,12]{1,0:T(8,128)}) %reduce-scatter.48.cloned.1.call-update) | async-done | bytes 3088
  1475.6 132.9 %reduce-scatter.46.cloned.1.call-done = f32[64,16]{1,0:T(8,128)} async-done(((f32[2048,16]{1,0:T(8,128)}), f32[64,16]{1,0:T(8,128)}) %reduce-scatter.46.cloned.1.call-update) | async-done | bytes 4112
  1609.9 24.9 %reduce-scatter.50.cloned.1.call-done = bf16[64,2048]{1,0:T(8,128)(2,1)} async-done(((bf16[256,2048]{1,0:T(8,128)(2,1)}), bf16[64,2048]{1,0:T(8,128)(2,1)}) %reduce-scatter.50.cloned.1.call-update) | async-done | bytes 262160
  1637.0 25.8 %reduce-scatter.28.cloned.1.call-done = bf16[64,2048]{1,0:T(8,128)(2,1)} async-done(((bf16[256,2048]{1,0:T(8,128)(2,1)}), bf16[64,2048]{1,0:T(8,128)(2,1)}) %reduce-scatter.28.cloned.1.call-update) | async-done | bytes 262160 | tf_op jit(solution)/shard_map/reduce_scatter | solution.py:549
  1662.8 1.8 convert_element_type.111
  1664.5 26.3 %reduce-scatter.36.cloned.1.call-done = bf16[64,2048]{1,0:T(8,128)(2,1)} async-done(((bf16[256,2048]{1,0:T(8,128)(2,1)}), bf16[64,2048]{1,0:T(8,128)(2,1)}) %reduce-scatter.36.cloned.1.call-update) | async-done | bytes 262160 | tf_op jit(solution)/shard_map/reduce_scatter | solution.py:549
  1690.9 1.8 convert_element_type.115
  1692.6 26.2 %reduce-scatter.32.cloned.1.call-done = bf16[64,2048]{1,0:T(8,128)(2,1)} async-done(((bf16[256,2048]{1,0:T(8,128)(2,1)}), bf16[64,2048]{1,0:T(8,128)(2,1)}) %reduce-scatter.32.cloned.1.call-update) | async-done | bytes 262160 | tf_op jit(solution)/shard_map/reduce_scatter | solution.py:549
  1718.8 1.8 convert_element_type.113
  (138 shorter events, 25.1 us)
Async XLA Ops:
  7.2 28.3 %copy-start = (bf16[2048,16]{0,1:T(8,128)(2,1)S(1)}, bf16[2048,16]{0,1:T(8,128)(2,1)}, u32[]{:S(2)}) copy-start(bf16[2048,16]{0,1:T(8,128)(2,1)} %param.27) | copy-start | bytes 196612
  7.2 277.5 %all-gather.3.cloned.1.call-start = ((), (), s32[]{:S(2)}) async-start(), calls=%async_computation.15 | async-start | bytes 10485760 | tf_op jit(solution)/shard_map/all_gather | solution.py:590
  7.2 11.5 slice-start
  10.1 25.4 %copy-start.26 = (f32[512]{0:T(512)}, f32[512]{0:T(512)S(1)}, u32[]{:S(2)}) copy-start(f32[512]{0:T(512)S(1)} %get-tuple-element.140) | copy-start | bytes 6148
  10.1 8.6 copy-start.7
  10.1 8.6 copy-start.24
  10.1 8.7 slice-start.1
  10.1 13.3 slice-start.2
  18.7 9.4 copy-start.9
  18.8 4.7 slice-start.3
  23.4 4.7 copy-start.10
  28.1 2.1 copy-start.11
  28.1 8.9 copy-start.33
  30.2 7.1 collective-permute-start
  37.3 0.8 copy-start.17
  89.1 14.3 copy-start.2
  103.4 1.0 copy-start.1
  112.0 9.8 copy-start.20
  119.8 2.0 copy-start.6
  120.4 3.1 copy-start.22
  123.5 310.6 %all-gather.5.cloned.1.call-start = ((), (), s32[]{:S(2)}) async-start(), calls=%async_computation.17 | async-start | bytes 10485760 | tf_op jit(solution)/shard_map/all_gather | solution.py:572
  124.3 519.5 %reduce-scatter.24.cloned.1.call-start = ((), (), s32[]{:S(2)}) async-start(), calls=%async_computation.18 | async-start | bytes 10485760 | tf_op jit(solution)/shard_map/reduce_scatter | solution.py:600
  284.7 18.7 %copy-start.32 = (bf16[2048,2048]{1,0:T(8,128)(2,1)S(1)}, bf16[2048,2048]{1,0:T(8,128)(2,1)}, u32[]{:S(2)}) copy-start(bf16[2048,2048]{1,0:T(8,128)(2,1)} %all-gather.3.cloned.1.call-done) | copy-start | bytes 25165828
  501.0 290.3 %reduce-scatter.22.cloned.1.call-start = ((), (), s32[]{:S(2)}) async-start(), calls=%async_computation.16 | async-start | bytes 10485760 | tf_op jit(solution)/shard_map/reduce_scatter | solution.py:606
  519.5 124.3 %copy-start.21 = (f32[2048]{0:T(1024)S(1)}, f32[2048]{0:T(1024)}, u32[]{:S(2)}) copy-start(f32[2048]{0:T(1024)} %param.31) | copy-start | bytes 24580
  519.5 124.3 %copy-start.23 = (f32[512]{0:T(512)S(1)}, f32[512]{0:T(512)}, u32[]{:S(2)}) copy-start(f32[512]{0:T(512)} %copy-done.22) | copy-start | bytes 6148
  519.5 271.8 %copy-start.13 = (bf16[512,2048]{1,0:T(8,128)(2,1)S(1)}, bf16[512,2048]{1,0:T(8,128)(2,1)}, u32[]{:S(2)}) copy-start(bf16[512,2048]{1,0:T(8,128)(2,1)} %param.35) | copy-start | bytes 6291460
  519.5 271.8 %copy-start.28 = (f32[512]{0:T(512)S(1)}, f32[512]{0:T(512)}, u32[]{:S(2)}) copy-start(f32[512]{0:T(512)} %get-tuple-element.141) | copy-start | bytes 6148
  519.5 496.4 %reduce-scatter.38.cloned.1.call-start = ((), (), s32[]{:S(2)}) async-start(), calls=%async_computation.25 | async-start | bytes 9437184 | tf_op jit(solution)/shard_map/reduce_scatter | solution.py:548
  791.3 7.3 copy-start.16
  796.6 2.0 copy-start.12
  805.5 212.8 %reduce-scatter.26.cloned.1.call-start = ((), (), s32[]{:S(2)}) async-start(), calls=%async_computation.19 | async-start | bytes 9437184 | tf_op jit(solution)/shard_map/reduce_scatter | solution.py:548
  817.1 10.4 copy-start.3
  827.5 1.2 copy-start.5
  855.2 1.0 copy-start.4
  856.2 64.4 %copy-start.8 = (bf16[512,2048]{1,0:T(8,128)(2,1)S(1)}, bf16[512,2048]{1,0:T(8,128)(2,1)}, u32[]{:S(2)}) copy-start(bf16[512,2048]{1,0:T(8,128)(2,1)} %param.21) | copy-start | bytes 6291460
  856.2 64.4 %copy-start.25 = (f32[2048]{0:T(1024)S(1)}, f32[2048]{0:T(1024)}, u32[]{:S(2)}) copy-start(f32[2048]{0:T(1024)} %param.23) | copy-start | bytes 24580
  856.2 64.4 %copy-start.27 = (f32[512]{0:T(512)S(1)}, f32[512]{0:T(512)}, u32[]{:S(2)}) copy-start(f32[512]{0:T(512)} %copy-done.26) | copy-start | bytes 6148
  912.6 6.5 collective-permute-start.1
  929.1 132.1 %reduce-scatter.44.cloned.1.call-start = ((), (), s32[]{:S(2)}) async-start(), calls=%async_computation.28 | async-start | bytes 6488064 | tf_op jit(solution)/shard_map/reduce_scatter | solution.py:616
  947.8 176.3 %reduce-scatter.42.cloned.1.call-start = ((), (), s32[]{:S(2)}) async-start(), calls=%async_computation.27 | async-start | bytes 6488064 | tf_op jit(solution)/shard_map/reduce_scatter | solution.py:615
  966.9 219.8 %reduce-scatter.40.cloned.1.call-start = ((), (), s32[]{:S(2)}) async-start(), calls=%async_computation.26 | async-start | bytes 6488064 | tf_op jit(solution)/shard_map/reduce_scatter | solution.py:614
  986.4 275.3 %reduce-scatter.34.cloned.1.call-start = ((), (), s32[]{:S(2)}) async-start(), calls=%async_computation.23 | async-start | bytes 9437184 | tf_op jit(solution)/shard_map/reduce_scatter | solution.py:548
  995.1 341.4 %reduce-scatter.30.cloned.1.call-start = ((), (), s32[]{:S(2)}) async-start(), calls=%async_computation.21 | async-start | bytes 9437184 | tf_op jit(solution)/shard_map/reduce_scatter | solution.py:548
  1003.8 0.9 copy-start.19
  1003.8 470.2 %reduce-scatter.48.cloned.1.call-start = ((), (), s32[]{:S(2)}) async-start(), calls=%async_computation.30 | async-start | bytes 1081344
  1007.8 6.0 copy-start.18
  1013.4 595.1 %reduce-scatter.46.cloned.1.call-start = ((), (), s32[]{:S(2)}) async-start(), calls=%async_computation.29 | async-start | bytes 1081344
  1015.8 619.0 %reduce-scatter.50.cloned.1.call-start = ((), (), s32[]{:S(2)}) async-start(), calls=%async_computation.31 | async-start | bytes 1310720
  1018.2 644.5 %reduce-scatter.28.cloned.1.call-start = ((), (), s32[]{:S(2)}) async-start(), calls=%async_computation.20 | async-start | bytes 1310720 | tf_op jit(solution)/shard_map/reduce_scatter | solution.py:549
  1018.8 672.0 %reduce-scatter.36.cloned.1.call-start = ((), (), s32[]{:S(2)}) async-start(), calls=%async_computation.24 | async-start | bytes 1310720 | tf_op jit(solution)/shard_map/reduce_scatter | solution.py:549
  1261.7 457.1 %reduce-scatter.32.cloned.1.call-start = ((), (), s32[]{:S(2)}) async-start(), calls=%async_computation.22 | async-start | bytes 1310720 | tf_op jit(solution)/shard_map/reduce_scatter | solution.py:549
  1261.8 10.7 copy-start.30
  1336.5 7.8 copy-start.14
  1336.5 7.8 copy-start.15
  1344.3 3.5 copy-start.31
  1344.3 45.3 %copy-start.29 = (f32[512]{0:T(512)S(1)}, f32[512]{0:T(512)}, u32[]{:S(2)}) copy-start(f32[512]{0:T(512)} %get-tuple-element.139) | copy-start | bytes 6148
Sparse Core Ops, SparseCore 0:
  123.6 160.9 all-gather.2
  286.2 147.8 all-gather.4
  501.1 142.6 reduce-scatter.23
  646.0 145.1 reduce-scatter.21
  805.6 71.9 reduce-scatter.37
  929.3 69.3 reduce-scatter.25
  1002.1 59.0 reduce-scatter.43
  1065.0 59.0 reduce-scatter.41
  1127.6 59.0 reduce-scatter.39
  1190.4 71.2 reduce-scatter.33
  1265.2 71.2 reduce-scatter.29
  1338.7 135.3 reduce-scatter.47
  1476.3 132.1 reduce-scatter.45
  1610.7 24.0 reduce-scatter.49
  1636.9 25.7 reduce-scatter.27
  1665.0 25.8 reduce-scatter.35
  1693.0 25.7 reduce-scatter.31

commit v2 on v1

--- a/solution.py
+++ b/solution.py
@@ -425,6 +425,7 @@
 
 
 GROUPS = 4
+HALVES = 2
 
 
 def chain_kernel(axis, forward, map_ref, add_ref, out_ref, sent, landed, send_sem, recv_sem):
@@ -567,9 +568,19 @@
     grad_out,
 ):
     tok_rows, model_width = tokens.shape
-    edge = CONV - 1
     offset = lax.axis_index("narrow") * tok_rows
-    cot_rows = lax.all_gather(grad_out, "narrow", axis=0, tiled=True)
+    half = tok_rows // HALVES
+    parts = [slice(at * half, (at + 1) * half) for at in range(HALVES)]
+
+    def gather(rows):
+        return lax.all_gather(rows, "narrow", axis=0, tiled=True)
+
+    def scatter(rows):
+        return lax.psum_scatter(rows, "narrow", scatter_dimension=0, tiled=True)
+
+    cot = []
+    for part in parts:
+        cot.append(gather(grad_out[part]))
     since = since_start(doc_lengths, offset, tok_rows)
     inputs = tokens.astype(F32)
     normed = rms_scale(inputs, attn_gain, 1e-06).astype(BF16)
@@ -587,38 +598,39 @@
     attn_mixed = mixer_join(out_add, out_map, entry, gain_row)
     hidden = inputs + matmul(attn_mixed, w_out)
     normed_mlp = rms_scale(hidden, mlp_gain, 1e-06).astype(BF16)
-    gathered = lax.all_gather(normed_mlp, "narrow", axis=0, tiled=True)
-    gate_proj = matmul(gathered, w_gate)
-    up_proj = matmul(gathered, w_up)
-    gate_sigmoid = jax.nn.sigmoid(gate_proj)
-    silu_gate = gate_proj * gate_sigmoid
-    activation = (silu_gate * up_proj).astype(BF16)
-    d_act = jnp.einsum("rd,fd->rf", cot_rows, w_down, preferred_element_type=F32)
-    d_gate = (d_act * up_proj * gate_sigmoid * (1.0 + gate_proj * (1.0 - gate_sigmoid))).astype(BF16)
-    d_up = (d_act * silu_gate).astype(BF16)
-    from_gate = jnp.einsum("rf,df->rd", d_gate, w_gate, preferred_element_type=F32)
-    d_normed_mlp = lax.psum_scatter(
-        (from_gate + jnp.einsum("rf,df->rd", d_up, w_up, preferred_element_type=F32)).astype(BF16),
-        "narrow",
-        scatter_dimension=0,
-        tiled=True,
-    ).astype(F32)
-    ffn_sum = lax.psum_scatter(
-        matmul(activation, w_down).astype(BF16), "narrow", scatter_dimension=0, tiled=True
-    ).astype(F32)
-    block_out = (hidden + ffn_sum).astype(BF16)
-    down_term_grad = dot_tn(activation, cot_rows)
-    gate_term_grad = dot_tn(gathered, d_gate)
-    up_term_grad = dot_tn(gathered, d_up)
+    normed_mlp, *cot = lax.optimization_barrier((normed_mlp, *cot))
+    gathered = [gather(normed_mlp[part]) for part in parts]
+    activation, d_gate, d_up, d_normed_parts = [], [], [], []
+    for at in range(HALVES):
+        gate_proj = matmul(gathered[at], w_gate)
+        up_proj = matmul(gathered[at], w_up)
+        gate_sigmoid = jax.nn.sigmoid(gate_proj)
+        silu_gate = gate_proj * gate_sigmoid
+        activation.append((silu_gate * up_proj).astype(BF16))
+        d_act = jnp.einsum("rd,fd->rf", cot[at], w_down, preferred_element_type=F32)
+        d_gate.append(
+            (d_act * up_proj * gate_sigmoid * (1.0 + gate_proj * (1.0 - gate_sigmoid))).astype(BF16)
+        )
+        d_up.append((d_act * silu_gate).astype(BF16))
+        d_normed_parts.append(scatter((dot_nt(d_gate[at], w_gate) + dot_nt(d_up[at], w_up)).astype(BF16)))
+    out_parts = [matmul(act, w_down).astype(BF16) for act in activation]
+    down_term_grad = sum(dot_tn(a, c) for a, c in zip(activation, cot)).astype(BF16)
+    gate_term_grad = sum(dot_tn(a, c) for a, c in zip(gathered, d_gate)).astype(BF16)
+    up_term_grad = sum(dot_tn(a, c) for a, c in zip(gathered, d_up)).astype(BF16)
+    (d_normed_parts, out_parts, down_term_grad, gate_term_grad, up_term_grad) = lax.optimization_barrier(
+        (d_normed_parts, out_parts, down_term_grad, gate_term_grad, up_term_grad)
+    )
+    d_normed_mlp = jnp.concatenate(d_normed_parts, axis=0).astype(F32)
+    ffn_parts = [scatter(part) for part in out_parts]
     grad_gate, grad_up, grad_down = (
-        lax.psum_scatter(gate_term_grad.astype(BF16), "dp", scatter_dimension=0, tiled=True).astype(F32),
-        lax.psum_scatter(up_term_grad.astype(BF16), "dp", scatter_dimension=0, tiled=True).astype(F32),
-        lax.psum_scatter(down_term_grad.astype(BF16), "dp", scatter_dimension=1, tiled=True).astype(F32),
+        lax.psum_scatter(gate_term_grad, "dp", scatter_dimension=0, tiled=True).astype(F32),
+        lax.psum_scatter(up_term_grad, "dp", scatter_dimension=0, tiled=True).astype(F32),
+        lax.psum_scatter(down_term_grad, "dp", scatter_dimension=1, tiled=True).astype(F32),
     )
     d_hidden_norm, mlp_gain_term = norm_back(hidden, mlp_gain, d_normed_mlp, 1e-06)
     d_hidden = grad_out.astype(F32) + d_hidden_norm
     d_branch = d_hidden.astype(BF16)
-    w_out_term = dot_tn(attn_mixed, d_branch)
+    w_out_term = dot_tn(d_branch, attn_mixed)
     d_mixed = dot_nt(d_branch, w_out)
     d_core, start_grad, out_gain_term = mixer_core_back(out_add, out_map, entry, gain_row, d_mixed)
     exit_grad = carry_chain(transfer, start_grad, "narrow", False)
@@ -626,6 +638,8 @@
         since, beta_logit, query, key, value, halo, conv_weight,
         new_add, new_map, inverse, starts, entry, exit_grad, d_core,
     )
+    ffn_parts, d_halo = lax.optimization_barrier((ffn_parts, d_halo))
+    block_out = (hidden + jnp.concatenate(ffn_parts, axis=0).astype(F32)).astype(BF16)
     after = shifted(d_halo.astype(BF16), "narrow", -1)
     d_query, d_key, d_value = (
         part.at[tok_rows - PAD :].add(after[place])
@@ -640,18 +654,35 @@
     d_normed = d_normed + jnp.einsum("rh,dh->rd", d_beta_low, w_beta, preferred_element_type=F32)
     d_input_norm, attn_gain_term = norm_back(inputs, attn_gain, d_normed, 1e-06)
     grad_tokens = (d_hidden + d_input_norm).astype(BF16)
-    both = ("dp", "narrow")
-    grad_query, grad_key, grad_value = (
-        scatter_all(term.astype(BF16), 0).astype(F32) for term in (query_term, key_term, value_term)
-    )
-    grad_w_out = scatter_all(w_out_term.astype(BF16), 1).astype(F32)
-    grad_beta, grad_conv, grad_attn_gain, grad_out_gain, grad_mlp_gain = (
-        lax.psum_scatter(beta_term, both, scatter_dimension=0, tiled=True),
-        lax.psum_scatter(conv_term, both, scatter_dimension=2, tiled=True),
-        lax.psum_scatter(attn_gain_term, both, scatter_dimension=0, tiled=True),
-        lax.psum_scatter(out_gain_term[0], both, scatter_dimension=0, tiled=True),
-        lax.psum_scatter(mlp_gain_term, both, scatter_dimension=0, tiled=True),
-    )
+    devices = lax.axis_size("dp") * lax.axis_size("narrow")
+    heads = w_beta.shape[1]
+    taps = 3 * CONV
+    gain_share = BLOCK // devices
+    gain_column = jnp.pad(
+        out_gain_term.reshape(devices, gain_share), ((0, 0), (0, model_width // devices - gain_share))
+    ).reshape(model_width, 1)
+    small = jnp.concatenate(
+        [
+            beta_term,
+            conv_term.reshape(taps, model_width).T,
+            attn_gain_term[:, None],
+            mlp_gain_term[:, None],
+            gain_column,
+        ],
+        axis=1,
+    )
+    small = jnp.pad(small, ((0, 0), (0, BLOCK - small.shape[1])))
+    small = lax.psum_scatter(small, ("dp", "narrow"), scatter_dimension=0, tiled=True)
+    grad_beta = small[:, :heads]
+    grad_conv = small[:, heads : heads + taps].T.reshape(3, CONV, -1)
+    grad_attn_gain = small[:, heads + taps]
+    grad_mlp_gain = small[:, heads + taps + 1]
+    grad_out_gain = small[:gain_share, heads + taps + 2]
+    grad_query, grad_key, grad_value, grad_w_out = (
+        scatter_all(term.astype(BF16), 0).astype(F32)
+        for term in (query_term, key_term, value_term, w_out_term)
+    )
+    grad_w_out = grad_w_out.T
     return (
         block_out,
         grad_tokens,

time: 1730 us -> 1430 us (0.83)
  waiting for transfers between devices: 1150 us -> 853 us
  blocking collectives: 40.1 us -> 0 us
  Pallas kernels: 162 us -> 194 us
    reduce_scatter x5 -> x7, waiting for transfers between devices: 430 us -> 226 us  [the longest x1 60.4 us: local(): lax.psum_scatter(up_term_grad, 'dp', scatter_dimension=0, tiled=True)]
    all_gather x2 -> x4, waiting for transfers between devices: 274 us -> 150 us  [gather(): return lax.all_gather(rows, 'narrow', axis=0, tiled=True)]
    reduce_scatter x4, waiting for transfers between devices: 126 us -> 233 us  [scatter_all(): part = lax.psum_scatter(value, 'dp', scatter_dimension=dim, tiled=True)]
    unnamed x20 -> x21, waiting for transfers between devices: 238 us -> 139 us
    dot_general x3, matrix products: 66.8 us -> 23.3 us  [the longest x2 22.6 us: local(): d_act = jnp.einsum('rd,fd->rf', cot[at], w_down, preferred_element_type=F32)]
    unnamed x1 -> x0, blocking collectives: 40.1 us -> none
    pallas_call x2, Pallas kernels: 39.3 us -> 71.1 us  [carry_chain(): pl.pallas_call(functools.partial(chain_kernel, axis, forward), in_specs=[...]
    dot_general x4 -> x8, matrix products: 41.2 us -> 69 us  [dot_nt(): return jnp.einsum('re,de->rd', left, right, preferred_element_type=F32)]
  transfers between devices with their start and end apart: 19 -> 22, of which waited for: 17 -> 19; matrix products, arithmetic and copies ran while one was open for 13% -> 23% of each run, Pallas kernels for 5% -> 14%
where the time goes in v2:
time: 1430 us; the launch traced here: 1420 us
  waiting for transfers between devices  853 us (60%)
  matrix products  288 us (20%)
  Pallas kernels  194 us (14%)
  other arithmetic  33.2 us (2%)
  local copies, waits for them, and re-layouts  28.9 us (2%)
  between operations  15.4 us (1%)
    reduce_scatter x4, waiting for transfers between devices, scatter_all(): part = lax.psum_scatter(value, 'dp', scatter_dimension=dim, tiled=True)  233 us
    all_gather x4, waiting for transfers between devices, gather(): return lax.all_gather(rows, 'narrow', axis=0, tiled=True)  150 us
    unnamed x21, waiting for transfers between devices  139 us
    reduce_scatter x4, waiting for transfers between devices, scatter_all(): return lax.psum_scatter(part, 'narrow', scatter_dimension=dim, tiled=True)  98.5 us
    dot_general x11, matrix products, matmul(): return jnp.dot(left, right, preferred_element_type=F32)  96.4 us
    dot_general x10, matrix products, dot_tn(): return jnp.einsum('rd,re->de', left, right, preferred_element_type=F32)  95.4 us
    pallas_call x2, Pallas kernels, carry_chain(): pl.pallas_call(functools.partial(chain_kernel, axis, forward), in_specs=[...  71.1 us
    dot_general x8, matrix products, dot_nt(): return jnp.einsum('re,de->rd', left, right, preferred_element_type=F32)  69 us
  transfers between devices with their start and end apart: 22, of which 19 were waited for; matrix products, arithmetic and copies ran while one was open for 23% of the time, Pallas kernels for 14%

profile of v2, /device:TPU:0, one launch (start us, length us, event | category | flops | bytes accessed | tf_op | source)
XLA Modules:
  0.0 1419.8 jit_solution(1732561931067966529)
XLA Ops:
  7.3 3.2 fusion.51
  12.5 7.2 fusion.42.value_ref
  19.7 4.6 fusion.46.query_ref
  24.4 4.6 fusion.44.key_ref
  31.1 5.1 collective-permute-start
  38.0 2.9 collective-permute-done.halo_ref
  41.7 49.7 %mixer_forward.1 = (bf16[512,2048]{1,0:T(8,128)(2,1)}, bf16[512,2048]{1,0:T(8,128)(2,1)}, bf16[512,2048]{1,0:T(8,128)(2,1)}, bf16[512,2048]{1,0:T(8,128)(2,1)}, ...) custom-call(s32[512,128]{1,0:T(8,128)} %broadcast_in_dim.19.since_ref, ...), custom_call_target="tpu_custom_call" | custom-call | tf_op jit(solution)/shard_map/mixer_forward/pallas_call | solution.py:180
  94.2 16.6 %carry_forward.1.entry_ref = f32[16,128,128]{2,1,0:T(8,128)S(1)} custom-call(bf16[16,128,128]{2,1,0:T(8,128)(2,1)S(1)} %slice.172.map_ref, f32[16,128,128]{2,1,0:T(8,128)S(1)} %slice.116.add_ref), custom_call_target="tpu_custom_call" | custom-call | tf_op jit(solution)/shard_map/carry_forward/pallas_call | solution.py:490
  111.8 7.6 mixer_join.1
  119.5 7.8 multiply_reduce_fusion
  129.6 48.0 %all-gather.5.cloned.1.call-done = bf16[1024,2048]{1,0:T(8,128)(2,1)} async-done(((bf16[256,2048]{1,0:T(8,128)(2,1)}), bf16[1024,2048]{1,0:T(8,128)(2,1)}) %all-gather.5.cloned.1.call-update) | async-done | bytes 4194320 | tf_op jit(solution)/shard_map/all_gather | solution.py:576
  179.1 11.9 fusion.53
  191.1 10.7 fusion.56
  202.2 64.7 %all-gather.11.cloned.1.call-done = bf16[1024,2048]{1,0:T(8,128)(2,1)} async-done(((bf16[256,2048]{1,0:T(8,128)(2,1)}), bf16[1024,2048]{1,0:T(8,128)(2,1)}) %all-gather.11.cloned.1.call-update) | async-done | bytes 4194320 | tf_op jit(solution)/shard_map/all_gather | solution.py:576
  266.9 11.8 fusion.57
  278.8 15.1 %multiply_convert_fusion = (bf16[1024,1408]{1,0:T(8,128)(2,1)}, bf16[1024,1408]{1,0:T(8,128)(2,1)}, bf16[1024,1408]{1,0:T(8,128)(2,1)}) fusion(f32[1024,1408]{1,0:T(8,128)} %fusion.57, f32[1024,1408]{1,0:T(8,128)} %fusion.56, bf16[1024,2048]{1,0:T(8,128)(2,1)S(1)} %copy-done.38, bf16[2048,1408]{1,0:T(8,128)(2,1)} %param.33), kind=kOutput, calls=%fused_computation.15 | convolution fusion | flops 5927206912 | bytes 30146560 | tf_op jit(solution)/shard_map/dot_general | solution.py:515
  293.9 8.7 fusion.58
  302.7 8.3 add_convert_fusion.3
  311.2 37.0 %all-gather.9.cloned.1.call-done = bf16[1024,2048]{1,0:T(8,128)(2,1)} async-done(((bf16[256,2048]{1,0:T(8,128)(2,1)}), bf16[1024,2048]{1,0:T(8,128)(2,1)}) %all-gather.9.cloned.1.call-update) | async-done | bytes 4194320 | tf_op jit(solution)/shard_map/all_gather | solution.py:576
  348.3 10.9 fusion.54
  359.2 13.4 multiply_convert_fusion.1
  374.3 8.3 convolution_convert_fusion.5
  382.5 11.2 convolution_convert_fusion.4
  393.7 9.8 fusion.55
  403.6 8.6 add_convert_fusion.4
  412.3 12.1 fusion.61
  424.3 9.9 fusion.60
  434.3 6.3 fusion.59
  440.6 8.0 add_convert_fusion.2
  448.6 13.0 add_convert_fusion
  461.5 12.8 add_convert_fusion.1
  474.4 30.9 %reduce-scatter.19.cloned.1.call-done = bf16[256,2048]{1,0:T(8,128)(2,1)} async-done(((bf16[1024,2048]{1,0:T(8,128)(2,1)}), bf16[256,2048]{1,0:T(8,128)(2,1)}) %reduce-scatter.19.cloned.1.call-update) | async-done | bytes 1048592 | tf_op jit(solution)/shard_map/reduce_scatter | solution.py:579
  506.2 3.9 fusion.8
  510.5 2.6 fusion.5
  515.3 6.9 convolution_convert_fusion
  522.4 11.4 fusion.20.up_ref
  533.8 9.9 mixer_core_back.1
  544.9 54.4 %carry_backward.1.exit_ref = f32[16,128,128]{2,1,0:T(8,128)S(1)} custom-call(bf16[16,128,128]{2,1,0:T(8,128)(2,1)S(1)} %copy-done.3, f32[16,128,128]{2,1,0:T(8,128)S(1)} %copy-done.5), custom_call_target="tpu_custom_call" | custom-call | tf_op jit(solution)/shard_map/carry_backward/pallas_call | solution.py:490
  600.3 55.4 %mixer_backward.1 = (bf16[512,2048]{1,0:T(8,128)(2,1)}, bf16[512,2048]{1,0:T(8,128)(2,1)}, bf16[512,2048]{1,0:T(8,128)(2,1)}, f32[3,8,2048]{2,1,0:T(8,128)}, f32[3,4,2048]{2,1,0:T(4,128)}, /*index=5*/f32[512,16]{1,0:T(8,128)}) custom-call(s32[512,128]{1,0:T(8,128)} %broadcast_in_dim.19.since_ref, f32[512,16]{1,0:T(8,128)} %fusion.48.beta_ref, ...), custom_call_target="tpu_custom_call" | custom-call | tf_op jit(solution)/shard_map/mixer_backward/pallas_call | solution.py:395
  655.7 20.0 %reduce-scatter.25.cloned.1.call-done = bf16[256,2048]{1,0:T(8,128)(2,1)} async-done(((bf16[1024,2048]{1,0:T(8,128)(2,1)}), bf16[256,2048]{1,0:T(8,128)(2,1)}) %reduce-scatter.25.cloned.1.call-update) | async-done | bytes 1048592 | tf_op jit(solution)/shard_map/reduce_scatter | solution.py:579
  678.4 4.8 collective-permute-done.1
  684.6 9.1 convolution_convert_fusion.3
  693.8 8.8 convolution_convert_fusion.1
  702.7 8.6 convolution_convert_fusion.2
  715.6 8.0 fusion.63
  723.7 7.2 fusion.64
  730.9 7.0 fusion.62
  737.9 3.5 fusion.18
  742.9 8.1 reduce-scatter.39.cloned.1.call-done
  751.0 74.9 %reduce-scatter.27.cloned.1.call-done = bf16[256,2048]{1,0:T(8,128)(2,1)} async-done(((bf16[2048,2048]{1,0:T(8,128)(2,1)}), bf16[256,2048]{1,0:T(8,128)(2,1)}) %reduce-scatter.27.cloned.1.call-update) | async-done | bytes 1048592 | tf_op jit(solution)/shard_map/reduce_scatter | solution.py:549
  826.0 74.7 %reduce-scatter.35.cloned.1.call-done = bf16[256,2048]{1,0:T(8,128)(2,1)} async-done(((bf16[2048,2048]{1,0:T(8,128)(2,1)}), bf16[256,2048]{1,0:T(8,128)(2,1)}) %reduce-scatter.35.cloned.1.call-update) | async-done | bytes 1048592 | tf_op jit(solution)/shard_map/reduce_scatter | solution.py:549
  900.8 74.9 %reduce-scatter.31.cloned.1.call-done = bf16[256,2048]{1,0:T(8,128)(2,1)} async-done(((bf16[2048,2048]{1,0:T(8,128)(2,1)}), bf16[256,2048]{1,0:T(8,128)(2,1)}) %reduce-scatter.31.cloned.1.call-update) | async-done | bytes 1048592 | tf_op jit(solution)/shard_map/reduce_scatter | solution.py:549
  975.8 4.7 add_convert_fusion.5
  981.6 2.5 fusion.15
  984.0 54.2 %reduce-scatter.47.cloned.1.call-done = bf16[1408,256]{1,0:T(8,128)(2,1)} async-done(((bf16[1408,2048]{1,0:T(8,128)(2,1)}), bf16[1408,256]{1,0:T(8,128)(2,1)}) %reduce-scatter.47.cloned.1.call-update) | async-done | bytes 720912 | tf_op jit(solution)/shard_map/reduce_scatter | solution.py:628
  1038.2 2.3 convert_element_type.144
  1040.6 60.4 %reduce-scatter.45.cloned.1.call-done = bf16[256,1408]{1,0:T(8,128)(2,1)} async-done(((bf16[2048,1408]{1,0:T(8,128)(2,1)}), bf16[256,1408]{1,0:T(8,128)(2,1)}) %reduce-scatter.45.cloned.1.call-update) | async-done | bytes 720912 | tf_op jit(solution)/shard_map/reduce_scatter | solution.py:627
  1101.0 2.3 convert_element_type.143
  1103.3 60.1 %reduce-scatter.43.cloned.1.call-done = bf16[256,1408]{1,0:T(8,128)(2,1)} async-done(((bf16[2048,1408]{1,0:T(8,128)(2,1)}), bf16[256,1408]{1,0:T(8,128)(2,1)}) %reduce-scatter.43.cloned.1.call-update) | async-done | bytes 720912 | tf_op jit(solution)/shard_map/reduce_scatter | solution.py:626
  1165.7 135.2 %reduce-scatter.49.cloned.1.call-done = f32[64,128]{1,0:T(8,128)} async-done(((f32[2048,128]{1,0:T(8,128)}), f32[64,128]{1,0:T(8,128)}) %reduce-scatter.49.cloned.1.call-update) | async-done | bytes 32784
  1307.3 19.5 %reduce-scatter.41.cloned.1.call-done = bf16[64,2048]{1,0:T(8,128)(2,1)} async-done(((bf16[256,2048]{1,0:T(8,128)(2,1)}), bf16[64,2048]{1,0:T(8,128)(2,1)}) %reduce-scatter.41.cloned.1.call-update) | async-done | bytes 262160 | tf_op jit(solution)/shard_map/reduce_scatter | solution.py:550
  1328.6 26.3 %reduce-scatter.29.cloned.1.call-done = bf16[64,2048]{1,0:T(8,128)(2,1)} async-done(((bf16[256,2048]{1,0:T(8,128)(2,1)}), bf16[64,2048]{1,0:T(8,128)(2,1)}) %reduce-scatter.29.cloned.1.call-update) | async-done | bytes 262160 | tf_op jit(solution)/shard_map/reduce_scatter | solution.py:550
  1356.6 26.3 %reduce-scatter.37.cloned.1.call-done = bf16[64,2048]{1,0:T(8,128)(2,1)} async-done(((bf16[256,2048]{1,0:T(8,128)(2,1)}), bf16[64,2048]{1,0:T(8,128)(2,1)}) %reduce-scatter.37.cloned.1.call-update) | async-done | bytes 262160 | tf_op jit(solution)/shard_map/reduce_scatter | solution.py:550
  1384.8 26.3 %reduce-scatter.33.cloned.1.call-done = bf16[64,2048]{1,0:T(8,128)(2,1)} async-done(((bf16[256,2048]{1,0:T(8,128)(2,1)}), bf16[64,2048]{1,0:T(8,128)(2,1)}) %reduce-scatter.33.cloned.1.call-update) | async-done | bytes 262160 | tf_op jit(solution)/shard_map/reduce_scatter | solution.py:550
  (218 shorter events, 49.5 us)
Async XLA Ops:
  7.2 29.3 %copy-start = (bf16[2048,16]{0,1:T(8,128)(2,1)S(1)}, bf16[2048,16]{0,1:T(8,128)(2,1)}, u32[]{:S(2)}) copy-start(bf16[2048,16]{0,1:T(8,128)(2,1)} %param.27) | copy-start | bytes 196612
  7.2 5.2 copy-start.25
  7.2 122.4 %all-gather.7.cloned.1.call-start = ((), (), s32[]{:S(2)}) async-start(), calls=%async_computation.17 | async-start | bytes 5242880 | tf_op jit(solution)/shard_map/all_gather | solution.py:576
  10.5 167.1 %all-gather.5.cloned.1.call-start = ((), (), s32[]{:S(2)}) async-start(), calls=%async_computation.16 | async-start | bytes 5242880 | tf_op jit(solution)/shard_map/all_gather | solution.py:576
  11.3 255.6 %all-gather.11.cloned.1.call-start = ((), (), s32[]{:S(2)}) async-start(), calls=%async_computation.20 | async-start | bytes 5242880 | tf_op jit(solution)/shard_map/all_gather | solution.py:576
  11.3 8.3 slice-start.2
  12.4 24.0 %copy-start.29 = (f32[512]{0:T(512)}, f32[512]{0:T(512)S(1)}, u32[]{:S(2)}) copy-start(f32[512]{0:T(512)S(1)} %get-tuple-element.128) | copy-start | bytes 6148
  12.4 7.2 slice-start.3
  12.4 11.9 slice-start
  24.4 11.8 copy-start.41
  31.1 9.8 collective-permute-start
  92.7 18.2 %copy-start.2 = (bf16[16,128,128]{2,1,0:T(8,128)(2,1)}, bf16[16,128,128]{2,1,0:T(8,128)(2,1)S(1)}, u32[]{:S(2)}) copy-start(bf16[16,128,128]{2,1,0:T(8,128)(2,1)S(1)} %slice.172.map_ref) | copy-start | bytes 1572868
  119.4 9.7 copy-start.23
  179.1 169.2 %all-gather.9.cloned.1.call-start = ((), (), s32[]{:S(2)}) async-start(), calls=%async_computation.18 | async-start | bytes 5242880 | tf_op jit(solution)/shard_map/all_gather | solution.py:576
  179.1 12.0 copy-start.35
  201.8 272.6 %reduce-scatter.21.cloned.1.call-start = ((), (), s32[]{:S(2)}) async-start(), calls=%async_computation.21 | async-start | bytes 5242880 | tf_op jit(solution)/shard_map/reduce_scatter | solution.py:579
  266.9 11.8 copy-start.38
  266.9 27.0 %slice-start.6 = ((s8[5767168]{0:T(1024)(128)(4,1)}), s8[4194304]{0:T(1024)(128)(4,1)S(1)}, s32[]{:S(2)}) async-start(s8[5767168]{0:T(1024)(128)(4,1)} %bitcast.109), calls=%async_computation.42 | async-start | bytes 8388608
  266.9 35.7 %slice-start.8 = ((s8[5767168]{0:T(1024)(128)(4,1)}), s8[4194304]{0:T(1024)(128)(4,1)S(1)}, s32[]{:S(2)}) async-start(s8[5767168]{0:T(1024)(128)(4,1)} %bitcast.111), calls=%async_computation.44 | async-start | bytes 8388608
  278.8 15.1 %slice-start.7 = ((s8[5767168]{0:T(1024)(128)(4,1)}), s8[1572864]{0:T(1024)(128)(4,1)S(1)}, s32[]{:S(2)}) async-start(s8[5767168]{0:T(1024)(128)(4,1)} %bitcast.109), calls=%async_computation.43 | async-start | bytes 3145728
  278.8 23.9 %slice-start.9 = ((s8[5767168]{0:T(1024)(128)(4,1)}), s8[1572864]{0:T(1024)(128)(4,1)S(1)}, s32[]{:S(2)}) async-start(s8[5767168]{0:T(1024)(128)(4,1)} %bitcast.111), calls=%async_computation.45 | async-start | bytes 3145728
  293.9 8.7 copy-start.49
  311.0 194.3 %reduce-scatter.19.cloned.1.call-start = ((), (), s32[]{:S(2)}) async-start(), calls=%async_computation.19 | async-start | bytes 5242880 | tf_op jit(solution)/shard_map/reduce_scatter | solution.py:579
  348.3 11.0 copy-start.39
  348.3 26.0 %slice-start.4 = ((s8[5767168]{0:T(1024)(128)(4,1)}), s8[4194304]{0:T(1024)(128)(4,1)S(1)}, s32[]{:S(2)}) async-start(s8[5767168]{0:T(1024)(128)(4,1)} %bitcast.107), calls=%async_computation.40 | async-start | bytes 8388608
  359.2 15.0 %slice-start.5 = ((s8[5767168]{0:T(1024)(128)(4,1)}), s8[1572864]{0:T(1024)(128)(4,1)S(1)}, s32[]{:S(2)}) async-start(s8[5767168]{0:T(1024)(128)(4,1)} %bitcast.107), calls=%async_computation.41 | async-start | bytes 3145728
  382.5 21.0 %slice-start.10 = ((s8[5767168]{0:T(1024)(128)(4,1)}), s8[1572864]{0:T(1024)(128)(4,1)S(1)}, s32[]{:S(2)}) async-start(s8[5767168]{0:T(1024)(128)(4,1)} %bitcast.113), calls=%async_computation.46 | async-start | bytes 3145728
  393.7 9.9 slice-start.11
  393.7 9.9 copy-start.47
  412.2 12.1 copy-start.46
  412.2 243.5 %reduce-scatter.23.cloned.1.call-start = ((), (), s32[]{:S(2)}) async-start(), calls=%async_computation.22 | async-start | bytes 5242880 | tf_op jit(solution)/shard_map/reduce_scatter | solution.py:579
  412.2 12.1 copy-start.40
  424.3 9.9 copy-start.37
  424.3 9.9 copy-start.44
  434.2 6.3 copy-start.36
  434.2 6.3 copy-start.45
  448.6 13.0 copy-start.48
  474.4 31.7 %copy-start.24 = (f32[2048]{0:T(1024)S(1)}, f32[2048]{0:T(1024)}, u32[]{:S(2)}) copy-start(f32[2048]{0:T(1024)} %param.31) | copy-start | bytes 24580
  474.4 31.8 %copy-start.28 = (f32[512]{0:T(512)S(1)}, f32[512]{0:T(512)}, u32[]{:S(2)}) copy-start(f32[512]{0:T(512)} %copy-done.27) | copy-start | bytes 6148
  474.4 31.8 %copy-start.17 = (bf16[256,2048]{1,0:T(8,128)(2,1)S(1)}, bf16[256,2048]{1,0:T(8,128)(2,1)}, u32[]{:S(2)}) copy-start(bf16[256,2048]{1,0:T(8,128)(2,1)} %reduce-scatter.21.cloned.1.call-done) | copy-start | bytes 3145732
  505.3 170.4 %reduce-scatter.25.cloned.1.call-start = ((), (), s32[]{:S(2)}) async-start(), calls=%async_computation.23 | async-start | bytes 5242880 | tf_op jit(solution)/shard_map/reduce_scatter | solution.py:579
  506.1 244.9 %reduce-scatter.39.cloned.1.call-start = ((), (), s32[]{:S(2)}) async-start(), calls=%async_computation.30 | async-start | bytes 9437184 | tf_op jit(solution)/shard_map/reduce_scatter | solution.py:549
  510.5 4.8 copy-start.18
  522.2 303.8 %reduce-scatter.27.cloned.1.call-start = ((), (), s32[]{:S(2)}) async-start(), calls=%async_computation.24 | async-start | bytes 9437184 | tf_op jit(solution)/shard_map/reduce_scatter | solution.py:549
  533.8 9.9 copy-start.3
  600.3 84.3 %copy-start.9 = (bf16[512,2048]{1,0:T(8,128)(2,1)S(1)}, bf16[512,2048]{1,0:T(8,128)(2,1)}, u32[]{:S(2)}) copy-start(bf16[512,2048]{1,0:T(8,128)(2,1)} %param.21) | copy-start | bytes 6291460
  600.3 84.3 %copy-start.26 = (f32[2048]{0:T(1024)S(1)}, f32[2048]{0:T(1024)}, u32[]{:S(2)}) copy-start(f32[2048]{0:T(1024)} %param.23) | copy-start | bytes 24580
  600.3 84.3 %copy-start.30 = (f32[512]{0:T(512)S(1)}, f32[512]{0:T(512)}, u32[]{:S(2)}) copy-start(f32[512]{0:T(512)} %copy-done.29) | copy-start | bytes 6148
  676.7 6.5 collective-permute-start.1
  693.8 207.0 %reduce-scatter.35.cloned.1.call-start = ((), (), s32[]{:S(2)}) async-start(), calls=%async_computation.28 | async-start | bytes 9437184 | tf_op jit(solution)/shard_map/reduce_scatter | solution.py:549
  702.7 273.1 %reduce-scatter.31.cloned.1.call-start = ((), (), s32[]{:S(2)}) async-start(), calls=%async_computation.26 | async-start | bytes 9437184 | tf_op jit(solution)/shard_map/reduce_scatter | solution.py:549
  711.3 326.9 %reduce-scatter.47.cloned.1.call-start = ((), (), s32[]{:S(2)}) async-start(), calls=%async_computation.34 | async-start | bytes 6488064 | tf_op jit(solution)/shard_map/reduce_scatter | solution.py:628
  712.1 388.9 %reduce-scatter.45.cloned.1.call-start = ((), (), s32[]{:S(2)}) async-start(), calls=%async_computation.33 | async-start | bytes 6488064 | tf_op jit(solution)/shard_map/reduce_scatter | solution.py:627
  712.7 450.7 %reduce-scatter.43.cloned.1.call-start = ((), (), s32[]{:S(2)}) async-start(), calls=%async_computation.32 | async-start | bytes 6488064 | tf_op jit(solution)/shard_map/reduce_scatter | solution.py:626
  713.3 587.6 %reduce-scatter.49.cloned.1.call-start = ((), (), s32[]{:S(2)}) async-start(), calls=%async_computation.35 | async-start | bytes 1081344
  715.6 8.1 copy-start.34
  723.7 7.2 copy-start.33
  742.8 232.9 %copy-start.19 = (bf16[256,2048]{1,0:T(8,128)(2,1)S(1)}, bf16[256,2048]{1,0:T(8,128)(2,1)}, u32[]{:S(2)}) copy-start(bf16[256,2048]{1,0:T(8,128)(2,1)} %reduce-scatter.23.cloned.1.call-done) | copy-start | bytes 3145732
  742.9 583.9 %reduce-scatter.41.cloned.1.call-start = ((), (), s32[]{:S(2)}) async-start(), calls=%async_computation.31 | async-start | bytes 1310720 | tf_op jit(solution)/shard_map/reduce_scatter | solution.py:550
  751.0 603.8 %reduce-scatter.29.cloned.1.call-start = ((), (), s32[]{:S(2)}) async-start(), calls=%async_computation.25 | async-start | bytes 1310720 | tf_op jit(solution)/shard_map/reduce_scatter | solution.py:550
  826.0 557.0 %reduce-scatter.37.cloned.1.call-start = ((), (), s32[]{:S(2)}) async-start(), calls=%async_computation.29 | async-start | bytes 1310720 | tf_op jit(solution)/shard_map/reduce_scatter | solution.py:550
  900.8 510.3 %reduce-scatter.33.cloned.1.call-start = ((), (), s32[]{:S(2)}) async-start(), calls=%async_computation.27 | async-start | bytes 1310720 | tf_op jit(solution)/shard_map/reduce_scatter | solution.py:550
  975.8 5.8 copy-start.15
  975.8 5.8 copy-start.31
  (20 other events, 54.2 us)
Sparse Core Ops, SparseCore 0:
  10.7 83.4 all-gather.6
  96.3 81.2 all-gather.4
  179.8 87.1 all-gather.10
  268.9 79.2 all-gather.8
  350.4 75.2 reduce-scatter.20
  428.0 77.2 reduce-scatter.18
  507.6 88.1 reduce-scatter.22
  598.2 77.4 reduce-scatter.24
  679.2 71.7 reduce-scatter.38
  754.7 71.2 reduce-scatter.26
  829.4 71.2 reduce-scatter.34
  904.4 71.2 reduce-scatter.30
  979.2 59.0 reduce-scatter.46
  1041.9 59.0 reduce-scatter.44
  1104.3 59.0 reduce-scatter.42
  1165.5 135.2 reduce-scatter.48
  1303.0 23.7 reduce-scatter.40
  1329.0 25.7 reduce-scatter.28
  1357.1 25.7 reduce-scatter.36
  1385.2 25.7 reduce-scatter.32

commit v3 on v2

--- a/solution.py
+++ b/solution.py
@@ -267,7 +267,7 @@
 def backward_kernel(
     since_ref, beta_ref, query_ref, key_ref, value_ref, halo_ref, taps_ref,
     new_add_ref, new_map_ref, inverse_ref, starts_ref, entry_ref, exit_ref, d_core_ref,
-    d_query_ref, d_key_ref, d_value_ref, d_halo_ref, d_taps_ref, d_beta_ref,
+    d_proj_ref, d_halo_ref, d_taps_ref, d_beta_ref,
     ext, back,
 ):
     rows = since_ref.shape[0]
@@ -354,7 +354,6 @@
         d_key = key_inv * (d_key - key * jnp.sum(d_key * key, axis=-1, keepdims=True))
         d_value = jnp.concatenate(d_values, axis=0)
         d_beta_all = d_beta_all + jnp.where(lane == head, jnp.concatenate(d_betas, axis=0), 0.0)
-        outs = (d_query_ref, d_key_ref, d_value_ref)
         for part, d_act in enumerate((d_query, d_key, d_value)):
             pre, gate, _ = fronts[part]
             taps = taps_ref[part, :, lanes]
@@ -374,7 +373,7 @@
                 total = term if total is None else total + term
             d_taps_ref[part, :, lanes] = jnp.concatenate(d_taps, axis=0)
             d_halo_ref[part, :, lanes] = total[:PAD].astype(d_halo_ref.dtype)
-            outs[part][:, lanes] = total[PAD:].astype(BF16)
+            d_proj_ref[part, :, lanes] = total[PAD:].astype(BF16)
 
     @pl.when(pl.program_id(0) == 0)
     def _():
@@ -391,7 +390,6 @@
     rows, width = query.shape
     heads = width // BLOCK
     blocks = rows // BLOCK
-    wide = jax.ShapeDtypeStruct((rows, width), BF16)
     return pl.pallas_call(
         backward_kernel,
         grid=(heads // HEADS_STEP,),
@@ -404,11 +402,10 @@
             per_head(BLOCK, BLOCK), per_head(BLOCK, BLOCK), head_spec(rows),
         ],
         out_specs=[
-            head_spec(rows), head_spec(rows), head_spec(rows),
-            lanes_spec(3, PAD), lanes_spec(3, CONV), whole_spec(beta_logit.shape),
+            lanes_spec(3, rows), lanes_spec(3, PAD), lanes_spec(3, CONV), whole_spec(beta_logit.shape),
         ],
         out_shape=[
-            wide, wide, wide,
+            jax.ShapeDtypeStruct((3, rows, width), BF16),
             jax.ShapeDtypeStruct((3, PAD, width), F32),
             jax.ShapeDtypeStruct((3, CONV, width), F32),
             jax.ShapeDtypeStruct(beta_logit.shape, F32),
@@ -503,6 +500,288 @@
         ),
         name="carry_forward" if forward else "carry_backward",
     )(map_part, add_part)
+
+
+WINDOW = 4
+LAG = 2
+SPLIT = 4
+
+
+def reduce_kernel(
+    left_ref, right_ref, small_ref, out_ref, small_out_ref,
+    left_own, left_away, left_sib, right_sib, small_sib, total, total_small, got2, got2_small, got3, got3_small, gotz, gotz_small,
+    left_send, left_recv, right_send, right_recv, small_send, small_recv,
+    send2, recv2, send3, recv3, sendz, recvz,
+):
+    dp = lax.axis_index("dp")
+    z = lax.axis_index("narrow")
+    core, x, y = dp % 2, (dp // 2) % 2, dp // 4
+    depth = lax.axis_size("narrow")
+    parts = right_ref.shape[0]
+    units = SPLIT * parts
+    rows = left_ref.shape[1] // 8
+    cols = right_ref.shape[2] // SPLIT
+    sib = dp + 1 - 2 * core
+    flip_x = dp + 2 * (1 - 2 * x)
+    flip_y = dp + 4 * (1 - 2 * y)
+
+    def peer_z(step):
+        return (z + step) % depth
+
+    barrier = pltpu.get_barrier_semaphore()
+    for target in (sib, flip_x, flip_y):
+        pl.semaphore_signal(barrier, inc=1, device_id={"dp": target}, device_id_type=MESH)
+    for step in range(1, depth):
+        pl.semaphore_signal(barrier, inc=1, device_id={"narrow": peer_z(step)}, device_id_type=MESH)
+    pl.semaphore_wait(barrier, 2 + depth)
+
+    def send(src, dst, send_sem, recv_sem, target):
+        return pltpu.make_async_remote_copy(
+            src_ref=src, dst_ref=dst, send_sem=send_sem, recv_sem=recv_sem,
+            device_id=target, device_id_type=MESH,
+        )
+
+    def stripe_rows(stripe, which):
+        return pl.ds(pl.multiple_of((stripe * 2 + which) * rows, rows), rows)
+
+    def left_copy(stripe):
+        return send(
+            left_away.at[stripe], left_sib.at[stripe],
+            left_send.at[stripe], left_recv.at[stripe], {"dp": sib},
+        )
+
+    def small_copy(stripe):
+        return send(
+            small_ref.at[stripe_rows(stripe, 1 - core)], small_sib.at[stripe],
+            small_send.at[stripe], small_recv.at[stripe], {"dp": sib},
+        )
+
+    def right_copy(part):
+        return send(right_ref.at[part], right_sib.at[part], right_send.at[part], right_recv.at[part], {"dp": sib})
+
+    right_copy(0).start()
+    for stripe in range(4):
+        small_copy(stripe).start()
+    for stripe in range(4):
+        turned = left_ref[:, stripe_rows(stripe, 1 - core)].astype(F32).T
+        left_away[stripe] = turned.astype(BF16)
+        left_copy(stripe).start()
+    for part in range(1, parts):
+        right_copy(part).start()
+    for stripe in range(4):
+        left_own[stripe] = left_ref[:, stripe_rows(stripe, core)].astype(F32).T.astype(BF16)
+
+    def order(unit):
+        e = unit % 2
+
+        def pick(even, odd):
+            return (1 - e) * even + e * odd
+
+        def away(j):
+            return pick(2 * j + 1 - x, 2 * (1 - y) + j)
+
+        def kept(j):
+            return pick(2 * j + x, 2 * y + j)
+
+        far = pick(1 - y, 1 - x)
+        near = pick(y, x)
+        return away, kept, pick(flip_x, flip_y), pick(flip_y, flip_x), far, near
+
+    def copy2(unit, j):
+        away, _, target, _, _, _ = order(unit)
+        return send(total.at[unit, away(j)], got2.at[unit, j], send2.at[unit, j], recv2.at[unit, j], {"dp": target})
+
+    def copy2_small(j):
+        away, _, target, _, _, _ = order(0)
+        return send(
+            total_small.at[away(j)], got2_small.at[j], send2.at[units, j], recv2.at[units, j], {"dp": target}
+        )
+
+    def copy3(unit):
+        _, kept, _, target, far, _ = order(unit)
+        return send(total.at[unit, kept(far)], got3.at[unit], send3.at[unit], recv3.at[unit], {"dp": target})
+
+    def copy3_small():
+        _, kept, _, target, far, _ = order(0)
+        return send(total_small.at[kept(far)], got3_small, send3.at[units], recv3.at[units], {"dp": target})
+
+    share = rows // depth
+
+    def share_rows(at):
+        return pl.ds(pl.multiple_of(at * share, share), share)
+
+    def copyz(unit, step):
+        _, kept, _, _, _, near = order(unit)
+        to = peer_z(step)
+        return send(
+            total.at[unit, kept(near), share_rows(to)], gotz.at[unit, step - 1],
+            sendz.at[unit, step - 1], recvz.at[unit, step - 1], {"narrow": to},
+        )
+
+    def copyz_small(step):
+        _, kept, _, _, _, near = order(0)
+        to = peer_z(step)
+        return send(
+            total_small.at[kept(near), share_rows(to)], gotz_small.at[step - 1],
+            sendz.at[units, step - 1], recvz.at[units, step - 1], {"narrow": to},
+        )
+
+    def add_to(dst, src):
+        step = 32
+
+        def one(at, _):
+            at = pl.ds(pl.multiple_of(at * step, step), step)
+            dst[at, :] = (dst[at, :].astype(F32) + src[at, :].astype(F32)).astype(dst.dtype)
+            return 0
+
+        lax.fori_loop(0, rows // step, one, 0)
+
+    for stripe in range(4):
+        small_copy(stripe).wait()
+        total_small[stripe] = small_ref[stripe_rows(stripe, core)] + small_sib[stripe]
+    for j in range(2):
+        copy2_small(j).start()
+    for stripe in range(4):
+        left_copy(stripe).wait()
+
+    tile = 512
+
+    def products(unit, _):
+        away, kept, _, _, _, _ = order(unit)
+        part = unit // SPLIT
+
+        @pl.when(unit % SPLIT == 0)
+        def _():
+            right_copy(part).wait()
+
+        def one(k, _):
+            j = k % 2
+            stripe = (k // 2) * kept(j) + (1 - k // 2) * away(j)
+            mine = left_own[stripe]
+            other = left_sib[stripe]
+            for at in range(cols // tile):
+                lanes = pl.ds(pl.multiple_of((unit % SPLIT) * cols + at * tile, tile), tile)
+                value = jnp.dot(mine, right_ref[part, :, lanes], preferred_element_type=F32)
+                value = value + jnp.dot(other, right_sib[part, :, lanes], preferred_element_type=F32)
+                total[unit, stripe, :, at * tile : (at + 1) * tile] = value.astype(BF16)
+
+            @pl.when((k < 2) & (unit < WINDOW))
+            def _():
+                copy2(unit, j).start()
+
+            return 0
+
+        lax.fori_loop(0, 4, one, 0)
+        return 0
+
+    lax.fori_loop(0, units, products, 0)
+
+    def second(unit):
+        _, kept, _, _, far, near = order(unit)
+        for j in range(2):
+            copy2(unit, j).wait()
+
+        @pl.when(unit + WINDOW < units)
+        def _():
+            for j in range(2):
+                copy2(unit + WINDOW, j).start()
+
+        add_to(total.at[unit, kept(far)], got2.at[unit, far])
+        copy3(unit).start()
+        add_to(total.at[unit, kept(near)], got2.at[unit, near])
+
+    def third(unit):
+        _, kept, _, _, _, near = order(unit)
+        copy3(unit).wait()
+        add_to(total.at[unit, kept(near)], got3.at[unit])
+        for step in range(1, depth):
+            copyz(unit, step).start()
+
+    def fourth(unit):
+        _, kept, _, _, _, near = order(unit)
+        for step in range(1, depth):
+            copyz(unit, step).wait()
+        value = total[unit, kept(near), share_rows(z), :].astype(F32)
+        for step in range(1, depth):
+            value = value + gotz[unit, step - 1].astype(F32)
+        out_ref[unit // SPLIT, :, pl.ds(pl.multiple_of((unit % SPLIT) * cols, cols), cols)] = value
+
+    _, kept, _, _, far, near = order(0)
+    for j in range(2):
+        copy2_small(j).wait()
+    add_to(total_small.at[kept(far)], got2_small.at[far])
+    copy3_small().start()
+    add_to(total_small.at[kept(near)], got2_small.at[near])
+
+    def stages(at, _):
+        @pl.when(at < units)
+        def _():
+            second(at)
+
+        @pl.when((at >= LAG) & (at < units + LAG))
+        def _():
+            third(at - LAG)
+
+        @pl.when(at >= 2 * LAG)
+        def _():
+            fourth(at - 2 * LAG)
+
+        return 0
+
+    lax.fori_loop(0, units, stages, 0)
+    copy3_small().wait()
+    add_to(total_small.at[kept(near)], got3_small)
+    for step in range(1, depth):
+        copyz_small(step).start()
+    lax.fori_loop(units, units + 2 * LAG, stages, 0)
+    for step in range(1, depth):
+        copyz_small(step).wait()
+    value = total_small[kept(near), share_rows(z), :]
+    for step in range(1, depth):
+        value = value + gotz_small[step - 1]
+    small_out_ref[...] = value
+
+
+def reduce_products(left, right, small):
+    tokens, height = left.shape
+    parts, _, width = right.shape
+    depth = lax.axis_size("narrow")
+    units = SPLIT * parts
+    rows, cols = height // 8, width // SPLIT
+    share = rows // depth
+    lanes = small.shape[1]
+    dma = pltpu.SemaphoreType.DMA
+    return pl.pallas_call(
+        reduce_kernel,
+        in_specs=[pl.BlockSpec(memory_space=pltpu.VMEM)] * 3,
+        out_specs=[pl.BlockSpec(memory_space=pltpu.VMEM)] * 2,
+        out_shape=[
+            jax.ShapeDtypeStruct((parts, share, width), F32),
+            jax.ShapeDtypeStruct((share, lanes), F32),
+        ],
+        scratch_shapes=[
+            pltpu.VMEM((4, rows, tokens), BF16),
+            pltpu.VMEM((4, rows, tokens), BF16),
+            pltpu.VMEM((4, rows, tokens), BF16),
+            pltpu.VMEM(right.shape, BF16),
+            pltpu.VMEM((4, rows, lanes), F32),
+            pltpu.VMEM((units, 4, rows, cols), BF16),
+            pltpu.VMEM((4, rows, lanes), F32),
+            pltpu.VMEM((units, 2, rows, cols), BF16),
+            pltpu.VMEM((2, rows, lanes), F32),
+            pltpu.VMEM((units, rows, cols), BF16),
+            pltpu.VMEM((rows, lanes), F32),
+            pltpu.VMEM((units, depth - 1, share, cols), BF16),
+            pltpu.VMEM((depth - 1, share, lanes), F32),
+            dma((4,)), dma((4,)), dma((parts,)), dma((parts,)), dma((4,)), dma((4,)),
+            dma((units + 1, 2)), dma((units + 1, 2)), dma((units + 1,)), dma((units + 1,)),
+            dma((units + 1, depth - 1)), dma((units + 1, depth - 1)),
+        ],
+        compiler_params=pltpu.CompilerParams(
+            collective_id=3, has_side_effects=True, vmem_limit_bytes=VMEM_LIMIT
+        ),
+        name="reduce_products",
+    )(left, right, small)
 
 
 def shifted(value, axis, steps):
@@ -621,7 +900,6 @@
         (d_normed_parts, out_parts, down_term_grad, gate_term_grad, up_term_grad)
     )
     d_normed_mlp = jnp.concatenate(d_normed_parts, axis=0).astype(F32)
-    ffn_parts = [scatter(part) for part in out_parts]
     grad_gate, grad_up, grad_down = (
         lax.psum_scatter(gate_term_grad, "dp", scatter_dimension=0, tiled=True).astype(F32),
         lax.psum_scatter(up_term_grad, "dp", scatter_dimension=0, tiled=True).astype(F32),
@@ -630,25 +908,21 @@
     d_hidden_norm, mlp_gain_term = norm_back(hidden, mlp_gain, d_normed_mlp, 1e-06)
     d_hidden = grad_out.astype(F32) + d_hidden_norm
     d_branch = d_hidden.astype(BF16)
-    w_out_term = dot_tn(d_branch, attn_mixed)
+    w_out_term = dot_tn(d_branch, attn_mixed).astype(BF16)
     d_mixed = dot_nt(d_branch, w_out)
     d_core, start_grad, out_gain_term = mixer_core_back(out_add, out_map, entry, gain_row, d_mixed)
     exit_grad = carry_chain(transfer, start_grad, "narrow", False)
-    d_query, d_key, d_value, d_halo, conv_term, d_beta = mixer_backward(
+    exit_grad, out_parts = lax.optimization_barrier((exit_grad, out_parts))
+    w_out_term = scatter_all(w_out_term, 0)
+    ffn_parts = [scatter(part) for part in out_parts]
+    d_proj, d_halo, conv_term, d_beta = mixer_backward(
         since, beta_logit, query, key, value, halo, conv_weight,
         new_add, new_map, inverse, starts, entry, exit_grad, d_core,
     )
-    ffn_parts, d_halo = lax.optimization_barrier((ffn_parts, d_halo))
-    block_out = (hidden + jnp.concatenate(ffn_parts, axis=0).astype(F32)).astype(BF16)
     after = shifted(d_halo.astype(BF16), "narrow", -1)
-    d_query, d_key, d_value = (
-        part.at[tok_rows - PAD :].add(after[place])
-        for place, part in enumerate((d_query, d_key, d_value))
-    )
+    d_proj = d_proj.at[:, tok_rows - PAD :].add(after)
+    d_query, d_key, d_value = d_proj[0], d_proj[1], d_proj[2]
     d_beta_low = d_beta.astype(BF16)
-    query_term = dot_tn(normed, d_query)
-    key_term = dot_tn(normed, d_key)
-    value_term = dot_tn(normed, d_value)
     beta_term = jnp.einsum("rd,rh->dh", normed, d_beta_low, preferred_element_type=F32)
     d_normed = dot_nt(d_query, w_query) + dot_nt(d_key, w_key) + dot_nt(d_value, w_value)
     d_normed = d_normed + jnp.einsum("rh,dh->rd", d_beta_low, w_beta, preferred_element_type=F32)
@@ -672,17 +946,20 @@
         axis=1,
     )
     small = jnp.pad(small, ((0, 0), (0, BLOCK - small.shape[1])))
-    small = lax.psum_scatter(small, ("dp", "narrow"), scatter_dimension=0, tiled=True)
+    if lax.axis_size("dp") == 8:
+        grads, small = reduce_products(normed, d_proj, small)
+    else:
+        grads = [scatter_all(dot_tn(normed, part).astype(BF16), 0).astype(F32) for part in (d_query, d_key, d_value)]
+        small = lax.psum_scatter(small, ("dp", "narrow"), scatter_dimension=0, tiled=True)
     grad_beta = small[:, :heads]
     grad_conv = small[:, heads : heads + taps].T.reshape(3, CONV, -1)
     grad_attn_gain = small[:, heads + taps]
     grad_mlp_gain = small[:, heads + taps + 1]
     grad_out_gain = small[:gain_share, heads + taps + 2]
-    grad_query, grad_key, grad_value, grad_w_out = (
-        scatter_all(term.astype(BF16), 0).astype(F32)
-        for term in (query_term, key_term, value_term, w_out_term)
-    )
-    grad_w_out = grad_w_out.T
+    ffn_parts, w_out_term, grads = lax.optimization_barrier((ffn_parts, w_out_term, grads))
+    block_out = (hidden + jnp.concatenate(ffn_parts, axis=0).astype(F32)).astype(BF16)
+    grad_query, grad_key, grad_value = grads[0], grads[1], grads[2]
+    grad_w_out = w_out_term.astype(F32).T
     return (
         block_out,
         grad_tokens,

time: 1430 us -> 1060 us (0.74)
  waiting for transfers between devices: 853 us -> 304 us
  Pallas kernels: 194 us -> 387 us
    reduce_scatter x4 -> x1, waiting for transfers between devices: 233 us -> 0.01 us  [scatter_all(): part = lax.psum_scatter(value, 'dp', scatter_dimension=dim, tiled=True)]
    pallas_call x0 -> x1, Pallas kernels: none -> 219 us  [reduce_products(): pl.pallas_call(reduce_kernel, in_specs=[pl.BlockSpec(memory_space=pltpu.V...]
    unnamed x21 -> x13, waiting for transfers between devices: 139 us -> 2.86 us
    reduce_scatter x4, waiting for transfers between devices: 50.9 us -> 123 us  [scatter(): return lax.psum_scatter(rows, 'narrow', scatter_dimension=0, tiled=True)]
    reduce_scatter x4 -> x1, waiting for transfers between devices: 98.5 us -> 30 us  [scatter_all(): return lax.psum_scatter(part, 'narrow', scatter_dimension=dim, tiled=True)]
    reduce_scatter x1, waiting for transfers between devices: 60.4 us -> 0.01 us  [local(): lax.psum_scatter(up_term_grad, 'dp', scatter_dimension=0, tiled=True)]
    reduce_scatter x1, waiting for transfers between devices: 60.1 us -> 0.01 us  [local(): lax.psum_scatter(gate_term_grad, 'dp', scatter_dimension=0, tiled=True)]
    reduce_scatter x1, waiting for transfers between devices: 54.2 us -> 0.01 us  [local(): lax.psum_scatter(down_term_grad, 'dp', scatter_dimension=1, tiled=True)]
  transfers between devices with their start and end apart: 22 -> 15, of which waited for: 19 -> 9; matrix products, arithmetic and copies ran while one was open for 23% -> 28% of each run, Pallas kernels for 14% -> 37%
where the time goes in v3:
time: 1060 us; the launch traced here: 1050 us
  Pallas kernels  387 us (37%)
  waiting for transfers between devices  304 us (29%)
  matrix products  274 us (26%)
  other arithmetic  32.4 us (3%)
  local copies, waits for them, and re-layouts  29.3 us (3%)
  between operations  14.9 us (1%)
    pallas_call x1, Pallas kernels, reduce_products(): pl.pallas_call(reduce_kernel, in_specs=[pl.BlockSpec(memory_space=pltpu.V...  219 us
    all_gather x4, waiting for transfers between devices, gather(): return lax.all_gather(rows, 'narrow', axis=0, tiled=True)  146 us
    reduce_scatter x4, waiting for transfers between devices, scatter(): return lax.psum_scatter(rows, 'narrow', scatter_dimension=0, tiled=True)  123 us
    dot_general x11, matrix products, matmul(): return jnp.dot(left, right, preferred_element_type=F32)  98.5 us
    dot_general x8, matrix products, dot_nt(): return jnp.einsum('re,de->rd', left, right, preferred_element_type=F32)  74.1 us
    dot_general x7, matrix products, dot_tn(): return jnp.einsum('rd,re->de', left, right, preferred_element_type=F32)  68.8 us
    pallas_call x1, Pallas kernels, mixer_backward(): pl.pallas_call(backward_kernel, grid=(heads // HEADS_STEP,), in_specs=[wh...  55.4 us
    pallas_call x1, Pallas kernels, mixer_forward(): pl.pallas_call(forward_kernel, grid=(heads // HEADS_STEP,), in_specs=[who...  49.7 us
  transfers between devices with their start and end apart: 15, of which 9 were waited for; matrix products, arithmetic and copies ran while one was open for 28% of the time, Pallas kernels for 37%

profile of v3, /device:TPU:0, one launch (start us, length us, event | category | flops | bytes accessed | tf_op | source)
XLA Modules:
  0.0 1050.5 jit_solution(10039517713244894228)
XLA Ops:
  7.3 3.2 fusion.33
  13.6 7.9 fusion.37.value_ref
  21.6 4.5 fusion.36.key_ref
  26.2 4.5 fusion.35.query_ref
  30.7 1.9 copy-done.14
  32.7 5.1 collective-permute-start
  38.1 3.0 fusion.34.beta_ref
  41.1 1.4 collective-permute-done.halo_ref
  43.3 49.7 %mixer_forward.1 = (bf16[512,2048]{1,0:T(8,128)(2,1)}, bf16[512,2048]{1,0:T(8,128)(2,1)}, bf16[512,2048]{1,0:T(8,128)(2,1)}, bf16[512,2048]{1,0:T(8,128)(2,1)}, ...) custom-call(s32[512,128]{1,0:T(8,128)} %broadcast_in_dim.19.since_ref, ...), custom_call_target="tpu_custom_call" | custom-call | tf_op jit(solution)/shard_map/mixer_forward/pallas_call | solution.py:180
  94.3 1.5 slice.92.add_ref
  95.8 19.5 %carry_forward.1.entry_ref = f32[16,128,128]{2,1,0:T(8,128)S(1)} custom-call(bf16[16,128,128]{2,1,0:T(8,128)(2,1)S(1)} %slice.140.map_ref, f32[16,128,128]{2,1,0:T(8,128)S(1)} %slice.92.add_ref), custom_call_target="tpu_custom_call" | custom-call | tf_op jit(solution)/shard_map/carry_forward/pallas_call | solution.py:487
  116.3 7.6 mixer_join.1
  123.9 7.8 multiply_reduce_fusion
  134.1 43.5 %all-gather.5.cloned.1.call-done = bf16[1024,2048]{1,0:T(8,128)(2,1)} async-done(((bf16[256,2048]{1,0:T(8,128)(2,1)}), bf16[1024,2048]{1,0:T(8,128)(2,1)}) %all-gather.5.cloned.1.call-update) | async-done | bytes 4194320 | tf_op jit(solution)/shard_map/all_gather | solution.py:855
  177.6 1.4 fusion.32
  179.1 12.0 %fusion.38 = f32[1024,1408]{1,0:T(8,128)} fusion(bf16[1024,2048]{1,0:T(8,128)(2,1)} %all-gather.5.cloned.1.call-done, bf16[1408,2048]{1,0:T(8,128)(2,1)} %param.30), kind=kOutput, calls=%fused_computation.92 | convolution fusion | flops 5905580032 | bytes 15728640 | tf_op jit(solution)/shard_map/rd,fd->rf/dot_general | solution.py:889
  191.1 10.5 %fusion.41 = f32[1024,1408]{1,0:T(8,128)} fusion(bf16[1024,2048]{1,0:T(8,128)(2,1)S(1)} %copy-done.34, bf16[1408,2048]{1,0:T(8,128)(2,1)} %param.30), kind=kOutput, calls=%fused_computation.95 | convolution fusion | flops 5905580032 | bytes 15728640 | tf_op jit(solution)/shard_map/rd,fd->rf/dot_general | solution.py:889
  202.1 65.2 %all-gather.11.cloned.1.call-done = bf16[1024,2048]{1,0:T(8,128)(2,1)} async-done(((bf16[256,2048]{1,0:T(8,128)(2,1)}), bf16[1024,2048]{1,0:T(8,128)(2,1)}) %all-gather.11.cloned.1.call-update) | async-done | bytes 4194320 | tf_op jit(solution)/shard_map/all_gather | solution.py:855
  267.3 11.8 %fusion.42 = f32[1024,1408]{1,0:T(8,128)} fusion(bf16[1024,2048]{1,0:T(8,128)(2,1)} %all-gather.11.cloned.1.call-done, bf16[2048,1408]{1,0:T(8,128)(2,1)} %param.28), kind=kOutput, calls=%fused_computation.96 | convolution fusion | flops 5905580032 | bytes 15728640 | tf_op jit(solution)/shard_map/dot_general | solution.py:794
  279.1 15.2 %multiply_convert_fusion = (bf16[1024,1408]{1,0:T(8,128)(2,1)}, bf16[1024,1408]{1,0:T(8,128)(2,1)}, bf16[1024,1408]{1,0:T(8,128)(2,1)}) fusion(f32[1024,1408]{1,0:T(8,128)} %fusion.42, f32[1024,1408]{1,0:T(8,128)} %fusion.41, bf16[1024,2048]{1,0:T(8,128)(2,1)S(1)} %copy-done.37, bf16[2048,1408]{1,0:T(8,128)(2,1)} %param.29), kind=kOutput, calls=%fused_computation.12 | convolution fusion | flops 5927206912 | bytes 30146560 | tf_op jit(solution)/shard_map/dot_general | solution.py:794
  294.3 8.7 fusion.43
  303.0 8.3 add_convert_fusion.3
  311.6 37.0 %all-gather.9.cloned.1.call-done = bf16[1024,2048]{1,0:T(8,128)(2,1)} async-done(((bf16[256,2048]{1,0:T(8,128)(2,1)}), bf16[1024,2048]{1,0:T(8,128)(2,1)}) %all-gather.9.cloned.1.call-update) | async-done | bytes 4194320 | tf_op jit(solution)/shard_map/all_gather | solution.py:855
  348.6 11.0 %fusion.39 = f32[1024,1408]{1,0:T(8,128)S(1)} fusion(bf16[1024,2048]{1,0:T(8,128)(2,1)} %all-gather.9.cloned.1.call-done, bf16[2048,1408]{1,0:T(8,128)(2,1)} %param.28), kind=kOutput, calls=%fused_computation.93 | convolution fusion | flops 5905580032 | bytes 15728640 | tf_op jit(solution)/shard_map/dot_general | solution.py:794
  359.6 13.4 %multiply_convert_fusion.1 = (bf16[1024,1408]{1,0:T(8,128)(2,1)S(1)}, bf16[1024,1408]{1,0:T(8,128)(2,1)}, bf16[1024,1408]{1,0:T(8,128)(2,1)}) fusion(f32[1024,1408]{1,0:T(8,128)S(1)} %fusion.39, f32[1024,1408]{1,0:T(8,128)} %fusion.38, bf16[1024,2048]{1,0:T(8,128)(2,1)S(1)} %copy-done.38, bf16[2048,1408]{1,0:T(8,128)(2,1)} %param.29), kind=kOutput, calls=%fused_computation.13 | convolution fusion | flops 5927206912 | bytes 30146560 | tf_op jit(solution)/shard_map/dot_general | solution.py:794
  373.1 1.6 copy-done.42
  374.7 8.2 convolution_convert_fusion.2
  382.9 11.2 %convolution_convert_fusion.1 = bf16[1024,2048]{1,0:T(8,128)(2,1)} fusion(bf16[1024,1408]{1,0:T(8,128)(2,1)} %get-tuple-element.154, bf16[1408,2048]{1,0:T(8,128)(2,1)} %param.30), kind=kOutput, calls=%fused_computation.45 | convolution fusion | flops 5907677184 | bytes 12845056 | tf_op jit(solution)/shard_map/dot_general | solution.py:794
  394.1 9.8 fusion.40
  404.0 8.6 add_convert_fusion.4
  412.6 12.1 %fusion.46 = f32[2048,1408]{1,0:T(8,128)} fusion(bf16[1024,2048]{1,0:T(8,128)(2,1)} %all-gather.9.cloned.1.call-done, bf16[1024,1408]{1,0:T(8,128)(2,1)} %get-tuple-element.159), kind=kOutput, calls=%fused_computation.100 | convolution fusion | flops 5905580032 | bytes 18612224 | tf_op jit(solution)/shard_map/rd,re->de/dot_general | solution.py:798
  424.7 9.9 fusion.45
  434.6 6.3 fusion.44
  441.0 8.1 add_convert_fusion.2
  449.0 12.9 %add_convert_fusion = bf16[2048,1408]{1,0:T(8,128)(2,1)} fusion(f32[2048,1408]{1,0:T(8,128)} %fusion.46, bf16[1024,2048]{1,0:T(8,128)(2,1)} %all-gather.11.cloned.1.call-done, bf16[1024,1408]{1,0:T(8,128)(2,1)S(1)} %copy-done.48), kind=kOutput, calls=%fused_computation | convolution fusion | flops 5911347200 | bytes 24379392 | tf_op jit(solution)/shard_map/rd,re->de/dot_general | solution.py:798
  461.9 12.8 %add_convert_fusion.1 = bf16[2048,1408]{1,0:T(8,128)(2,1)} fusion(f32[2048,1408]{1,0:T(8,128)} %fusion.45, bf16[1024,2048]{1,0:T(8,128)(2,1)} %all-gather.11.cloned.1.call-done, bf16[1024,1408]{1,0:T(8,128)(2,1)} %get-tuple-element.155), kind=kOutput, calls=%fused_computation.1 | convolution fusion | flops 5911347200 | bytes 24379392 | tf_op jit(solution)/shard_map/rd,re->de/dot_general | solution.py:798
  474.7 30.9 %reduce-scatter.10.cloned.1.call-done = bf16[256,2048]{1,0:T(8,128)(2,1)} async-done(((bf16[1024,2048]{1,0:T(8,128)(2,1)}), bf16[256,2048]{1,0:T(8,128)(2,1)}) %reduce-scatter.10.cloned.1.call-update) | async-done | bytes 1048592 | tf_op jit(solution)/shard_map/reduce_scatter | solution.py:858
  505.6 4.2 fusion.8
  509.9 2.9 fusion.5
  512.9 2.0 copy-done.15
  514.8 6.8 convolution_convert_fusion
  523.8 12.1 %fusion.23.up_ref = f32[512,2048]{1,0:T(8,128)} fusion(bf16[2048,2048]{1,0:T(8,128)(2,1)} %param.26, f32[512,2048]{1,0:T(8,128)} %copy-done.15), kind=kOutput, calls=%fused_computation.56 | convolution fusion | flops 4296015872 | bytes 16777216 | tf_op jit(solution)/shard_map/re,de->rd/dot_general | solution.py:802
  535.9 10.1 mixer_core_back.1
  547.3 25.8 %carry_backward.1.exit_ref = f32[16,128,128]{2,1,0:T(8,128)S(1)} custom-call(bf16[16,128,128]{2,1,0:T(8,128)(2,1)S(1)} %copy-done.3, f32[16,128,128]{2,1,0:T(8,128)S(1)} %copy-done.5), custom_call_target="tpu_custom_call" | custom-call | tf_op jit(solution)/shard_map/carry_backward/pallas_call | solution.py:487
  574.8 55.4 %mixer_backward.1 = (bf16[3,512,2048]{2,1,0:T(8,128)(2,1)}, f32[3,8,2048]{2,1,0:T(8,128)}, f32[3,4,2048]{2,1,0:T(4,128)}, f32[512,16]{1,0:T(8,128)}) custom-call(s32[512,128]{1,0:T(8,128)} %broadcast_in_dim.19.since_ref, f32[512,16]{1,0:T(8,128)} %fusion.34.beta_ref, f32[512,2048]{1,0:T(8,128)} %copy-done.14, f32[512,2048]{1,0:T(8,128)} %copy-done.13, ...), custom_call_target="tpu_custom_call" | custom-call | tf_op jit(solution)/shard_map/mixer_backward/pallas_call | solution.py:393
  631.1 1.5 collective-permute-start.1
  632.6 1.4 fusion.26
  637.6 1.5 add_dynamic-update-slice_fusion.right_ref
  639.2 10.8 %fusion.19 = f32[512,2048]{1,0:T(8,128)} fusion(bf16[2048,2048]{1,0:T(8,128)(2,1)} %param.22, bf16[3,512,2048]{2,1,0:T(8,128)(2,1)} %add_dynamic-update-slice_fusion.right_ref), kind=kOutput, calls=%fused_computation.48 | convolution fusion | flops 4294967296 | bytes 14680064 | tf_op jit(solution)/shard_map/re,de->rd/dot_general | solution.py:802
  650.0 9.7 fusion.20
  659.7 6.1 fusion.21
  665.9 9.1 fusion.18
  676.5 219.1 %reduce_products.1 = (f32[3,64,2048]{2,1,0:T(8,128)}, f32[64,128]{1,0:T(8,128)}) custom-call(bf16[512,2048]{1,0:T(8,128)(2,1)} %copy-done.10, bf16[3,512,2048]{2,1,0:T(8,128)(2,1)} %add_dynamic-update-slice_fusion.right_ref, f32[2048,128]{1,0:T(8,128)} %pad.11.small_ref), custom_call_target="tpu_custom_call" | custom-call | tf_op jit(solution)/shard_map/reduce_products/pallas_call | solution.py:754
  895.6 1.4 copy.53
  899.9 1.5 slice_reduce_fusion
  901.5 5.9 fusion.17
  907.4 2.4 convert_element_type.120
  909.8 2.3 convert_element_type.119
  912.1 2.3 convert_element_type.118
  914.5 9.3 reduce-scatter.14.cloned.1.call-done
  923.8 82.8 %reduce-scatter.16.cloned.1.call-done = bf16[256,2048]{1,0:T(8,128)(2,1)} async-done(((bf16[1024,2048]{1,0:T(8,128)(2,1)}), bf16[256,2048]{1,0:T(8,128)(2,1)}) %reduce-scatter.16.cloned.1.call-update) | async-done | bytes 1048592 | tf_op jit(solution)/shard_map/reduce_scatter | solution.py:858
  1006.6 30.0 %reduce-scatter.20.cloned.1.call-done = bf16[64,2048]{1,0:T(8,128)(2,1)} async-done(((bf16[256,2048]{1,0:T(8,128)(2,1)}), bf16[64,2048]{1,0:T(8,128)(2,1)}) %reduce-scatter.20.cloned.1.call-update) | async-done | bytes 262160 | tf_op jit(solution)/shard_map/reduce_scatter | solution.py:829
  1036.5 1.9 convert_bitcast_fusion
  1039.6 4.2 add_convert_fusion.5
  (194 shorter events, 24.9 us)
Async XLA Ops:
  7.2 30.9 %copy-start = (bf16[2048,16]{0,1:T(8,128)(2,1)S(1)}, bf16[2048,16]{0,1:T(8,128)(2,1)}, u32[]{:S(2)}) copy-start(bf16[2048,16]{0,1:T(8,128)(2,1)} %param.23) | copy-start | bytes 196612
  7.2 5.8 copy-start.26
  7.2 126.9 %all-gather.7.cloned.1.call-start = ((), (), s32[]{:S(2)}) async-start(), calls=%async_computation.10 | async-start | bytes 5242880 | tf_op jit(solution)/shard_map/all_gather | solution.py:855
  10.5 167.0 %all-gather.5.cloned.1.call-start = ((), (), s32[]{:S(2)}) async-start(), calls=%async_computation.9 | async-start | bytes 5242880 | tf_op jit(solution)/shard_map/all_gather | solution.py:855
  11.3 256.0 %all-gather.11.cloned.1.call-start = ((), (), s32[]{:S(2)}) async-start(), calls=%async_computation.13 | async-start | bytes 5242880 | tf_op jit(solution)/shard_map/all_gather | solution.py:855
  13.0 8.6 slice-start
  13.6 12.5 %copy-start.10 = (bf16[512,2048]{1,0:T(8,128)(2,1)}, bf16[512,2048]{1,0:T(8,128)(2,1)S(1)}, u32[]{:S(2)}) copy-start(bf16[512,2048]{1,0:T(8,128)(2,1)S(1)} %fusion.11.left_ref) | copy-start | bytes 6291460
  13.6 8.0 slice-start.1
  13.6 12.5 %slice-start.2 = ((s8[8388608]{0:T(1024)(128)(4,1)}), s8[4194304]{0:T(1024)(128)(4,1)S(1)}, s32[]{:S(2)}) async-start(s8[8388608]{0:T(1024)(128)(4,1)} %bitcast.94), calls=%async_computation.24 | async-start | bytes 8388608
  21.5 4.6 copy-start.12
  21.6 4.6 slice-start.3
  26.2 11.6 %copy-start.40 = (s32[1,4]{1,0:T(1,128)S(1)}, s32[1,4]{1,0:T(1,128)}, u32[]{:S(2)}) copy-start(s32[1,4]{1,0:T(1,128)} %param.18) | copy-start | bytes 52
  32.7 9.8 collective-permute-start
  94.3 21.0 %copy-start.2 = (bf16[16,128,128]{2,1,0:T(8,128)(2,1)}, bf16[16,128,128]{2,1,0:T(8,128)(2,1)S(1)}, u32[]{:S(2)}) copy-start(bf16[16,128,128]{2,1,0:T(8,128)(2,1)S(1)} %slice.140.map_ref) | copy-start | bytes 1572868
  123.9 9.7 copy-start.24
  179.0 169.5 %all-gather.9.cloned.1.call-start = ((), (), s32[]{:S(2)}) async-start(), calls=%async_computation.11 | async-start | bytes 5242880 | tf_op jit(solution)/shard_map/all_gather | solution.py:855
  179.1 12.0 %copy-start.34 = (bf16[1024,2048]{1,0:T(8,128)(2,1)S(1)}, bf16[1024,2048]{1,0:T(8,128)(2,1)}, u32[]{:S(2)}) copy-start(bf16[1024,2048]{1,0:T(8,128)(2,1)} %all-gather.7.cloned.1.call-done) | copy-start | bytes 12582916
  201.6 273.1 %reduce-scatter.12.cloned.1.call-start = ((), (), s32[]{:S(2)}) async-start(), calls=%async_computation.14 | async-start | bytes 5242880 | tf_op jit(solution)/shard_map/reduce_scatter | solution.py:858
  267.3 11.8 %copy-start.37 = (bf16[1024,2048]{1,0:T(8,128)(2,1)S(1)}, bf16[1024,2048]{1,0:T(8,128)(2,1)}, u32[]{:S(2)}) copy-start(bf16[1024,2048]{1,0:T(8,128)(2,1)} %all-gather.11.cloned.1.call-done) | copy-start | bytes 12582916
  267.3 27.0 %slice-start.8 = ((s8[5767168]{0:T(1024)(128)(4,1)}), s8[4194304]{0:T(1024)(128)(4,1)S(1)}, s32[]{:S(2)}) async-start(s8[5767168]{0:T(1024)(128)(4,1)} %bitcast.100), calls=%async_computation.30 | async-start | bytes 8388608
  267.3 35.7 %slice-start.10 = ((s8[5767168]{0:T(1024)(128)(4,1)}), s8[4194304]{0:T(1024)(128)(4,1)S(1)}, s32[]{:S(2)}) async-start(s8[5767168]{0:T(1024)(128)(4,1)} %bitcast.102), calls=%async_computation.32 | async-start | bytes 8388608
  279.1 15.2 %slice-start.9 = ((s8[5767168]{0:T(1024)(128)(4,1)}), s8[1572864]{0:T(1024)(128)(4,1)S(1)}, s32[]{:S(2)}) async-start(s8[5767168]{0:T(1024)(128)(4,1)} %bitcast.100), calls=%async_computation.31 | async-start | bytes 3145728
  279.1 23.9 %slice-start.11 = ((s8[5767168]{0:T(1024)(128)(4,1)}), s8[1572864]{0:T(1024)(128)(4,1)S(1)}, s32[]{:S(2)}) async-start(s8[5767168]{0:T(1024)(128)(4,1)} %bitcast.102), calls=%async_computation.33 | async-start | bytes 3145728
  294.3 8.7 copy-start.47
  311.4 194.2 %reduce-scatter.10.cloned.1.call-start = ((), (), s32[]{:S(2)}) async-start(), calls=%async_computation.12 | async-start | bytes 5242880 | tf_op jit(solution)/shard_map/reduce_scatter | solution.py:858
  348.6 11.0 %copy-start.38 = (bf16[1024,2048]{1,0:T(8,128)(2,1)S(1)}, bf16[1024,2048]{1,0:T(8,128)(2,1)}, u32[]{:S(2)}) copy-start(bf16[1024,2048]{1,0:T(8,128)(2,1)} %all-gather.9.cloned.1.call-done) | copy-start | bytes 12582916
  348.6 26.1 %slice-start.6 = ((s8[5767168]{0:T(1024)(128)(4,1)}), s8[4194304]{0:T(1024)(128)(4,1)S(1)}, s32[]{:S(2)}) async-start(s8[5767168]{0:T(1024)(128)(4,1)} %bitcast.98), calls=%async_computation.28 | async-start | bytes 8388608
  359.6 15.1 %slice-start.7 = ((s8[5767168]{0:T(1024)(128)(4,1)}), s8[1572864]{0:T(1024)(128)(4,1)S(1)}, s32[]{:S(2)}) async-start(s8[5767168]{0:T(1024)(128)(4,1)} %bitcast.98), calls=%async_computation.29 | async-start | bytes 3145728
  382.9 21.0 %slice-start.12 = ((s8[5767168]{0:T(1024)(128)(4,1)}), s8[1572864]{0:T(1024)(128)(4,1)S(1)}, s32[]{:S(2)}) async-start(s8[5767168]{0:T(1024)(128)(4,1)} %bitcast.104), calls=%async_computation.34 | async-start | bytes 3145728
  394.1 9.9 slice-start.13
  394.1 9.9 copy-start.46
  412.6 12.1 %copy-start.45 = (bf16[1024,1408]{1,0:T(8,128)(2,1)S(1)}, bf16[1024,1408]{1,0:T(8,128)(2,1)}, u32[]{:S(2)}) copy-start(bf16[1024,1408]{1,0:T(8,128)(2,1)} %get-tuple-element.158) | copy-start | bytes 8650756
  412.6 253.3 %reduce-scatter.18.cloned.1.call-start = ((), (), s32[]{:S(2)}) async-start(), calls=%async_computation.17 | async-start | bytes 9437184 | tf_op jit(solution)/shard_map/reduce_scatter | solution.py:828
  412.6 12.1 %copy-start.39 = (bf16[1024,2048]{1,0:T(8,128)(2,1)S(1)}, bf16[1024,2048]{1,0:T(8,128)(2,1)}, u32[]{:S(2)}) copy-start(bf16[1024,2048]{1,0:T(8,128)(2,1)} %all-gather.9.cloned.1.call-done) | copy-start | bytes 12582916
  424.7 9.9 copy-start.36
  424.7 9.9 copy-start.43
  434.6 6.3 copy-start.35
  434.6 6.3 copy-start.44
  440.9 8.1 copy-start.48
  461.9 43.7 %copy-start.25 = (f32[2048]{0:T(1024)S(1)}, f32[2048]{0:T(1024)}, u32[]{:S(2)}) copy-start(f32[2048]{0:T(1024)} %param.27) | copy-start | bytes 24580
  461.9 43.7 %copy-start.31 = (f32[512]{0:T(512)S(1)}, f32[512]{0:T(512)}, u32[]{:S(2)}) copy-start(f32[512]{0:T(512)} %copy-done.30) | copy-start | bytes 6148
  474.7 35.2 %copy-start.16 = (bf16[512,2048]{1,0:T(8,128)(2,1)S(1)}, bf16[512,2048]{1,0:T(8,128)(2,1)}, u32[]{:S(2)}) copy-start(bf16[512,2048]{1,0:T(8,128)(2,1)} %param.31) | copy-start | bytes 6291460
  474.7 35.2 %copy-start.33 = (f32[512]{0:T(512)S(1)}, f32[512]{0:T(512)}, u32[]{:S(2)}) copy-start(f32[512]{0:T(512)} %get-tuple-element.169) | copy-start | bytes 6148
  509.9 4.9 copy-start.18
  521.7 385.7 %reduce-scatter.26.cloned.1.call-start = ((), (), s32[]{:S(2)}) async-start(), calls=%async_computation.21 | async-start | bytes 6488064 | tf_op jit(solution)/shard_map/reduce_scatter | solution.py:906
  522.4 387.4 %reduce-scatter.24.cloned.1.call-start = ((), (), s32[]{:S(2)}) async-start(), calls=%async_computation.20 | async-start | bytes 6488064 | tf_op jit(solution)/shard_map/reduce_scatter | solution.py:905
  523.2 389.0 %reduce-scatter.22.cloned.1.call-start = ((), (), s32[]{:S(2)}) async-start(), calls=%async_computation.19 | async-start | bytes 6488064 | tf_op jit(solution)/shard_map/reduce_scatter | solution.py:904
  523.8 400.0 %reduce-scatter.14.cloned.1.call-start = ((), (), s32[]{:S(2)}) async-start(), calls=%async_computation.15 | async-start | bytes 5242880 | tf_op jit(solution)/shard_map/reduce_scatter | solution.py:858
  535.9 10.2 copy-start.3
  574.1 432.4 %reduce-scatter.16.cloned.1.call-start = ((), (), s32[]{:S(2)}) async-start(), calls=%async_computation.16 | async-start | bytes 5242880 | tf_op jit(solution)/shard_map/reduce_scatter | solution.py:858
  574.7 461.8 %reduce-scatter.20.cloned.1.call-start = ((), (), s32[]{:S(2)}) async-start(), calls=%async_computation.18 | async-start | bytes 1310720 | tf_op jit(solution)/shard_map/reduce_scatter | solution.py:829
  574.7 57.9 %copy-start.11 = (bf16[512,2048]{1,0:T(8,128)(2,1)S(1)}, bf16[512,2048]{1,0:T(8,128)(2,1)}, u32[]{:S(2)}) copy-start(bf16[512,2048]{1,0:T(8,128)(2,1)} %copy-done.10) | copy-start | bytes 6291460
  574.7 59.8 %copy-start.41 = (f32[1,128]{1,0:T(1,128)S(1)}, f32[1,128]{1,0:T(1,128)}, u32[]{:S(2)}) copy-start(f32[1,128]{1,0:T(1,128)} %get-tuple-element.82) | copy-start | bytes 1540
  631.1 6.5 collective-permute-start.1
  639.2 10.8 %copy-start.17 = (bf16[3,512,2048]{2,1,0:T(8,128)(2,1)S(1)}, bf16[3,512,2048]{2,1,0:T(8,128)(2,1)}, u32[]{:S(2)}) copy-start(bf16[3,512,2048]{2,1,0:T(8,128)(2,1)} %add_dynamic-update-slice_fusion.right_ref) | copy-start | bytes 18874372
  639.2 20.4 %slice-start.4 = ((s8[8388608]{0:T(1024)(128)(4,1)}), s8[4194304]{0:T(1024)(128)(4,1)S(1)}, s32[]{:S(2)}) async-start(s8[8388608]{0:T(1024)(128)(4,1)} %bitcast.96), calls=%async_computation.26 | async-start | bytes 8388608
  650.0 9.7 slice-start.5
  659.6 6.2 copy-start.9
  659.7 6.2 copy-start.20
  659.7 6.2 copy-start.27
  659.7 6.2 copy-start.29
  676.5 225.0 %copy-start.32 = (f32[512]{0:T(512)S(1)}, f32[512]{0:T(512)}, u32[]{:S(2)}) copy-start(f32[512]{0:T(512)} %get-tuple-element.167) | copy-start | bytes 6148
  907.4 131.0 %copy-start.19 = (f32[3,64,2048]{2,1,0:T(8,128)S(1)}, f32[3,64,2048]{2,1,0:T(8,128)}, u32[]{:S(2)}) copy-start(f32[3,64,2048]{2,1,0:T(8,128)} %get-tuple-element.87) | copy-start | bytes 4718596
  923.8 115.8 %copy-start.21 = (bf16[256,2048]{1,0:T(8,128)(2,1)S(1)}, bf16[256,2048]{1,0:T(8,128)(2,1)}, u32[]{:S(2)}) copy-start(bf16[256,2048]{1,0:T(8,128)(2,1)} %reduce-scatter.14.cloned.1.call-done) | copy-start | bytes 3145732
  (14 other events, 29.4 us)
Sparse Core Ops, SparseCore 0:
  10.7 83.4 all-gather.6
  96.3 81.1 all-gather.4
  179.7 87.4 all-gather.10
  269.3 79.2 all-gather.8
  350.7 75.2 reduce-scatter.11
  428.3 77.2 reduce-scatter.9
  521.8 71.7 reduce-scatter.17
  597.5 59.0 reduce-scatter.25
  660.0 80.0 reduce-scatter.23
  743.8 82.4 reduce-scatter.21
  828.6 95.1 reduce-scatter.13
  926.0 80.4 reduce-scatter.15
  1008.8 27.6 reduce-scatter.19

commit v4 on v3

--- a/solution.py
+++ b/solution.py
@@ -784,6 +784,196 @@
     )(left, right, small)
 
 
+def ffn_grads_kernel(*refs):
+    lefts = [refs[0:HALVES], refs[0:HALVES], refs[HALVES : 2 * HALVES]]
+    rights = [refs[(2 + m) * HALVES : (3 + m) * HALVES] for m in range(3)]
+    (
+        out_ref, left_buf, right_buf, away, landed, total, got2, got3,
+        left_sem, right_sem, send1, recv1, send2, recv2, send3, recv3,
+    ) = refs[5 * HALVES :]
+    dp = lax.axis_index("dp")
+    core, x, y = dp % 2, (dp // 2) % 2, dp // 4
+    rows = total.shape[2]
+    half = rows // 2
+    part = left_buf.shape[1] // HALVES
+    sib = dp + 1 - 2 * core
+    flip_x = dp + 2 * (1 - 2 * x)
+    flip_y = dp + 4 * (1 - 2 * y)
+    barrier = pltpu.get_barrier_semaphore()
+    for target in (sib, flip_x, flip_y):
+        pl.semaphore_signal(barrier, inc=1, device_id={"dp": target}, device_id_type=MESH)
+
+    def load_left(m, k, start):
+        own = k // 4
+        block = (k % 4) * 2 + own * core + (1 - own) * (1 - core)
+        lanes = pl.ds(pl.multiple_of(block * rows, rows), rows)
+        for at in range(HALVES):
+            copy = pltpu.make_async_copy(
+                lefts[m][at].at[:, lanes], left_buf.at[k % 2, at * part : (at + 1) * part], left_sem.at[k % 2, at]
+            )
+            if start:
+                copy.start()
+            else:
+                copy.wait()
+
+    def load_right(m, start):
+        for at in range(HALVES):
+            copy = pltpu.make_async_copy(
+                rights[m][at], right_buf.at[m % 2, at * part : (at + 1) * part], right_sem.at[m % 2, at]
+            )
+            if start:
+                copy.start()
+            else:
+                copy.wait()
+
+    def send(src, dst, send_sem, recv_sem, target):
+        return pltpu.make_async_remote_copy(
+            src_ref=src, dst_ref=dst, send_sem=send_sem, recv_sem=recv_sem,
+            device_id={"dp": target}, device_id_type=MESH,
+        )
+
+    def copy1(m, stripe):
+        return send(away.at[m, stripe], landed.at[m, stripe], send1.at[m, stripe], recv1.at[m, stripe], sib)
+
+    def band(h):
+        return pl.ds(h * half, half)
+
+    def order(h):
+        if h == 0:
+            return (lambda j: 2 * j + 1 - x), (lambda j: 2 * j + x), flip_x, flip_y, 1 - y, y
+        return (lambda j: 2 * (1 - y) + j), (lambda j: 2 * y + j), flip_y, flip_x, 1 - x, x
+
+    def copy2(m, h, j):
+        gone, _, target, _, _, _ = order(h)
+        return send(
+            total.at[m, gone(j), band(h)], got2.at[m, h, j], send2.at[2 * m + h, j], recv2.at[2 * m + h, j], target
+        )
+
+    def copy3(m, h):
+        _, kept, _, target, far, _ = order(h)
+        return send(total.at[m, kept(far), band(h)], got3.at[m, h], send3.at[m, h], recv3.at[m, h], target)
+
+    def add_to(dst, src):
+        step = 32
+
+        def one(at, _):
+            at = pl.ds(pl.multiple_of(at * step, step), step)
+            dst[at, :] = (dst[at, :].astype(F32) + src[at, :].astype(F32)).astype(dst.dtype)
+            return 0
+
+        lax.fori_loop(0, dst.shape[0] // step, one, 0)
+
+    def compute(m):
+        load_right(m, False)
+        if m + 1 < 3:
+            load_right(m + 1, True)
+
+        def one(k, _):
+            @pl.when(k < 7)
+            def _():
+                load_left(m, k + 1, True)
+
+            if m + 1 < 3:
+                @pl.when(k == 7)
+                def _():
+                    load_left(m + 1, 0, True)
+
+            load_left(m, k, False)
+            value = lax.dot_general(
+                left_buf[k % 2], right_buf[m % 2], (((0,), (0,)), ((), ())), preferred_element_type=F32
+            ).astype(BF16)
+
+            @pl.when(k < 4)
+            def _():
+                away[m, k] = value
+                copy1(m, k).start()
+
+            @pl.when(k >= 4)
+            def _():
+                total[m, k - 4] = value
+
+            return 0
+
+        lax.fori_loop(0, 8, one, 0)
+
+        def join(stripe, _):
+            copy1(m, stripe).wait()
+            add_to(total.at[m, stripe], landed.at[m, stripe])
+            return 0
+
+        lax.fori_loop(0, 4, join, 0)
+        for h in range(2):
+            for j in range(2):
+                copy2(m, h, j).start()
+
+    def second(m):
+        for h in range(2):
+            _, kept, _, _, far, near = order(h)
+            for j in range(2):
+                copy2(m, h, j).wait()
+            add_to(total.at[m, kept(far), band(h)], got2.at[m, h, far])
+            copy3(m, h).start()
+            add_to(total.at[m, kept(near), band(h)], got2.at[m, h, near])
+
+    def third(m):
+        for h in range(2):
+            _, kept, _, _, _, near = order(h)
+            copy3(m, h).wait()
+            step = 32
+
+            def one(at, _):
+                at = at * step
+                value = total[m, kept(near), pl.ds(pl.multiple_of(h * half + at, step), step), :].astype(F32)
+                value = value + got3[m, h, pl.ds(pl.multiple_of(at, step), step), :].astype(F32)
+                out_ref[m, pl.ds(pl.multiple_of(h * half + at, step), step), :] = value
+                return 0
+
+            lax.fori_loop(0, half // step, one, 0)
+
+    load_right(0, True)
+    load_left(0, 0, True)
+    pl.semaphore_wait(barrier, 3)
+    compute(0)
+    compute(1)
+    second(0)
+    compute(2)
+    third(0)
+    second(1)
+    third(1)
+    second(2)
+    third(2)
+
+
+def ffn_grads(lefts, rights):
+    part, height = lefts[0][0].shape
+    width = rights[0][0].shape[1]
+    rows = height // 8
+    half = rows // 2
+    dma = pltpu.SemaphoreType.DMA
+    operands = [ref for group in (*lefts, *rights) for ref in group]
+    return pl.pallas_call(
+        ffn_grads_kernel,
+        in_specs=[pl.BlockSpec(memory_space=pl.ANY)] * len(operands),
+        out_specs=pl.BlockSpec(memory_space=pltpu.VMEM),
+        out_shape=jax.ShapeDtypeStruct((3, rows, width), F32),
+        scratch_shapes=[
+            pltpu.VMEM((2, HALVES * part, rows), BF16),
+            pltpu.VMEM((2, HALVES * part, width), BF16),
+            pltpu.VMEM((3, 4, rows, width), BF16),
+            pltpu.VMEM((3, 4, rows, width), BF16),
+            pltpu.VMEM((3, 4, rows, width), BF16),
+            pltpu.VMEM((3, 2, 2, half, width), BF16),
+            pltpu.VMEM((3, 2, half, width), BF16),
+            dma((2, HALVES)), dma((2, HALVES)), dma((3, 4)), dma((3, 4)),
+            dma((6, 2)), dma((6, 2)), dma((3, 2)), dma((3, 2)),
+        ],
+        compiler_params=pltpu.CompilerParams(
+            collective_id=4, has_side_effects=True, vmem_limit_bytes=60 * 1024 * 1024
+        ),
+        name="ffn_grads",
+    )(*operands)
+
+
 def shifted(value, axis, steps):
     count = lax.axis_size(axis)
     first, last = (max(0, -steps), min(count, count - steps))
@@ -893,18 +1083,18 @@
         d_up.append((d_act * silu_gate).astype(BF16))
         d_normed_parts.append(scatter((dot_nt(d_gate[at], w_gate) + dot_nt(d_up[at], w_up)).astype(BF16)))
     out_parts = [matmul(act, w_down).astype(BF16) for act in activation]
-    down_term_grad = sum(dot_tn(a, c) for a, c in zip(activation, cot)).astype(BF16)
-    gate_term_grad = sum(dot_tn(a, c) for a, c in zip(gathered, d_gate)).astype(BF16)
-    up_term_grad = sum(dot_tn(a, c) for a, c in zip(gathered, d_up)).astype(BF16)
-    (d_normed_parts, out_parts, down_term_grad, gate_term_grad, up_term_grad) = lax.optimization_barrier(
-        (d_normed_parts, out_parts, down_term_grad, gate_term_grad, up_term_grad)
-    )
+    if lax.axis_size("dp") == 8:
+        ffn_sums = ffn_grads((gathered, cot), (d_gate, d_up, activation))
+    else:
+        ffn_sums = [
+            lax.psum_scatter(
+                sum(dot_tn(a, c) for a, c in zip(left, right)).astype(BF16), "dp", scatter_dimension=0, tiled=True
+            )
+            for left, right in ((gathered, d_gate), (gathered, d_up), (cot, activation))
+        ]
+    d_normed_parts, out_parts, ffn_sums = lax.optimization_barrier((d_normed_parts, out_parts, ffn_sums))
+    grad_gate, grad_up, grad_down = ffn_sums[0].astype(F32), ffn_sums[1].astype(F32), ffn_sums[2].astype(F32).T
     d_normed_mlp = jnp.concatenate(d_normed_parts, axis=0).astype(F32)
-    grad_gate, grad_up, grad_down = (
-        lax.psum_scatter(gate_term_grad, "dp", scatter_dimension=0, tiled=True).astype(F32),
-        lax.psum_scatter(up_term_grad, "dp", scatter_dimension=0, tiled=True).astype(F32),
-        lax.psum_scatter(down_term_grad, "dp", scatter_dimension=1, tiled=True).astype(F32),
-    )
     d_hidden_norm, mlp_gain_term = norm_back(hidden, mlp_gain, d_normed_mlp, 1e-06)
     d_hidden = grad_out.astype(F32) + d_hidden_norm
     d_branch = d_hidden.astype(BF16)

time: 1060 us -> 888 us (0.84)
  waiting for transfers between devices: 304 us -> 151 us
  matrix products: 274 us -> 220 us
  Pallas kernels: 387 us -> 429 us
    reduce_scatter x4, waiting for transfers between devices: 123 us -> 0.04 us  [scatter(): return lax.psum_scatter(rows, 'narrow', scatter_dimension=0, tiled=True)]
    pallas_call x0 -> x1, Pallas kernels: none -> 98.8 us  [ffn_grads(): pl.pallas_call(ffn_grads_kernel, in_specs=[pl.BlockSpec(memory_space=pl.A...]
    dot_general x7 -> x1, matrix products: 68.8 us -> 6.91 us  [dot_tn(): return jnp.einsum('rd,re->de', left, right, preferred_element_type=F32)]
    pallas_call x1, Pallas kernels: 219 us -> 166 us  [reduce_products(): pl.pallas_call(reduce_kernel, in_specs=[pl.BlockSpec(memory_space=pltpu.V...]
    reduce_scatter x1, waiting for transfers between devices: 30 us -> 0.02 us  [scatter_all(): return lax.psum_scatter(part, 'narrow', scatter_dimension=dim, tiled=True)]
  transfers between devices with their start and end apart: 15 -> 12, of which waited for: 9 -> 5; matrix products, arithmetic and copies ran while one was open for 28% -> 27% of each run, Pallas kernels for 37% -> 49%
where the time goes in v4:
time: 888 us; the launch traced here: 881 us
  Pallas kernels  429 us (48%)
  matrix products  220 us (25%)
  waiting for transfers between devices  151 us (17%)
  local copies, waits for them, and re-layouts  32.2 us (4%)
  other arithmetic  25.2 us (3%)
  between operations  15.4 us (2%)
    pallas_call x1, Pallas kernels, reduce_products(): pl.pallas_call(reduce_kernel, in_specs=[pl.BlockSpec(memory_space=pltpu.V...  166 us
    all_gather x4, waiting for transfers between devices, gather(): return lax.all_gather(rows, 'narrow', axis=0, tiled=True)  142 us
    dot_general x11, matrix products, matmul(): return jnp.dot(left, right, preferred_element_type=F32)  102 us
    pallas_call x1, Pallas kernels, ffn_grads(): pl.pallas_call(ffn_grads_kernel, in_specs=[pl.BlockSpec(memory_space=pl.A...  98.8 us
    dot_general x8, matrix products, dot_nt(): return jnp.einsum('re,de->rd', left, right, preferred_element_type=F32)  81.3 us
    pallas_call x1, Pallas kernels, mixer_backward(): pl.pallas_call(backward_kernel, grid=(heads // HEADS_STEP,), in_specs=[wh...  55.7 us
    pallas_call x1, Pallas kernels, mixer_forward(): pl.pallas_call(forward_kernel, grid=(heads // HEADS_STEP,), in_specs=[who...  49.7 us
    pallas_call x2, Pallas kernels, carry_chain(): pl.pallas_call(functools.partial(chain_kernel, axis, forward), in_specs=[...  41.2 us
  transfers between devices with their start and end apart: 12, of which 5 were waited for; matrix products, arithmetic and copies ran while one was open for 27% of the time, Pallas kernels for 49%

profile of v4, /device:TPU:0, one launch (start us, length us, event | category | flops | bytes accessed | tf_op | source)
XLA Modules:
  0.0 880.5 jit_solution(14958762113336094083)
XLA Ops:
  7.3 3.2 fusion.33
  13.6 7.9 fusion.37.value_ref
  21.6 4.5 fusion.35.query_ref
  26.2 4.5 fusion.36.key_ref
  30.7 2.0 copy-done.14
  32.8 5.4 collective-permute-start
  38.5 3.0 fusion.34.beta_ref
  41.5 1.1 collective-permute-done.halo_ref
  42.6 0.8 broadcast_in_dim.19.since_ref
  43.4 49.7 %mixer_forward.1 = (bf16[512,2048]{1,0:T(8,128)(2,1)}, bf16[512,2048]{1,0:T(8,128)(2,1)}, bf16[512,2048]{1,0:T(8,128)(2,1)}, bf16[512,2048]{1,0:T(8,128)(2,1)}, ...) custom-call(s32[512,128]{1,0:T(8,128)} %broadcast_in_dim.19.since_ref, ...), custom_call_target="tpu_custom_call" | custom-call | tf_op jit(solution)/shard_map/mixer_forward/pallas_call | solution.py:180
  93.1 1.3 slice.155.map_ref
  94.4 1.5 slice.101.add_ref
  96.0 19.7 %carry_forward.1.entry_ref = f32[16,128,128]{2,1,0:T(8,128)S(1)} custom-call(bf16[16,128,128]{2,1,0:T(8,128)(2,1)S(1)} %slice.155.map_ref, f32[16,128,128]{2,1,0:T(8,128)S(1)} %slice.101.add_ref), custom_call_target="tpu_custom_call" | custom-call | tf_op jit(solution)/shard_map/carry_forward/pallas_call | solution.py:487
  115.7 1.0 copy-done.1
  116.7 7.7 mixer_join.1
  124.4 7.8 multiply_reduce_fusion
  132.8 1.3 copy-done.6
  134.6 43.0 %all-gather.7.cloned.1.call-done.refs_3_ = bf16[1024,2048]{1,0:T(8,128)(2,1)} async-done(((bf16[256,2048]{1,0:T(8,128)(2,1)}), bf16[1024,2048]{1,0:T(8,128)(2,1)}) %all-gather.7.cloned.1.call-update) | async-done | bytes 4194320 | tf_op jit(solution)/shard_map/all_gather | solution.py:1045
  177.6 1.4 fusion.32
  179.1 11.9 %fusion.41 = f32[1024,1408]{1,0:T(8,128)} fusion(bf16[1024,2048]{1,0:T(8,128)(2,1)} %all-gather.7.cloned.1.call-done.refs_3_, bf16[1408,2048]{1,0:T(8,128)(2,1)} %param.30), kind=kOutput, calls=%fused_computation.95 | convolution fusion | flops 5905580032 | bytes 15728640 | tf_op jit(solution)/shard_map/rd,fd->rf/dot_general | solution.py:1079
  191.0 10.5 %fusion.38 = f32[1024,1408]{1,0:T(8,128)} fusion(bf16[1024,2048]{1,0:T(8,128)(2,1)S(1)} %copy-done.18, bf16[1408,2048]{1,0:T(8,128)(2,1)} %param.30), kind=kOutput, calls=%fused_computation.92 | convolution fusion | flops 5905580032 | bytes 15728640 | tf_op jit(solution)/shard_map/rd,fd->rf/dot_general | solution.py:1079
  201.8 65.6 %all-gather.11.cloned.1.call-done.refs_1_ = bf16[1024,2048]{1,0:T(8,128)(2,1)} async-done(((bf16[256,2048]{1,0:T(8,128)(2,1)}), bf16[1024,2048]{1,0:T(8,128)(2,1)}) %all-gather.11.cloned.1.call-update) | async-done | bytes 4194320 | tf_op jit(solution)/shard_map/all_gather | solution.py:1045
  267.4 11.9 %fusion.42 = f32[1024,1408]{1,0:T(8,128)} fusion(bf16[1024,2048]{1,0:T(8,128)(2,1)} %all-gather.11.cloned.1.call-done.refs_1_, bf16[2048,1408]{1,0:T(8,128)(2,1)} %param.28), kind=kOutput, calls=%fused_computation.96 | convolution fusion | flops 5905580032 | bytes 15728640 | tf_op jit(solution)/shard_map/dot_general | solution.py:984
  279.3 14.2 %multiply_convert_fusion = (bf16[1024,1408]{1,0:T(8,128)(2,1)}, bf16[1024,1408]{1,0:T(8,128)(2,1)S(1)}, bf16[1024,1408]{1,0:T(8,128)(2,1)S(1)}) fusion(f32[1024,1408]{1,0:T(8,128)} %fusion.42, f32[1024,1408]{1,0:T(8,128)} %fusion.41, bf16[1024,2048]{1,0:T(8,128)(2,1)S(1)} %copy-done.19, bf16[2048,1408]{1,0:T(8,128)(2,1)} %param.29), kind=kOutput, calls=%fused_computation.9 | convolution fusion | flops 5927206912 | bytes 30146560 | tf_op jit(solution)/shard_map/dot_general | solution.py:984
  293.6 8.9 %fusion.43 = f32[1024,2048]{1,0:T(8,128)} fusion(bf16[1024,1408]{1,0:T(8,128)(2,1)S(1)} %get-tuple-element.151.refs_5_, bf16[2048,1408]{1,0:T(8,128)(2,1)S(1)} %bitcast.97), kind=kOutput, calls=%fused_computation.97 | convolution fusion | flops 5905580032 | bytes 17039360 | tf_op jit(solution)/shard_map/re,de->rd/dot_general | solution.py:992
  302.5 12.3 %add_convert_fusion = bf16[1024,2048]{1,0:T(8,128)(2,1)} fusion(f32[1024,2048]{1,0:T(8,128)} %fusion.43, bf16[1024,1408]{1,0:T(8,128)(2,1)S(1)} %get-tuple-element.152.refs_7_, bf16[2048,1408]{1,0:T(8,128)(2,1)} %param.29), kind=kOutput, calls=%fused_computation.6 | convolution fusion | flops 5909774336 | bytes 21233664 | tf_op jit(solution)/shard_map/re,de->rd/dot_general | solution.py:992
  315.0 33.7 %all-gather.9.cloned.1.call-done.refs_0_ = bf16[1024,2048]{1,0:T(8,128)(2,1)} async-done(((bf16[256,2048]{1,0:T(8,128)(2,1)}), bf16[1024,2048]{1,0:T(8,128)(2,1)}) %all-gather.9.cloned.1.call-update) | async-done | bytes 4194320 | tf_op jit(solution)/shard_map/all_gather | solution.py:1045
  348.7 11.9 %fusion.39 = f32[1024,1408]{1,0:T(8,128)} fusion(bf16[1024,2048]{1,0:T(8,128)(2,1)} %all-gather.9.cloned.1.call-done.refs_0_, bf16[2048,1408]{1,0:T(8,128)(2,1)} %param.28), kind=kOutput, calls=%fused_computation.93 | convolution fusion | flops 5905580032 | bytes 15728640 | tf_op jit(solution)/shard_map/dot_general | solution.py:984
  360.6 14.3 %multiply_convert_fusion.1 = (bf16[1024,1408]{1,0:T(8,128)(2,1)}, bf16[1024,1408]{1,0:T(8,128)(2,1)S(1)}, bf16[1024,1408]{1,0:T(8,128)(2,1)S(1)}) fusion(f32[1024,1408]{1,0:T(8,128)} %fusion.39, f32[1024,1408]{1,0:T(8,128)} %fusion.38, bf16[1024,2048]{1,0:T(8,128)(2,1)S(1)} %copy-done.20, bf16[2048,1408]{1,0:T(8,128)(2,1)} %param.29), kind=kOutput, calls=%fused_computation.10 | convolution fusion | flops 5927206912 | bytes 30146560 | tf_op jit(solution)/shard_map/dot_general | solution.py:984
  374.9 8.9 %fusion.40 = f32[1024,2048]{1,0:T(8,128)} fusion(bf16[1024,1408]{1,0:T(8,128)(2,1)S(1)} %get-tuple-element.154.refs_4_, bf16[2048,1408]{1,0:T(8,128)(2,1)S(1)} %bitcast.99), kind=kOutput, calls=%fused_computation.94 | convolution fusion | flops 5905580032 | bytes 17039360 | tf_op jit(solution)/shard_map/re,de->rd/dot_general | solution.py:992
  383.9 12.3 %add_convert_fusion.1 = bf16[1024,2048]{1,0:T(8,128)(2,1)} fusion(f32[1024,2048]{1,0:T(8,128)} %fusion.40, bf16[1024,1408]{1,0:T(8,128)(2,1)S(1)} %get-tuple-element.155.refs_6_, bf16[2048,1408]{1,0:T(8,128)(2,1)} %param.29), kind=kOutput, calls=%fused_computation.7 | convolution fusion | flops 5909774336 | bytes 21233664 | tf_op jit(solution)/shard_map/re,de->rd/dot_general | solution.py:992
  396.6 98.8 %ffn_grads.1 = f32[3,256,1408]{2,1,0:T(8,128)} custom-call(bf16[1024,2048]{1,0:T(8,128)(2,1)} %all-gather.9.cloned.1.call-done.refs_0_, bf16[1024,2048]{1,0:T(8,128)(2,1)} %all-gather.11.cloned.1.call-done.refs_1_, bf16[1024,2048]{1,0:T(8,128)(2,1)} %all-gather.5.cloned.1.call-done.refs_2_, bf16[1024,2048]{1,0:T(8,128)(2,1)} %all-gather.7.cloned.1.call-done.refs_3_, ...), custom_call_target="tpu_custom_call" | custom-call | tf_op jit(solution)/shard_map/ffn_grads/pallas_call | solution.py:954
  495.4 10.8 %convolution_convert_fusion.1 = bf16[1024,2048]{1,0:T(8,128)(2,1)} fusion(bf16[1024,1408]{1,0:T(8,128)(2,1)S(1)} %copy-done.21, bf16[1408,2048]{1,0:T(8,128)(2,1)} %param.30), kind=kOutput, calls=%fused_computation.42 | convolution fusion | flops 5907677184 | bytes 12845056 | tf_op jit(solution)/shard_map/dot_general | solution.py:984
  506.2 11.1 %convolution_convert_fusion.2 = bf16[1024,2048]{1,0:T(8,128)(2,1)} fusion(bf16[1024,1408]{1,0:T(8,128)(2,1)} %get-tuple-element.153.refs_8_, bf16[1408,2048]{1,0:T(8,128)(2,1)} %param.30), kind=kOutput, calls=%fused_computation.43 | convolution fusion | flops 5907677184 | bytes 12845056 | tf_op jit(solution)/shard_map/dot_general | solution.py:984
  517.4 4.2 fusion.8
  522.0 2.9 fusion.5
  525.0 2.0 copy-done.15
  526.9 6.9 convolution_convert_fusion
  533.9 12.1 %fusion.23.up_ref = f32[512,2048]{1,0:T(8,128)} fusion(bf16[2048,2048]{1,0:T(8,128)(2,1)} %param.26, f32[512,2048]{1,0:T(8,128)} %copy-done.15), kind=kOutput, calls=%fused_computation.56 | convolution fusion | flops 4296015872 | bytes 16777216 | tf_op jit(solution)/shard_map/re,de->rd/dot_general | solution.py:992
  546.1 10.1 %mixer_core_back.1 = (bf16[512,2048]{1,0:T(8,128)(2,1)}, f32[16,128,128]{2,1,0:T(8,128)}, f32[1,128]{1,0:T(1,128)}) custom-call(bf16[512,2048]{1,0:T(8,128)(2,1)} %get-tuple-element.57.out_add_ref, bf16[512,2048]{1,0:T(8,128)(2,1)} %get-tuple-element.58.out_map_ref, f32[16,128,128]{2,1,0:T(8,128)} %copy-done.1, f32[1,128]{1,0:T(1,128)} %bitcast.88, ...), custom_call_target="tpu_custom_call" | custom-call | tf_op jit(solution)/shard_map/mixer_core_back/pallas_call | solution.py:250
  556.2 1.3 copy-done.5
  557.4 21.4 %carry_backward.1.exit_ref = f32[16,128,128]{2,1,0:T(8,128)S(1)} custom-call(bf16[16,128,128]{2,1,0:T(8,128)(2,1)S(1)} %copy-done.3, f32[16,128,128]{2,1,0:T(8,128)S(1)} %copy-done.5), custom_call_target="tpu_custom_call" | custom-call | tf_op jit(solution)/shard_map/carry_backward/pallas_call | solution.py:487
  578.9 1.0 copy-done.4
  580.7 55.7 %mixer_backward.1 = (bf16[3,512,2048]{2,1,0:T(8,128)(2,1)}, f32[3,8,2048]{2,1,0:T(8,128)}, f32[3,4,2048]{2,1,0:T(4,128)}, f32[512,16]{1,0:T(8,128)}) custom-call(s32[512,128]{1,0:T(8,128)} %broadcast_in_dim.19.since_ref, f32[512,16]{1,0:T(8,128)} %fusion.34.beta_ref, f32[512,2048]{1,0:T(8,128)} %copy-done.13, f32[512,2048]{1,0:T(8,128)} %copy-done.14, ...), custom_call_target="tpu_custom_call" | custom-call | tf_op jit(solution)/shard_map/mixer_backward/pallas_call | solution.py:393
  636.4 0.9 convert_element_type.92
  637.4 1.4 collective-permute-start.1
  638.8 1.9 slice_bitcast_fusion.6
  642.5 1.5 copy.57
  644.1 6.1 collective-permute-done.1
  650.1 1.5 add_dynamic-update-slice_fusion.right_ref
  651.7 10.7 %fusion.19 = f32[512,2048]{1,0:T(8,128)} fusion(bf16[2048,2048]{1,0:T(8,128)(2,1)} %param.22, bf16[3,512,2048]{2,1,0:T(8,128)(2,1)} %add_dynamic-update-slice_fusion.right_ref), kind=kOutput, calls=%fused_computation.45 | convolution fusion | flops 4294967296 | bytes 14680064 | tf_op jit(solution)/shard_map/re,de->rd/dot_general | solution.py:992
  662.4 9.9 %fusion.20 = f32[512,2048]{1,0:T(8,128)} fusion(bf16[2048,2048]{1,0:T(8,128)(2,1)} %param.21, bf16[3,512,2048]{2,1,0:T(8,128)(2,1)S(1)} %copy-done.17), kind=kOutput, calls=%fused_computation.47 | convolution fusion | flops 4294967296 | bytes 14680064 | tf_op jit(solution)/shard_map/re,de->rd/dot_general | solution.py:992
  672.4 6.2 fusion.21
  678.6 6.9 fusion.18
  686.0 1.0 pad.11.small_ref
  687.0 165.7 %reduce_products.1 = (f32[3,64,2048]{2,1,0:T(8,128)}, f32[64,128]{1,0:T(8,128)}) custom-call(bf16[512,2048]{1,0:T(8,128)(2,1)} %copy-done.10, bf16[3,512,2048]{2,1,0:T(8,128)(2,1)} %add_dynamic-update-slice_fusion.right_ref, f32[2048,128]{1,0:T(8,128)} %pad.11.small_ref), custom_call_target="tpu_custom_call" | custom-call | tf_op jit(solution)/shard_map/reduce_products/pallas_call | solution.py:754
  852.7 0.8 slice_bitcast_fusion.12
  854.3 1.4 copy.56
  855.7 1.4 slice_reduce_fusion.2
  857.1 1.5 slice_reduce_fusion
  858.6 5.9 fusion.17
  864.6 2.7 slice_bitcast_fusion.9
  867.3 1.8 convert_bitcast_fusion
  869.0 4.2 add_convert_fusion.2
  (164 shorter events, 9.9 us)
Async XLA Ops:
  7.2 31.3 %copy-start = (bf16[2048,16]{0,1:T(8,128)(2,1)S(1)}, bf16[2048,16]{0,1:T(8,128)(2,1)}, u32[]{:S(2)}) copy-start(bf16[2048,16]{0,1:T(8,128)(2,1)} %param.23) | copy-start | bytes 196612
  7.2 4.1 copy-start.8
  7.2 5.8 copy-start.34
  7.2 127.3 %all-gather.5.cloned.1.call-start = ((), (), s32[]{:S(2)}) async-start(), calls=%async_computation.6 | async-start | bytes 5242880 | tf_op jit(solution)/shard_map/all_gather | solution.py:1045
  10.5 167.1 %all-gather.7.cloned.1.call-start = ((), (), s32[]{:S(2)}) async-start(), calls=%async_computation.7 | async-start | bytes 5242880 | tf_op jit(solution)/shard_map/all_gather | solution.py:1045
  11.3 256.1 %all-gather.11.cloned.1.call-start = ((), (), s32[]{:S(2)}) async-start(), calls=%async_computation.10 | async-start | bytes 5242880 | tf_op jit(solution)/shard_map/all_gather | solution.py:1045
  13.0 8.6 slice-start.4
  13.6 12.5 %copy-start.10 = (bf16[512,2048]{1,0:T(8,128)(2,1)}, bf16[512,2048]{1,0:T(8,128)(2,1)S(1)}, u32[]{:S(2)}) copy-start(bf16[512,2048]{1,0:T(8,128)(2,1)S(1)} %fusion.11.left_ref) | copy-start | bytes 6291460
  13.6 8.0 slice-start.5
  13.6 12.5 %slice-start.2 = ((s8[8388608]{0:T(1024)(128)(4,1)}), s8[4194304]{0:T(1024)(128)(4,1)S(1)}, s32[]{:S(2)}) async-start(s8[8388608]{0:T(1024)(128)(4,1)} %bitcast.90), calls=%async_computation.18 | async-start | bytes 8388608
  21.5 4.6 copy-start.12
  21.6 4.6 slice-start.3
  26.2 4.5 copy-start.13
  26.2 12.0 %copy-start.42 = (s32[1,4]{1,0:T(1,128)S(1)}, s32[1,4]{1,0:T(1,128)}, u32[]{:S(2)}) copy-start(s32[1,4]{1,0:T(1,128)} %param.18) | copy-start | bytes 52
  30.7 2.1 copy-start.14
  32.8 9.8 %collective-permute-start = (bf16[3,8,2048]{2,1,0:T(8,128)(2,1)S(1)}, bf16[3,8,2048]{2,1,0:T(8,128)(2,1)S(1)}, u32[]{:S(2)}, u32[]{:S(2)}) collective-permute-start(bf16[3,8,2048]{2,1,0:T(8,128)(2,1)S(1)} %pad_maximum_fusion.1), channel_id=1, source_target_pairs={{0,1},{1,2},{2,3},{4,5},{5,6},{6,7},{8,9},{9,10},{10,11},{12,13},{... | collective-permute-start | bytes 294920 | tf_op jit(solution)/shard_map/ppermute | solution.py:980
  94.4 21.3 %copy-start.2 = (bf16[16,128,128]{2,1,0:T(8,128)(2,1)}, bf16[16,128,128]{2,1,0:T(8,128)(2,1)S(1)}, u32[]{:S(2)}) copy-start(bf16[16,128,128]{2,1,0:T(8,128)(2,1)S(1)} %slice.155.map_ref) | copy-start | bytes 1572868
  124.3 9.8 %copy-start.32 = (f32[2048]{0:T(1024)S(1)}, f32[2048]{0:T(1024)}, u32[]{:S(2)}) copy-start(f32[2048]{0:T(1024)} %param.27) | copy-start | bytes 24580
  132.1 2.0 copy-start.6
  132.8 1.3 copy-start.38
  179.1 169.7 %all-gather.9.cloned.1.call-start = ((), (), s32[]{:S(2)}) async-start(), calls=%async_computation.8 | async-start | bytes 5242880 | tf_op jit(solution)/shard_map/all_gather | solution.py:1045
  179.1 11.9 %copy-start.18 = (bf16[1024,2048]{1,0:T(8,128)(2,1)S(1)}, bf16[1024,2048]{1,0:T(8,128)(2,1)}, u32[]{:S(2)}) copy-start(bf16[1024,2048]{1,0:T(8,128)(2,1)} %all-gather.5.cloned.1.call-done.refs_2_) | copy-start | bytes 12582916
  201.6 315.8 %reduce-scatter.9.cloned.1.call-start = ((), (), s32[]{:S(2)}) async-start(), calls=%async_computation.11 | async-start | bytes 5242880 | tf_op jit(solution)/shard_map/reduce_scatter | solution.py:1048
  267.4 11.9 %copy-start.19 = (bf16[1024,2048]{1,0:T(8,128)(2,1)S(1)}, bf16[1024,2048]{1,0:T(8,128)(2,1)}, u32[]{:S(2)}) copy-start(bf16[1024,2048]{1,0:T(8,128)(2,1)} %all-gather.11.cloned.1.call-done.refs_1_) | copy-start | bytes 12582916
  267.4 26.1 %slice-start.8 = ((s8[5767168]{0:T(1024)(128)(4,1)}), s8[4194304]{0:T(1024)(128)(4,1)S(1)}, s32[]{:S(2)}) async-start(s8[5767168]{0:T(1024)(128)(4,1)} %bitcast.96), calls=%async_computation.24 | async-start | bytes 8388608
  279.3 14.2 %slice-start.9 = ((s8[5767168]{0:T(1024)(128)(4,1)}), s8[1572864]{0:T(1024)(128)(4,1)S(1)}, s32[]{:S(2)}) async-start(s8[5767168]{0:T(1024)(128)(4,1)} %bitcast.96), calls=%async_computation.25 | async-start | bytes 3145728
  293.5 9.0 %copy-start.22 = (bf16[1024,1408]{1,0:T(8,128)(2,1)}, bf16[1024,1408]{1,0:T(8,128)(2,1)S(1)}, u32[]{:S(2)}) copy-start(bf16[1024,1408]{1,0:T(8,128)(2,1)S(1)} %get-tuple-element.151.refs_5_) | copy-start | bytes 8650756
  293.5 9.0 %copy-start.23 = (bf16[1024,1408]{1,0:T(8,128)(2,1)}, bf16[1024,1408]{1,0:T(8,128)(2,1)S(1)}, u32[]{:S(2)}) copy-start(bf16[1024,1408]{1,0:T(8,128)(2,1)S(1)} %get-tuple-element.152.refs_7_) | copy-start | bytes 8650756
  314.8 202.6 %reduce-scatter.7.cloned.1.call-start = ((), (), s32[]{:S(2)}) async-start(), calls=%async_computation.9 | async-start | bytes 5242880 | tf_op jit(solution)/shard_map/reduce_scatter | solution.py:1048
  348.7 11.9 %copy-start.20 = (bf16[1024,2048]{1,0:T(8,128)(2,1)S(1)}, bf16[1024,2048]{1,0:T(8,128)(2,1)}, u32[]{:S(2)}) copy-start(bf16[1024,2048]{1,0:T(8,128)(2,1)} %all-gather.9.cloned.1.call-done.refs_0_) | copy-start | bytes 12582916
  348.7 26.2 %slice-start.10 = ((s8[5767168]{0:T(1024)(128)(4,1)}), s8[4194304]{0:T(1024)(128)(4,1)S(1)}, s32[]{:S(2)}) async-start(s8[5767168]{0:T(1024)(128)(4,1)} %bitcast.98), calls=%async_computation.26 | async-start | bytes 8388608
  360.6 14.3 %slice-start.11 = ((s8[5767168]{0:T(1024)(128)(4,1)}), s8[1572864]{0:T(1024)(128)(4,1)S(1)}, s32[]{:S(2)}) async-start(s8[5767168]{0:T(1024)(128)(4,1)} %bitcast.98), calls=%async_computation.27 | async-start | bytes 3145728
  374.9 8.9 %copy-start.24 = (bf16[1024,1408]{1,0:T(8,128)(2,1)}, bf16[1024,1408]{1,0:T(8,128)(2,1)S(1)}, u32[]{:S(2)}) copy-start(bf16[1024,1408]{1,0:T(8,128)(2,1)S(1)} %get-tuple-element.154.refs_4_) | copy-start | bytes 8650756
  374.9 8.9 %copy-start.25 = (bf16[1024,1408]{1,0:T(8,128)(2,1)}, bf16[1024,1408]{1,0:T(8,128)(2,1)S(1)}, u32[]{:S(2)}) copy-start(bf16[1024,1408]{1,0:T(8,128)(2,1)S(1)} %get-tuple-element.155.refs_6_) | copy-start | bytes 8650756
  396.1 282.4 %reduce-scatter.15.cloned.1.call-start = ((), (), s32[]{:S(2)}) async-start(), calls=%async_computation.14 | async-start | bytes 9437184 | tf_op jit(solution)/shard_map/reduce_scatter | solution.py:1018
  396.6 98.8 %copy-start.21 = (bf16[1024,1408]{1,0:T(8,128)(2,1)S(1)}, bf16[1024,1408]{1,0:T(8,128)(2,1)}, u32[]{:S(2)}) copy-start(bf16[1024,1408]{1,0:T(8,128)(2,1)} %get-tuple-element.150.refs_9_) | copy-start | bytes 8650756
  506.2 11.2 %copy-start.33 = (f32[2048]{0:T(1024)S(1)}, f32[2048]{0:T(1024)}, u32[]{:S(2)}) copy-start(f32[2048]{0:T(1024)} %param.27) | copy-start | bytes 24580
  506.2 11.2 %copy-start.39 = (f32[512]{0:T(512)S(1)}, f32[512]{0:T(512)}, u32[]{:S(2)}) copy-start(f32[512]{0:T(512)} %copy-done.38) | copy-start | bytes 6148
  517.3 4.4 copy-start.16
  517.3 4.4 copy-start.41
  517.4 4.6 copy-start.7
  522.0 4.9 copy-start.26
  525.0 2.0 copy-start.15
  533.9 330.7 %reduce-scatter.11.cloned.1.call-start = ((), (), s32[]{:S(2)}) async-start(), calls=%async_computation.12 | async-start | bytes 5242880 | tf_op jit(solution)/shard_map/reduce_scatter | solution.py:1048
  546.1 10.1 %copy-start.3 = (bf16[16,128,128]{2,1,0:T(8,128)(2,1)S(1)}, bf16[16,128,128]{2,1,0:T(8,128)(2,1)}, u32[]{:S(2)}) copy-start(bf16[16,128,128]{2,1,0:T(8,128)(2,1)} %copy-done.2) | copy-start | bytes 1572868
  556.2 1.3 copy-start.5
  579.9 284.7 %reduce-scatter.13.cloned.1.call-start = ((), (), s32[]{:S(2)}) async-start(), calls=%async_computation.13 | async-start | bytes 5242880 | tf_op jit(solution)/shard_map/reduce_scatter | solution.py:1048
  579.9 58.9 %slice-start = ((s8[4325376]{0:T(1024)(128)(4,1)}), s8[131072]{0:T(1024)(128)(4,1)S(1)}, s32[]{:S(2)}) async-start(s8[4325376]{0:T(1024)(128)(4,1)} %bitcast.81), calls=%async_computation.16 | async-start | bytes 262144
  580.6 284.0 %reduce-scatter.17.cloned.1.call-start = ((), (), s32[]{:S(2)}) async-start(), calls=%async_computation.15 | async-start | bytes 1310720 | tf_op jit(solution)/shard_map/reduce_scatter | solution.py:1019
  580.7 58.2 %slice-start.1 = ((s8[4325376]{0:T(1024)(128)(4,1)}), s8[4194304]{0:T(1024)(128)(4,1)S(1)}, s32[]{:S(2)}) async-start(s8[4325376]{0:T(1024)(128)(4,1)} %bitcast.81), calls=%async_computation.17 | async-start | bytes 8388608
  637.3 3.4 copy-start.11
  637.3 3.4 copy-start.27
  637.3 3.8 copy-start.31
  637.4 4.3 copy-start.43
  637.4 12.8 %collective-permute-start.1 = (bf16[3,8,2048]{2,1,0:T(8,128)(2,1)S(1)}, bf16[3,8,2048]{2,1,0:T(8,128)(2,1)S(1)}, u32[]{:S(2)}, u32[]{:S(2)}) collective-permute-start(bf16[3,8,2048]{2,1,0:T(8,128)(2,1)S(1)} %convert_element_type.92), channel_id=1, source_target_pairs={{1,0},{2,1},{3,2},{5,4},{6,5},{7,6},{9,8},{10,9},{11,10},{13,12},{... | collective-permute-start | bytes 294920 | tf_op jit(solution)/shard_map/ppermute | solution.py:980
  651.7 10.7 %copy-start.17 = (bf16[3,512,2048]{2,1,0:T(8,128)(2,1)S(1)}, bf16[3,512,2048]{2,1,0:T(8,128)(2,1)}, u32[]{:S(2)}) copy-start(bf16[3,512,2048]{2,1,0:T(8,128)(2,1)} %add_dynamic-update-slice_fusion.right_ref) | copy-start | bytes 18874372
  651.7 20.7 %slice-start.6 = ((s8[8388608]{0:T(1024)(128)(4,1)}), s8[4194304]{0:T(1024)(128)(4,1)S(1)}, s32[]{:S(2)}) async-start(s8[8388608]{0:T(1024)(128)(4,1)} %bitcast.94), calls=%async_computation.22 | async-start | bytes 8388608
  662.4 9.9 %slice-start.7 = ((s8[8388608]{0:T(1024)(128)(4,1)}), s8[4194304]{0:T(1024)(128)(4,1)S(1)}, s32[]{:S(2)}) async-start(s8[8388608]{0:T(1024)(128)(4,1)} %bitcast.94), calls=%async_computation.23 | async-start | bytes 8388608
  672.4 6.2 copy-start.9
  672.4 6.2 copy-start.35
  672.4 6.2 copy-start.37
  687.0 171.6 %copy-start.40 = (f32[512]{0:T(512)S(1)}, f32[512]{0:T(512)}, u32[]{:S(2)}) copy-start(f32[512]{0:T(512)} %get-tuple-element.166) | copy-start | bytes 6148
  864.5 4.5 copy-start.28
  864.5 4.5 copy-start.29
  (4 other events, 3.4 us)
Sparse Core Ops, SparseCore 0:
  10.7 83.4 all-gather.4
  96.3 81.2 all-gather.6
  179.7 87.6 all-gather.10
  269.4 79.2 all-gather.8
  350.9 75.2 reduce-scatter.8
  428.5 77.2 reduce-scatter.6
  534.0 69.5 reduce-scatter.14
  605.9 78.8 reduce-scatter.10
  687.1 99.7 reduce-scatter.12
  789.2 51.7 reduce-scatter.16

commit v5 on v4

--- a/solution.py
+++ b/solution.py
@@ -264,18 +264,17 @@
     )(out_add, out_map, entry, gain, up)
 
 
-def backward_kernel(
-    since_ref, beta_ref, query_ref, key_ref, value_ref, halo_ref, taps_ref,
+def backward_heads(
+    step, since_ref, beta_ref, query_ref, key_ref, value_ref, halo_ref, taps_ref,
     new_add_ref, new_map_ref, inverse_ref, starts_ref, entry_ref, exit_ref, d_core_ref,
-    d_proj_ref, d_halo_ref, d_taps_ref, d_beta_ref,
-    ext, back,
+    d_taps_ref, d_beta_ref, ext, back, emit,
 ):
     rows = since_ref.shape[0]
     blocks = rows // BLOCK
     since = since_ref[...]
     jobs = []
     for sub in range(HEADS_STEP):
-        head = pl.program_id(0) * HEADS_STEP + sub
+        head = step * HEADS_STEP + sub
         lanes = slice(sub * BLOCK, (sub + 1) * BLOCK)
         fronts = []
         for part, ref in enumerate((query_ref, key_ref, value_ref)):
@@ -359,7 +358,7 @@
             taps = taps_ref[part, :, lanes]
             source = ext.at[sub * 3 + part]
             d_pre = d_act * gate * (1.0 + pre * (1.0 - gate))
-            room = back.at[sub * 3 + part]
+            room = back.at[(sub * 3 + part) % 2]
             total = None
             d_taps = []
             for lag in range(CONV):
@@ -372,16 +371,25 @@
                 term = room[lag, lag : lag + PAD + rows, :]
                 total = term if total is None else total + term
             d_taps_ref[part, :, lanes] = jnp.concatenate(d_taps, axis=0)
-            d_halo_ref[part, :, lanes] = total[:PAD].astype(d_halo_ref.dtype)
-            d_proj_ref[part, :, lanes] = total[PAD:].astype(BF16)
-
-    @pl.when(pl.program_id(0) == 0)
+            emit(part, lanes, total)
+
+    @pl.when(step == 0)
     def _():
         d_beta_ref[...] = d_beta_all
 
-    @pl.when(pl.program_id(0) > 0)
+    @pl.when(step > 0)
     def _():
         d_beta_ref[...] += d_beta_all
+
+
+def backward_kernel(*refs):
+    d_proj_ref, d_halo_ref, d_taps_ref, d_beta_ref, ext, back = refs[14:]
+
+    def emit(part, lanes, total):
+        d_halo_ref[part, :, lanes] = total[:PAD]
+        d_proj_ref[part, :, lanes] = total[PAD:].astype(BF16)
+
+    backward_heads(pl.program_id(0), *refs[:14], d_taps_ref, d_beta_ref, ext, back, emit)
 
 
 def mixer_backward(
@@ -412,7 +420,7 @@
         ],
         scratch_shapes=[
             pltpu.VMEM((3 * HEADS_STEP, PAD + rows, BLOCK), F32),
-            pltpu.VMEM((3 * HEADS_STEP, CONV, PAD + rows + PAD, BLOCK), F32),
+            pltpu.VMEM((2, CONV, PAD + rows + PAD, BLOCK), F32),
         ],
         compiler_params=params(),
         name="mixer_backward",
@@ -502,74 +510,155 @@
     )(map_part, add_part)
 
 
-WINDOW = 4
-LAG = 2
-SPLIT = 4
-
-
-def reduce_kernel(
-    left_ref, right_ref, small_ref, out_ref, small_out_ref,
-    left_own, left_away, left_sib, right_sib, small_sib, total, total_small, got2, got2_small, got3, got3_small, gotz, gotz_small,
-    left_send, left_recv, right_send, right_recv, small_send, small_recv,
-    send2, recv2, send3, recv3, sendz, recvz,
-):
-    dp = lax.axis_index("dp")
-    z = lax.axis_index("narrow")
+def bits(dp):
     core, x, y = dp % 2, (dp // 2) % 2, dp // 4
+    return core, x, y, dp + 1 - 2 * core, dp + 2 * (1 - 2 * x), dp + 4 * (1 - 2 * y)
+
+
+def remote(src, dst, send_sem, recv_sem, target):
+    return pltpu.make_async_remote_copy(
+        src_ref=src, dst_ref=dst, send_sem=send_sem, recv_sem=recv_sem, device_id=target, device_id_type=MESH
+    )
+
+
+def meet(dp_targets, narrow_targets):
+    barrier = pltpu.get_barrier_semaphore()
+    for target in dp_targets:
+        pl.semaphore_signal(barrier, inc=1, device_id={"dp": target}, device_id_type=MESH)
+    for target in narrow_targets:
+        pl.semaphore_signal(barrier, inc=1, device_id={"narrow": target}, device_id_type=MESH)
+    pl.semaphore_wait(barrier, len(dp_targets) + len(narrow_targets))
+
+
+def add_rows(dst, src, step):
+    def one(at, _):
+        at = pl.ds(pl.multiple_of(at * step, step), step)
+        dst[at, :] = (dst[at, :].astype(F32) + src[at, :].astype(F32)).astype(dst.dtype)
+        return 0
+
+    lax.fori_loop(0, dst.shape[0] // step, one, 0)
+
+
+def small_kernel(small_ref, out_ref, landed, total, got2, got3, gotz, send1, recv1, send2, recv2, send3, recv3, sendz, recvz):
+    dp, z = lax.axis_index("dp"), lax.axis_index("narrow")
+    core, x, y, sib, flip_x, flip_y = bits(dp)
     depth = lax.axis_size("narrow")
-    parts = right_ref.shape[0]
-    units = SPLIT * parts
-    rows = left_ref.shape[1] // 8
-    cols = right_ref.shape[2] // SPLIT
-    sib = dp + 1 - 2 * core
-    flip_x = dp + 2 * (1 - 2 * x)
-    flip_y = dp + 4 * (1 - 2 * y)
-
-    def peer_z(step):
-        return (z + step) % depth
-
-    barrier = pltpu.get_barrier_semaphore()
-    for target in (sib, flip_x, flip_y):
-        pl.semaphore_signal(barrier, inc=1, device_id={"dp": target}, device_id_type=MESH)
-    for step in range(1, depth):
-        pl.semaphore_signal(barrier, inc=1, device_id={"narrow": peer_z(step)}, device_id_type=MESH)
-    pl.semaphore_wait(barrier, 2 + depth)
-
-    def send(src, dst, send_sem, recv_sem, target):
-        return pltpu.make_async_remote_copy(
-            src_ref=src, dst_ref=dst, send_sem=send_sem, recv_sem=recv_sem,
-            device_id=target, device_id_type=MESH,
-        )
+    rows = small_ref.shape[0] // 8
+    share = rows // depth
+    peers = [(z + step) % depth for step in range(1, depth)]
+    meet((sib, flip_x, flip_y), peers)
 
     def stripe_rows(stripe, which):
         return pl.ds(pl.multiple_of((stripe * 2 + which) * rows, rows), rows)
 
+    def share_rows(at):
+        return pl.ds(pl.multiple_of(at * share, share), share)
+
+    first = [
+        remote(small_ref.at[stripe_rows(k, 1 - core)], landed.at[k], send1.at[k], recv1.at[k], {"dp": sib})
+        for k in range(4)
+    ]
+    for copy in first:
+        copy.start()
+    for k in range(4):
+        first[k].wait()
+        total[k] = small_ref[stripe_rows(k, core), :] + landed[k]
+    second = [
+        remote(total.at[2 * j + 1 - x], got2.at[j], send2.at[j], recv2.at[j], {"dp": flip_x}) for j in range(2)
+    ]
+    for copy in second:
+        copy.start()
+    for copy in second:
+        copy.wait()
+    third = remote(total.at[2 * (1 - y) + x], got3, send3, recv3, {"dp": flip_y})
+    total[2 * (1 - y) + x] = total[2 * (1 - y) + x] + got2[1 - y]
+    third.start()
+    third.wait()
+    mine = 2 * y + x
+    total[mine] = total[mine] + got2[y] + got3[...]
+    last = [
+        remote(total.at[mine, share_rows(to)], gotz.at[k], sendz.at[k], recvz.at[k], {"narrow": to})
+        for k, to in enumerate(peers)
+    ]
+    for copy in last:
+        copy.start()
+    value = total[mine, share_rows(z), :]
+    for k, copy in enumerate(last):
+        copy.wait()
+        value = value + gotz[k]
+    out_ref[...] = value
+
+
+def reduce_small(small):
+    height, lanes = small.shape
+    depth = lax.axis_size("narrow")
+    rows = height // 8
+    share = rows // depth
+    dma = pltpu.SemaphoreType.DMA
+    return pl.pallas_call(
+        small_kernel,
+        in_specs=[pl.BlockSpec(memory_space=pltpu.VMEM)],
+        out_specs=pl.BlockSpec(memory_space=pltpu.VMEM),
+        out_shape=jax.ShapeDtypeStruct((share, lanes), F32),
+        scratch_shapes=[
+            pltpu.VMEM((4, rows, lanes), F32),
+            pltpu.VMEM((4, rows, lanes), F32),
+            pltpu.VMEM((2, rows, lanes), F32),
+            pltpu.VMEM((rows, lanes), F32),
+            pltpu.VMEM((depth - 1, share, lanes), F32),
+            dma((4,)), dma((4,)), dma((2,)), dma((2,)), dma(()), dma(()), dma((depth - 1,)), dma((depth - 1,)),
+        ],
+        compiler_params=pltpu.CompilerParams(
+            collective_id=3, has_side_effects=True, vmem_limit_bytes=16 * 1024 * 1024
+        ),
+        name="reduce_small",
+    )(small)
+
+
+RING = 3
+HELD = 6
+
+
+def fused_kernel(*refs):
+    heads_in = refs[:14]
+    since_ref = refs[0]
+    (
+        w_query_ref, w_key_ref, w_value_ref, normed_hbm,
+        grad_hbm, d_normed_hbm, d_taps_ref, d_beta_ref,
+        ext, back, left_own, left_away, left_sib, d_proj, d_proj_sib, halo_out, halo_in,
+        total, got2, got3, gotz, d_normed, grad,
+        local_sem, left_send, left_recv, right_send, right_recv, halo_send, halo_recv,
+        send2, recv2, send3, recv3, sendz, recvz,
+    ) = refs[14:]
+    step = pl.program_id(0)
+    units = pl.num_programs(0) - 1
+    dp, z = lax.axis_index("dp"), lax.axis_index("narrow")
+    core, x, y, sib, flip_x, flip_y = bits(dp)
+    depth = lax.axis_size("narrow")
+    tokens = since_ref.shape[0]
+    rows = left_own.shape[1]
+    cols = d_proj.shape[3]
+    share = rows // depth
+    peers = [(z + k) % depth for k in range(1, depth)]
+
+    def stripe_lanes(stripe, which):
+        return pl.ds(pl.multiple_of((stripe * 2 + which) * rows, rows), rows)
+
     def left_copy(stripe):
-        return send(
-            left_away.at[stripe], left_sib.at[stripe],
-            left_send.at[stripe], left_recv.at[stripe], {"dp": sib},
+        return remote(
+            left_away.at[stripe], left_sib.at[stripe], left_send.at[stripe], left_recv.at[stripe], {"dp": sib}
         )
 
-    def small_copy(stripe):
-        return send(
-            small_ref.at[stripe_rows(stripe, 1 - core)], small_sib.at[stripe],
-            small_send.at[stripe], small_recv.at[stripe], {"dp": sib},
+    def right_copy(unit):
+        return remote(
+            d_proj.at[unit % RING], d_proj_sib.at[unit % RING],
+            right_send.at[unit % RING], right_recv.at[unit % RING], {"dp": sib},
         )
 
-    def right_copy(part):
-        return send(right_ref.at[part], right_sib.at[part], right_send.at[part], right_recv.at[part], {"dp": sib})
-
-    right_copy(0).start()
-    for stripe in range(4):
-        small_copy(stripe).start()
-    for stripe in range(4):
-        turned = left_ref[:, stripe_rows(stripe, 1 - core)].astype(F32).T
-        left_away[stripe] = turned.astype(BF16)
-        left_copy(stripe).start()
-    for part in range(1, parts):
-        right_copy(part).start()
-    for stripe in range(4):
-        left_own[stripe] = left_ref[:, stripe_rows(stripe, core)].astype(F32).T.astype(BF16)
+    def halo_copy(unit):
+        return remote(
+            halo_out.at[unit], halo_in.at[unit], halo_send.at[unit], halo_recv.at[unit], {"narrow": z - 1}
+        )
 
     def order(unit):
         e = unit % 2
@@ -583,205 +672,253 @@
         def kept(j):
             return pick(2 * j + x, 2 * y + j)
 
-        far = pick(1 - y, 1 - x)
-        near = pick(y, x)
-        return away, kept, pick(flip_x, flip_y), pick(flip_y, flip_x), far, near
+        return away, kept, pick(flip_x, flip_y), pick(flip_y, flip_x), pick(1 - y, 1 - x), pick(y, x)
 
     def copy2(unit, j):
         away, _, target, _, _, _ = order(unit)
-        return send(total.at[unit, away(j)], got2.at[unit, j], send2.at[unit, j], recv2.at[unit, j], {"dp": target})
-
-    def copy2_small(j):
-        away, _, target, _, _, _ = order(0)
-        return send(
-            total_small.at[away(j)], got2_small.at[j], send2.at[units, j], recv2.at[units, j], {"dp": target}
-        )
+        return remote(total.at[unit % HELD, away(j)], got2.at[unit, j], send2.at[unit, j], recv2.at[unit, j], {"dp": target})
 
     def copy3(unit):
         _, kept, _, target, far, _ = order(unit)
-        return send(total.at[unit, kept(far)], got3.at[unit], send3.at[unit], recv3.at[unit], {"dp": target})
-
-    def copy3_small():
-        _, kept, _, target, far, _ = order(0)
-        return send(total_small.at[kept(far)], got3_small, send3.at[units], recv3.at[units], {"dp": target})
-
-    share = rows // depth
-
-    def share_rows(at):
-        return pl.ds(pl.multiple_of(at * share, share), share)
-
-    def copyz(unit, step):
+        return remote(total.at[unit % HELD, kept(far)], got3.at[unit], send3.at[unit], recv3.at[unit], {"dp": target})
+
+    def copyz(unit, part, k):
         _, kept, _, _, _, near = order(unit)
-        to = peer_z(step)
-        return send(
-            total.at[unit, kept(near), share_rows(to)], gotz.at[unit, step - 1],
-            sendz.at[unit, step - 1], recvz.at[unit, step - 1], {"narrow": to},
+        at = pl.ds(pl.multiple_of(part * rows + peers[k] * share, share), share)
+        return remote(
+            total.at[unit % HELD, kept(near), at], gotz.at[unit, k, part * share : (part + 1) * share],
+            sendz.at[unit, k, part], recvz.at[unit, k, part], {"narrow": peers[k]},
         )
 
-    def copyz_small(step):
-        _, kept, _, _, _, near = order(0)
-        to = peer_z(step)
-        return send(
-            total_small.at[kept(near), share_rows(to)], gotz_small.at[step - 1],
-            sendz.at[units, step - 1], recvz.at[units, step - 1], {"narrow": to},
-        )
-
-    def add_to(dst, src):
-        step = 32
-
-        def one(at, _):
-            at = pl.ds(pl.multiple_of(at * step, step), step)
-            dst[at, :] = (dst[at, :].astype(F32) + src[at, :].astype(F32)).astype(dst.dtype)
-            return 0
-
-        lax.fori_loop(0, rows // step, one, 0)
-
-    for stripe in range(4):
-        small_copy(stripe).wait()
-        total_small[stripe] = small_ref[stripe_rows(stripe, core)] + small_sib[stripe]
-    for j in range(2):
-        copy2_small(j).start()
-    for stripe in range(4):
-        left_copy(stripe).wait()
-
-    tile = 512
-
-    def products(unit, _):
+    @pl.when(step == 0)
+    def _():
+        loads = [
+            pltpu.make_async_copy(
+                normed_hbm.at[:, stripe_lanes(k % 4, 1 - core if k < 4 else core)], d_proj.at[k // 3, k % 3], local_sem.at[k]
+            )
+            for k in range(8)
+        ]
+        for load in loads:
+            load.start()
+        back[:, :, 0:PAD, :] = jnp.zeros((2, CONV, PAD, BLOCK), F32)
+        back[:, :, PAD + tokens :, :] = jnp.zeros((2, CONV, PAD, BLOCK), F32)
+        d_normed[...] = jnp.zeros_like(d_normed)
+        meet((sib, flip_x, flip_y), peers)
+        for stripe in range(4):
+            loads[stripe].wait()
+            left_away[stripe] = d_proj[stripe // 3, stripe % 3].astype(F32).T.astype(BF16)
+            left_copy(stripe).start()
+        for stripe in range(4):
+            loads[4 + stripe].wait()
+            left_own[stripe] = d_proj[(4 + stripe) // 3, (4 + stripe) % 3].astype(F32).T.astype(BF16)
+
+    @pl.when(step >= 1)
+    def _():
+        unit = step - 1
+
+        @pl.when(z < depth - 1)
+        def _():
+            halo_copy(unit).wait_recv()
+            for part in range(3):
+                extra = jnp.concatenate([jnp.zeros((PAD, cols), F32), halo_in[unit, part]], axis=0)
+                tail = slice(tokens - 2 * PAD, tokens)
+                d_proj[unit % RING, part, tail, :] = (
+                    d_proj[unit % RING, part, tail, :].astype(F32) + extra
+                ).astype(BF16)
+
+        @pl.when(z > 0)
+        def _():
+            halo_copy(unit).wait_send()
+
+        right_copy(unit).start()
+
+    @pl.when(step < units)
+    def _():
+        def emit(part, lanes, value):
+            halo_out[step, part, :, lanes] = value[:PAD]
+            d_proj[step % RING, part, :, lanes] = value[PAD:].astype(BF16)
+
+        backward_heads(step, *heads_in, d_taps_ref, d_beta_ref, ext, back, emit)
+
+        @pl.when(z > 0)
+        def _():
+            halo_copy(step).start()
+
+    @pl.when(step == 1)
+    def _():
+        for stripe in range(4):
+            left_copy(stripe).wait()
+
+    @pl.when(step >= 1)
+    def _():
+        unit = step - 1
         away, kept, _, _, _, _ = order(unit)
-        part = unit // SPLIT
-
-        @pl.when(unit % SPLIT == 0)
-        def _():
-            right_copy(part).wait()
+        right_copy(unit).wait()
 
         def one(k, _):
             j = k % 2
             stripe = (k // 2) * kept(j) + (1 - k // 2) * away(j)
-            mine = left_own[stripe]
-            other = left_sib[stripe]
-            for at in range(cols // tile):
-                lanes = pl.ds(pl.multiple_of((unit % SPLIT) * cols + at * tile, tile), tile)
-                value = jnp.dot(mine, right_ref[part, :, lanes], preferred_element_type=F32)
-                value = value + jnp.dot(other, right_sib[part, :, lanes], preferred_element_type=F32)
-                total[unit, stripe, :, at * tile : (at + 1) * tile] = value.astype(BF16)
-
-            @pl.when((k < 2) & (unit < WINDOW))
+            for part in range(3):
+                value = jnp.dot(left_own[stripe], d_proj[unit % RING, part], preferred_element_type=F32)
+                value = value + jnp.dot(left_sib[stripe], d_proj_sib[unit % RING, part], preferred_element_type=F32)
+                total[unit % HELD, stripe, part * rows : (part + 1) * rows, :] = value.astype(BF16)
+
+            @pl.when(k < 2)
             def _():
                 copy2(unit, j).start()
 
             return 0
 
         lax.fori_loop(0, 4, one, 0)
-        return 0
-
-    lax.fori_loop(0, units, products, 0)
+
+        def normed_part(at, _):
+            at = pl.ds(pl.multiple_of(at * 512, 512), 512)
+            value = d_normed[:, at]
+            for part, ref in enumerate((w_query_ref, w_key_ref, w_value_ref)):
+                value = value + lax.dot_general(
+                    d_proj[unit % RING, part], ref[at, :], (((1,), (1,)), ((), ())), preferred_element_type=F32
+                )
+            d_normed[:, at] = value
+            return 0
+
+        lax.fori_loop(0, d_normed.shape[1] // 512, normed_part, 0)
 
     def second(unit):
         _, kept, _, _, far, near = order(unit)
         for j in range(2):
             copy2(unit, j).wait()
-
-        @pl.when(unit + WINDOW < units)
-        def _():
-            for j in range(2):
-                copy2(unit + WINDOW, j).start()
-
-        add_to(total.at[unit, kept(far)], got2.at[unit, far])
+        add_rows(total.at[unit % HELD, kept(far)], got2.at[unit, far], 64)
         copy3(unit).start()
-        add_to(total.at[unit, kept(near)], got2.at[unit, near])
+        add_rows(total.at[unit % HELD, kept(near)], got2.at[unit, near], 64)
 
     def third(unit):
         _, kept, _, _, _, near = order(unit)
         copy3(unit).wait()
-        add_to(total.at[unit, kept(near)], got3.at[unit])
-        for step in range(1, depth):
-            copyz(unit, step).start()
+        add_rows(total.at[unit % HELD, kept(near)], got3.at[unit], 64)
+        for k in range(depth - 1):
+            for part in range(3):
+                copyz(unit, part, k).start()
 
     def fourth(unit):
         _, kept, _, _, _, near = order(unit)
-        for step in range(1, depth):
-            copyz(unit, step).wait()
-        value = total[unit, kept(near), share_rows(z), :].astype(F32)
-        for step in range(1, depth):
-            value = value + gotz[unit, step - 1].astype(F32)
-        out_ref[unit // SPLIT, :, pl.ds(pl.multiple_of((unit % SPLIT) * cols, cols), cols)] = value
-
-    _, kept, _, _, far, near = order(0)
-    for j in range(2):
-        copy2_small(j).wait()
-    add_to(total_small.at[kept(far)], got2_small.at[far])
-    copy3_small().start()
-    add_to(total_small.at[kept(near)], got2_small.at[near])
-
-    def stages(at, _):
-        @pl.when(at < units)
+        for k in range(depth - 1):
+            for part in range(3):
+                copyz(unit, part, k).wait()
+        for part in range(3):
+            at = pl.ds(pl.multiple_of(part * rows + z * share, share), share)
+            value = total[unit % HELD, kept(near), at, :].astype(F32)
+            for k in range(depth - 1):
+                value = value + gotz[unit, k, part * share : (part + 1) * share, :].astype(F32)
+            grad[part, :, pl.ds(pl.multiple_of(unit * cols, cols), cols)] = value
+
+    def stages(at):
+        @pl.when((at >= 3) & (at < units + 3))
         def _():
-            second(at)
-
-        @pl.when((at >= LAG) & (at < units + LAG))
+            second(at - 3)
+
+        @pl.when((at >= 4) & (at < units + 4))
         def _():
-            third(at - LAG)
-
-        @pl.when(at >= 2 * LAG)
+            third(at - 4)
+
+        @pl.when(at >= 5)
         def _():
-            fourth(at - 2 * LAG)
-
-        return 0
-
-    lax.fori_loop(0, units, stages, 0)
-    copy3_small().wait()
-    add_to(total_small.at[kept(near)], got3_small)
-    for step in range(1, depth):
-        copyz_small(step).start()
-    lax.fori_loop(units, units + 2 * LAG, stages, 0)
-    for step in range(1, depth):
-        copyz_small(step).wait()
-    value = total_small[kept(near), share_rows(z), :]
-    for step in range(1, depth):
-        value = value + gotz_small[step - 1]
-    small_out_ref[...] = value
-
-
-def reduce_products(left, right, small):
-    tokens, height = left.shape
-    parts, _, width = right.shape
+            fourth(at - 5)
+
+    stages(step)
+
+    @pl.when(step == units)
+    def _():
+        save = pltpu.make_async_copy(d_normed, d_normed_hbm, local_sem.at[0])
+        save.start()
+
+        def one(at, _):
+            stages(at)
+            return 0
+
+        lax.fori_loop(units + 1, units + 5, one, 0)
+        save.wait()
+        store = pltpu.make_async_copy(grad, grad_hbm, local_sem.at[1])
+        store.start()
+        store.wait()
+
+
+def fused_backward(
+    since, beta_logit, query, key, value, halo, taps, new_add, new_map, inverse, starts, entry, exit_grad, d_core,
+    w_query, w_key, w_value, normed,
+):
+    tokens, width = query.shape
+    heads = width // BLOCK
+    blocks = tokens // BLOCK
+    units = heads // HEADS_STEP
+    cols = HEADS_STEP * BLOCK
     depth = lax.axis_size("narrow")
-    units = SPLIT * parts
-    rows, cols = height // 8, width // SPLIT
+    rows = width // 8
     share = rows // depth
-    lanes = small.shape[1]
     dma = pltpu.SemaphoreType.DMA
+
+    def now(step):
+        return jnp.minimum(step, units - 1)
+
+    def before(step):
+        return jnp.maximum(step - 1, 0)
+
+    def whole(shape):
+        return pl.BlockSpec(shape, lambda h: (0,) * len(shape))
+
+    wide = pl.BlockSpec((tokens, cols), lambda h: (0, now(h)))
+
+    def lanes(first, second):
+        return pl.BlockSpec((first, second, cols), lambda h: (0, 0, now(h)))
+
+    def each(*tail):
+        return pl.BlockSpec((HEADS_STEP,) + tail, lambda h: (now(h),) + (0,) * len(tail))
+
+    weight = pl.BlockSpec((width, cols), lambda h: (0, before(h)))
+    anywhere = pl.BlockSpec(memory_space=pl.ANY)
     return pl.pallas_call(
-        reduce_kernel,
-        in_specs=[pl.BlockSpec(memory_space=pltpu.VMEM)] * 3,
-        out_specs=[pl.BlockSpec(memory_space=pltpu.VMEM)] * 2,
+        fused_kernel,
+        grid=(units + 1,),
+        in_specs=[
+            whole(since.shape), whole(beta_logit.shape), wide, wide, wide, lanes(3, PAD), lanes(3, CONV),
+            wide, wide, each(blocks, BLOCK, BLOCK), each(blocks, BLOCK, 2 * BLOCK),
+            each(BLOCK, BLOCK), each(BLOCK, BLOCK), wide,
+            weight, weight, weight, anywhere,
+        ],
+        out_specs=[anywhere, anywhere, lanes(3, CONV), whole(beta_logit.shape)],
         out_shape=[
-            jax.ShapeDtypeStruct((parts, share, width), F32),
-            jax.ShapeDtypeStruct((share, lanes), F32),
+            jax.ShapeDtypeStruct((3, share, width), F32),
+            jax.ShapeDtypeStruct((tokens, width), F32),
+            jax.ShapeDtypeStruct((3, CONV, width), F32),
+            jax.ShapeDtypeStruct(beta_logit.shape, F32),
         ],
         scratch_shapes=[
+            pltpu.VMEM((3 * HEADS_STEP, PAD + tokens, BLOCK), F32),
+            pltpu.VMEM((2, CONV, PAD + tokens + PAD, BLOCK), F32),
             pltpu.VMEM((4, rows, tokens), BF16),
             pltpu.VMEM((4, rows, tokens), BF16),
             pltpu.VMEM((4, rows, tokens), BF16),
-            pltpu.VMEM(right.shape, BF16),
-            pltpu.VMEM((4, rows, lanes), F32),
-            pltpu.VMEM((units, 4, rows, cols), BF16),
-            pltpu.VMEM((4, rows, lanes), F32),
-            pltpu.VMEM((units, 2, rows, cols), BF16),
-            pltpu.VMEM((2, rows, lanes), F32),
-            pltpu.VMEM((units, rows, cols), BF16),
-            pltpu.VMEM((rows, lanes), F32),
-            pltpu.VMEM((units, depth - 1, share, cols), BF16),
-            pltpu.VMEM((depth - 1, share, lanes), F32),
-            dma((4,)), dma((4,)), dma((parts,)), dma((parts,)), dma((4,)), dma((4,)),
-            dma((units + 1, 2)), dma((units + 1, 2)), dma((units + 1,)), dma((units + 1,)),
-            dma((units + 1, depth - 1)), dma((units + 1, depth - 1)),
+            pltpu.VMEM((RING, 3, tokens, cols), BF16),
+            pltpu.VMEM((RING, 3, tokens, cols), BF16),
+            pltpu.VMEM((units, 3, PAD, cols), F32),
+            pltpu.VMEM((units, 3, PAD, cols), F32),
+            pltpu.VMEM((HELD, 4, 3 * rows, cols), BF16),
+            pltpu.VMEM((units, 2, 3 * rows, cols), BF16),
+            pltpu.VMEM((units, 3 * rows, cols), BF16),
+            pltpu.VMEM((units, depth - 1, 3 * share, cols), BF16),
+            pltpu.VMEM((tokens, width), F32),
+            pltpu.VMEM((3, share, width), F32),
+            dma((8,)), dma((4,)), dma((4,)), dma((RING,)), dma((RING,)), dma((units,)), dma((units,)),
+            dma((units, 2)), dma((units, 2)), dma((units,)), dma((units,)),
+            dma((units, depth - 1, 3)), dma((units, depth - 1, 3)),
         ],
         compiler_params=pltpu.CompilerParams(
-            collective_id=3, has_side_effects=True, vmem_limit_bytes=VMEM_LIMIT
+            collective_id=5, has_side_effects=True, vmem_limit_bytes=61 * 1024 * 1024
         ),
-        name="reduce_products",
-    )(left, right, small)
+        name="fused_backward",
+    )(
+        since, beta_logit, query, key, value, halo, taps, new_add, new_map, inverse, starts, entry, exit_grad, d_core,
+        w_query, w_key, w_value, normed,
+    )
 
 
 def ffn_grads_kernel(*refs):
@@ -1047,9 +1184,7 @@
     def scatter(rows):
         return lax.psum_scatter(rows, "narrow", scatter_dimension=0, tiled=True)
 
-    cot = []
-    for part in parts:
-        cot.append(gather(grad_out[part]))
+    cot = gather(grad_out)
     since = since_start(doc_lengths, offset, tok_rows)
     inputs = tokens.astype(F32)
     normed = rms_scale(inputs, attn_gain, 1e-06).astype(BF16)
@@ -1067,7 +1202,9 @@
     attn_mixed = mixer_join(out_add, out_map, entry, gain_row)
     hidden = inputs + matmul(attn_mixed, w_out)
     normed_mlp = rms_scale(hidden, mlp_gain, 1e-06).astype(BF16)
-    normed_mlp, *cot = lax.optimization_barrier((normed_mlp, *cot))
+    normed_mlp, cot = lax.optimization_barrier((normed_mlp, cot))
+    cot = cot.reshape(-1, tok_rows, model_width)
+    cot = [cot[:, part].reshape(-1, model_width) for part in parts]
     gathered = [gather(normed_mlp[part]) for part in parts]
     activation, d_gate, d_up, d_normed_parts = [], [], [], []
     for at in range(HALVES):
@@ -1105,16 +1242,20 @@
     exit_grad, out_parts = lax.optimization_barrier((exit_grad, out_parts))
     w_out_term = scatter_all(w_out_term, 0)
     ffn_parts = [scatter(part) for part in out_parts]
-    d_proj, d_halo, conv_term, d_beta = mixer_backward(
+    mixer_args = (
         since, beta_logit, query, key, value, halo, conv_weight,
         new_add, new_map, inverse, starts, entry, exit_grad, d_core,
     )
-    after = shifted(d_halo.astype(BF16), "narrow", -1)
-    d_proj = d_proj.at[:, tok_rows - PAD :].add(after)
-    d_query, d_key, d_value = d_proj[0], d_proj[1], d_proj[2]
+    if lax.axis_size("dp") == 8:
+        grads, d_normed, conv_term, d_beta = fused_backward(*mixer_args, w_query, w_key, w_value, normed)
+    else:
+        d_proj, d_halo, conv_term, d_beta = mixer_backward(*mixer_args)
+        after = shifted(d_halo.astype(BF16), "narrow", -1)
+        d_proj = d_proj.at[:, tok_rows - PAD :].add(after)
+        d_normed = sum(dot_nt(part, w) for part, w in zip(d_proj, (w_query, w_key, w_value)))
+        grads = jnp.stack([scatter_all(dot_tn(normed, part).astype(BF16), 0).astype(F32) for part in d_proj])
     d_beta_low = d_beta.astype(BF16)
     beta_term = jnp.einsum("rd,rh->dh", normed, d_beta_low, preferred_element_type=F32)
-    d_normed = dot_nt(d_query, w_query) + dot_nt(d_key, w_key) + dot_nt(d_value, w_value)
     d_normed = d_normed + jnp.einsum("rh,dh->rd", d_beta_low, w_beta, preferred_element_type=F32)
     d_input_norm, attn_gain_term = norm_back(inputs, attn_gain, d_normed, 1e-06)
     grad_tokens = (d_hidden + d_input_norm).astype(BF16)
@@ -1137,9 +1278,8 @@
     )
     small = jnp.pad(small, ((0, 0), (0, BLOCK - small.shape[1])))
     if lax.axis_size("dp") == 8:
-        grads, small = reduce_products(normed, d_proj, small)
+        small = reduce_small(small)
     else:
-        grads = [scatter_all(dot_tn(normed, part).astype(BF16), 0).astype(F32) for part in (d_query, d_key, d_value)]
         small = lax.psum_scatter(small, ("dp", "narrow"), scatter_dimension=0, tiled=True)
     grad_beta = small[:, :heads]
     grad_conv = small[:, heads : heads + taps].T.reshape(3, CONV, -1)

time: 888 us -> 867 us (0.976)
  matrix products: 220 us -> 192 us
    dot_general x8 -> x5, matrix products: 81.3 us -> 54.5 us  [dot_nt(): return jnp.einsum('re,de->rd', left, right, preferred_element_type=F32)]
    reduce_scatter x1, waiting for transfers between devices: 0.02 us -> 24 us  [scatter_all(): return lax.psum_scatter(part, 'narrow', scatter_dimension=dim, tiled=True)]
    all_gather x4 -> x3, waiting for transfers between devices: 142 us -> 123 us  [gather(): return lax.all_gather(rows, 'narrow', axis=0, tiled=True)]
  transfers between devices with their start and end apart: 12 -> 10, of which waited for: 5 -> 5; matrix products, arithmetic and copies ran while one was open for 27% -> 25% of each run, Pallas kernels for 49% -> 51%
where the time goes in v5:
time: 867 us; the launch traced here: 859 us
  Pallas kernels  436 us (50%)
  matrix products  192 us (22%)
  waiting for transfers between devices  150 us (17%)
  local copies, waits for them, and re-layouts  33.9 us (4%)
  other arithmetic  24.9 us (3%)
  between operations  15 us (2%)
    pallas_call x1, Pallas kernels, fused_backward(): pl.pallas_call(fused_kernel, grid=(units + 1,), in_specs=[whole(since.sha...  189 us
    all_gather x3, waiting for transfers between devices, gather(): return lax.all_gather(rows, 'narrow', axis=0, tiled=True)  123 us
    dot_general x11, matrix products, matmul(): return jnp.dot(left, right, preferred_element_type=F32)  102 us
    pallas_call x1, Pallas kernels, ffn_grads(): pl.pallas_call(ffn_grads_kernel, in_specs=[pl.BlockSpec(memory_space=pl.A...  98.6 us
    dot_general x5, matrix products, dot_nt(): return jnp.einsum('re,de->rd', left, right, preferred_element_type=F32)  54.5 us
    pallas_call x1, Pallas kernels, mixer_forward(): pl.pallas_call(forward_kernel, grid=(heads // HEADS_STEP,), in_specs=[who...  49.7 us
    pallas_call x2, Pallas kernels, carry_chain(): pl.pallas_call(functools.partial(chain_kernel, axis, forward), in_specs=[...  49.5 us
    pallas_call x1, Pallas kernels, reduce_small(): pl.pallas_call(small_kernel, in_specs=[pl.BlockSpec(memory_space=pltpu.VM...  32.1 us
  transfers between devices with their start and end apart: 10, of which 5 were waited for; matrix products, arithmetic and copies ran while one was open for 25% of the time, Pallas kernels for 51%

profile of v5, /device:TPU:0, one launch (start us, length us, event | category | flops | bytes accessed | tf_op | source)
XLA Modules:
  0.0 858.8 jit_solution(3736784734372019741)
XLA Ops:
  7.3 0.7 all-gather.4.cloned.1.call-update
  8.0 2.1 fusion.9
  11.8 7.9 fusion.35.value_ref.refs_4_
  19.9 4.5 fusion.33.query_ref.refs_2_
  24.4 4.5 fusion.34.key_ref.refs_3_
  29.0 2.0 copy-done.13
  31.0 5.1 collective-permute-start
  36.4 3.0 fusion.32.beta_ref.refs_1_
  39.4 1.4 collective-permute-done.halo_ref.refs_5_
  40.8 0.8 broadcast_in_dim.19.since_ref.refs_0_
  41.6 49.7 %mixer_forward.1 = (bf16[512,2048]{1,0:T(8,128)(2,1)}, bf16[512,2048]{1,0:T(8,128)(2,1)}, bf16[512,2048]{1,0:T(8,128)(2,1)}, bf16[512,2048]{1,0:T(8,128)(2,1)}, ...) custom-call(s32[512,128]{1,0:T(8,128)} %broadcast_in_dim.19.since_ref.refs_0_, ...), custom_call_target="tpu_custom_call" | custom-call | tf_op jit(solution)/shard_map/mixer_forward/pallas_call | solution.py:180
  91.3 1.3 slice.110.map_ref
  92.6 1.5 slice.68.add_ref
  94.2 27.8 %carry_forward.1.entry_ref.refs_11_ = f32[16,128,128]{2,1,0:T(8,128)S(1)} custom-call(bf16[16,128,128]{2,1,0:T(8,128)(2,1)S(1)} %slice.110.map_ref, f32[16,128,128]{2,1,0:T(8,128)S(1)} %slice.68.add_ref), custom_call_target="tpu_custom_call" | custom-call | tf_op jit(solution)/shard_map/carry_forward/pallas_call | solution.py:495
  122.0 1.0 copy-done.1
  123.0 7.6 mixer_join.1
  130.6 7.8 multiply_reduce_fusion
  138.4 0.6 multiply_multiply_fusion.1
  139.0 1.3 copy-done.6
  140.7 30.4 %all-gather.4.cloned.1.call-done = bf16[2048,2048]{1,0:T(8,128)(2,1)} async-done(((bf16[512,2048]{1,0:T(8,128)(2,1)}), bf16[2048,2048]{1,0:T(8,128)(2,1)}) %all-gather.4.cloned.1.call-update) | async-done | bytes 8388624 | tf_op jit(solution)/shard_map/all_gather | solution.py:1182
  171.1 1.4 fusion.31
  172.9 4.0 fusion.30
  176.9 13.0 %fusion.39 = f32[1024,1408]{1,0:T(8,128)} fusion(bf16[1024,2048]{1,0:T(8,128)(2,1)S(1)} %bitcast.73, bf16[1408,2048]{1,0:T(8,128)(2,1)} %param.28), kind=kOutput, calls=%fused_computation.88 | convolution fusion | flops 5905580032 | bytes 15728640 | tf_op jit(solution)/shard_map/rd,fd->rf/dot_general | solution.py:1216
  189.9 8.5 fusion.36
  198.7 59.0 %all-gather.8.cloned.1.call-done.refs_1_ = bf16[1024,2048]{1,0:T(8,128)(2,1)} async-done(((bf16[256,2048]{1,0:T(8,128)(2,1)}), bf16[1024,2048]{1,0:T(8,128)(2,1)}) %all-gather.8.cloned.1.call-update) | async-done | bytes 4194320 | tf_op jit(solution)/shard_map/all_gather | solution.py:1182
  257.7 12.0 %fusion.40 = f32[1024,1408]{1,0:T(8,128)} fusion(bf16[1024,2048]{1,0:T(8,128)(2,1)} %all-gather.8.cloned.1.call-done.refs_1_, bf16[2048,1408]{1,0:T(8,128)(2,1)} %param.26), kind=kOutput, calls=%fused_computation.89 | convolution fusion | flops 5905580032 | bytes 15728640 | tf_op jit(solution)/shard_map/dot_general | solution.py:1121
  269.7 14.2 %multiply_convert_fusion = (bf16[1024,1408]{1,0:T(8,128)(2,1)}, bf16[1024,1408]{1,0:T(8,128)(2,1)S(1)}, bf16[1024,1408]{1,0:T(8,128)(2,1)S(1)}) fusion(f32[1024,1408]{1,0:T(8,128)} %fusion.40, f32[1024,1408]{1,0:T(8,128)} %fusion.39, bf16[1024,2048]{1,0:T(8,128)(2,1)S(1)} %copy-done.18, bf16[2048,1408]{1,0:T(8,128)(2,1)} %param.27), kind=kOutput, calls=%fused_computation.9 | convolution fusion | flops 5927206912 | bytes 30146560 | tf_op jit(solution)/shard_map/dot_general | solution.py:1121
  283.9 8.8 %fusion.41 = f32[1024,2048]{1,0:T(8,128)} fusion(bf16[1024,1408]{1,0:T(8,128)(2,1)S(1)} %get-tuple-element.133.refs_5_, bf16[2048,1408]{1,0:T(8,128)(2,1)S(1)} %bitcast.89), kind=kOutput, calls=%fused_computation.90 | convolution fusion | flops 5905580032 | bytes 17039360 | tf_op jit(solution)/shard_map/re,de->rd/dot_general | solution.py:1129
  292.8 12.2 %add_convert_fusion = bf16[1024,2048]{1,0:T(8,128)(2,1)} fusion(f32[1024,2048]{1,0:T(8,128)} %fusion.41, bf16[1024,1408]{1,0:T(8,128)(2,1)S(1)} %get-tuple-element.134.refs_7_, bf16[2048,1408]{1,0:T(8,128)(2,1)} %param.27), kind=kOutput, calls=%fused_computation.6 | convolution fusion | flops 5909774336 | bytes 21233664 | tf_op jit(solution)/shard_map/re,de->rd/dot_general | solution.py:1129
  305.6 33.6 %all-gather.6.cloned.1.call-done.refs_0_ = bf16[1024,2048]{1,0:T(8,128)(2,1)} async-done(((bf16[256,2048]{1,0:T(8,128)(2,1)}), bf16[1024,2048]{1,0:T(8,128)(2,1)}) %all-gather.6.cloned.1.call-update) | async-done | bytes 4194320 | tf_op jit(solution)/shard_map/all_gather | solution.py:1182
  339.2 12.0 %fusion.37 = f32[1024,1408]{1,0:T(8,128)} fusion(bf16[1024,2048]{1,0:T(8,128)(2,1)} %all-gather.6.cloned.1.call-done.refs_0_, bf16[2048,1408]{1,0:T(8,128)(2,1)} %param.26), kind=kOutput, calls=%fused_computation.86 | convolution fusion | flops 5905580032 | bytes 15728640 | tf_op jit(solution)/shard_map/dot_general | solution.py:1121
  351.2 14.3 %multiply_convert_fusion.1 = (bf16[1024,1408]{1,0:T(8,128)(2,1)}, bf16[1024,1408]{1,0:T(8,128)(2,1)S(1)}, bf16[1024,1408]{1,0:T(8,128)(2,1)S(1)}) fusion(f32[1024,1408]{1,0:T(8,128)} %fusion.37, f32[1024,1408]{1,0:T(8,128)} %fusion.36, bf16[1024,2048]{1,0:T(8,128)(2,1)S(1)} %copy-done.19, bf16[2048,1408]{1,0:T(8,128)(2,1)} %param.27), kind=kOutput, calls=%fused_computation.10 | convolution fusion | flops 5927206912 | bytes 30146560 | tf_op jit(solution)/shard_map/dot_general | solution.py:1121
  365.5 8.9 %fusion.38 = f32[1024,2048]{1,0:T(8,128)} fusion(bf16[1024,1408]{1,0:T(8,128)(2,1)S(1)} %get-tuple-element.136.refs_4_, bf16[2048,1408]{1,0:T(8,128)(2,1)S(1)} %bitcast.91), kind=kOutput, calls=%fused_computation.87 | convolution fusion | flops 5905580032 | bytes 17039360 | tf_op jit(solution)/shard_map/re,de->rd/dot_general | solution.py:1129
  374.4 12.3 %add_convert_fusion.1 = bf16[1024,2048]{1,0:T(8,128)(2,1)} fusion(f32[1024,2048]{1,0:T(8,128)} %fusion.38, bf16[1024,1408]{1,0:T(8,128)(2,1)S(1)} %get-tuple-element.137.refs_6_, bf16[2048,1408]{1,0:T(8,128)(2,1)} %param.27), kind=kOutput, calls=%fused_computation.7 | convolution fusion | flops 5909774336 | bytes 21233664 | tf_op jit(solution)/shard_map/re,de->rd/dot_general | solution.py:1129
  387.0 98.6 %ffn_grads.1 = f32[3,256,1408]{2,1,0:T(8,128)} custom-call(bf16[1024,2048]{1,0:T(8,128)(2,1)} %all-gather.6.cloned.1.call-done.refs_0_, bf16[1024,2048]{1,0:T(8,128)(2,1)} %all-gather.8.cloned.1.call-done.refs_1_, bf16[1024,2048]{1,0:T(8,128)(2,1)} %bitcast.76, bf16[1024,2048]{1,0:T(8,128)(2,1)} %bitcast.74, bf16[1024,1408]{1,0:T(8,128)(2,1)} %copy-done.23, ...), custom_call_target="tpu_custom_call" | custom-call | tf_op jit(solution)/shard_map/ffn_grads/pallas_call | solution.py:1091
  485.6 10.8 %convolution_convert_fusion.1 = bf16[1024,2048]{1,0:T(8,128)(2,1)} fusion(bf16[1024,1408]{1,0:T(8,128)(2,1)S(1)} %copy-done.20, bf16[1408,2048]{1,0:T(8,128)(2,1)} %param.28), kind=kOutput, calls=%fused_computation.41 | convolution fusion | flops 5907677184 | bytes 12845056 | tf_op jit(solution)/shard_map/dot_general | solution.py:1121
  496.4 11.1 %convolution_convert_fusion.2 = bf16[1024,2048]{1,0:T(8,128)(2,1)} fusion(bf16[1024,1408]{1,0:T(8,128)(2,1)} %get-tuple-element.135.refs_8_, bf16[1408,2048]{1,0:T(8,128)(2,1)} %param.28), kind=kOutput, calls=%fused_computation.42 | convolution fusion | flops 5907677184 | bytes 12845056 | tf_op jit(solution)/shard_map/dot_general | solution.py:1121
  507.7 4.2 fusion.8
  512.3 2.9 fusion.5
  515.3 2.0 copy-done.14
  517.3 6.8 convolution_convert_fusion
  524.2 12.2 %fusion.20.up_ref = f32[512,2048]{1,0:T(8,128)} fusion(bf16[2048,2048]{1,0:T(8,128)(2,1)} %param.24, f32[512,2048]{1,0:T(8,128)} %copy-done.14), kind=kOutput, calls=%fused_computation.49 | convolution fusion | flops 4296015872 | bytes 16777216 | tf_op jit(solution)/shard_map/re,de->rd/dot_general | solution.py:1129
  536.4 10.1 %mixer_core_back.1 = (bf16[512,2048]{1,0:T(8,128)(2,1)}, f32[16,128,128]{2,1,0:T(8,128)}, f32[1,128]{1,0:T(1,128)}) custom-call(bf16[512,2048]{1,0:T(8,128)(2,1)} %get-tuple-element.42.out_add_ref, bf16[512,2048]{1,0:T(8,128)(2,1)} %get-tuple-element.43.out_map_ref, f32[16,128,128]{2,1,0:T(8,128)} %copy-done.1, f32[1,128]{1,0:T(1,128)} %bitcast.86, ...), custom_call_target="tpu_custom_call" | custom-call | tf_op jit(solution)/shard_map/mixer_core_back/pallas_call | solution.py:250
  546.5 1.4 copy-done.5
  547.9 21.6 %carry_backward.1.refs_12_ = f32[16,128,128]{2,1,0:T(8,128)S(1)} custom-call(bf16[16,128,128]{2,1,0:T(8,128)(2,1)S(1)} %copy-done.3, f32[16,128,128]{2,1,0:T(8,128)S(1)} %copy-done.5), custom_call_target="tpu_custom_call" | custom-call | tf_op jit(solution)/shard_map/carry_backward/pallas_call | solution.py:495
  569.5 1.0 copy-done.4
  570.6 0.7 reduce-scatter.13.cloned.1.call-update
  571.3 188.5 %fused_backward.1 = (f32[3,64,2048]{2,1,0:T(8,128)}, f32[512,2048]{1,0:T(8,128)}, f32[3,4,2048]{2,1,0:T(4,128)}, f32[512,16]{1,0:T(8,128)}) custom-call(s32[512,128]{1,0:T(8,128)} %broadcast_in_dim.19.since_ref.refs_0_, f32[512,16]{1,0:T(8,128)} %fusion.32.beta_ref.refs_1_, f32[512,2048]{1,0:T(8,128)} %copy-done.12, f32[512,2048]{1,0:T(8,128)} %copy-done.13, ...), custom_call_target="tpu_custom_call" | custom-call | tf_op jit(solution)/shard_map/fused_backward/pallas_call | solution.py:878
  759.9 1.1 reshape.125
  761.5 0.7 reduce.9
  762.3 2.0 fusion.22
  764.4 5.6 fusion.18
  770.5 32.1 %reduce_small.1 = f32[64,128]{1,0:T(8,128)S(1)} custom-call(f32[2048,128]{1,0:T(8,128)S(1)} %pad.9.small_ref), custom_call_target="tpu_custom_call" | custom-call | tf_op jit(solution)/shard_map/reduce_small/pallas_call | solution.py:598
  802.8 0.6 reshape.128
  803.4 0.7 copy.56
  804.1 4.4 slice_bitcast_fusion
  808.4 2.9 copy.57
  811.4 0.7 slice_reduce_fusion.2
  812.1 0.7 slice_reduce_fusion
  812.8 6.5 fusion.15
  819.3 24.0 %reduce-scatter.17.cloned.1.call-done = bf16[64,2048]{1,0:T(8,128)(2,1)} async-done(((bf16[256,2048]{1,0:T(8,128)(2,1)}), bf16[64,2048]{1,0:T(8,128)(2,1)}) %reduce-scatter.17.cloned.1.call-update) | async-done | bytes 262160 | tf_op jit(solution)/shard_map/reduce_scatter | solution.py:1156
  843.3 2.5 slice_bitcast_fusion.3
  845.8 1.8 convert_bitcast_fusion
  847.6 4.2 add_convert_fusion.2
  (143 shorter events, 6.0 us)
Async XLA Ops:
  7.2 29.2 %copy-start = (bf16[2048,16]{0,1:T(8,128)(2,1)S(1)}, bf16[2048,16]{0,1:T(8,128)(2,1)}, u32[]{:S(2)}) copy-start(bf16[2048,16]{0,1:T(8,128)(2,1)} %param.21) | copy-start | bytes 196612
  7.2 4.1 copy-start.8
  7.2 4.1 copy-start.29
  7.2 163.9 %all-gather.4.cloned.1.call-start = ((), (), s32[]{:S(2)}) async-start(), calls=%async_computation.6 | async-start | bytes 10485760 | tf_op jit(solution)/shard_map/all_gather | solution.py:1182
  8.0 249.8 %all-gather.8.cloned.1.call-start = ((), (), s32[]{:S(2)}) async-start(), calls=%async_computation.9 | async-start | bytes 5242880 | tf_op jit(solution)/shard_map/all_gather | solution.py:1182
  10.7 0.6 copy-start.33
  11.3 8.6 slice-start
  11.8 12.5 %copy-start.10 = (bf16[512,2048]{1,0:T(8,128)(2,1)}, bf16[512,2048]{1,0:T(8,128)(2,1)S(1)}, u32[]{:S(2)}) copy-start(bf16[512,2048]{1,0:T(8,128)(2,1)S(1)} %fusion.11.refs_17_) | copy-start | bytes 6291460
  11.8 8.0 slice-start.1
  11.8 12.5 %slice-start.2 = ((s8[8388608]{0:T(1024)(128)(4,1)}), s8[4194304]{0:T(1024)(128)(4,1)S(1)}, s32[]{:S(2)}) async-start(s8[8388608]{0:T(1024)(128)(4,1)} %bitcast.80), calls=%async_computation.17 | async-start | bytes 8388608
  19.8 4.6 copy-start.11
  19.8 4.6 slice-start.3
  24.4 4.5 copy-start.12
  24.4 11.7 %copy-start.39 = (s32[1,4]{1,0:T(1,128)S(1)}, s32[1,4]{1,0:T(1,128)}, u32[]{:S(2)}) copy-start(s32[1,4]{1,0:T(1,128)} %param.16) | copy-start | bytes 52
  28.9 2.1 copy-start.13
  31.0 9.8 %collective-permute-start = (bf16[3,8,2048]{2,1,0:T(8,128)(2,1)S(1)}, bf16[3,8,2048]{2,1,0:T(8,128)(2,1)S(1)}, u32[]{:S(2)}, u32[]{:S(2)}) collective-permute-start(bf16[3,8,2048]{2,1,0:T(8,128)(2,1)S(1)} %pad_maximum_fusion.1), channel_id=1, source_target_pairs={{0,1},{1,2},{2,3},{4,5},{5,6},{6,7},{8,9},{9,10},{10,11},{12,13},{... | collective-permute-start | bytes 294920 | tf_op jit(solution)/shard_map/ppermute | solution.py:1117
  40.8 0.8 copy-start.28
  92.6 29.4 %copy-start.2 = (bf16[16,128,128]{2,1,0:T(8,128)(2,1)}, bf16[16,128,128]{2,1,0:T(8,128)(2,1)S(1)}, u32[]{:S(2)}) copy-start(bf16[16,128,128]{2,1,0:T(8,128)(2,1)S(1)} %slice.110.map_ref) | copy-start | bytes 1572868
  122.0 1.0 copy-start.1
  130.6 9.7 %copy-start.31 = (f32[2048]{0:T(1024)S(1)}, f32[2048]{0:T(1024)}, u32[]{:S(2)}) copy-start(f32[2048]{0:T(1024)} %param.25) | copy-start | bytes 24580
  138.4 2.0 copy-start.6
  139.0 1.3 copy-start.35
  172.6 166.6 %all-gather.6.cloned.1.call-start = ((), (), s32[]{:S(2)}) async-start(), calls=%async_computation.7 | async-start | bytes 5242880 | tf_op jit(solution)/shard_map/all_gather | solution.py:1182
  172.8 17.0 %slice-start.8 = ((s8[5767168]{0:T(1024)(128)(4,1)}), s8[4194304]{0:T(1024)(128)(4,1)S(1)}, s32[]{:S(2)}) async-start(s8[5767168]{0:T(1024)(128)(4,1)} %bitcast.92), calls=%async_computation.23 | async-start | bytes 8388608
  176.8 13.0 %copy-start.15 = (bf16[4,256,2048]{2,1,0:T(8,128)(2,1)}, bf16[4,256,2048]{2,1,0:T(8,128)(2,1)S(1)}, u32[]{:S(2)}) copy-start(bf16[4,256,2048]{2,1,0:T(8,128)(2,1)S(1)} %get-tuple-element.138) | copy-start | bytes 12582916
  176.8 13.0 %copy-start.16 = (bf16[4,256,2048]{2,1,0:T(8,128)(2,1)}, bf16[4,256,2048]{2,1,0:T(8,128)(2,1)S(1)}, u32[]{:S(2)}) copy-start(bf16[4,256,2048]{2,1,0:T(8,128)(2,1)S(1)} %get-tuple-element.139) | copy-start | bytes 12582916
  176.8 13.0 %slice-start.9 = ((s8[5767168]{0:T(1024)(128)(4,1)}), s8[1572864]{0:T(1024)(128)(4,1)S(1)}, s32[]{:S(2)}) async-start(s8[5767168]{0:T(1024)(128)(4,1)} %bitcast.92), calls=%async_computation.24 | async-start | bytes 3145728
  198.4 309.2 %reduce-scatter.9.cloned.1.call-start = ((), (), s32[]{:S(2)}) async-start(), calls=%async_computation.10 | async-start | bytes 5242880 | tf_op jit(solution)/shard_map/reduce_scatter | solution.py:1185
  257.7 12.0 %copy-start.18 = (bf16[1024,2048]{1,0:T(8,128)(2,1)S(1)}, bf16[1024,2048]{1,0:T(8,128)(2,1)}, u32[]{:S(2)}) copy-start(bf16[1024,2048]{1,0:T(8,128)(2,1)} %all-gather.8.cloned.1.call-done.refs_1_) | copy-start | bytes 12582916
  257.7 26.2 %slice-start.4 = ((s8[5767168]{0:T(1024)(128)(4,1)}), s8[4194304]{0:T(1024)(128)(4,1)S(1)}, s32[]{:S(2)}) async-start(s8[5767168]{0:T(1024)(128)(4,1)} %bitcast.88), calls=%async_computation.19 | async-start | bytes 8388608
  269.7 14.2 %slice-start.5 = ((s8[5767168]{0:T(1024)(128)(4,1)}), s8[1572864]{0:T(1024)(128)(4,1)S(1)}, s32[]{:S(2)}) async-start(s8[5767168]{0:T(1024)(128)(4,1)} %bitcast.88), calls=%async_computation.20 | async-start | bytes 3145728
  283.9 8.9 %copy-start.21 = (bf16[1024,1408]{1,0:T(8,128)(2,1)}, bf16[1024,1408]{1,0:T(8,128)(2,1)S(1)}, u32[]{:S(2)}) copy-start(bf16[1024,1408]{1,0:T(8,128)(2,1)S(1)} %get-tuple-element.133.refs_5_) | copy-start | bytes 8650756
  283.9 8.9 %copy-start.22 = (bf16[1024,1408]{1,0:T(8,128)(2,1)}, bf16[1024,1408]{1,0:T(8,128)(2,1)S(1)}, u32[]{:S(2)}) copy-start(bf16[1024,1408]{1,0:T(8,128)(2,1)S(1)} %get-tuple-element.134.refs_7_) | copy-start | bytes 8650756
  305.0 202.6 %reduce-scatter.7.cloned.1.call-start = ((), (), s32[]{:S(2)}) async-start(), calls=%async_computation.8 | async-start | bytes 5242880 | tf_op jit(solution)/shard_map/reduce_scatter | solution.py:1185
  339.2 12.0 %copy-start.19 = (bf16[1024,2048]{1,0:T(8,128)(2,1)S(1)}, bf16[1024,2048]{1,0:T(8,128)(2,1)}, u32[]{:S(2)}) copy-start(bf16[1024,2048]{1,0:T(8,128)(2,1)} %all-gather.6.cloned.1.call-done.refs_0_) | copy-start | bytes 12582916
  339.2 26.2 %slice-start.6 = ((s8[5767168]{0:T(1024)(128)(4,1)}), s8[4194304]{0:T(1024)(128)(4,1)S(1)}, s32[]{:S(2)}) async-start(s8[5767168]{0:T(1024)(128)(4,1)} %bitcast.90), calls=%async_computation.21 | async-start | bytes 8388608
  351.2 14.3 %slice-start.7 = ((s8[5767168]{0:T(1024)(128)(4,1)}), s8[1572864]{0:T(1024)(128)(4,1)S(1)}, s32[]{:S(2)}) async-start(s8[5767168]{0:T(1024)(128)(4,1)} %bitcast.90), calls=%async_computation.22 | async-start | bytes 3145728
  365.4 9.0 %copy-start.23 = (bf16[1024,1408]{1,0:T(8,128)(2,1)}, bf16[1024,1408]{1,0:T(8,128)(2,1)S(1)}, u32[]{:S(2)}) copy-start(bf16[1024,1408]{1,0:T(8,128)(2,1)S(1)} %get-tuple-element.136.refs_4_) | copy-start | bytes 8650756
  365.4 9.0 %copy-start.24 = (bf16[1024,1408]{1,0:T(8,128)(2,1)}, bf16[1024,1408]{1,0:T(8,128)(2,1)S(1)}, u32[]{:S(2)}) copy-start(bf16[1024,1408]{1,0:T(8,128)(2,1)S(1)} %get-tuple-element.137.refs_6_) | copy-start | bytes 8650756
  386.7 415.9 %reduce-scatter.15.cloned.1.call-start = ((), (), s32[]{:S(2)}) async-start(), calls=%async_computation.13 | async-start | bytes 9437184 | tf_op jit(solution)/shard_map/reduce_scatter | solution.py:1155
  386.9 98.7 %copy-start.20 = (bf16[1024,1408]{1,0:T(8,128)(2,1)S(1)}, bf16[1024,1408]{1,0:T(8,128)(2,1)}, u32[]{:S(2)}) copy-start(bf16[1024,1408]{1,0:T(8,128)(2,1)} %get-tuple-element.132.refs_9_) | copy-start | bytes 8650756
  496.4 11.2 %copy-start.32 = (f32[2048]{0:T(1024)S(1)}, f32[2048]{0:T(1024)}, u32[]{:S(2)}) copy-start(f32[2048]{0:T(1024)} %param.25) | copy-start | bytes 24580
  496.4 11.2 %copy-start.36 = (f32[512]{0:T(512)S(1)}, f32[512]{0:T(512)}, u32[]{:S(2)}) copy-start(f32[512]{0:T(512)} %copy-done.35) | copy-start | bytes 6148
  507.6 4.4 copy-start.17
  507.6 4.4 copy-start.38
  507.7 4.6 copy-start.7
  512.3 5.0 copy-start.25
  515.3 2.0 copy-start.14
  524.1 295.2 %reduce-scatter.11.cloned.1.call-start = ((), (), s32[]{:S(2)}) async-start(), calls=%async_computation.11 | async-start | bytes 5242880 | tf_op jit(solution)/shard_map/reduce_scatter | solution.py:1185
  536.4 10.1 %copy-start.3 = (bf16[16,128,128]{2,1,0:T(8,128)(2,1)S(1)}, bf16[16,128,128]{2,1,0:T(8,128)(2,1)}, u32[]{:S(2)}) copy-start(bf16[16,128,128]{2,1,0:T(8,128)(2,1)} %copy-done.2) | copy-start | bytes 1572868
  546.5 1.4 copy-start.5
  569.5 1.0 copy-start.4
  570.5 248.8 %reduce-scatter.13.cloned.1.call-start = ((), (), s32[]{:S(2)}) async-start(), calls=%async_computation.12 | async-start | bytes 5242880 | tf_op jit(solution)/shard_map/reduce_scatter | solution.py:1185
  571.3 272.0 %reduce-scatter.17.cloned.1.call-start = ((), (), s32[]{:S(2)}) async-start(), calls=%async_computation.14 | async-start | bytes 1310720 | tf_op jit(solution)/shard_map/reduce_scatter | solution.py:1156
  571.3 190.2 %copy-start.40 = (f32[1,128]{1,0:T(1,128)S(1)}, f32[1,128]{1,0:T(1,128)}, u32[]{:S(2)}) copy-start(f32[1,128]{1,0:T(1,128)} %get-tuple-element.66) | copy-start | bytes 1540
  571.3 193.0 %copy-start.30 = (f32[2048]{0:T(1024)S(1)}, f32[2048]{0:T(1024)}, u32[]{:S(2)}) copy-start(f32[2048]{0:T(1024)} %param.17) | copy-start | bytes 24580
  571.3 193.0 %copy-start.34 = (f32[512]{0:T(512)S(1)}, f32[512]{0:T(512)}, u32[]{:S(2)}) copy-start(f32[512]{0:T(512)} %copy-done.33) | copy-start | bytes 6148
  759.9 4.5 copy-start.9
  804.1 8.7 %copy-start.37 = (f32[512]{0:T(512)S(1)}, f32[512]{0:T(512)}, u32[]{:S(2)}) copy-start(f32[512]{0:T(512)} %get-tuple-element.148) | copy-start | bytes 6148
  819.3 28.3 %copy-start.26 = (bf16[256,2048]{1,0:T(8,128)(2,1)S(1)}, bf16[256,2048]{1,0:T(8,128)(2,1)}, u32[]{:S(2)}) copy-start(bf16[256,2048]{1,0:T(8,128)(2,1)} %reduce-scatter.11.cloned.1.call-done) | copy-start | bytes 3145732
  819.3 28.3 %copy-start.27 = (bf16[256,2048]{1,0:T(8,128)(2,1)S(1)}, bf16[256,2048]{1,0:T(8,128)(2,1)}, u32[]{:S(2)}) copy-start(bf16[256,2048]{1,0:T(8,128)(2,1)} %reduce-scatter.13.cloned.1.call-done) | copy-start | bytes 3145732
Sparse Core Ops, SparseCore 0:
  9.6 161.4 all-gather.3
  173.2 84.4 all-gather.7
  259.9 79.2 all-gather.5
  341.3 75.2 reduce-scatter.8
  418.9 77.2 reduce-scatter.6
  524.3 69.4 reduce-scatter.14
  596.1 103.4 reduce-scatter.10
  701.9 110.1 reduce-scatter.12
  814.5 28.7 reduce-scatter.16

commit v6 on v5

--- a/solution.py
+++ b/solution.py
@@ -616,18 +616,18 @@
 
 
 RING = 3
-HELD = 6
+HELD = 5
 
 
 def fused_kernel(*refs):
     heads_in = refs[:14]
     since_ref = refs[0]
     (
-        w_query_ref, w_key_ref, w_value_ref, normed_hbm,
+        w_query_ref, w_key_ref, w_value_ref, mixed_ref, normed_hbm, branch_hbm,
         grad_hbm, d_normed_hbm, d_taps_ref, d_beta_ref,
-        ext, back, left_own, left_away, left_sib, d_proj, d_proj_sib, halo_out, halo_in,
+        ext, back, left_own, left_sib, d_proj, d_proj_sib, halo_out, halo_in,
         total, got2, got3, gotz, d_normed, grad,
-        local_sem, left_send, left_recv, right_send, right_recv, halo_send, halo_recv,
+        local_sem, grad_sem, left_send, left_recv, right_send, right_recv, halo_send, halo_recv,
         send2, recv2, send3, recv3, sendz, recvz,
     ) = refs[14:]
     step = pl.program_id(0)
@@ -636,7 +636,8 @@
     core, x, y, sib, flip_x, flip_y = bits(dp)
     depth = lax.axis_size("narrow")
     tokens = since_ref.shape[0]
-    rows = left_own.shape[1]
+    parts = d_proj_sib.shape[1]
+    rows = left_own.shape[2]
     cols = d_proj.shape[3]
     share = rows // depth
     peers = [(z + k) % depth for k in range(1, depth)]
@@ -644,16 +645,25 @@
     def stripe_lanes(stripe, which):
         return pl.ds(pl.multiple_of((stripe * 2 + which) * rows, rows), rows)
 
-    def left_copy(stripe):
+    def left_copy(k):
+        source = (normed_hbm, branch_hbm)[k // 4]
         return remote(
-            left_away.at[stripe], left_sib.at[stripe], left_send.at[stripe], left_recv.at[stripe], {"dp": sib}
+            source.at[:, stripe_lanes(k % 4, 1 - core)], d_proj_sib.at[1 + k // 4, k % 4],
+            left_send.at[k], left_recv.at[k], {"dp": sib},
         )
 
-    def right_copy(unit):
-        return remote(
-            d_proj.at[unit % RING], d_proj_sib.at[unit % RING],
-            right_send.at[unit % RING], right_recv.at[unit % RING], {"dp": sib},
-        )
+    def right_copies(unit):
+        slot = unit % RING
+        return [
+            remote(
+                d_proj.at[slot], d_proj_sib.at[slot, 0 : parts - 1],
+                right_send.at[slot, 0], right_recv.at[slot, 0], {"dp": sib},
+            ),
+            remote(
+                mixed_ref, d_proj_sib.at[slot, parts - 1],
+                right_send.at[slot, 1], right_recv.at[slot, 1], {"dp": sib},
+            ),
+        ]
 
     def halo_copy(unit):
         return remote(
@@ -694,7 +704,8 @@
     def _():
         loads = [
             pltpu.make_async_copy(
-                normed_hbm.at[:, stripe_lanes(k % 4, 1 - core if k < 4 else core)], d_proj.at[k // 3, k % 3], local_sem.at[k]
+                (normed_hbm, branch_hbm)[k // 4].at[:, stripe_lanes(k % 4, core)],
+                d_proj.at[k // 3, k % 3], local_sem.at[k],
             )
             for k in range(8)
         ]
@@ -704,13 +715,17 @@
         back[:, :, PAD + tokens :, :] = jnp.zeros((2, CONV, PAD, BLOCK), F32)
         d_normed[...] = jnp.zeros_like(d_normed)
         meet((sib, flip_x, flip_y), peers)
-        for stripe in range(4):
-            loads[stripe].wait()
-            left_away[stripe] = d_proj[stripe // 3, stripe % 3].astype(F32).T.astype(BF16)
-            left_copy(stripe).start()
-        for stripe in range(4):
-            loads[4 + stripe].wait()
-            left_own[stripe] = d_proj[(4 + stripe) // 3, (4 + stripe) % 3].astype(F32).T.astype(BF16)
+        for k in range(8):
+            left_copy(k).start()
+        for k in range(8):
+            loads[k].wait()
+            left_own[k // 4, k % 4] = d_proj[k // 3, k % 3].astype(F32).T.astype(BF16)
+
+    @pl.when(step == 1)
+    def _():
+        for k in range(8):
+            left_copy(k).wait()
+            left_sib[k // 4, k % 4] = d_proj_sib[1 + k // 4, k % 4].astype(F32).T.astype(BF16)
 
     @pl.when(step >= 1)
     def _():
@@ -730,7 +745,8 @@
         def _():
             halo_copy(unit).wait_send()
 
-        right_copy(unit).start()
+        for copy in right_copies(unit):
+            copy.start()
 
     @pl.when(step < units)
     def _():
@@ -744,23 +760,23 @@
         def _():
             halo_copy(step).start()
 
-    @pl.when(step == 1)
-    def _():
-        for stripe in range(4):
-            left_copy(stripe).wait()
-
     @pl.when(step >= 1)
     def _():
         unit = step - 1
         away, kept, _, _, _, _ = order(unit)
-        right_copy(unit).wait()
+        for copy in right_copies(unit):
+            copy.wait()
 
         def one(k, _):
             j = k % 2
             stripe = (k // 2) * kept(j) + (1 - k // 2) * away(j)
-            for part in range(3):
-                value = jnp.dot(left_own[stripe], d_proj[unit % RING, part], preferred_element_type=F32)
-                value = value + jnp.dot(left_sib[stripe], d_proj_sib[unit % RING, part], preferred_element_type=F32)
+            for part in range(parts):
+                which = part // (parts - 1)
+                mine = d_proj[unit % RING, part] if which == 0 else mixed_ref[...]
+                value = jnp.dot(left_own[which, stripe], mine, preferred_element_type=F32)
+                value = value + jnp.dot(
+                    left_sib[which, stripe], d_proj_sib[unit % RING, part], preferred_element_type=F32
+                )
                 total[unit % HELD, stripe, part * rows : (part + 1) * rows, :] = value.astype(BF16)
 
             @pl.when(k < 2)
@@ -791,25 +807,34 @@
         copy3(unit).start()
         add_rows(total.at[unit % HELD, kept(near)], got2.at[unit, near], 64)
 
+    def grad_copy(unit):
+        at = pl.ds(pl.multiple_of(unit * cols, cols), cols)
+        return pltpu.make_async_copy(grad.at[unit % 2], grad_hbm.at[:, :, at], grad_sem.at[unit % 2])
+
     def third(unit):
         _, kept, _, _, _, near = order(unit)
         copy3(unit).wait()
         add_rows(total.at[unit % HELD, kept(near)], got3.at[unit], 64)
         for k in range(depth - 1):
-            for part in range(3):
+            for part in range(parts):
                 copyz(unit, part, k).start()
 
     def fourth(unit):
         _, kept, _, _, _, near = order(unit)
         for k in range(depth - 1):
-            for part in range(3):
+            for part in range(parts):
                 copyz(unit, part, k).wait()
-        for part in range(3):
+        @pl.when(unit >= 2)
+        def _():
+            grad_copy(unit - 2).wait()
+
+        for part in range(parts):
             at = pl.ds(pl.multiple_of(part * rows + z * share, share), share)
             value = total[unit % HELD, kept(near), at, :].astype(F32)
             for k in range(depth - 1):
                 value = value + gotz[unit, k, part * share : (part + 1) * share, :].astype(F32)
-            grad[part, :, pl.ds(pl.multiple_of(unit * cols, cols), cols)] = value
+            grad[unit % 2, part] = value
+        grad_copy(unit).start()
 
     def stages(at):
         @pl.when((at >= 3) & (at < units + 3))
@@ -837,14 +862,13 @@
 
         lax.fori_loop(units + 1, units + 5, one, 0)
         save.wait()
-        store = pltpu.make_async_copy(grad, grad_hbm, local_sem.at[1])
-        store.start()
-        store.wait()
+        grad_copy(units - 2).wait()
+        grad_copy(units - 1).wait()
 
 
 def fused_backward(
     since, beta_logit, query, key, value, halo, taps, new_add, new_map, inverse, starts, entry, exit_grad, d_core,
-    w_query, w_key, w_value, normed,
+    w_query, w_key, w_value, mixed, normed, branch,
 ):
     tokens, width = query.shape
     heads = width // BLOCK
@@ -873,7 +897,9 @@
     def each(*tail):
         return pl.BlockSpec((HEADS_STEP,) + tail, lambda h: (now(h),) + (0,) * len(tail))
 
-    weight = pl.BlockSpec((width, cols), lambda h: (0, before(h)))
+    weight = pl.BlockSpec((width, cols), lambda h: (0, before(h)), pipeline_mode=pl.Buffered(1))
+    mixed_spec = pl.BlockSpec((tokens, cols), lambda h: (0, before(h)))
+    parts = 4
     anywhere = pl.BlockSpec(memory_space=pl.ANY)
     return pl.pallas_call(
         fused_kernel,
@@ -882,11 +908,11 @@
             whole(since.shape), whole(beta_logit.shape), wide, wide, wide, lanes(3, PAD), lanes(3, CONV),
             wide, wide, each(blocks, BLOCK, BLOCK), each(blocks, BLOCK, 2 * BLOCK),
             each(BLOCK, BLOCK), each(BLOCK, BLOCK), wide,
-            weight, weight, weight, anywhere,
+            weight, weight, weight, mixed_spec, anywhere, anywhere,
         ],
         out_specs=[anywhere, anywhere, lanes(3, CONV), whole(beta_logit.shape)],
         out_shape=[
-            jax.ShapeDtypeStruct((3, share, width), F32),
+            jax.ShapeDtypeStruct((parts, share, width), F32),
             jax.ShapeDtypeStruct((tokens, width), F32),
             jax.ShapeDtypeStruct((3, CONV, width), F32),
             jax.ShapeDtypeStruct(beta_logit.shape, F32),
@@ -894,30 +920,29 @@
         scratch_shapes=[
             pltpu.VMEM((3 * HEADS_STEP, PAD + tokens, BLOCK), F32),
             pltpu.VMEM((2, CONV, PAD + tokens + PAD, BLOCK), F32),
-            pltpu.VMEM((4, rows, tokens), BF16),
-            pltpu.VMEM((4, rows, tokens), BF16),
-            pltpu.VMEM((4, rows, tokens), BF16),
+            pltpu.VMEM((2, 4, rows, tokens), BF16),
+            pltpu.VMEM((2, 4, rows, tokens), BF16),
             pltpu.VMEM((RING, 3, tokens, cols), BF16),
-            pltpu.VMEM((RING, 3, tokens, cols), BF16),
+            pltpu.VMEM((RING, parts, tokens, cols), BF16),
             pltpu.VMEM((units, 3, PAD, cols), F32),
             pltpu.VMEM((units, 3, PAD, cols), F32),
-            pltpu.VMEM((HELD, 4, 3 * rows, cols), BF16),
-            pltpu.VMEM((units, 2, 3 * rows, cols), BF16),
-            pltpu.VMEM((units, 3 * rows, cols), BF16),
-            pltpu.VMEM((units, depth - 1, 3 * share, cols), BF16),
+            pltpu.VMEM((HELD, 4, parts * rows, cols), BF16),
+            pltpu.VMEM((units, 2, parts * rows, cols), BF16),
+            pltpu.VMEM((units, parts * rows, cols), BF16),
+            pltpu.VMEM((units, depth - 1, parts * share, cols), BF16),
             pltpu.VMEM((tokens, width), F32),
-            pltpu.VMEM((3, share, width), F32),
-            dma((8,)), dma((4,)), dma((4,)), dma((RING,)), dma((RING,)), dma((units,)), dma((units,)),
+            pltpu.VMEM((2, parts, share, cols), F32),
+            dma((8,)), dma((2,)), dma((8,)), dma((8,)), dma((RING, 2)), dma((RING, 2)), dma((units,)), dma((units,)),
             dma((units, 2)), dma((units, 2)), dma((units,)), dma((units,)),
-            dma((units, depth - 1, 3)), dma((units, depth - 1, 3)),
+            dma((units, depth - 1, parts)), dma((units, depth - 1, parts)),
         ],
         compiler_params=pltpu.CompilerParams(
-            collective_id=5, has_side_effects=True, vmem_limit_bytes=61 * 1024 * 1024
+            collective_id=5, has_side_effects=True, vmem_limit_bytes=62 * 1024 * 1024
         ),
         name="fused_backward",
     )(
         since, beta_logit, query, key, value, halo, taps, new_add, new_map, inverse, starts, entry, exit_grad, d_core,
-        w_query, w_key, w_value, normed,
+        w_query, w_key, w_value, mixed, normed, branch,
     )
 
 
@@ -1188,10 +1213,10 @@
     since = since_start(doc_lengths, offset, tok_rows)
     inputs = tokens.astype(F32)
     normed = rms_scale(inputs, attn_gain, 1e-06).astype(BF16)
-    query, key, value = (matmul(normed, w) for w in (w_query, w_key, w_value))
+    query, key, value = (matmul(normed, w).astype(BF16) for w in (w_query, w_key, w_value))
     beta_logit = matmul(normed, w_beta)
     halo = shifted(
-        jnp.stack([part[tok_rows - PAD :].astype(BF16) for part in (query, key, value)]), "narrow", 1
+        jnp.stack([part[tok_rows - PAD :] for part in (query, key, value)]), "narrow", 1
     )
     out_add, out_map, new_add, new_map, inverse, starts, end = mixer_forward(
         since, beta_logit, query, key, value, halo, conv_weight
@@ -1206,7 +1231,7 @@
     cot = cot.reshape(-1, tok_rows, model_width)
     cot = [cot[:, part].reshape(-1, model_width) for part in parts]
     gathered = [gather(normed_mlp[part]) for part in parts]
-    activation, d_gate, d_up, d_normed_parts = [], [], [], []
+    activation, d_gate, d_up, d_normed_parts, out_parts = [], [], [], [], []
     for at in range(HALVES):
         gate_proj = matmul(gathered[at], w_gate)
         up_proj = matmul(gathered[at], w_up)
@@ -1218,8 +1243,13 @@
             (d_act * up_proj * gate_sigmoid * (1.0 + gate_proj * (1.0 - gate_sigmoid))).astype(BF16)
         )
         d_up.append((d_act * silu_gate).astype(BF16))
-        d_normed_parts.append(scatter((dot_nt(d_gate[at], w_gate) + dot_nt(d_up[at], w_up)).astype(BF16)))
-    out_parts = [matmul(act, w_down).astype(BF16) for act in activation]
+        d_part = (dot_nt(d_gate[at], w_gate) + dot_nt(d_up[at], w_up)).astype(BF16)
+        out_parts.append(matmul(activation[at], w_down).astype(BF16))
+        if at + 1 < HALVES:
+            d_part, out_parts[at], gathered[at + 1] = lax.optimization_barrier(
+                (d_part, out_parts[at], gathered[at + 1])
+            )
+        d_normed_parts.append(scatter(d_part))
     if lax.axis_size("dp") == 8:
         ffn_sums = ffn_grads((gathered, cot), (d_gate, d_up, activation))
     else:
@@ -1235,25 +1265,26 @@
     d_hidden_norm, mlp_gain_term = norm_back(hidden, mlp_gain, d_normed_mlp, 1e-06)
     d_hidden = grad_out.astype(F32) + d_hidden_norm
     d_branch = d_hidden.astype(BF16)
-    w_out_term = dot_tn(d_branch, attn_mixed).astype(BF16)
     d_mixed = dot_nt(d_branch, w_out)
     d_core, start_grad, out_gain_term = mixer_core_back(out_add, out_map, entry, gain_row, d_mixed)
     exit_grad = carry_chain(transfer, start_grad, "narrow", False)
     exit_grad, out_parts = lax.optimization_barrier((exit_grad, out_parts))
-    w_out_term = scatter_all(w_out_term, 0)
     ffn_parts = [scatter(part) for part in out_parts]
     mixer_args = (
         since, beta_logit, query, key, value, halo, conv_weight,
         new_add, new_map, inverse, starts, entry, exit_grad, d_core,
     )
     if lax.axis_size("dp") == 8:
-        grads, d_normed, conv_term, d_beta = fused_backward(*mixer_args, w_query, w_key, w_value, normed)
+        grads, d_normed, conv_term, d_beta = fused_backward(
+            *mixer_args, w_query, w_key, w_value, attn_mixed, normed, d_branch
+        )
     else:
         d_proj, d_halo, conv_term, d_beta = mixer_backward(*mixer_args)
         after = shifted(d_halo.astype(BF16), "narrow", -1)
         d_proj = d_proj.at[:, tok_rows - PAD :].add(after)
         d_normed = sum(dot_nt(part, w) for part, w in zip(d_proj, (w_query, w_key, w_value)))
-        grads = jnp.stack([scatter_all(dot_tn(normed, part).astype(BF16), 0).astype(F32) for part in d_proj])
+        pairs = [(normed, part) for part in d_proj] + [(d_branch, attn_mixed)]
+        grads = jnp.stack([scatter_all(dot_tn(a, c).astype(BF16), 0).astype(F32) for a, c in pairs])
     d_beta_low = d_beta.astype(BF16)
     beta_term = jnp.einsum("rd,rh->dh", normed, d_beta_low, preferred_element_type=F32)
     d_normed = d_normed + jnp.einsum("rh,dh->rd", d_beta_low, w_beta, preferred_element_type=F32)
@@ -1286,10 +1317,10 @@
     grad_attn_gain = small[:, heads + taps]
     grad_mlp_gain = small[:, heads + taps + 1]
     grad_out_gain = small[:gain_share, heads + taps + 2]
-    ffn_parts, w_out_term, grads = lax.optimization_barrier((ffn_parts, w_out_term, grads))
+    ffn_parts, grads = lax.optimization_barrier((ffn_parts, grads))
     block_out = (hidden + jnp.concatenate(ffn_parts, axis=0).astype(F32)).astype(BF16)
     grad_query, grad_key, grad_value = grads[0], grads[1], grads[2]
-    grad_w_out = w_out_term.astype(F32).T
+    grad_w_out = grads[3].T
     return (
         block_out,
         grad_tokens,

time: 867 us -> 863 us (level)
  Pallas kernels: 436 us -> 477 us
  waiting for transfers between devices: 150 us -> 124 us
  matrix products: 192 us -> 180 us
    pallas_call x1, Pallas kernels: 189 us -> 237 us  [fused_backward(): pl.pallas_call(fused_kernel, grid=(units + 1,), in_specs=[whole(since.sha...]
    reduce_scatter x2 -> x0, waiting for transfers between devices: 24 us -> none  [the longest x1 24 us: scatter_all(): return lax.psum_scatter(part, 'narrow', scatter_dimension=dim, tiled=True)]
    pallas_call x1, Pallas kernels: 32.1 us -> 21.2 us  [reduce_small(): pl.pallas_call(small_kernel, in_specs=[pl.BlockSpec(memory_space=pltpu.VM...]
  transfers between devices with their start and end apart: 10 -> 8, of which waited for: 5 -> 4; matrix products, arithmetic and copies ran while one was open for 25% -> 23% of each run, Pallas kernels for 51% -> 52%
where the time goes in v6:
time: 863 us; the launch traced here: 857 us
  Pallas kernels  477 us (55%)
  matrix products  180 us (21%)
  waiting for transfers between devices  124 us (14%)
  local copies, waits for them, and re-layouts  33 us (4%)
  other arithmetic  20.5 us (2%)
  between operations  15.3 us (2%)
    pallas_call x1, Pallas kernels, fused_backward(): pl.pallas_call(fused_kernel, grid=(units + 1,), in_specs=[whole(since.sha...  237 us
    all_gather x3, waiting for transfers between devices, gather(): return lax.all_gather(rows, 'narrow', axis=0, tiled=True)  122 us
    dot_general x11, matrix products, matmul(): return jnp.dot(left, right, preferred_element_type=F32)  99.1 us
    pallas_call x1, Pallas kernels, ffn_grads(): pl.pallas_call(ffn_grads_kernel, in_specs=[pl.BlockSpec(memory_space=pl.A...  98.7 us
    dot_general x5, matrix products, dot_nt(): return jnp.einsum('re,de->rd', left, right, preferred_element_type=F32)  51.6 us
    pallas_call x2, Pallas kernels, carry_chain(): pl.pallas_call(functools.partial(chain_kernel, axis, forward), in_specs=[...  51.5 us
    pallas_call x1, Pallas kernels, mixer_forward(): pl.pallas_call(forward_kernel, grid=(heads // HEADS_STEP,), in_specs=[who...  50.8 us
    dot_general x2, matrix products, local(): d_act = jnp.einsum('rd,fd->rf', cot[at], w_down, preferred_element_type=F32)  21.5 us
  transfers between devices with their start and end apart: 8, of which 4 were waited for; matrix products, arithmetic and copies ran while one was open for 23% of the time, Pallas kernels for 52%

profile of v6, /device:TPU:0, one launch (start us, length us, event | category | flops | bytes accessed | tf_op | source)
XLA Modules:
  0.0 856.8 jit_solution(14150135697173594768)
XLA Ops:
  7.3 0.7 all-gather.4.cloned.1.call-update
  8.0 2.1 fusion.9
  10.1 0.6 multiply_multiply_fusion
  10.7 0.6 copy-done.34
  11.3 0.5 fusion.11.refs_18_
  11.9 9.2 %convolution_convert_fusion.4.query_ref.refs_2_ = bf16[512,2048]{1,0:T(8,128)(2,1)S(1)} fusion(bf16[512,2048]{1,0:T(8,128)(2,1)S(1)} %fusion.11.refs_18_, bf16[2048,2048]{1,0:T(8,128)(2,1)} %refs_14_.1), kind=kOutput, calls=%fused_computation.44 | convolution fusion | flops 4296015872 | bytes 12582912 | tf_op jit(solution)/shard_map/dot_general | solution.py:1146
  21.2 4.8 convolution_convert_fusion.2.value_ref.refs_4_
  26.0 4.8 convolution_convert_fusion.3.key_ref.refs_3_
  30.8 1.3 copy-done.18
  32.1 5.5 collective-permute-start
  37.9 3.0 fusion.27.beta_ref.refs_1_
  40.9 1.0 collective-permute-done.halo_ref.refs_5_
  41.9 0.8 broadcast_in_dim.19.since_ref.refs_0_
  42.7 50.8 %mixer_forward.1 = (bf16[512,2048]{1,0:T(8,128)(2,1)}, bf16[512,2048]{1,0:T(8,128)(2,1)}, bf16[512,2048]{1,0:T(8,128)(2,1)}, bf16[512,2048]{1,0:T(8,128)(2,1)}, ...) custom-call(s32[512,128]{1,0:T(8,128)} %broadcast_in_dim.19.since_ref.refs_0_, ...), custom_call_target="tpu_custom_call" | custom-call | tf_op jit(solution)/shard_map/mixer_forward/pallas_call | solution.py:180
  93.5 1.3 slice.106.map_ref
  94.8 1.5 slice.68.add_ref
  96.3 26.7 %carry_forward.1.entry_ref.refs_11_ = f32[16,128,128]{2,1,0:T(8,128)S(1)} custom-call(bf16[16,128,128]{2,1,0:T(8,128)(2,1)S(1)} %slice.106.map_ref, f32[16,128,128]{2,1,0:T(8,128)S(1)} %slice.68.add_ref), custom_call_target="tpu_custom_call" | custom-call | tf_op jit(solution)/shard_map/carry_forward/pallas_call | solution.py:495
  123.1 1.0 copy-done.1
  124.0 7.6 mixer_join.1.refs_17_
  131.6 7.8 multiply_reduce_fusion
  139.4 0.6 multiply_multiply_fusion.1
  140.0 1.3 copy-done.6
  141.8 29.3 %all-gather.4.cloned.1.call-done = bf16[2048,2048]{1,0:T(8,128)(2,1)} async-done(((bf16[512,2048]{1,0:T(8,128)(2,1)}), bf16[2048,2048]{1,0:T(8,128)(2,1)}) %all-gather.4.cloned.1.call-update) | async-done | bytes 8388624 | tf_op jit(solution)/shard_map/all_gather | solution.py:1207
  171.1 1.4 fusion.26
  172.8 4.0 fusion.25
  176.8 12.9 %fusion.28 = f32[1024,1408]{1,0:T(8,128)} fusion(bf16[1024,2048]{1,0:T(8,128)(2,1)S(1)} %bitcast.77, bf16[1408,2048]{1,0:T(8,128)(2,1)} %param.28), kind=kOutput, calls=%fused_computation.79 | convolution fusion | flops 5905580032 | bytes 15728640 | tf_op jit(solution)/shard_map/rd,fd->rf/dot_general | solution.py:1241
  189.8 8.5 fusion.31
  198.6 64.6 %all-gather.6.cloned.1.call-done.refs_0_ = bf16[1024,2048]{1,0:T(8,128)(2,1)} async-done(((bf16[256,2048]{1,0:T(8,128)(2,1)}), bf16[1024,2048]{1,0:T(8,128)(2,1)}) %all-gather.6.cloned.1.call-update) | async-done | bytes 4194320 | tf_op jit(solution)/shard_map/all_gather | solution.py:1207
  263.2 10.9 %fusion.29 = f32[1024,1408]{1,0:T(8,128)S(1)} fusion(bf16[1024,2048]{1,0:T(8,128)(2,1)} %all-gather.6.cloned.1.call-done.refs_0_, bf16[2048,1408]{1,0:T(8,128)(2,1)} %param.26), kind=kOutput, calls=%fused_computation.80 | convolution fusion | flops 5905580032 | bytes 15728640 | tf_op jit(solution)/shard_map/dot_general | solution.py:1146
  274.2 13.5 %multiply_convert_fusion.3 = (bf16[1024,1408]{1,0:T(8,128)(2,1)S(1)}, bf16[1024,1408]{1,0:T(8,128)(2,1)}, bf16[1024,1408]{1,0:T(8,128)(2,1)}) fusion(f32[1024,1408]{1,0:T(8,128)S(1)} %fusion.29, f32[1024,1408]{1,0:T(8,128)} %fusion.28, bf16[1024,2048]{1,0:T(8,128)(2,1)S(1)} %copy-done.20, bf16[2048,1408]{1,0:T(8,128)(2,1)} %param.27), kind=kOutput, calls=%fused_computation.13 | convolution fusion | flops 5927206912 | bytes 30146560 | tf_op jit(solution)/shard_map/dot_general | solution.py:1146
  287.6 8.3 convolution_convert_fusion.1
  295.9 9.8 %fusion.30 = f32[1024,2048]{1,0:T(8,128)S(1)} fusion(bf16[1024,1408]{1,0:T(8,128)(2,1)} %get-tuple-element.140.refs_4_, bf16[2048,1408]{1,0:T(8,128)(2,1)} %param.26), kind=kOutput, calls=%fused_computation.81 | convolution fusion | flops 5905580032 | bytes 17039360 | tf_op jit(solution)/shard_map/re,de->rd/dot_general | solution.py:1154
  305.7 11.0 %add_convert_fusion.1 = bf16[1024,2048]{1,0:T(8,128)(2,1)} fusion(f32[1024,2048]{1,0:T(8,128)S(1)} %fusion.30, bf16[1024,1408]{1,0:T(8,128)(2,1)S(1)} %copy-done.23, bf16[2048,1408]{1,0:T(8,128)(2,1)} %param.27), kind=kOutput, calls=%fused_computation.7 | convolution fusion | flops 5909774336 | bytes 21233664 | tf_op jit(solution)/shard_map/re,de->rd/dot_general | solution.py:1154
  316.7 27.9 %all-gather.8.cloned.1.call-done.refs_1_ = bf16[1024,2048]{1,0:T(8,128)(2,1)} async-done(((bf16[256,2048]{1,0:T(8,128)(2,1)}), bf16[1024,2048]{1,0:T(8,128)(2,1)}) %all-gather.8.cloned.1.call-update) | async-done | bytes 4194320 | tf_op jit(solution)/shard_map/all_gather | solution.py:1207
  345.2 11.8 %fusion.32 = f32[1024,1408]{1,0:T(8,128)} fusion(bf16[1024,2048]{1,0:T(8,128)(2,1)} %all-gather.8.cloned.1.call-done.refs_1_, bf16[2048,1408]{1,0:T(8,128)(2,1)} %param.26), kind=kOutput, calls=%fused_computation.83 | convolution fusion | flops 5905580032 | bytes 15728640 | tf_op jit(solution)/shard_map/dot_general | solution.py:1146
  357.0 14.3 %multiply_convert_fusion = (bf16[1024,1408]{1,0:T(8,128)(2,1)}, bf16[1024,1408]{1,0:T(8,128)(2,1)S(1)}, bf16[1024,1408]{1,0:T(8,128)(2,1)S(1)}) fusion(f32[1024,1408]{1,0:T(8,128)} %fusion.32, f32[1024,1408]{1,0:T(8,128)} %fusion.31, bf16[1024,2048]{1,0:T(8,128)(2,1)S(1)} %copy-done.21, bf16[2048,1408]{1,0:T(8,128)(2,1)} %param.27), kind=kOutput, calls=%fused_computation.8 | convolution fusion | flops 5927206912 | bytes 30146560 | tf_op jit(solution)/shard_map/dot_general | solution.py:1146
  371.3 8.9 %fusion.33 = f32[1024,2048]{1,0:T(8,128)} fusion(bf16[1024,1408]{1,0:T(8,128)(2,1)S(1)} %get-tuple-element.137.refs_5_, bf16[2048,1408]{1,0:T(8,128)(2,1)S(1)} %bitcast.91), kind=kOutput, calls=%fused_computation.84 | convolution fusion | flops 5905580032 | bytes 17039360 | tf_op jit(solution)/shard_map/re,de->rd/dot_general | solution.py:1154
  380.2 12.2 %add_convert_fusion = bf16[1024,2048]{1,0:T(8,128)(2,1)} fusion(f32[1024,2048]{1,0:T(8,128)} %fusion.33, bf16[1024,1408]{1,0:T(8,128)(2,1)S(1)} %get-tuple-element.138.refs_7_, bf16[2048,1408]{1,0:T(8,128)(2,1)} %param.27), kind=kOutput, calls=%fused_computation.6 | convolution fusion | flops 5909774336 | bytes 21233664 | tf_op jit(solution)/shard_map/re,de->rd/dot_general | solution.py:1154
  392.7 98.7 %ffn_grads.1 = f32[3,256,1408]{2,1,0:T(8,128)} custom-call(bf16[1024,2048]{1,0:T(8,128)(2,1)} %all-gather.6.cloned.1.call-done.refs_0_, bf16[1024,2048]{1,0:T(8,128)(2,1)} %all-gather.8.cloned.1.call-done.refs_1_, bf16[1024,2048]{1,0:T(8,128)(2,1)} %bitcast.78, bf16[1024,2048]{1,0:T(8,128)(2,1)} %bitcast.76, bf16[1024,1408]{1,0:T(8,128)(2,1)} %get-tuple-element.140.refs_4_, ...), custom_call_target="tpu_custom_call" | custom-call | tf_op jit(solution)/shard_map/ffn_grads/pallas_call | solution.py:1116
  491.5 10.9 %convolution_convert_fusion = bf16[1024,2048]{1,0:T(8,128)(2,1)} fusion(bf16[1024,1408]{1,0:T(8,128)(2,1)S(1)} %copy-done.24, bf16[1408,2048]{1,0:T(8,128)(2,1)} %param.28), kind=kOutput, calls=%fused_computation.40 | convolution fusion | flops 5907677184 | bytes 12845056 | tf_op jit(solution)/shard_map/dot_general | solution.py:1146
  502.4 4.2 fusion.8
  507.1 2.8 fusion.24.refs_19_
  509.9 1.3 copy-done.19
  511.3 9.6 %fusion.34.up_ref = f32[512,2048]{1,0:T(8,128)} fusion(bf16[512,2048]{1,0:T(8,128)(2,1)S(1)} %fusion.24.refs_19_, bf16[2048,2048]{1,0:T(8,128)(2,1)} %param.24), kind=kOutput, calls=%fused_computation.85 | convolution fusion | flops 4294967296 | bytes 14680064 | tf_op jit(solution)/shard_map/re,de->rd/dot_general | solution.py:1154
  520.9 9.8 %mixer_core_back.1 = (bf16[512,2048]{1,0:T(8,128)(2,1)}, f32[16,128,128]{2,1,0:T(8,128)}, f32[1,128]{1,0:T(1,128)}) custom-call(bf16[512,2048]{1,0:T(8,128)(2,1)} %get-tuple-element.44.out_add_ref, bf16[512,2048]{1,0:T(8,128)(2,1)} %get-tuple-element.45.out_map_ref, f32[16,128,128]{2,1,0:T(8,128)} %copy-done.1, f32[1,128]{1,0:T(1,128)} %bitcast.88, ...), custom_call_target="tpu_custom_call" | custom-call | tf_op jit(solution)/shard_map/mixer_core_back/pallas_call | solution.py:250
  530.7 1.2 copy-done.5
  532.0 24.8 %carry_backward.1.refs_12_ = f32[16,128,128]{2,1,0:T(8,128)S(1)} custom-call(bf16[16,128,128]{2,1,0:T(8,128)(2,1)S(1)} %copy-done.3, f32[16,128,128]{2,1,0:T(8,128)S(1)} %copy-done.5), custom_call_target="tpu_custom_call" | custom-call | tf_op jit(solution)/shard_map/carry_backward/pallas_call | solution.py:495
  556.7 1.0 copy-done.4
  557.8 0.7 reduce-scatter.11.cloned.1.call-update
  558.5 0.5 broadcast.103
  559.0 0.7 reduce.9
  559.9 237.0 %fused_backward.1 = (f32[4,64,2048]{2,1,0:T(8,128)}, f32[512,2048]{1,0:T(8,128)}, f32[3,4,2048]{2,1,0:T(4,128)}, f32[512,16]{1,0:T(8,128)}) custom-call(s32[512,128]{1,0:T(8,128)} %broadcast_in_dim.19.since_ref.refs_0_, f32[512,16]{1,0:T(8,128)} %fusion.27.beta_ref.refs_1_, bf16[512,2048]{1,0:T(8,128)(2,1)} %copy-done.16, bf16[512,2048]{1,0:T(8,128)(2,1)} %copy-done.18, ...), custom_call_target="tpu_custom_call" | custom-call | tf_op jit(solution)/shard_map/fused_backward/pallas_call | solution.py:904
  796.9 0.9 reshape.125
  797.8 2.0 fusion.19
  799.9 6.1 fusion.18
  806.5 21.2 %reduce_small.1 = f32[64,128]{1,0:T(8,128)S(1)} custom-call(f32[2048,128]{1,0:T(8,128)S(1)} %pad.9.small_ref), custom_call_target="tpu_custom_call" | custom-call | tf_op jit(solution)/shard_map/reduce_small/pallas_call | solution.py:598
  827.7 0.7 copy.56
  828.5 0.6 reshape.128
  829.2 4.5 slice_bitcast_fusion
  833.6 3.0 copy.57
  836.7 0.7 slice_reduce_fusion.2
  837.4 0.7 slice_reduce_fusion
  838.1 3.0 slice_bitcast_fusion.3
  841.3 8.2 fusion.15
  (132 shorter events, 3.7 us)
Async XLA Ops:
  7.2 30.7 %copy-start = (bf16[2048,16]{0,1:T(8,128)(2,1)S(1)}, bf16[2048,16]{0,1:T(8,128)(2,1)}, u32[]{:S(2)}) copy-start(bf16[2048,16]{0,1:T(8,128)(2,1)} %param.21) | copy-start | bytes 196612
  7.2 4.1 copy-start.9
  7.2 4.1 copy-start.30
  7.2 163.9 %all-gather.4.cloned.1.call-start = ((), (), s32[]{:S(2)}) async-start(), calls=%async_computation.4 | async-start | bytes 10485760 | tf_op jit(solution)/shard_map/all_gather | solution.py:1207
  8.0 255.2 %all-gather.6.cloned.1.call-start = ((), (), s32[]{:S(2)}) async-start(), calls=%async_computation.5 | async-start | bytes 5242880 | tf_op jit(solution)/shard_map/all_gather | solution.py:1207
  10.7 0.6 copy-start.34
  11.3 9.9 %slice-start.2 = ((s8[8388608]{0:T(1024)(128)(4,1)}), s8[4194304]{0:T(1024)(128)(4,1)S(1)}, s32[]{:S(2)}) async-start(s8[8388608]{0:T(1024)(128)(4,1)} %bitcast.81), calls=%async_computation.13 | async-start | bytes 8388608
  11.8 14.1 %copy-start.11 = (bf16[512,2048]{1,0:T(8,128)(2,1)}, bf16[512,2048]{1,0:T(8,128)(2,1)S(1)}, u32[]{:S(2)}) copy-start(bf16[512,2048]{1,0:T(8,128)(2,1)S(1)} %fusion.11.refs_18_) | copy-start | bytes 6291460
  11.8 9.3 %slice-start.3 = ((s8[8388608]{0:T(1024)(128)(4,1)}), s8[4194304]{0:T(1024)(128)(4,1)S(1)}, s32[]{:S(2)}) async-start(s8[8388608]{0:T(1024)(128)(4,1)} %bitcast.81), calls=%async_computation.14 | async-start | bytes 8388608
  11.8 14.1 %slice-start = ((s8[8388608]{0:T(1024)(128)(4,1)}), s8[4194304]{0:T(1024)(128)(4,1)S(1)}, s32[]{:S(2)}) async-start(s8[8388608]{0:T(1024)(128)(4,1)} %bitcast.79), calls=%async_computation.11 | async-start | bytes 8388608
  21.1 4.9 copy-start.16
  21.1 4.9 slice-start.1
  26.0 4.8 copy-start.17
  26.0 11.6 %copy-start.38 = (s32[1,4]{1,0:T(1,128)S(1)}, s32[1,4]{1,0:T(1,128)}, u32[]{:S(2)}) copy-start(s32[1,4]{1,0:T(1,128)} %param.16) | copy-start | bytes 52
  30.8 1.3 copy-start.18
  32.1 9.8 %collective-permute-start = (bf16[3,8,2048]{2,1,0:T(8,128)(2,1)S(1)}, bf16[3,8,2048]{2,1,0:T(8,128)(2,1)S(1)}, u32[]{:S(2)}, u32[]{:S(2)}) collective-permute-start(bf16[3,8,2048]{2,1,0:T(8,128)(2,1)S(1)} %pad_maximum_fusion.1), channel_id=1, source_target_pairs={{0,1},{1,2},{2,3},{4,5},{5,6},{6,7},{8,9},{9,10},{10,11},{12,13},{... | collective-permute-start | bytes 294920 | tf_op jit(solution)/shard_map/ppermute | solution.py:1142
  41.9 0.8 copy-start.27
  94.8 28.2 %copy-start.2 = (bf16[16,128,128]{2,1,0:T(8,128)(2,1)}, bf16[16,128,128]{2,1,0:T(8,128)(2,1)S(1)}, u32[]{:S(2)}) copy-start(bf16[16,128,128]{2,1,0:T(8,128)(2,1)S(1)} %slice.106.map_ref) | copy-start | bytes 1572868
  123.1 1.0 copy-start.1
  131.6 9.7 %copy-start.28 = (f32[2048]{0:T(1024)S(1)}, f32[2048]{0:T(1024)}, u32[]{:S(2)}) copy-start(f32[2048]{0:T(1024)} %param.25) | copy-start | bytes 24580
  139.4 1.9 copy-start.6
  140.0 1.3 copy-start.32
  172.6 172.1 %all-gather.8.cloned.1.call-start = ((), (), s32[]{:S(2)}) async-start(), calls=%async_computation.6 | async-start | bytes 5242880 | tf_op jit(solution)/shard_map/all_gather | solution.py:1207
  172.8 17.0 %slice-start.6 = ((s8[5767168]{0:T(1024)(128)(4,1)}), s8[4194304]{0:T(1024)(128)(4,1)S(1)}, s32[]{:S(2)}) async-start(s8[5767168]{0:T(1024)(128)(4,1)} %bitcast.92), calls=%async_computation.17 | async-start | bytes 8388608
  176.8 13.0 %copy-start.14 = (bf16[4,256,2048]{2,1,0:T(8,128)(2,1)}, bf16[4,256,2048]{2,1,0:T(8,128)(2,1)S(1)}, u32[]{:S(2)}) copy-start(bf16[4,256,2048]{2,1,0:T(8,128)(2,1)S(1)} %get-tuple-element.143) | copy-start | bytes 12582916
  176.8 13.0 %copy-start.13 = (bf16[4,256,2048]{2,1,0:T(8,128)(2,1)}, bf16[4,256,2048]{2,1,0:T(8,128)(2,1)S(1)}, u32[]{:S(2)}) copy-start(bf16[4,256,2048]{2,1,0:T(8,128)(2,1)S(1)} %get-tuple-element.142) | copy-start | bytes 12582916
  176.8 13.0 %slice-start.7 = ((s8[5767168]{0:T(1024)(128)(4,1)}), s8[1572864]{0:T(1024)(128)(4,1)S(1)}, s32[]{:S(2)}) async-start(s8[5767168]{0:T(1024)(128)(4,1)} %bitcast.92), calls=%async_computation.18 | async-start | bytes 3145728
  198.3 304.0 %reduce-scatter.5.cloned.1.call-start = ((), (), s32[]{:S(2)}) async-start(), calls=%async_computation.7 | async-start | bytes 5242880 | tf_op jit(solution)/shard_map/reduce_scatter | solution.py:1210
  263.2 10.9 %copy-start.20 = (bf16[1024,2048]{1,0:T(8,128)(2,1)S(1)}, bf16[1024,2048]{1,0:T(8,128)(2,1)}, u32[]{:S(2)}) copy-start(bf16[1024,2048]{1,0:T(8,128)(2,1)} %all-gather.6.cloned.1.call-done.refs_0_) | copy-start | bytes 12582916
  263.2 24.4 %slice-start.8 = ((s8[5767168]{0:T(1024)(128)(4,1)}), s8[4194304]{0:T(1024)(128)(4,1)S(1)}, s32[]{:S(2)}) async-start(s8[5767168]{0:T(1024)(128)(4,1)} %bitcast.94), calls=%async_computation.19 | async-start | bytes 8388608
  274.2 13.5 %slice-start.9 = ((s8[5767168]{0:T(1024)(128)(4,1)}), s8[1572864]{0:T(1024)(128)(4,1)S(1)}, s32[]{:S(2)}) async-start(s8[5767168]{0:T(1024)(128)(4,1)} %bitcast.94), calls=%async_computation.20 | async-start | bytes 3145728
  287.6 8.3 copy-start.22
  295.9 9.8 %copy-start.23 = (bf16[1024,1408]{1,0:T(8,128)(2,1)S(1)}, bf16[1024,1408]{1,0:T(8,128)(2,1)}, u32[]{:S(2)}) copy-start(bf16[1024,1408]{1,0:T(8,128)(2,1)} %get-tuple-element.141.refs_6_) | copy-start | bytes 8650756
  344.7 157.7 %reduce-scatter.7.cloned.1.call-start = ((), (), s32[]{:S(2)}) async-start(), calls=%async_computation.8 | async-start | bytes 5242880 | tf_op jit(solution)/shard_map/reduce_scatter | solution.py:1210
  345.2 11.8 %copy-start.21 = (bf16[1024,2048]{1,0:T(8,128)(2,1)S(1)}, bf16[1024,2048]{1,0:T(8,128)(2,1)}, u32[]{:S(2)}) copy-start(bf16[1024,2048]{1,0:T(8,128)(2,1)} %all-gather.8.cloned.1.call-done.refs_1_) | copy-start | bytes 12582916
  345.2 26.1 %slice-start.4 = ((s8[5767168]{0:T(1024)(128)(4,1)}), s8[4194304]{0:T(1024)(128)(4,1)S(1)}, s32[]{:S(2)}) async-start(s8[5767168]{0:T(1024)(128)(4,1)} %bitcast.90), calls=%async_computation.15 | async-start | bytes 8388608
  357.0 14.3 %slice-start.5 = ((s8[5767168]{0:T(1024)(128)(4,1)}), s8[1572864]{0:T(1024)(128)(4,1)S(1)}, s32[]{:S(2)}) async-start(s8[5767168]{0:T(1024)(128)(4,1)} %bitcast.90), calls=%async_computation.16 | async-start | bytes 3145728
  371.3 8.9 %copy-start.25 = (bf16[1024,1408]{1,0:T(8,128)(2,1)}, bf16[1024,1408]{1,0:T(8,128)(2,1)S(1)}, u32[]{:S(2)}) copy-start(bf16[1024,1408]{1,0:T(8,128)(2,1)S(1)} %get-tuple-element.137.refs_5_) | copy-start | bytes 8650756
  371.3 8.9 %copy-start.26 = (bf16[1024,1408]{1,0:T(8,128)(2,1)}, bf16[1024,1408]{1,0:T(8,128)(2,1)S(1)}, u32[]{:S(2)}) copy-start(bf16[1024,1408]{1,0:T(8,128)(2,1)S(1)} %get-tuple-element.138.refs_7_) | copy-start | bytes 8650756
  392.5 445.6 %reduce-scatter.9.cloned.1.call-start = ((), (), s32[]{:S(2)}) async-start(), calls=%async_computation.9 | async-start | bytes 5242880 | tf_op jit(solution)/shard_map/reduce_scatter | solution.py:1210
  392.7 98.8 %copy-start.24 = (bf16[1024,1408]{1,0:T(8,128)(2,1)S(1)}, bf16[1024,1408]{1,0:T(8,128)(2,1)}, u32[]{:S(2)}) copy-start(bf16[1024,1408]{1,0:T(8,128)(2,1)} %get-tuple-element.136.refs_9_) | copy-start | bytes 8650756
  491.5 10.9 %copy-start.29 = (f32[2048]{0:T(1024)S(1)}, f32[2048]{0:T(1024)}, u32[]{:S(2)}) copy-start(f32[2048]{0:T(1024)} %param.25) | copy-start | bytes 24580
  491.5 10.9 %copy-start.33 = (f32[512]{0:T(512)S(1)}, f32[512]{0:T(512)}, u32[]{:S(2)}) copy-start(f32[512]{0:T(512)} %copy-done.32) | copy-start | bytes 6148
  502.4 4.3 copy-start.12
  502.4 4.3 copy-start.36
  502.4 4.7 copy-start.7
  509.9 1.3 copy-start.19
  520.9 9.8 %copy-start.3 = (bf16[16,128,128]{2,1,0:T(8,128)(2,1)S(1)}, bf16[16,128,128]{2,1,0:T(8,128)(2,1)}, u32[]{:S(2)}) copy-start(bf16[16,128,128]{2,1,0:T(8,128)(2,1)} %copy-done.2) | copy-start | bytes 1572868
  530.7 1.2 copy-start.5
  556.7 1.0 copy-start.4
  557.7 1.3 copy-start.39
  557.7 280.4 %reduce-scatter.11.cloned.1.call-start = ((), (), s32[]{:S(2)}) async-start(), calls=%async_computation.10 | async-start | bytes 5242880 | tf_op jit(solution)/shard_map/reduce_scatter | solution.py:1210
  559.9 240.0 %copy-start.31 = (f32[2048]{0:T(1024)S(1)}, f32[2048]{0:T(1024)}, u32[]{:S(2)}) copy-start(f32[2048]{0:T(1024)} %param.17) | copy-start | bytes 24580
  559.9 240.0 %copy-start.35 = (f32[512]{0:T(512)S(1)}, f32[512]{0:T(512)}, u32[]{:S(2)}) copy-start(f32[512]{0:T(512)} %copy-done.34) | copy-start | bytes 6148
  829.2 11.9 %copy-start.15 = (bf16[256,2048]{1,0:T(8,128)(2,1)S(1)}, bf16[256,2048]{1,0:T(8,128)(2,1)}, u32[]{:S(2)}) copy-start(bf16[256,2048]{1,0:T(8,128)(2,1)} %reduce-scatter.5.cloned.1.call-done) | copy-start | bytes 3145732
  833.6 7.5 copy-start.10
  833.6 7.5 copy-start.37
  838.1 3.2 copy-start.8
Sparse Core Ops, SparseCore 0:
  9.6 161.4 all-gather.3
  173.2 89.9 all-gather.5
  265.4 79.2 all-gather.7
  346.8 75.2 reduce-scatter.4
  424.4 77.2 reduce-scatter.6
  557.8 79.4 reduce-scatter.8
  639.7 128.4 reduce-scatter.10

commit v7 on v6

--- a/solution.py
+++ b/solution.py
@@ -224,18 +224,21 @@
     )(out_add, out_map, entry, gain)
 
 
-def core_back_kernel(out_add_ref, out_map_ref, entry_ref, gain_ref, up_ref, d_core_ref, start_ref, gain_out_ref):
+def core_back_kernel(
+    out_add_ref, out_map_ref, entry_ref, gain_ref, branch_ref, w_out_ref, d_core_ref, start_ref, gain_out_ref
+):
     @pl.when(pl.program_id(0) == 0)
     def _():
         gain_out_ref[...] = jnp.zeros_like(gain_out_ref)
 
+    upstream = mm_nt(branch_ref[...], w_out_ref[...])
     for sub in range(HEADS_STEP):
         lanes = slice(sub * BLOCK, (sub + 1) * BLOCK)
         out_map = out_map_ref[:, lanes]
         core = out_add_ref[:, lanes].astype(F32) + mm(out_map, entry_ref[sub])
         scale = lax.rsqrt(jnp.mean(core * core, axis=-1, keepdims=True) + 1e-05)
         unit = core * scale
-        up = up_ref[:, lanes].astype(F32)
+        up = upstream[:, lanes]
         gain_out_ref[...] += jnp.sum(up * unit, axis=0, keepdims=True)
         scaled = up * gain_ref[...]
         d_core = scale * (scaled - unit * jnp.mean(scaled * unit, axis=-1, keepdims=True))
@@ -244,14 +247,15 @@
         start_ref[sub] = mm_tn(out_map, d_core)
 
 
-def mixer_core_back(out_add, out_map, entry, gain, up):
+def mixer_core_back(out_add, out_map, entry, gain, branch, w_out):
     rows, width = out_add.shape
     heads = width // BLOCK
     return pl.pallas_call(
         core_back_kernel,
         grid=(heads // HEADS_STEP,),
         in_specs=[
-            head_spec(rows), head_spec(rows), per_head(BLOCK, BLOCK), whole_spec((1, BLOCK)), head_spec(rows),
+            head_spec(rows), head_spec(rows), per_head(BLOCK, BLOCK), whole_spec((1, BLOCK)),
+            whole_spec(branch.shape), pl.BlockSpec((HEADS_STEP * BLOCK, width), lambda h: (h, 0)),
         ],
         out_specs=[head_spec(rows), per_head(BLOCK, BLOCK), whole_spec((1, BLOCK))],
         out_shape=[
@@ -261,7 +265,7 @@
         ],
         compiler_params=params(),
         name="mixer_core_back",
-    )(out_add, out_map, entry, gain, up)
+    )(out_add, out_map, entry, gain, branch, w_out)
 
 
 def backward_heads(
@@ -429,7 +433,7 @@
     )
 
 
-GROUPS = 4
+GROUPS = 8
 HALVES = 2
 
 
@@ -950,7 +954,7 @@
     lefts = [refs[0:HALVES], refs[0:HALVES], refs[HALVES : 2 * HALVES]]
     rights = [refs[(2 + m) * HALVES : (3 + m) * HALVES] for m in range(3)]
     (
-        out_ref, left_buf, right_buf, away, landed, total, got2, got3,
+        gate_ref, up_ref, down_ref, left_buf, right_buf, away, landed, total, got2, got3,
         left_sem, right_sem, send1, recv1, send2, recv2, send3, recv3,
     ) = refs[5 * HALVES :]
     dp = lax.axis_index("dp")
@@ -1081,13 +1085,17 @@
         for h in range(2):
             _, kept, _, _, _, near = order(h)
             copy3(m, h).wait()
+            if m == 2:
+                value = total[m, kept(near), band(h), :].astype(F32) + got3[m, h].astype(F32)
+                down_ref[:, band(h)] = value.T
+                continue
             step = 32
 
             def one(at, _):
                 at = at * step
                 value = total[m, kept(near), pl.ds(pl.multiple_of(h * half + at, step), step), :].astype(F32)
                 value = value + got3[m, h, pl.ds(pl.multiple_of(at, step), step), :].astype(F32)
-                out_ref[m, pl.ds(pl.multiple_of(h * half + at, step), step), :] = value
+                (gate_ref, up_ref)[m][pl.ds(pl.multiple_of(h * half + at, step), step), :] = value
                 return 0
 
             lax.fori_loop(0, half // step, one, 0)
@@ -1116,8 +1124,12 @@
     return pl.pallas_call(
         ffn_grads_kernel,
         in_specs=[pl.BlockSpec(memory_space=pl.ANY)] * len(operands),
-        out_specs=pl.BlockSpec(memory_space=pltpu.VMEM),
-        out_shape=jax.ShapeDtypeStruct((3, rows, width), F32),
+        out_specs=[pl.BlockSpec(memory_space=pltpu.VMEM)] * 3,
+        out_shape=[
+            jax.ShapeDtypeStruct((rows, width), F32),
+            jax.ShapeDtypeStruct((rows, width), F32),
+            jax.ShapeDtypeStruct((width, rows), F32),
+        ],
         scratch_shapes=[
             pltpu.VMEM((2, HALVES * part, rows), BF16),
             pltpu.VMEM((2, HALVES * part, width), BF16),
@@ -1259,17 +1271,21 @@
             )
             for left, right in ((gathered, d_gate), (gathered, d_up), (cot, activation))
         ]
+        ffn_sums[2] = ffn_sums[2].T
     d_normed_parts, out_parts, ffn_sums = lax.optimization_barrier((d_normed_parts, out_parts, ffn_sums))
-    grad_gate, grad_up, grad_down = ffn_sums[0].astype(F32), ffn_sums[1].astype(F32), ffn_sums[2].astype(F32).T
+    quarters = out_parts[0].reshape(-1, 2, half // 2, model_width)
+    out_first, out_second = (quarters[:, at].reshape(-1, model_width) for at in range(2))
+    out_rest = [out_second, *out_parts[1:]]
+    ffn_parts = [scatter(out_first)]
+    grad_gate, grad_up, grad_down = (value.astype(F32) for value in ffn_sums)
     d_normed_mlp = jnp.concatenate(d_normed_parts, axis=0).astype(F32)
     d_hidden_norm, mlp_gain_term = norm_back(hidden, mlp_gain, d_normed_mlp, 1e-06)
     d_hidden = grad_out.astype(F32) + d_hidden_norm
     d_branch = d_hidden.astype(BF16)
-    d_mixed = dot_nt(d_branch, w_out)
-    d_core, start_grad, out_gain_term = mixer_core_back(out_add, out_map, entry, gain_row, d_mixed)
+    d_core, start_grad, out_gain_term = mixer_core_back(out_add, out_map, entry, gain_row, d_branch, w_out)
     exit_grad = carry_chain(transfer, start_grad, "narrow", False)
-    exit_grad, out_parts = lax.optimization_barrier((exit_grad, out_parts))
-    ffn_parts = [scatter(part) for part in out_parts]
+    exit_grad, out_rest = lax.optimization_barrier((exit_grad, out_rest))
+    ffn_parts += [scatter(part) for part in out_rest]
     mixer_args = (
         since, beta_logit, query, key, value, halo, conv_weight,
         new_add, new_map, inverse, starts, entry, exit_grad, d_core,

time: 863 us -> 848 us (0.983)
  waiting for transfers between devices: 124 us -> 113 us
    pallas_call x1, Pallas kernels: 237 us -> 222 us  [fused_backward(): pl.pallas_call(fused_kernel, grid=(units + 1,), in_specs=[whole(since.sha...]
    all_gather x3, waiting for transfers between devices: 122 us -> 110 us  [gather(): return lax.all_gather(rows, 'narrow', axis=0, tiled=True)]
    dot_general x5 -> x4, matrix products: 51.6 us -> 40.8 us  [dot_nt(): return jnp.einsum('re,de->rd', left, right, preferred_element_type=F32)]
    pallas_call x2, Pallas kernels: 51.5 us -> 60.7 us  [carry_chain(): pl.pallas_call(functools.partial(chain_kernel, axis, forward), in_specs=[...]
  transfers between devices with their start and end apart: 8 -> 9, of which waited for: 4 -> 4; matrix products, arithmetic and copies ran while one was open for 23% -> 24% of each run, Pallas kernels for 52% -> 57%
where the time goes in v7:
time: 848 us; the launch traced here: 843 us
  Pallas kernels  477 us (56%)
  matrix products  176 us (21%)
  waiting for transfers between devices  113 us (13%)
  local copies, waits for them, and re-layouts  34.9 us (4%)
  other arithmetic  21 us (2%)
  between operations  15.2 us (2%)
    pallas_call x1, Pallas kernels, fused_backward(): pl.pallas_call(fused_kernel, grid=(units + 1,), in_specs=[whole(since.sha...  222 us
    all_gather x3, waiting for transfers between devices, gather(): return lax.all_gather(rows, 'narrow', axis=0, tiled=True)  110 us
    dot_general x11, matrix products, matmul(): return jnp.dot(left, right, preferred_element_type=F32)  105 us
    pallas_call x1, Pallas kernels, ffn_grads(): pl.pallas_call(ffn_grads_kernel, in_specs=[pl.BlockSpec(memory_space=pl.A...  98.7 us
    pallas_call x2, Pallas kernels, carry_chain(): pl.pallas_call(functools.partial(chain_kernel, axis, forward), in_specs=[...  60.7 us
    pallas_call x1, Pallas kernels, mixer_forward(): pl.pallas_call(forward_kernel, grid=(heads // HEADS_STEP,), in_specs=[who...  50.7 us
    dot_general x4, matrix products, dot_nt(): return jnp.einsum('re,de->rd', left, right, preferred_element_type=F32)  40.8 us
    pallas_call x1, Pallas kernels, reduce_small(): pl.pallas_call(small_kernel, in_specs=[pl.BlockSpec(memory_space=pltpu.VM...  21.6 us
  transfers between devices with their start and end apart: 9, of which 4 were waited for; matrix products, arithmetic and copies ran while one was open for 24% of the time, Pallas kernels for 57%

profile of v7, /device:TPU:0, one launch (start us, length us, event | category | flops | bytes accessed | tf_op | source)
XLA Modules:
  0.0 842.7 jit_solution(10727032523303006704)
XLA Ops:
  7.3 0.7 all-gather.4.cloned.1.call-update
  8.0 2.1 fusion.9
  10.1 0.6 multiply_multiply_fusion
  10.7 0.6 copy-done.38
  11.3 0.5 fusion.11.refs_18_
  11.9 9.2 %convolution_convert_fusion.4.query_ref.refs_2_ = bf16[512,2048]{1,0:T(8,128)(2,1)S(1)} fusion(bf16[512,2048]{1,0:T(8,128)(2,1)S(1)} %fusion.11.refs_18_, bf16[2048,2048]{1,0:T(8,128)(2,1)} %refs_14_.1), kind=kOutput, calls=%fused_computation.44 | convolution fusion | flops 4296015872 | bytes 12582912 | tf_op jit(solution)/shard_map/dot_general | solution.py:1158
  21.2 4.8 convolution_convert_fusion.2.value_ref.refs_4_
  26.0 4.8 convolution_convert_fusion.3.key_ref.refs_3_
  30.8 1.3 copy-done.19
  32.2 5.5 collective-permute-start
  37.9 3.0 fusion.28.beta_ref.refs_1_
  40.9 1.0 collective-permute-done.halo_ref.refs_5_
  41.9 0.8 broadcast_in_dim.19.since_ref.refs_0_
  42.8 50.7 %mixer_forward.1 = (bf16[512,2048]{1,0:T(8,128)(2,1)}, bf16[512,2048]{1,0:T(8,128)(2,1)}, bf16[512,2048]{1,0:T(8,128)(2,1)}, bf16[512,2048]{1,0:T(8,128)(2,1)}, ...) custom-call(s32[512,128]{1,0:T(8,128)} %broadcast_in_dim.19.since_ref.refs_0_, ...), custom_call_target="tpu_custom_call" | custom-call | tf_op jit(solution)/shard_map/mixer_forward/pallas_call | solution.py:180
  93.5 1.3 slice.101.map_ref
  94.8 1.5 slice.65.add_ref
  96.3 26.7 %carry_forward.1.entry_ref.refs_11_ = f32[16,128,128]{2,1,0:T(8,128)S(1)} custom-call(bf16[16,128,128]{2,1,0:T(8,128)(2,1)S(1)} %slice.101.map_ref, f32[16,128,128]{2,1,0:T(8,128)S(1)} %slice.65.add_ref), custom_call_target="tpu_custom_call" | custom-call | tf_op jit(solution)/shard_map/carry_forward/pallas_call | solution.py:499
  123.1 1.0 copy-done.1
  124.0 7.6 mixer_join.1.refs_17_
  131.7 7.8 multiply_reduce_fusion
  139.4 0.6 multiply_multiply_fusion.1
  140.1 1.3 copy-done.6
  141.9 29.2 %all-gather.4.cloned.1.call-done = bf16[2048,2048]{1,0:T(8,128)(2,1)} async-done(((bf16[512,2048]{1,0:T(8,128)(2,1)}), bf16[2048,2048]{1,0:T(8,128)(2,1)}) %all-gather.4.cloned.1.call-update) | async-done | bytes 8388624 | tf_op jit(solution)/shard_map/all_gather | solution.py:1219
  171.1 1.4 fusion.27
  172.8 4.0 fusion.25
  176.8 12.9 %fusion.29 = f32[1024,1408]{1,0:T(8,128)} fusion(bf16[1024,2048]{1,0:T(8,128)(2,1)S(1)} %bitcast.74, bf16[1408,2048]{1,0:T(8,128)(2,1)} %param.28), kind=kOutput, calls=%fused_computation.77 | convolution fusion | flops 5905580032 | bytes 15728640 | tf_op jit(solution)/shard_map/rd,fd->rf/dot_general | solution.py:1253
  189.8 8.5 %fusion.32 = f32[1024,1408]{1,0:T(8,128)} fusion(bf16[1024,2048]{1,0:T(8,128)(2,1)S(1)} %bitcast.72, bf16[1408,2048]{1,0:T(8,128)(2,1)S(1)} %bitcast.97), kind=kOutput, calls=%fused_computation.80 | convolution fusion | flops 5905580032 | bytes 15728640 | tf_op jit(solution)/shard_map/rd,fd->rf/dot_general | solution.py:1253
  198.6 57.6 %all-gather.6.cloned.1.call-done.refs_0_ = bf16[1024,2048]{1,0:T(8,128)(2,1)} async-done(((bf16[256,2048]{1,0:T(8,128)(2,1)}), bf16[1024,2048]{1,0:T(8,128)(2,1)}) %all-gather.6.cloned.1.call-update) | async-done | bytes 4194320 | tf_op jit(solution)/shard_map/all_gather | solution.py:1219
  256.2 11.9 %fusion.30 = f32[1024,1408]{1,0:T(8,128)} fusion(bf16[1024,2048]{1,0:T(8,128)(2,1)} %all-gather.6.cloned.1.call-done.refs_0_, bf16[2048,1408]{1,0:T(8,128)(2,1)} %param.26), kind=kOutput, calls=%fused_computation.78 | convolution fusion | flops 5905580032 | bytes 15728640 | tf_op jit(solution)/shard_map/dot_general | solution.py:1158
  268.1 12.7 %multiply_convert_fusion.3 = (bf16[1024,1408]{1,0:T(8,128)(2,1)S(1)}, bf16[1024,1408]{1,0:T(8,128)(2,1)S(1)}, bf16[1024,1408]{1,0:T(8,128)(2,1)S(1)}) fusion(f32[1024,1408]{1,0:T(8,128)} %fusion.30, f32[1024,1408]{1,0:T(8,128)} %fusion.29, bf16[1024,2048]{1,0:T(8,128)(2,1)S(1)} %copy-done.20, bf16[2048,1408]{1,0:T(8,128)(2,1)} %param.27), kind=kOutput, calls=%fused_computation.13 | convolution fusion | flops 5927206912 | bytes 30146560 | tf_op jit(solution)/shard_map/dot_general | solution.py:1158
  280.8 13.9 %convolution_convert_fusion.1 = bf16[1024,2048]{1,0:T(8,128)(2,1)} fusion(bf16[1024,1408]{1,0:T(8,128)(2,1)S(1)} %get-tuple-element.151.refs_8_, bf16[1408,2048]{1,0:T(8,128)(2,1)} %param.28), kind=kOutput, calls=%fused_computation.41 | convolution fusion | flops 5907677184 | bytes 12845056 | tf_op jit(solution)/shard_map/dot_general | solution.py:1158
  294.7 9.0 %fusion.31 = f32[1024,2048]{1,0:T(8,128)} fusion(bf16[1024,1408]{1,0:T(8,128)(2,1)S(1)} %get-tuple-element.152.refs_4_, bf16[2048,1408]{1,0:T(8,128)(2,1)S(1)} %bitcast.91), kind=kOutput, calls=%fused_computation.79 | convolution fusion | flops 5905580032 | bytes 17039360 | tf_op jit(solution)/shard_map/re,de->rd/dot_general | solution.py:1166
  303.7 10.5 %add_convert_fusion.1 = bf16[1024,2048]{1,0:T(8,128)(2,1)} fusion(f32[1024,2048]{1,0:T(8,128)} %fusion.31, bf16[1024,1408]{1,0:T(8,128)(2,1)S(1)} %get-tuple-element.153.refs_6_, bf16[2048,1408]{1,0:T(8,128)(2,1)S(1)} %bitcast.95), kind=kOutput, calls=%fused_computation.7 | convolution fusion | flops 5909774336 | bytes 21233664 | tf_op jit(solution)/shard_map/re,de->rd/dot_general | solution.py:1166
  314.3 23.4 %all-gather.8.cloned.1.call-done.refs_1_ = bf16[1024,2048]{1,0:T(8,128)(2,1)} async-done(((bf16[256,2048]{1,0:T(8,128)(2,1)}), bf16[1024,2048]{1,0:T(8,128)(2,1)}) %all-gather.8.cloned.1.call-update) | async-done | bytes 4194320 | tf_op jit(solution)/shard_map/all_gather | solution.py:1219
  338.1 12.0 %fusion.33 = f32[1024,1408]{1,0:T(8,128)} fusion(bf16[1024,2048]{1,0:T(8,128)(2,1)} %all-gather.8.cloned.1.call-done.refs_1_, bf16[2048,1408]{1,0:T(8,128)(2,1)} %param.26), kind=kOutput, calls=%fused_computation.81 | convolution fusion | flops 5905580032 | bytes 15728640 | tf_op jit(solution)/shard_map/dot_general | solution.py:1158
  350.2 14.3 %multiply_convert_fusion = (bf16[1024,1408]{1,0:T(8,128)(2,1)}, bf16[1024,1408]{1,0:T(8,128)(2,1)S(1)}, bf16[1024,1408]{1,0:T(8,128)(2,1)S(1)}) fusion(f32[1024,1408]{1,0:T(8,128)} %fusion.33, f32[1024,1408]{1,0:T(8,128)} %fusion.32, bf16[1024,2048]{1,0:T(8,128)(2,1)S(1)} %copy-done.21, bf16[2048,1408]{1,0:T(8,128)(2,1)} %param.27), kind=kOutput, calls=%fused_computation.8 | convolution fusion | flops 5927206912 | bytes 30146560 | tf_op jit(solution)/shard_map/dot_general | solution.py:1158
  364.5 9.0 %fusion.34 = f32[1024,2048]{1,0:T(8,128)} fusion(bf16[1024,1408]{1,0:T(8,128)(2,1)S(1)} %get-tuple-element.149.refs_5_, bf16[2048,1408]{1,0:T(8,128)(2,1)S(1)} %bitcast.93), kind=kOutput, calls=%fused_computation.82 | convolution fusion | flops 5905580032 | bytes 17039360 | tf_op jit(solution)/shard_map/re,de->rd/dot_general | solution.py:1166
  373.5 12.3 %add_convert_fusion = bf16[1024,2048]{1,0:T(8,128)(2,1)} fusion(f32[1024,2048]{1,0:T(8,128)} %fusion.34, bf16[1024,1408]{1,0:T(8,128)(2,1)S(1)} %get-tuple-element.150.refs_7_, bf16[2048,1408]{1,0:T(8,128)(2,1)} %param.27), kind=kOutput, calls=%fused_computation.6 | convolution fusion | flops 5909774336 | bytes 21233664 | tf_op jit(solution)/shard_map/re,de->rd/dot_general | solution.py:1166
  386.0 98.7 %ffn_grads.1 = (f32[256,1408]{1,0:T(8,128)}, f32[256,1408]{1,0:T(8,128)}, f32[1408,256]{1,0:T(8,128)}) custom-call(bf16[1024,2048]{1,0:T(8,128)(2,1)} %all-gather.6.cloned.1.call-done.refs_0_, bf16[1024,2048]{1,0:T(8,128)(2,1)} %all-gather.8.cloned.1.call-done.refs_1_, bf16[1024,2048]{1,0:T(8,128)(2,1)} %bitcast.75, bf16[1024,2048]{1,0:T(8,128)(2,1)} %bitcast.73, ...), custom_call_target="tpu_custom_call" | custom-call | tf_op jit(solution)/shard_map/ffn_grads/pallas_call | solution.py:1124
  484.7 10.8 %convolution_convert_fusion = bf16[1024,2048]{1,0:T(8,128)(2,1)} fusion(bf16[1024,1408]{1,0:T(8,128)(2,1)S(1)} %copy-done.25, bf16[1408,2048]{1,0:T(8,128)(2,1)} %param.28), kind=kOutput, calls=%fused_computation.40 | convolution fusion | flops 5907677184 | bytes 12845056 | tf_op jit(solution)/shard_map/dot_general | solution.py:1158
  495.5 4.9 fusion.26
  500.5 3.9 fusion.8
  505.1 3.1 fusion.24.branch_ref.refs_19_
  508.2 15.3 %mixer_core_back.1 = (bf16[512,2048]{1,0:T(8,128)(2,1)}, f32[16,128,128]{2,1,0:T(8,128)}, f32[1,128]{1,0:T(1,128)}) custom-call(bf16[512,2048]{1,0:T(8,128)(2,1)} %get-tuple-element.50.out_add_ref, bf16[512,2048]{1,0:T(8,128)(2,1)} %get-tuple-element.51.out_map_ref, f32[16,128,128]{2,1,0:T(8,128)} %copy-done.1, f32[1,128]{1,0:T(1,128)} %bitcast.88, ...), custom_call_target="tpu_custom_call" | custom-call | tf_op jit(solution)/shard_map/mixer_core_back/pallas_call | solution.py:253
  523.6 1.2 copy-done.5
  524.8 34.0 %carry_backward.1.refs_12_ = f32[16,128,128]{2,1,0:T(8,128)S(1)} custom-call(bf16[16,128,128]{2,1,0:T(8,128)(2,1)S(1)} %copy-done.3, f32[16,128,128]{2,1,0:T(8,128)S(1)} %copy-done.5), custom_call_target="tpu_custom_call" | custom-call | tf_op jit(solution)/shard_map/carry_backward/pallas_call | solution.py:499
  558.9 1.0 copy-done.4
  561.1 0.7 reduce.9
  562.0 222.0 %fused_backward.1 = (f32[4,64,2048]{2,1,0:T(8,128)}, f32[512,2048]{1,0:T(8,128)}, f32[3,4,2048]{2,1,0:T(4,128)}, f32[512,16]{1,0:T(8,128)}) custom-call(s32[512,128]{1,0:T(8,128)} %broadcast_in_dim.19.since_ref.refs_0_, f32[512,16]{1,0:T(8,128)} %fusion.28.beta_ref.refs_1_, bf16[512,2048]{1,0:T(8,128)(2,1)} %copy-done.17, bf16[512,2048]{1,0:T(8,128)(2,1)} %copy-done.19, ...), custom_call_target="tpu_custom_call" | custom-call | tf_op jit(solution)/shard_map/fused_backward/pallas_call | solution.py:908
  784.0 0.9 reshape.129
  784.9 2.0 fusion.19
  787.0 6.2 fusion.18
  793.2 1.3 copy.59
  794.6 1.3 pad.9.small_ref
  795.9 21.6 %reduce_small.1 = f32[64,128]{1,0:T(8,128)S(1)} custom-call(f32[2048,128]{1,0:T(8,128)S(1)} %pad.9.small_ref), custom_call_target="tpu_custom_call" | custom-call | tf_op jit(solution)/shard_map/reduce_small/pallas_call | solution.py:602
  817.5 0.7 copy.61
  818.3 0.6 reshape.132
  818.9 0.7 slice_reduce_fusion.2
  819.6 0.7 slice_reduce_fusion
  820.4 3.0 slice_bitcast_fusion
  823.6 8.7 %fusion.15 = (bf16[512,2048]{1,0:T(8,128)(2,1)}, bf16[512,2048]{1,0:T(8,128)(2,1)}) fusion(bf16[512,2048]{1,0:T(8,128)(2,1)S(1)} %copy-done.10, f32[512]{0:T(512)S(1)} %broadcast_multiply_fusion, f32[512]{0:T(512)S(1)} %copy-done.41, f32[2048]{0:T(1024)S(1)} %copy-done.35, f32[512]{0:T(512)S(1)} %copy-done.39, f32[512,2048]{1,0:T(8,128)} %get-tuple-element.78, ...), kind=kLoop, calls=%fused_computation.33 | loop fusion | flops 29360128 | bytes 25194496 | tf_op jit(solution)/shard_map/convert_element_type | solution.py:1308
  832.2 1.1 copy.68
  833.3 1.1 copy.69
  834.4 1.1 copy.70
  (149 shorter events, 4.8 us)
Async XLA Ops:
  7.2 30.7 %copy-start = (bf16[2048,16]{0,1:T(8,128)(2,1)S(1)}, bf16[2048,16]{0,1:T(8,128)(2,1)}, u32[]{:S(2)}) copy-start(bf16[2048,16]{0,1:T(8,128)(2,1)} %param.21) | copy-start | bytes 196612
  7.2 4.1 copy-start.9
  7.2 4.1 copy-start.34
  7.2 163.9 %all-gather.4.cloned.1.call-start = ((), (), s32[]{:S(2)}) async-start(), calls=%async_computation.5 | async-start | bytes 10485760 | tf_op jit(solution)/shard_map/all_gather | solution.py:1219
  8.0 248.2 %all-gather.6.cloned.1.call-start = ((), (), s32[]{:S(2)}) async-start(), calls=%async_computation.6 | async-start | bytes 5242880 | tf_op jit(solution)/shard_map/all_gather | solution.py:1219
  11.3 9.9 %slice-start.2 = ((s8[8388608]{0:T(1024)(128)(4,1)}), s8[4194304]{0:T(1024)(128)(4,1)S(1)}, s32[]{:S(2)}) async-start(s8[8388608]{0:T(1024)(128)(4,1)} %bitcast.78), calls=%async_computation.15 | async-start | bytes 8388608
  11.8 14.1 %copy-start.11 = (bf16[512,2048]{1,0:T(8,128)(2,1)}, bf16[512,2048]{1,0:T(8,128)(2,1)S(1)}, u32[]{:S(2)}) copy-start(bf16[512,2048]{1,0:T(8,128)(2,1)S(1)} %fusion.11.refs_18_) | copy-start | bytes 6291460
  11.8 9.3 %slice-start.3 = ((s8[8388608]{0:T(1024)(128)(4,1)}), s8[4194304]{0:T(1024)(128)(4,1)S(1)}, s32[]{:S(2)}) async-start(s8[8388608]{0:T(1024)(128)(4,1)} %bitcast.78), calls=%async_computation.16 | async-start | bytes 8388608
  11.8 14.1 %slice-start = ((s8[8388608]{0:T(1024)(128)(4,1)}), s8[4194304]{0:T(1024)(128)(4,1)S(1)}, s32[]{:S(2)}) async-start(s8[8388608]{0:T(1024)(128)(4,1)} %bitcast.76), calls=%async_computation.13 | async-start | bytes 8388608
  21.1 4.9 copy-start.17
  21.1 4.9 slice-start.1
  26.0 4.8 copy-start.18
  26.0 11.6 %copy-start.42 = (s32[1,4]{1,0:T(1,128)S(1)}, s32[1,4]{1,0:T(1,128)}, u32[]{:S(2)}) copy-start(s32[1,4]{1,0:T(1,128)} %param.16) | copy-start | bytes 52
  30.8 1.4 copy-start.19
  32.2 9.8 %collective-permute-start = (bf16[3,8,2048]{2,1,0:T(8,128)(2,1)S(1)}, bf16[3,8,2048]{2,1,0:T(8,128)(2,1)S(1)}, u32[]{:S(2)}, u32[]{:S(2)}) collective-permute-start(bf16[3,8,2048]{2,1,0:T(8,128)(2,1)S(1)} %pad_maximum_fusion.1), channel_id=1, source_target_pairs={{0,1},{1,2},{2,3},{4,5},{5,6},{6,7},{8,9},{9,10},{10,11},{12,13},{... | collective-permute-start | bytes 294920 | tf_op jit(solution)/shard_map/ppermute | solution.py:1154
  41.9 0.8 copy-start.31
  94.8 28.2 %copy-start.2 = (bf16[16,128,128]{2,1,0:T(8,128)(2,1)}, bf16[16,128,128]{2,1,0:T(8,128)(2,1)S(1)}, u32[]{:S(2)}) copy-start(bf16[16,128,128]{2,1,0:T(8,128)(2,1)S(1)} %slice.101.map_ref) | copy-start | bytes 1572868
  123.1 1.0 copy-start.1
  131.7 9.8 %copy-start.32 = (f32[2048]{0:T(1024)S(1)}, f32[2048]{0:T(1024)}, u32[]{:S(2)}) copy-start(f32[2048]{0:T(1024)} %param.25) | copy-start | bytes 24580
  139.4 2.0 copy-start.6
  140.1 1.4 copy-start.36
  172.6 165.1 %all-gather.8.cloned.1.call-start = ((), (), s32[]{:S(2)}) async-start(), calls=%async_computation.7 | async-start | bytes 5242880 | tf_op jit(solution)/shard_map/all_gather | solution.py:1219
  172.8 17.0 %slice-start.10 = ((s8[5767168]{0:T(1024)(128)(4,1)}), s8[4194304]{0:T(1024)(128)(4,1)S(1)}, s32[]{:S(2)}) async-start(s8[5767168]{0:T(1024)(128)(4,1)} %bitcast.96), calls=%async_computation.23 | async-start | bytes 8388608
  176.8 13.0 %copy-start.14 = (bf16[4,256,2048]{2,1,0:T(8,128)(2,1)}, bf16[4,256,2048]{2,1,0:T(8,128)(2,1)S(1)}, u32[]{:S(2)}) copy-start(bf16[4,256,2048]{2,1,0:T(8,128)(2,1)S(1)} %get-tuple-element.155) | copy-start | bytes 12582916
  176.8 13.0 %copy-start.13 = (bf16[4,256,2048]{2,1,0:T(8,128)(2,1)}, bf16[4,256,2048]{2,1,0:T(8,128)(2,1)S(1)}, u32[]{:S(2)}) copy-start(bf16[4,256,2048]{2,1,0:T(8,128)(2,1)S(1)} %get-tuple-element.154) | copy-start | bytes 12582916
  176.8 13.0 %slice-start.11 = ((s8[5767168]{0:T(1024)(128)(4,1)}), s8[1572864]{0:T(1024)(128)(4,1)S(1)}, s32[]{:S(2)}) async-start(s8[5767168]{0:T(1024)(128)(4,1)} %bitcast.96), calls=%async_computation.24 | async-start | bytes 3145728
  198.3 297.2 %reduce-scatter.6.cloned.1.call-start = ((), (), s32[]{:S(2)}) async-start(), calls=%async_computation.8 | async-start | bytes 5242880 | tf_op jit(solution)/shard_map/reduce_scatter | solution.py:1222
  256.2 11.9 %copy-start.20 = (bf16[1024,2048]{1,0:T(8,128)(2,1)S(1)}, bf16[1024,2048]{1,0:T(8,128)(2,1)}, u32[]{:S(2)}) copy-start(bf16[1024,2048]{1,0:T(8,128)(2,1)} %all-gather.6.cloned.1.call-done.refs_0_) | copy-start | bytes 12582916
  256.2 38.5 %slice-start.4 = ((s8[5767168]{0:T(1024)(128)(4,1)}), s8[4194304]{0:T(1024)(128)(4,1)S(1)}, s32[]{:S(2)}) async-start(s8[5767168]{0:T(1024)(128)(4,1)} %bitcast.90), calls=%async_computation.17 | async-start | bytes 8388608
  268.1 26.6 %slice-start.5 = ((s8[5767168]{0:T(1024)(128)(4,1)}), s8[1572864]{0:T(1024)(128)(4,1)S(1)}, s32[]{:S(2)}) async-start(s8[5767168]{0:T(1024)(128)(4,1)} %bitcast.90), calls=%async_computation.18 | async-start | bytes 3145728
  280.8 13.9 %copy-start.22 = (bf16[1024,1408]{1,0:T(8,128)(2,1)}, bf16[1024,1408]{1,0:T(8,128)(2,1)S(1)}, u32[]{:S(2)}) copy-start(bf16[1024,1408]{1,0:T(8,128)(2,1)S(1)} %get-tuple-element.151.refs_8_) | copy-start | bytes 8650756
  280.8 13.9 %copy-start.23 = (bf16[1024,1408]{1,0:T(8,128)(2,1)}, bf16[1024,1408]{1,0:T(8,128)(2,1)S(1)}, u32[]{:S(2)}) copy-start(bf16[1024,1408]{1,0:T(8,128)(2,1)S(1)} %get-tuple-element.152.refs_4_) | copy-start | bytes 8650756
  280.8 22.9 %copy-start.24 = (bf16[1024,1408]{1,0:T(8,128)(2,1)}, bf16[1024,1408]{1,0:T(8,128)(2,1)S(1)}, u32[]{:S(2)}) copy-start(bf16[1024,1408]{1,0:T(8,128)(2,1)S(1)} %get-tuple-element.153.refs_6_) | copy-start | bytes 8650756
  280.8 22.9 %slice-start.8 = ((s8[5767168]{0:T(1024)(128)(4,1)}), s8[4194304]{0:T(1024)(128)(4,1)S(1)}, s32[]{:S(2)}) async-start(s8[5767168]{0:T(1024)(128)(4,1)} %bitcast.94), calls=%async_computation.21 | async-start | bytes 8388608
  294.7 9.0 %slice-start.9 = ((s8[5767168]{0:T(1024)(128)(4,1)}), s8[1572864]{0:T(1024)(128)(4,1)S(1)}, s32[]{:S(2)}) async-start(s8[5767168]{0:T(1024)(128)(4,1)} %bitcast.94), calls=%async_computation.22 | async-start | bytes 3145728
  337.7 157.8 %reduce-scatter.8.cloned.1.call-start = ((), (), s32[]{:S(2)}) async-start(), calls=%async_computation.9 | async-start | bytes 5242880 | tf_op jit(solution)/shard_map/reduce_scatter | solution.py:1222
  338.1 12.0 %copy-start.21 = (bf16[1024,2048]{1,0:T(8,128)(2,1)S(1)}, bf16[1024,2048]{1,0:T(8,128)(2,1)}, u32[]{:S(2)}) copy-start(bf16[1024,2048]{1,0:T(8,128)(2,1)} %all-gather.8.cloned.1.call-done.refs_1_) | copy-start | bytes 12582916
  338.1 26.3 %slice-start.6 = ((s8[5767168]{0:T(1024)(128)(4,1)}), s8[4194304]{0:T(1024)(128)(4,1)S(1)}, s32[]{:S(2)}) async-start(s8[5767168]{0:T(1024)(128)(4,1)} %bitcast.92), calls=%async_computation.19 | async-start | bytes 8388608
  350.1 14.3 %slice-start.7 = ((s8[5767168]{0:T(1024)(128)(4,1)}), s8[1572864]{0:T(1024)(128)(4,1)S(1)}, s32[]{:S(2)}) async-start(s8[5767168]{0:T(1024)(128)(4,1)} %bitcast.92), calls=%async_computation.20 | async-start | bytes 3145728
  364.5 9.0 %copy-start.26 = (bf16[1024,1408]{1,0:T(8,128)(2,1)}, bf16[1024,1408]{1,0:T(8,128)(2,1)S(1)}, u32[]{:S(2)}) copy-start(bf16[1024,1408]{1,0:T(8,128)(2,1)S(1)} %get-tuple-element.149.refs_5_) | copy-start | bytes 8650756
  364.5 9.0 %copy-start.27 = (bf16[1024,1408]{1,0:T(8,128)(2,1)}, bf16[1024,1408]{1,0:T(8,128)(2,1)S(1)}, u32[]{:S(2)}) copy-start(bf16[1024,1408]{1,0:T(8,128)(2,1)S(1)} %get-tuple-element.150.refs_7_) | copy-start | bytes 8650756
  385.7 434.6 %reduce-scatter.10.cloned.1.call-start = ((), (), s32[]{:S(2)}) async-start(), calls=%async_computation.10 | async-start | bytes 2621440 | tf_op jit(solution)/shard_map/reduce_scatter | solution.py:1222
  386.0 98.7 %copy-start.25 = (bf16[1024,1408]{1,0:T(8,128)(2,1)S(1)}, bf16[1024,1408]{1,0:T(8,128)(2,1)}, u32[]{:S(2)}) copy-start(bf16[1024,1408]{1,0:T(8,128)(2,1)} %get-tuple-element.148.refs_9_) | copy-start | bytes 8650756
  495.5 5.0 copy-start.15
  495.5 5.0 copy-start.33
  495.5 5.0 copy-start.37
  500.4 4.1 copy-start.12
  500.4 4.1 copy-start.40
  500.4 319.9 %reduce-scatter.12.cloned.1.call-start = ((), (), s32[]{:S(2)}) async-start(), calls=%async_computation.11 | async-start | bytes 2621440 | tf_op jit(solution)/shard_map/reduce_scatter | solution.py:1222
  500.5 4.3 copy-start.7
  500.5 4.6 copy-start.16
  508.2 15.3 %copy-start.3 = (bf16[16,128,128]{2,1,0:T(8,128)(2,1)S(1)}, bf16[16,128,128]{2,1,0:T(8,128)(2,1)}, u32[]{:S(2)}) copy-start(bf16[16,128,128]{2,1,0:T(8,128)(2,1)} %copy-done.2) | copy-start | bytes 1572868
  523.6 1.2 copy-start.5
  524.8 36.3 %copy-start.43 = (f32[1,128]{1,0:T(1,128)S(1)}, f32[1,128]{1,0:T(1,128)}, u32[]{:S(2)}) copy-start(f32[1,128]{1,0:T(1,128)} %get-tuple-element.81) | copy-start | bytes 1540
  558.9 1.0 copy-start.4
  559.8 260.5 %reduce-scatter.14.cloned.1.call-start = ((), (), s32[]{:S(2)}) async-start(), calls=%async_computation.12 | async-start | bytes 5242880 | tf_op jit(solution)/shard_map/reduce_scatter | solution.py:1222
  562.0 225.0 %copy-start.35 = (f32[2048]{0:T(1024)S(1)}, f32[2048]{0:T(1024)}, u32[]{:S(2)}) copy-start(f32[2048]{0:T(1024)} %param.17) | copy-start | bytes 24580
  562.0 225.0 %copy-start.39 = (f32[512]{0:T(512)S(1)}, f32[512]{0:T(512)}, u32[]{:S(2)}) copy-start(f32[512]{0:T(512)} %copy-done.38) | copy-start | bytes 6148
  793.2 30.1 %copy-start.10 = (bf16[512,2048]{1,0:T(8,128)(2,1)S(1)}, bf16[512,2048]{1,0:T(8,128)(2,1)}, u32[]{:S(2)}) copy-start(bf16[512,2048]{1,0:T(8,128)(2,1)} %param.15) | copy-start | bytes 6291460
  793.2 30.1 %copy-start.41 = (f32[512]{0:T(512)S(1)}, f32[512]{0:T(512)}, u32[]{:S(2)}) copy-start(f32[512]{0:T(512)} %get-tuple-element.166) | copy-start | bytes 6148
  820.3 3.2 copy-start.8
  823.6 8.7 %copy-start.30 = (f32[256,1408]{1,0:T(8,128)S(1)}, f32[256,1408]{1,0:T(8,128)}, u32[]{:S(2)}) copy-start(f32[256,1408]{1,0:T(8,128)} %get-tuple-element.200) | copy-start | bytes 4325380
  823.6 9.8 %copy-start.29 = (f32[256,1408]{1,0:T(8,128)S(1)}, f32[256,1408]{1,0:T(8,128)}, u32[]{:S(2)}) copy-start(f32[256,1408]{1,0:T(8,128)} %get-tuple-element.201) | copy-start | bytes 4325380
  832.2 2.2 copy-start.28
  (1 other events, 0.6 us)
Sparse Core Ops, SparseCore 0:
  9.6 161.4 all-gather.3
  173.2 82.8 all-gather.5
  258.3 79.2 all-gather.7
  339.8 75.2 reduce-scatter.5
  417.4 77.2 reduce-scatter.7
  500.6 54.6 reduce-scatter.9
  560.0 43.5 reduce-scatter.11
  605.9 107.8 reduce-scatter.13

commit v8 on v7

--- a/solution.py
+++ b/solution.py
@@ -621,6 +621,7 @@
 
 RING = 3
 HELD = 5
+LAG = 2
 
 
 def fused_kernel(*refs):
@@ -674,33 +675,29 @@
             halo_out.at[unit], halo_in.at[unit], halo_send.at[unit], halo_recv.at[unit], {"narrow": z - 1}
         )
 
-    def order(unit):
-        e = unit % 2
-
-        def pick(even, odd):
-            return (1 - e) * even + e * odd
-
-        def away(j):
-            return pick(2 * j + 1 - x, 2 * (1 - y) + j)
-
-        def kept(j):
-            return pick(2 * j + x, 2 * y + j)
-
-        return away, kept, pick(flip_x, flip_y), pick(flip_y, flip_x), pick(1 - y, 1 - x), pick(y, x)
-
-    def copy2(unit, j):
-        away, _, target, _, _, _ = order(unit)
-        return remote(total.at[unit % HELD, away(j)], got2.at[unit, j], send2.at[unit, j], recv2.at[unit, j], {"dp": target})
-
-    def copy3(unit):
-        _, kept, _, target, far, _ = order(unit)
-        return remote(total.at[unit % HELD, kept(far)], got3.at[unit], send3.at[unit], recv3.at[unit], {"dp": target})
+    near = 2 * y + x
+    fars = (2 * (1 - y) + x, 2 * y + 1 - x)
+
+    def band(e):
+        return pl.ds(2 * e * rows, 2 * rows)
+
+    def copy2(unit, e, j):
+        away = (2 * j + 1 - x, 2 * (1 - y) + j)[e]
+        return remote(
+            total.at[unit % HELD, away, band(e)], got2.at[unit, e, j],
+            send2.at[unit, e, j], recv2.at[unit, e, j], {"dp": (flip_x, flip_y)[e]},
+        )
+
+    def copy3(unit, e):
+        return remote(
+            total.at[unit % HELD, fars[e], band(e)], got3.at[unit, e],
+            send3.at[unit, e], recv3.at[unit, e], {"dp": (flip_y, flip_x)[e]},
+        )
 
     def copyz(unit, part, k):
-        _, kept, _, _, _, near = order(unit)
         at = pl.ds(pl.multiple_of(part * rows + peers[k] * share, share), share)
         return remote(
-            total.at[unit % HELD, kept(near), at], gotz.at[unit, k, part * share : (part + 1) * share],
+            total.at[unit % HELD, near, at], gotz.at[unit, k, part * share : (part + 1) * share],
             sendz.at[unit, k, part], recvz.at[unit, k, part], {"narrow": peers[k]},
         )
 
@@ -767,13 +764,12 @@
     @pl.when(step >= 1)
     def _():
         unit = step - 1
-        away, kept, _, _, _, _ = order(unit)
         for copy in right_copies(unit):
             copy.wait()
 
         def one(k, _):
-            j = k % 2
-            stripe = (k // 2) * kept(j) + (1 - k // 2) * away(j)
+            to_x, to_y = 1 - k // 2, 1 - k % 2
+            stripe = 2 * (to_y * (1 - y) + (1 - to_y) * y) + to_x * (1 - x) + (1 - to_x) * x
             for part in range(parts):
                 which = part // (parts - 1)
                 mine = d_proj[unit % RING, part] if which == 0 else mixed_ref[...]
@@ -783,9 +779,18 @@
                 )
                 total[unit % HELD, stripe, part * rows : (part + 1) * rows, :] = value.astype(BF16)
 
-            @pl.when(k < 2)
+            @pl.when(k == 0)
             def _():
-                copy2(unit, j).start()
+                copy2(unit, 0, 1 - y).start()
+                copy2(unit, 1, 1 - x).start()
+
+            @pl.when(k == 1)
+            def _():
+                copy2(unit, 0, y).start()
+
+            @pl.when(k == 2)
+            def _():
+                copy2(unit, 1, x).start()
 
             return 0
 
@@ -804,27 +809,27 @@
         lax.fori_loop(0, d_normed.shape[1] // 512, normed_part, 0)
 
     def second(unit):
-        _, kept, _, _, far, near = order(unit)
-        for j in range(2):
-            copy2(unit, j).wait()
-        add_rows(total.at[unit % HELD, kept(far)], got2.at[unit, far], 64)
-        copy3(unit).start()
-        add_rows(total.at[unit % HELD, kept(near)], got2.at[unit, near], 64)
+        for e in range(2):
+            for j in range(2):
+                copy2(unit, e, j).wait()
+            add_rows(total.at[unit % HELD, fars[e], band(e)], got2.at[unit, e, (1 - y, 1 - x)[e]], 64)
+            copy3(unit, e).start()
+        for e in range(2):
+            add_rows(total.at[unit % HELD, near, band(e)], got2.at[unit, e, (y, x)[e]], 64)
 
     def grad_copy(unit):
         at = pl.ds(pl.multiple_of(unit * cols, cols), cols)
         return pltpu.make_async_copy(grad.at[unit % 2], grad_hbm.at[:, :, at], grad_sem.at[unit % 2])
 
     def third(unit):
-        _, kept, _, _, _, near = order(unit)
-        copy3(unit).wait()
-        add_rows(total.at[unit % HELD, kept(near)], got3.at[unit], 64)
-        for k in range(depth - 1):
-            for part in range(parts):
-                copyz(unit, part, k).start()
+        for e in range(2):
+            copy3(unit, e).wait()
+            add_rows(total.at[unit % HELD, near, band(e)], got3.at[unit, e], 64)
+            for k in range(depth - 1):
+                for part in (2 * e, 2 * e + 1):
+                    copyz(unit, part, k).start()
 
     def fourth(unit):
-        _, kept, _, _, _, near = order(unit)
         for k in range(depth - 1):
             for part in range(parts):
                 copyz(unit, part, k).wait()
@@ -834,24 +839,24 @@
 
         for part in range(parts):
             at = pl.ds(pl.multiple_of(part * rows + z * share, share), share)
-            value = total[unit % HELD, kept(near), at, :].astype(F32)
+            value = total[unit % HELD, near, at, :].astype(F32)
             for k in range(depth - 1):
                 value = value + gotz[unit, k, part * share : (part + 1) * share, :].astype(F32)
             grad[unit % 2, part] = value
         grad_copy(unit).start()
 
     def stages(at):
-        @pl.when((at >= 3) & (at < units + 3))
+        @pl.when((at >= LAG) & (at < units + LAG))
         def _():
-            second(at - 3)
-
-        @pl.when((at >= 4) & (at < units + 4))
+            second(at - LAG)
+
+        @pl.when((at >= LAG + 1) & (at < units + LAG + 1))
         def _():
-            third(at - 4)
-
-        @pl.when(at >= 5)
+            third(at - LAG - 1)
+
+        @pl.when(at >= LAG + 2)
         def _():
-            fourth(at - 5)
+            fourth(at - LAG - 2)
 
     stages(step)
 
@@ -864,7 +869,7 @@
             stages(at)
             return 0
 
-        lax.fori_loop(units + 1, units + 5, one, 0)
+        lax.fori_loop(units + 1, units + LAG + 2, one, 0)
         save.wait()
         grad_copy(units - 2).wait()
         grad_copy(units - 1).wait()
@@ -931,13 +936,13 @@
             pltpu.VMEM((units, 3, PAD, cols), F32),
             pltpu.VMEM((units, 3, PAD, cols), F32),
             pltpu.VMEM((HELD, 4, parts * rows, cols), BF16),
-            pltpu.VMEM((units, 2, parts * rows, cols), BF16),
-            pltpu.VMEM((units, parts * rows, cols), BF16),
+            pltpu.VMEM((units, 2, 2, 2 * rows, cols), BF16),
+            pltpu.VMEM((units, 2, 2 * rows, cols), BF16),
             pltpu.VMEM((units, depth - 1, parts * share, cols), BF16),
             pltpu.VMEM((tokens, width), F32),
             pltpu.VMEM((2, parts, share, cols), F32),
             dma((8,)), dma((2,)), dma((8,)), dma((8,)), dma((RING, 2)), dma((RING, 2)), dma((units,)), dma((units,)),
-            dma((units, 2)), dma((units, 2)), dma((units,)), dma((units,)),
+            dma((units, 2, 2)), dma((units, 2, 2)), dma((units, 2)), dma((units, 2)),
             dma((units, depth - 1, parts)), dma((units, depth - 1, parts)),
         ],
         compiler_params=pltpu.CompilerParams(
@@ -1256,11 +1261,13 @@
         )
         d_up.append((d_act * silu_gate).astype(BF16))
         d_part = (dot_nt(d_gate[at], w_gate) + dot_nt(d_up[at], w_up)).astype(BF16)
-        out_parts.append(matmul(activation[at], w_down).astype(BF16))
+        out_part = matmul(activation[at], w_down).astype(BF16)
         if at + 1 < HALVES:
-            d_part, out_parts[at], gathered[at + 1] = lax.optimization_barrier(
-                (d_part, out_parts[at], gathered[at + 1])
-            )
+            quarters = out_part.reshape(-1, 2, half // 2, model_width)
+            out_parts += [quarters[:, side].reshape(-1, model_width) for side in range(2)]
+            d_part, out_parts, gathered[at + 1] = lax.optimization_barrier((d_part, out_parts, gathered[at + 1]))
+        else:
+            out_parts.append(out_part)
         d_normed_parts.append(scatter(d_part))
     if lax.axis_size("dp") == 8:
         ffn_sums = ffn_grads((gathered, cot), (d_gate, d_up, activation))
@@ -1273,9 +1280,7 @@
         ]
         ffn_sums[2] = ffn_sums[2].T
     d_normed_parts, out_parts, ffn_sums = lax.optimization_barrier((d_normed_parts, out_parts, ffn_sums))
-    quarters = out_parts[0].reshape(-1, 2, half // 2, model_width)
-    out_first, out_second = (quarters[:, at].reshape(-1, model_width) for at in range(2))
-    out_rest = [out_second, *out_parts[1:]]
+    out_first, *out_rest = out_parts
     ffn_parts = [scatter(out_first)]
     grad_gate, grad_up, grad_down = (value.astype(F32) for value in ffn_sums)
     d_normed_mlp = jnp.concatenate(d_normed_parts, axis=0).astype(F32)

time: 848 us -> 838 us (0.988)
  no operation moved by 1% of the time
where the time goes in v8:
time: 838 us; the launch traced here: 833 us
  Pallas kernels  471 us (56%)
  matrix products  172 us (21%)
  waiting for transfers between devices  113 us (13%)
  local copies, waits for them, and re-layouts  32.9 us (4%)
  other arithmetic  21.3 us (3%)
  between operations  15.2 us (2%)
    pallas_call x1, Pallas kernels, fused_backward(): pl.pallas_call(fused_kernel, grid=(units + 1,), in_specs=[whole(since.sha...  218 us
    all_gather x3, waiting for transfers between devices, gather(): return lax.all_gather(rows, 'narrow', axis=0, tiled=True)  111 us
    dot_general x11, matrix products, matmul(): return jnp.dot(left, right, preferred_element_type=F32)  102 us
    pallas_call x1, Pallas kernels, ffn_grads(): pl.pallas_call(ffn_grads_kernel, in_specs=[pl.BlockSpec(memory_space=pl.A...  98.6 us
    pallas_call x2, Pallas kernels, carry_chain(): pl.pallas_call(functools.partial(chain_kernel, axis, forward), in_specs=[...  61.3 us
    pallas_call x1, Pallas kernels, mixer_forward(): pl.pallas_call(forward_kernel, grid=(heads // HEADS_STEP,), in_specs=[who...  50.7 us
    dot_general x4, matrix products, dot_nt(): return jnp.einsum('re,de->rd', left, right, preferred_element_type=F32)  40.8 us
    dot_general x2, matrix products, local(): d_act = jnp.einsum('rd,fd->rf', cot[at], w_down, preferred_element_type=F32)  21.5 us
  transfers between devices with their start and end apart: 9, of which 4 were waited for; matrix products, arithmetic and copies ran while one was open for 24% of the time, Pallas kernels for 57%

profile of v8, /device:TPU:0, one launch (start us, length us, event | category | flops | bytes accessed | tf_op | source)
XLA Modules:
  0.0 832.7 jit_solution(11322878478498758886)
XLA Ops:
  7.3 0.7 all-gather.4.cloned.1.call-update
  8.0 2.1 fusion.9
  10.1 0.6 multiply_multiply_fusion
  11.9 9.2 %convolution_convert_fusion.4.query_ref.refs_2_ = bf16[512,2048]{1,0:T(8,128)(2,1)S(1)} fusion(bf16[512,2048]{1,0:T(8,128)(2,1)S(1)} %fusion.11.refs_18_, bf16[2048,2048]{1,0:T(8,128)(2,1)} %refs_14_.1), kind=kOutput, calls=%fused_computation.44 | convolution fusion | flops 4296015872 | bytes 12582912 | tf_op jit(solution)/shard_map/dot_general | solution.py:1163
  21.2 4.8 convolution_convert_fusion.2.value_ref.refs_4_
  26.0 4.8 convolution_convert_fusion.3.key_ref.refs_3_
  30.8 1.3 copy-done.19
  32.2 5.5 collective-permute-start
  37.9 3.0 fusion.28.beta_ref.refs_1_
  40.9 1.0 collective-permute-done.halo_ref.refs_5_
  41.9 0.8 broadcast_in_dim.19.since_ref.refs_0_
  42.8 50.7 %mixer_forward.1 = (bf16[512,2048]{1,0:T(8,128)(2,1)}, bf16[512,2048]{1,0:T(8,128)(2,1)}, bf16[512,2048]{1,0:T(8,128)(2,1)}, bf16[512,2048]{1,0:T(8,128)(2,1)}, ...) custom-call(s32[512,128]{1,0:T(8,128)} %broadcast_in_dim.19.since_ref.refs_0_, ...), custom_call_target="tpu_custom_call" | custom-call | tf_op jit(solution)/shard_map/mixer_forward/pallas_call | solution.py:180
  93.5 1.3 slice.101.map_ref
  94.8 1.5 slice.65.add_ref
  96.3 26.7 %carry_forward.1.entry_ref.refs_11_ = f32[16,128,128]{2,1,0:T(8,128)S(1)} custom-call(bf16[16,128,128]{2,1,0:T(8,128)(2,1)S(1)} %slice.101.map_ref, f32[16,128,128]{2,1,0:T(8,128)S(1)} %slice.65.add_ref), custom_call_target="tpu_custom_call" | custom-call | tf_op jit(solution)/shard_map/carry_forward/pallas_call | solution.py:499
  123.1 1.0 copy-done.1
  124.0 7.6 mixer_join.1.refs_17_
  131.7 7.8 multiply_reduce_fusion
  139.4 0.6 multiply_multiply_fusion.1
  140.1 1.3 copy-done.6
  141.8 29.3 %all-gather.4.cloned.1.call-done = bf16[2048,2048]{1,0:T(8,128)(2,1)} async-done(((bf16[512,2048]{1,0:T(8,128)(2,1)}), bf16[2048,2048]{1,0:T(8,128)(2,1)}) %all-gather.4.cloned.1.call-update) | async-done | bytes 8388624 | tf_op jit(solution)/shard_map/all_gather | solution.py:1224
  171.1 1.4 fusion.27
  172.8 4.0 fusion.25
  176.8 13.0 %fusion.29 = f32[1024,1408]{1,0:T(8,128)} fusion(bf16[1024,2048]{1,0:T(8,128)(2,1)S(1)} %bitcast.74, bf16[1408,2048]{1,0:T(8,128)(2,1)} %param.28), kind=kOutput, calls=%fused_computation.77 | convolution fusion | flops 5905580032 | bytes 15728640 | tf_op jit(solution)/shard_map/rd,fd->rf/dot_general | solution.py:1258
  189.8 8.5 %fusion.32 = f32[1024,1408]{1,0:T(8,128)} fusion(bf16[1024,2048]{1,0:T(8,128)(2,1)S(1)} %bitcast.72, bf16[1408,2048]{1,0:T(8,128)(2,1)S(1)} %bitcast.97), kind=kOutput, calls=%fused_computation.80 | convolution fusion | flops 5905580032 | bytes 15728640 | tf_op jit(solution)/shard_map/rd,fd->rf/dot_general | solution.py:1258
  198.6 57.6 %all-gather.6.cloned.1.call-done.refs_0_ = bf16[1024,2048]{1,0:T(8,128)(2,1)} async-done(((bf16[256,2048]{1,0:T(8,128)(2,1)}), bf16[1024,2048]{1,0:T(8,128)(2,1)}) %all-gather.6.cloned.1.call-update) | async-done | bytes 4194320 | tf_op jit(solution)/shard_map/all_gather | solution.py:1224
  256.2 11.8 %fusion.30 = f32[1024,1408]{1,0:T(8,128)} fusion(bf16[1024,2048]{1,0:T(8,128)(2,1)} %all-gather.6.cloned.1.call-done.refs_0_, bf16[2048,1408]{1,0:T(8,128)(2,1)} %param.26), kind=kOutput, calls=%fused_computation.78 | convolution fusion | flops 5905580032 | bytes 15728640 | tf_op jit(solution)/shard_map/dot_general | solution.py:1163
  268.0 12.7 %multiply_convert_fusion.3 = (bf16[1024,1408]{1,0:T(8,128)(2,1)S(1)}, bf16[1024,1408]{1,0:T(8,128)(2,1)S(1)}, bf16[1024,1408]{1,0:T(8,128)(2,1)S(1)}) fusion(f32[1024,1408]{1,0:T(8,128)} %fusion.30, f32[1024,1408]{1,0:T(8,128)} %fusion.29, bf16[1024,2048]{1,0:T(8,128)(2,1)S(1)} %copy-done.20, bf16[2048,1408]{1,0:T(8,128)(2,1)} %param.27), kind=kOutput, calls=%fused_computation.13 | convolution fusion | flops 5927206912 | bytes 30146560 | tf_op jit(solution)/shard_map/dot_general | solution.py:1163
  280.7 10.9 %convolution_convert_fusion.1 = bf16[1024,2048]{1,0:T(8,128)(2,1)S(1)} fusion(bf16[1024,1408]{1,0:T(8,128)(2,1)S(1)} %get-tuple-element.155.refs_8_, bf16[1408,2048]{1,0:T(8,128)(2,1)} %param.28), kind=kOutput, calls=%fused_computation.41 | convolution fusion | flops 5907677184 | bytes 12845056 | tf_op jit(solution)/shard_map/dot_general | solution.py:1163
  291.6 2.7 fusion.26
  294.3 9.0 %fusion.31 = f32[1024,2048]{1,0:T(8,128)} fusion(bf16[1024,1408]{1,0:T(8,128)(2,1)S(1)} %get-tuple-element.156.refs_4_, bf16[2048,1408]{1,0:T(8,128)(2,1)S(1)} %bitcast.91), kind=kOutput, calls=%fused_computation.79 | convolution fusion | flops 5905580032 | bytes 17039360 | tf_op jit(solution)/shard_map/re,de->rd/dot_general | solution.py:1171
  303.4 10.5 %add_convert_fusion.1 = bf16[1024,2048]{1,0:T(8,128)(2,1)} fusion(f32[1024,2048]{1,0:T(8,128)} %fusion.31, bf16[1024,1408]{1,0:T(8,128)(2,1)S(1)} %get-tuple-element.157.refs_6_, bf16[2048,1408]{1,0:T(8,128)(2,1)S(1)} %bitcast.95), kind=kOutput, calls=%fused_computation.7 | convolution fusion | flops 5909774336 | bytes 21233664 | tf_op jit(solution)/shard_map/re,de->rd/dot_general | solution.py:1171
  313.9 23.7 %all-gather.8.cloned.1.call-done.refs_1_ = bf16[1024,2048]{1,0:T(8,128)(2,1)} async-done(((bf16[256,2048]{1,0:T(8,128)(2,1)}), bf16[1024,2048]{1,0:T(8,128)(2,1)}) %all-gather.8.cloned.1.call-update) | async-done | bytes 4194320 | tf_op jit(solution)/shard_map/all_gather | solution.py:1224
  338.1 12.0 %fusion.33 = f32[1024,1408]{1,0:T(8,128)} fusion(bf16[1024,2048]{1,0:T(8,128)(2,1)} %all-gather.8.cloned.1.call-done.refs_1_, bf16[2048,1408]{1,0:T(8,128)(2,1)} %param.26), kind=kOutput, calls=%fused_computation.81 | convolution fusion | flops 5905580032 | bytes 15728640 | tf_op jit(solution)/shard_map/dot_general | solution.py:1163
  350.2 14.3 %multiply_convert_fusion = (bf16[1024,1408]{1,0:T(8,128)(2,1)}, bf16[1024,1408]{1,0:T(8,128)(2,1)S(1)}, bf16[1024,1408]{1,0:T(8,128)(2,1)S(1)}) fusion(f32[1024,1408]{1,0:T(8,128)} %fusion.33, f32[1024,1408]{1,0:T(8,128)} %fusion.32, bf16[1024,2048]{1,0:T(8,128)(2,1)S(1)} %copy-done.21, bf16[2048,1408]{1,0:T(8,128)(2,1)} %param.27), kind=kOutput, calls=%fused_computation.8 | convolution fusion | flops 5927206912 | bytes 30146560 | tf_op jit(solution)/shard_map/dot_general | solution.py:1163
  364.5 9.0 %fusion.34 = f32[1024,2048]{1,0:T(8,128)} fusion(bf16[1024,1408]{1,0:T(8,128)(2,1)S(1)} %get-tuple-element.153.refs_5_, bf16[2048,1408]{1,0:T(8,128)(2,1)S(1)} %bitcast.93), kind=kOutput, calls=%fused_computation.82 | convolution fusion | flops 5905580032 | bytes 17039360 | tf_op jit(solution)/shard_map/re,de->rd/dot_general | solution.py:1171
  373.5 12.3 %add_convert_fusion = bf16[1024,2048]{1,0:T(8,128)(2,1)} fusion(f32[1024,2048]{1,0:T(8,128)} %fusion.34, bf16[1024,1408]{1,0:T(8,128)(2,1)S(1)} %get-tuple-element.154.refs_7_, bf16[2048,1408]{1,0:T(8,128)(2,1)} %param.27), kind=kOutput, calls=%fused_computation.6 | convolution fusion | flops 5909774336 | bytes 21233664 | tf_op jit(solution)/shard_map/re,de->rd/dot_general | solution.py:1171
  386.0 98.6 %ffn_grads.1 = (f32[256,1408]{1,0:T(8,128)}, f32[256,1408]{1,0:T(8,128)}, f32[1408,256]{1,0:T(8,128)}) custom-call(bf16[1024,2048]{1,0:T(8,128)(2,1)} %all-gather.6.cloned.1.call-done.refs_0_, bf16[1024,2048]{1,0:T(8,128)(2,1)} %all-gather.8.cloned.1.call-done.refs_1_, bf16[1024,2048]{1,0:T(8,128)(2,1)} %bitcast.75, bf16[1024,2048]{1,0:T(8,128)(2,1)} %bitcast.73, ...), custom_call_target="tpu_custom_call" | custom-call | tf_op jit(solution)/shard_map/ffn_grads/pallas_call | solution.py:1129
  484.6 10.8 %convolution_convert_fusion = bf16[1024,2048]{1,0:T(8,128)(2,1)} fusion(bf16[1024,1408]{1,0:T(8,128)(2,1)S(1)} %copy-done.25, bf16[1408,2048]{1,0:T(8,128)(2,1)} %param.28), kind=kOutput, calls=%fused_computation.40 | convolution fusion | flops 5907677184 | bytes 12845056 | tf_op jit(solution)/shard_map/dot_general | solution.py:1163
  495.6 4.2 fusion.8
  499.8 0.6 copy-done.7
  500.7 3.2 fusion.24.branch_ref.refs_19_
  503.9 15.3 %mixer_core_back.1 = (bf16[512,2048]{1,0:T(8,128)(2,1)}, f32[16,128,128]{2,1,0:T(8,128)}, f32[1,128]{1,0:T(1,128)}) custom-call(bf16[512,2048]{1,0:T(8,128)(2,1)} %get-tuple-element.52.out_add_ref, bf16[512,2048]{1,0:T(8,128)(2,1)} %get-tuple-element.53.out_map_ref, f32[16,128,128]{2,1,0:T(8,128)} %copy-done.1, f32[1,128]{1,0:T(1,128)} %bitcast.88, ...), custom_call_target="tpu_custom_call" | custom-call | tf_op jit(solution)/shard_map/mixer_core_back/pallas_call | solution.py:253
  519.2 1.2 copy-done.5
  520.5 34.6 %carry_backward.1.refs_12_ = f32[16,128,128]{2,1,0:T(8,128)S(1)} custom-call(bf16[16,128,128]{2,1,0:T(8,128)(2,1)S(1)} %copy-done.3, f32[16,128,128]{2,1,0:T(8,128)S(1)} %copy-done.5), custom_call_target="tpu_custom_call" | custom-call | tf_op jit(solution)/shard_map/carry_backward/pallas_call | solution.py:499
  555.1 1.0 copy-done.4
  556.2 0.7 reduce-scatter.14.cloned.1.call-update
  557.4 0.7 reduce.9
  558.3 217.5 %fused_backward.1 = (f32[4,64,2048]{2,1,0:T(8,128)}, f32[512,2048]{1,0:T(8,128)}, f32[3,4,2048]{2,1,0:T(4,128)}, f32[512,16]{1,0:T(8,128)}) custom-call(s32[512,128]{1,0:T(8,128)} %broadcast_in_dim.19.since_ref.refs_0_, f32[512,16]{1,0:T(8,128)} %fusion.28.beta_ref.refs_1_, bf16[512,2048]{1,0:T(8,128)(2,1)} %copy-done.17, bf16[512,2048]{1,0:T(8,128)(2,1)} %copy-done.19, ...), custom_call_target="tpu_custom_call" | custom-call | tf_op jit(solution)/shard_map/fused_backward/pallas_call | solution.py:913
  775.8 0.9 reshape.129
  776.7 2.0 fusion.19
  778.8 6.2 fusion.18
  785.1 1.3 copy.59
  786.4 1.3 pad.9.small_ref
  787.7 19.9 %reduce_small.1 = f32[64,128]{1,0:T(8,128)S(1)} custom-call(f32[2048,128]{1,0:T(8,128)S(1)} %pad.9.small_ref), custom_call_target="tpu_custom_call" | custom-call | tf_op jit(solution)/shard_map/reduce_small/pallas_call | solution.py:602
  807.6 0.7 copy.61
  808.4 0.6 reshape.132
  809.0 0.7 slice_reduce_fusion.2
  809.7 0.7 slice_reduce_fusion
  810.4 3.0 slice_bitcast_fusion
  813.6 8.7 %fusion.15 = (bf16[512,2048]{1,0:T(8,128)(2,1)}, bf16[512,2048]{1,0:T(8,128)(2,1)}) fusion(bf16[512,2048]{1,0:T(8,128)(2,1)S(1)} %copy-done.10, f32[512]{0:T(512)S(1)} %broadcast_multiply_fusion, f32[512]{0:T(512)S(1)} %copy-done.41, f32[2048]{0:T(1024)S(1)} %copy-done.35, f32[512]{0:T(512)S(1)} %copy-done.39, f32[512,2048]{1,0:T(8,128)} %get-tuple-element.82, ...), kind=kLoop, calls=%fused_computation.33 | loop fusion | flops 29360128 | bytes 25194496 | tf_op jit(solution)/shard_map/convert_element_type | solution.py:1313
  822.3 1.1 copy.68
  823.4 1.1 copy.69
  824.5 1.1 copy.70
  (149 shorter events, 4.8 us)
Async XLA Ops:
  7.2 30.7 %copy-start = (bf16[2048,16]{0,1:T(8,128)(2,1)S(1)}, bf16[2048,16]{0,1:T(8,128)(2,1)}, u32[]{:S(2)}) copy-start(bf16[2048,16]{0,1:T(8,128)(2,1)} %param.21) | copy-start | bytes 196612
  7.2 4.1 copy-start.9
  7.2 4.1 copy-start.34
  7.2 163.9 %all-gather.4.cloned.1.call-start = ((), (), s32[]{:S(2)}) async-start(), calls=%async_computation.5 | async-start | bytes 10485760 | tf_op jit(solution)/shard_map/all_gather | solution.py:1224
  8.0 248.2 %all-gather.6.cloned.1.call-start = ((), (), s32[]{:S(2)}) async-start(), calls=%async_computation.6 | async-start | bytes 5242880 | tf_op jit(solution)/shard_map/all_gather | solution.py:1224
  11.3 9.9 %slice-start.2 = ((s8[8388608]{0:T(1024)(128)(4,1)}), s8[4194304]{0:T(1024)(128)(4,1)S(1)}, s32[]{:S(2)}) async-start(s8[8388608]{0:T(1024)(128)(4,1)} %bitcast.78), calls=%async_computation.15 | async-start | bytes 8388608
  11.8 14.1 %copy-start.11 = (bf16[512,2048]{1,0:T(8,128)(2,1)}, bf16[512,2048]{1,0:T(8,128)(2,1)S(1)}, u32[]{:S(2)}) copy-start(bf16[512,2048]{1,0:T(8,128)(2,1)S(1)} %fusion.11.refs_18_) | copy-start | bytes 6291460
  11.8 9.3 %slice-start.3 = ((s8[8388608]{0:T(1024)(128)(4,1)}), s8[4194304]{0:T(1024)(128)(4,1)S(1)}, s32[]{:S(2)}) async-start(s8[8388608]{0:T(1024)(128)(4,1)} %bitcast.78), calls=%async_computation.16 | async-start | bytes 8388608
  11.8 14.1 %slice-start = ((s8[8388608]{0:T(1024)(128)(4,1)}), s8[4194304]{0:T(1024)(128)(4,1)S(1)}, s32[]{:S(2)}) async-start(s8[8388608]{0:T(1024)(128)(4,1)} %bitcast.76), calls=%async_computation.13 | async-start | bytes 8388608
  21.1 4.9 copy-start.17
  21.1 4.9 slice-start.1
  26.0 4.8 copy-start.18
  26.0 11.6 %copy-start.42 = (s32[1,4]{1,0:T(1,128)S(1)}, s32[1,4]{1,0:T(1,128)}, u32[]{:S(2)}) copy-start(s32[1,4]{1,0:T(1,128)} %param.16) | copy-start | bytes 52
  30.8 1.4 copy-start.19
  32.2 9.8 %collective-permute-start = (bf16[3,8,2048]{2,1,0:T(8,128)(2,1)S(1)}, bf16[3,8,2048]{2,1,0:T(8,128)(2,1)S(1)}, u32[]{:S(2)}, u32[]{:S(2)}) collective-permute-start(bf16[3,8,2048]{2,1,0:T(8,128)(2,1)S(1)} %pad_maximum_fusion.1), channel_id=1, source_target_pairs={{0,1},{1,2},{2,3},{4,5},{5,6},{6,7},{8,9},{9,10},{10,11},{12,13},{... | collective-permute-start | bytes 294920 | tf_op jit(solution)/shard_map/ppermute | solution.py:1159
  41.9 0.8 copy-start.31
  94.8 28.2 %copy-start.2 = (bf16[16,128,128]{2,1,0:T(8,128)(2,1)}, bf16[16,128,128]{2,1,0:T(8,128)(2,1)S(1)}, u32[]{:S(2)}) copy-start(bf16[16,128,128]{2,1,0:T(8,128)(2,1)S(1)} %slice.101.map_ref) | copy-start | bytes 1572868
  123.1 1.0 copy-start.1
  131.7 9.8 %copy-start.32 = (f32[2048]{0:T(1024)S(1)}, f32[2048]{0:T(1024)}, u32[]{:S(2)}) copy-start(f32[2048]{0:T(1024)} %param.25) | copy-start | bytes 24580
  139.4 2.0 copy-start.6
  140.1 1.3 copy-start.36
  172.6 165.1 %all-gather.8.cloned.1.call-start = ((), (), s32[]{:S(2)}) async-start(), calls=%async_computation.7 | async-start | bytes 5242880 | tf_op jit(solution)/shard_map/all_gather | solution.py:1224
  172.8 17.0 %slice-start.10 = ((s8[5767168]{0:T(1024)(128)(4,1)}), s8[4194304]{0:T(1024)(128)(4,1)S(1)}, s32[]{:S(2)}) async-start(s8[5767168]{0:T(1024)(128)(4,1)} %bitcast.96), calls=%async_computation.23 | async-start | bytes 8388608
  176.8 13.0 %copy-start.14 = (bf16[4,256,2048]{2,1,0:T(8,128)(2,1)}, bf16[4,256,2048]{2,1,0:T(8,128)(2,1)S(1)}, u32[]{:S(2)}) copy-start(bf16[4,256,2048]{2,1,0:T(8,128)(2,1)S(1)} %get-tuple-element.159) | copy-start | bytes 12582916
  176.8 13.0 %copy-start.13 = (bf16[4,256,2048]{2,1,0:T(8,128)(2,1)}, bf16[4,256,2048]{2,1,0:T(8,128)(2,1)S(1)}, u32[]{:S(2)}) copy-start(bf16[4,256,2048]{2,1,0:T(8,128)(2,1)S(1)} %get-tuple-element.158) | copy-start | bytes 12582916
  176.8 13.0 %slice-start.11 = ((s8[5767168]{0:T(1024)(128)(4,1)}), s8[1572864]{0:T(1024)(128)(4,1)S(1)}, s32[]{:S(2)}) async-start(s8[5767168]{0:T(1024)(128)(4,1)} %bitcast.96), calls=%async_computation.24 | async-start | bytes 3145728
  198.3 297.1 %reduce-scatter.6.cloned.1.call-start = ((), (), s32[]{:S(2)}) async-start(), calls=%async_computation.8 | async-start | bytes 5242880 | tf_op jit(solution)/shard_map/reduce_scatter | solution.py:1227
  256.2 11.8 %copy-start.20 = (bf16[1024,2048]{1,0:T(8,128)(2,1)S(1)}, bf16[1024,2048]{1,0:T(8,128)(2,1)}, u32[]{:S(2)}) copy-start(bf16[1024,2048]{1,0:T(8,128)(2,1)} %all-gather.6.cloned.1.call-done.refs_0_) | copy-start | bytes 12582916
  256.2 38.1 %slice-start.4 = ((s8[5767168]{0:T(1024)(128)(4,1)}), s8[4194304]{0:T(1024)(128)(4,1)S(1)}, s32[]{:S(2)}) async-start(s8[5767168]{0:T(1024)(128)(4,1)} %bitcast.90), calls=%async_computation.17 | async-start | bytes 8388608
  268.0 26.3 %slice-start.5 = ((s8[5767168]{0:T(1024)(128)(4,1)}), s8[1572864]{0:T(1024)(128)(4,1)S(1)}, s32[]{:S(2)}) async-start(s8[5767168]{0:T(1024)(128)(4,1)} %bitcast.90), calls=%async_computation.18 | async-start | bytes 3145728
  280.7 10.9 %copy-start.22 = (bf16[1024,1408]{1,0:T(8,128)(2,1)}, bf16[1024,1408]{1,0:T(8,128)(2,1)S(1)}, u32[]{:S(2)}) copy-start(bf16[1024,1408]{1,0:T(8,128)(2,1)S(1)} %get-tuple-element.155.refs_8_) | copy-start | bytes 8650756
  280.7 13.6 %copy-start.23 = (bf16[1024,1408]{1,0:T(8,128)(2,1)}, bf16[1024,1408]{1,0:T(8,128)(2,1)S(1)}, u32[]{:S(2)}) copy-start(bf16[1024,1408]{1,0:T(8,128)(2,1)S(1)} %get-tuple-element.156.refs_4_) | copy-start | bytes 8650756
  280.7 22.6 %copy-start.24 = (bf16[1024,1408]{1,0:T(8,128)(2,1)}, bf16[1024,1408]{1,0:T(8,128)(2,1)S(1)}, u32[]{:S(2)}) copy-start(bf16[1024,1408]{1,0:T(8,128)(2,1)S(1)} %get-tuple-element.157.refs_6_) | copy-start | bytes 8650756
  291.6 11.7 %slice-start.8 = ((s8[5767168]{0:T(1024)(128)(4,1)}), s8[4194304]{0:T(1024)(128)(4,1)S(1)}, s32[]{:S(2)}) async-start(s8[5767168]{0:T(1024)(128)(4,1)} %bitcast.94), calls=%async_computation.21 | async-start | bytes 8388608
  294.3 9.0 %slice-start.9 = ((s8[5767168]{0:T(1024)(128)(4,1)}), s8[1572864]{0:T(1024)(128)(4,1)S(1)}, s32[]{:S(2)}) async-start(s8[5767168]{0:T(1024)(128)(4,1)} %bitcast.94), calls=%async_computation.22 | async-start | bytes 3145728
  337.7 157.8 %reduce-scatter.8.cloned.1.call-start = ((), (), s32[]{:S(2)}) async-start(), calls=%async_computation.9 | async-start | bytes 5242880 | tf_op jit(solution)/shard_map/reduce_scatter | solution.py:1227
  338.1 12.0 %copy-start.21 = (bf16[1024,2048]{1,0:T(8,128)(2,1)S(1)}, bf16[1024,2048]{1,0:T(8,128)(2,1)}, u32[]{:S(2)}) copy-start(bf16[1024,2048]{1,0:T(8,128)(2,1)} %all-gather.8.cloned.1.call-done.refs_1_) | copy-start | bytes 12582916
  338.1 26.3 %slice-start.6 = ((s8[5767168]{0:T(1024)(128)(4,1)}), s8[4194304]{0:T(1024)(128)(4,1)S(1)}, s32[]{:S(2)}) async-start(s8[5767168]{0:T(1024)(128)(4,1)} %bitcast.92), calls=%async_computation.19 | async-start | bytes 8388608
  350.1 14.3 %slice-start.7 = ((s8[5767168]{0:T(1024)(128)(4,1)}), s8[1572864]{0:T(1024)(128)(4,1)S(1)}, s32[]{:S(2)}) async-start(s8[5767168]{0:T(1024)(128)(4,1)} %bitcast.92), calls=%async_computation.20 | async-start | bytes 3145728
  364.5 9.0 %copy-start.26 = (bf16[1024,1408]{1,0:T(8,128)(2,1)}, bf16[1024,1408]{1,0:T(8,128)(2,1)S(1)}, u32[]{:S(2)}) copy-start(bf16[1024,1408]{1,0:T(8,128)(2,1)S(1)} %get-tuple-element.153.refs_5_) | copy-start | bytes 8650756
  364.5 9.0 %copy-start.27 = (bf16[1024,1408]{1,0:T(8,128)(2,1)}, bf16[1024,1408]{1,0:T(8,128)(2,1)S(1)}, u32[]{:S(2)}) copy-start(bf16[1024,1408]{1,0:T(8,128)(2,1)S(1)} %get-tuple-element.154.refs_7_) | copy-start | bytes 8650756
  385.7 424.7 %reduce-scatter.10.cloned.1.call-start = ((), (), s32[]{:S(2)}) async-start(), calls=%async_computation.10 | async-start | bytes 2621440 | tf_op jit(solution)/shard_map/reduce_scatter | solution.py:1227
  386.0 98.6 %copy-start.25 = (bf16[1024,1408]{1,0:T(8,128)(2,1)S(1)}, bf16[1024,1408]{1,0:T(8,128)(2,1)}, u32[]{:S(2)}) copy-start(bf16[1024,1408]{1,0:T(8,128)(2,1)} %get-tuple-element.152.refs_9_) | copy-start | bytes 8650756
  484.6 10.9 %copy-start.33 = (f32[2048]{0:T(1024)S(1)}, f32[2048]{0:T(1024)}, u32[]{:S(2)}) copy-start(f32[2048]{0:T(1024)} %param.25) | copy-start | bytes 24580
  484.6 10.9 %copy-start.37 = (f32[512]{0:T(512)S(1)}, f32[512]{0:T(512)}, u32[]{:S(2)}) copy-start(f32[512]{0:T(512)} %copy-done.36) | copy-start | bytes 6148
  495.4 4.4 copy-start.12
  495.4 4.4 copy-start.15
  495.4 4.4 copy-start.40
  495.5 314.9 %reduce-scatter.12.cloned.1.call-start = ((), (), s32[]{:S(2)}) async-start(), calls=%async_computation.11 | async-start | bytes 2621440 | tf_op jit(solution)/shard_map/reduce_scatter | solution.py:1227
  495.5 4.9 copy-start.7
  495.5 5.2 copy-start.16
  503.9 15.3 %copy-start.3 = (bf16[16,128,128]{2,1,0:T(8,128)(2,1)S(1)}, bf16[16,128,128]{2,1,0:T(8,128)(2,1)}, u32[]{:S(2)}) copy-start(bf16[16,128,128]{2,1,0:T(8,128)(2,1)} %copy-done.2) | copy-start | bytes 1572868
  519.2 1.2 copy-start.5
  520.5 36.9 %copy-start.43 = (f32[1,128]{1,0:T(1,128)S(1)}, f32[1,128]{1,0:T(1,128)}, u32[]{:S(2)}) copy-start(f32[1,128]{1,0:T(1,128)} %get-tuple-element.85) | copy-start | bytes 1540
  555.1 1.0 copy-start.4
  556.1 254.3 %reduce-scatter.14.cloned.1.call-start = ((), (), s32[]{:S(2)}) async-start(), calls=%async_computation.12 | async-start | bytes 5242880 | tf_op jit(solution)/shard_map/reduce_scatter | solution.py:1227
  558.2 220.5 %copy-start.35 = (f32[2048]{0:T(1024)S(1)}, f32[2048]{0:T(1024)}, u32[]{:S(2)}) copy-start(f32[2048]{0:T(1024)} %param.17) | copy-start | bytes 24580
  558.2 220.5 %copy-start.39 = (f32[512]{0:T(512)S(1)}, f32[512]{0:T(512)}, u32[]{:S(2)}) copy-start(f32[512]{0:T(512)} %copy-done.38) | copy-start | bytes 6148
  785.0 28.4 %copy-start.10 = (bf16[512,2048]{1,0:T(8,128)(2,1)S(1)}, bf16[512,2048]{1,0:T(8,128)(2,1)}, u32[]{:S(2)}) copy-start(bf16[512,2048]{1,0:T(8,128)(2,1)} %param.15) | copy-start | bytes 6291460
  785.0 28.4 %copy-start.41 = (f32[512]{0:T(512)S(1)}, f32[512]{0:T(512)}, u32[]{:S(2)}) copy-start(f32[512]{0:T(512)} %get-tuple-element.170) | copy-start | bytes 6148
  810.4 3.2 copy-start.8
  813.6 8.7 %copy-start.30 = (f32[256,1408]{1,0:T(8,128)S(1)}, f32[256,1408]{1,0:T(8,128)}, u32[]{:S(2)}) copy-start(f32[256,1408]{1,0:T(8,128)} %get-tuple-element.204) | copy-start | bytes 4325380
  813.6 9.8 %copy-start.29 = (f32[256,1408]{1,0:T(8,128)S(1)}, f32[256,1408]{1,0:T(8,128)}, u32[]{:S(2)}) copy-start(f32[256,1408]{1,0:T(8,128)} %get-tuple-element.205) | copy-start | bytes 4325380
  822.3 2.2 copy-start.28
  (1 other events, 0.6 us)
Sparse Core Ops, SparseCore 0:
  9.6 161.4 all-gather.3
  173.2 82.8 all-gather.5
  258.3 79.2 all-gather.7
  339.8 75.2 reduce-scatter.5
  417.4 77.2 reduce-scatter.7
  496.8 55.4 reduce-scatter.9
  556.2 43.5 reduce-scatter.11
  602.1 115.8 reduce-scatter.13

commit v9 on v8

--- a/solution.py
+++ b/solution.py
@@ -547,26 +547,22 @@
     dp, z = lax.axis_index("dp"), lax.axis_index("narrow")
     core, x, y, sib, flip_x, flip_y = bits(dp)
     depth = lax.axis_size("narrow")
-    rows = small_ref.shape[0] // 8
-    share = rows // depth
+    cols = small_ref.shape[1] // 8
     peers = [(z + step) % depth for step in range(1, depth)]
     meet((sib, flip_x, flip_y), peers)
 
-    def stripe_rows(stripe, which):
-        return pl.ds(pl.multiple_of((stripe * 2 + which) * rows, rows), rows)
-
-    def share_rows(at):
-        return pl.ds(pl.multiple_of(at * share, share), share)
+    def stripe_lanes(stripe, which):
+        return pl.ds(pl.multiple_of((stripe * 2 + which) * cols, cols), cols)
 
     first = [
-        remote(small_ref.at[stripe_rows(k, 1 - core)], landed.at[k], send1.at[k], recv1.at[k], {"dp": sib})
+        remote(small_ref.at[:, stripe_lanes(k, 1 - core)], landed.at[k], send1.at[k], recv1.at[k], {"dp": sib})
         for k in range(4)
     ]
     for copy in first:
         copy.start()
     for k in range(4):
         first[k].wait()
-        total[k] = small_ref[stripe_rows(k, core), :] + landed[k]
+        total[k] = small_ref[:, stripe_lanes(k, core)] + landed[k]
     second = [
         remote(total.at[2 * j + 1 - x], got2.at[j], send2.at[j], recv2.at[j], {"dp": flip_x}) for j in range(2)
     ]
@@ -581,12 +577,11 @@
     mine = 2 * y + x
     total[mine] = total[mine] + got2[y] + got3[...]
     last = [
-        remote(total.at[mine, share_rows(to)], gotz.at[k], sendz.at[k], recvz.at[k], {"narrow": to})
-        for k, to in enumerate(peers)
+        remote(total.at[mine], gotz.at[k], sendz.at[k], recvz.at[k], {"narrow": to}) for k, to in enumerate(peers)
     ]
     for copy in last:
         copy.start()
-    value = total[mine, share_rows(z), :]
+    value = total[mine]
     for k, copy in enumerate(last):
         copy.wait()
         value = value + gotz[k]
@@ -594,22 +589,21 @@
 
 
 def reduce_small(small):
-    height, lanes = small.shape
+    rows, width = small.shape
     depth = lax.axis_size("narrow")
-    rows = height // 8
-    share = rows // depth
+    cols = width // 8
     dma = pltpu.SemaphoreType.DMA
     return pl.pallas_call(
         small_kernel,
         in_specs=[pl.BlockSpec(memory_space=pltpu.VMEM)],
         out_specs=pl.BlockSpec(memory_space=pltpu.VMEM),
-        out_shape=jax.ShapeDtypeStruct((share, lanes), F32),
+        out_shape=jax.ShapeDtypeStruct((rows, cols), F32),
         scratch_shapes=[
-            pltpu.VMEM((4, rows, lanes), F32),
-            pltpu.VMEM((4, rows, lanes), F32),
-            pltpu.VMEM((2, rows, lanes), F32),
-            pltpu.VMEM((rows, lanes), F32),
-            pltpu.VMEM((depth - 1, share, lanes), F32),
+            pltpu.VMEM((4, rows, cols), F32),
+            pltpu.VMEM((4, rows, cols), F32),
+            pltpu.VMEM((2, rows, cols), F32),
+            pltpu.VMEM((rows, cols), F32),
+            pltpu.VMEM((depth - 1, rows, cols), F32),
             dma((4,)), dma((4,)), dma((2,)), dma((2,)), dma(()), dma(()), dma((depth - 1,)), dma((depth - 1,)),
         ],
         compiler_params=pltpu.CompilerParams(
@@ -1307,7 +1301,7 @@
         pairs = [(normed, part) for part in d_proj] + [(d_branch, attn_mixed)]
         grads = jnp.stack([scatter_all(dot_tn(a, c).astype(BF16), 0).astype(F32) for a, c in pairs])
     d_beta_low = d_beta.astype(BF16)
-    beta_term = jnp.einsum("rd,rh->dh", normed, d_beta_low, preferred_element_type=F32)
+    beta_term = jnp.einsum("rh,rd->hd", d_beta_low, normed, preferred_element_type=F32)
     d_normed = d_normed + jnp.einsum("rh,dh->rd", d_beta_low, w_beta, preferred_element_type=F32)
     d_input_norm, attn_gain_term = norm_back(inputs, attn_gain, d_normed, 1e-06)
     grad_tokens = (d_hidden + d_input_norm).astype(BF16)
@@ -1315,29 +1309,32 @@
     heads = w_beta.shape[1]
     taps = 3 * CONV
     gain_share = BLOCK // devices
-    gain_column = jnp.pad(
-        out_gain_term.reshape(devices, gain_share), ((0, 0), (0, model_width // devices - gain_share))
-    ).reshape(model_width, 1)
+    per_device = model_width // devices
+    gain_row_term = jnp.pad(
+        out_gain_term.reshape(devices, gain_share), ((0, 0), (0, per_device - gain_share))
+    ).reshape(1, model_width)
     small = jnp.concatenate(
         [
             beta_term,
-            conv_term.reshape(taps, model_width).T,
-            attn_gain_term[:, None],
-            mlp_gain_term[:, None],
-            gain_column,
-        ],
-        axis=1,
+            conv_term.reshape(taps, model_width),
+            attn_gain_term[None, :],
+            mlp_gain_term[None, :],
+            gain_row_term,
+            jnp.zeros((-(heads + taps + 3) % 8, model_width), F32),
+        ],
+        axis=0,
     )
-    small = jnp.pad(small, ((0, 0), (0, BLOCK - small.shape[1])))
     if lax.axis_size("dp") == 8:
-        small = reduce_small(small)
+        small = lax.dynamic_slice_in_dim(
+            reduce_small(small), lax.axis_index("narrow") * per_device, per_device, axis=1
+        )
     else:
-        small = lax.psum_scatter(small, ("dp", "narrow"), scatter_dimension=0, tiled=True)
-    grad_beta = small[:, :heads]
-    grad_conv = small[:, heads : heads + taps].T.reshape(3, CONV, -1)
-    grad_attn_gain = small[:, heads + taps]
-    grad_mlp_gain = small[:, heads + taps + 1]
-    grad_out_gain = small[:gain_share, heads + taps + 2]
+        small = lax.psum_scatter(small, ("dp", "narrow"), scatter_dimension=1, tiled=True)
+    grad_beta = small[:heads].T
+    grad_conv = small[heads : heads + taps].reshape(3, CONV, per_device)
+    grad_attn_gain = small[heads + taps]
+    grad_mlp_gain = small[heads + taps + 1]
+    grad_out_gain = small[heads + taps + 2, :gain_share]
     ffn_parts, grads = lax.optimization_barrier((ffn_parts, grads))
     block_out = (hidden + jnp.concatenate(ffn_parts, axis=0).astype(F32)).astype(BF16)
     grad_query, grad_key, grad_value = grads[0], grads[1], grads[2]

time: 838 us -> 833 us (level)
  transfers between devices with their start and end apart: 9 -> 9, of which waited for: 4 -> 4; matrix products, arithmetic and copies ran while one was open for 24% -> 25% of each run, Pallas kernels for 57% -> 56%
where the time goes in v9:
time: 833 us; the launch traced here: 827 us
  Pallas kernels  465 us (56%)
  matrix products  173 us (21%)
  waiting for transfers between devices  113 us (14%)
  local copies, waits for them, and re-layouts  32.5 us (4%)
  other arithmetic  21.3 us (3%)
  between operations  15.2 us (2%)
    pallas_call x1, Pallas kernels, fused_backward(): pl.pallas_call(fused_kernel, grid=(units + 1,), in_specs=[whole(since.sha...  218 us
    all_gather x3, waiting for transfers between devices, gather(): return lax.all_gather(rows, 'narrow', axis=0, tiled=True)  111 us
    dot_general x11, matrix products, matmul(): return jnp.dot(left, right, preferred_element_type=F32)  102 us
    pallas_call x1, Pallas kernels, ffn_grads(): pl.pallas_call(ffn_grads_kernel, in_specs=[pl.BlockSpec(memory_space=pl.A...  98.6 us
    pallas_call x2, Pallas kernels, carry_chain(): pl.pallas_call(functools.partial(chain_kernel, axis, forward), in_specs=[...  61.3 us
    pallas_call x1, Pallas kernels, mixer_forward(): pl.pallas_call(forward_kernel, grid=(heads // HEADS_STEP,), in_specs=[who...  50.7 us
    dot_general x4, matrix products, dot_nt(): return jnp.einsum('re,de->rd', left, right, preferred_element_type=F32)  40.7 us
    dot_general x2, matrix products, local(): d_act = jnp.einsum('rd,fd->rf', cot[at], w_down, preferred_element_type=F32)  21.4 us
  transfers between devices with their start and end apart: 9, of which 4 were waited for; matrix products, arithmetic and copies ran while one was open for 25% of the time, Pallas kernels for 56%

profile of v9, /device:TPU:0, one launch (start us, length us, event | category | flops | bytes accessed | tf_op | source)
XLA Modules:
  0.0 826.8 jit_solution(16162181666331463278)
XLA Ops:
  7.3 0.7 all-gather.4.cloned.1.call-update
  8.0 2.1 fusion.9
  10.1 0.6 multiply_multiply_fusion
  10.7 0.6 copy-done.38
  11.8 9.2 %convolution_convert_fusion.4.query_ref.refs_2_ = bf16[512,2048]{1,0:T(8,128)(2,1)S(1)} fusion(bf16[512,2048]{1,0:T(8,128)(2,1)S(1)} %fusion.11.refs_18_, bf16[2048,2048]{1,0:T(8,128)(2,1)} %refs_14_.1), kind=kOutput, calls=%fused_computation.44 | convolution fusion | flops 4296015872 | bytes 12582912 | tf_op jit(solution)/shard_map/dot_general | solution.py:1157
  21.1 4.8 convolution_convert_fusion.2.value_ref.refs_4_
  26.0 4.8 convolution_convert_fusion.3.key_ref.refs_3_
  30.8 1.3 copy-done.19
  32.1 5.5 collective-permute-start
  37.9 3.0 fusion.28.beta_ref.refs_1_
  40.9 1.0 collective-permute-done.halo_ref.refs_5_
  41.9 0.8 broadcast_in_dim.21.since_ref.refs_0_
  42.8 50.7 %mixer_forward.1 = (bf16[512,2048]{1,0:T(8,128)(2,1)}, bf16[512,2048]{1,0:T(8,128)(2,1)}, bf16[512,2048]{1,0:T(8,128)(2,1)}, bf16[512,2048]{1,0:T(8,128)(2,1)}, ...) custom-call(s32[512,128]{1,0:T(8,128)} %broadcast_in_dim.21.since_ref.refs_0_, ...), custom_call_target="tpu_custom_call" | custom-call | tf_op jit(solution)/shard_map/mixer_forward/pallas_call | solution.py:180
  93.5 1.3 slice.97.map_ref
  94.8 1.5 slice.65.add_ref
  96.4 26.7 %carry_forward.1.entry_ref.refs_11_ = f32[16,128,128]{2,1,0:T(8,128)S(1)} custom-call(bf16[16,128,128]{2,1,0:T(8,128)(2,1)S(1)} %slice.97.map_ref, f32[16,128,128]{2,1,0:T(8,128)S(1)} %slice.65.add_ref), custom_call_target="tpu_custom_call" | custom-call | tf_op jit(solution)/shard_map/carry_forward/pallas_call | solution.py:499
  123.1 1.0 copy-done.1
  124.1 7.6 mixer_join.1.refs_17_
  131.7 7.8 multiply_reduce_fusion
  139.4 0.6 multiply_multiply_fusion.1
  140.1 1.4 copy-done.6
  141.9 29.2 %all-gather.4.cloned.1.call-done = bf16[2048,2048]{1,0:T(8,128)(2,1)} async-done(((bf16[512,2048]{1,0:T(8,128)(2,1)}), bf16[2048,2048]{1,0:T(8,128)(2,1)}) %all-gather.4.cloned.1.call-update) | async-done | bytes 8388624 | tf_op jit(solution)/shard_map/all_gather | solution.py:1218
  171.1 1.4 fusion.27
  172.8 4.0 fusion.25
  176.8 12.9 %fusion.29 = f32[1024,1408]{1,0:T(8,128)} fusion(bf16[1024,2048]{1,0:T(8,128)(2,1)S(1)} %bitcast.77, bf16[1408,2048]{1,0:T(8,128)(2,1)} %param.28), kind=kOutput, calls=%fused_computation.77 | convolution fusion | flops 5905580032 | bytes 15728640 | tf_op jit(solution)/shard_map/rd,fd->rf/dot_general | solution.py:1252
  189.8 8.5 %fusion.32 = f32[1024,1408]{1,0:T(8,128)} fusion(bf16[1024,2048]{1,0:T(8,128)(2,1)S(1)} %bitcast.75, bf16[1408,2048]{1,0:T(8,128)(2,1)S(1)} %bitcast.99), kind=kOutput, calls=%fused_computation.80 | convolution fusion | flops 5905580032 | bytes 15728640 | tf_op jit(solution)/shard_map/rd,fd->rf/dot_general | solution.py:1252
  198.5 57.6 %all-gather.6.cloned.1.call-done.refs_0_ = bf16[1024,2048]{1,0:T(8,128)(2,1)} async-done(((bf16[256,2048]{1,0:T(8,128)(2,1)}), bf16[1024,2048]{1,0:T(8,128)(2,1)}) %all-gather.6.cloned.1.call-update) | async-done | bytes 4194320 | tf_op jit(solution)/shard_map/all_gather | solution.py:1218
  256.2 11.8 %fusion.30 = f32[1024,1408]{1,0:T(8,128)} fusion(bf16[1024,2048]{1,0:T(8,128)(2,1)} %all-gather.6.cloned.1.call-done.refs_0_, bf16[2048,1408]{1,0:T(8,128)(2,1)} %param.26), kind=kOutput, calls=%fused_computation.78 | convolution fusion | flops 5905580032 | bytes 15728640 | tf_op jit(solution)/shard_map/dot_general | solution.py:1157
  268.0 12.7 %multiply_convert_fusion.3 = (bf16[1024,1408]{1,0:T(8,128)(2,1)S(1)}, bf16[1024,1408]{1,0:T(8,128)(2,1)S(1)}, bf16[1024,1408]{1,0:T(8,128)(2,1)S(1)}) fusion(f32[1024,1408]{1,0:T(8,128)} %fusion.30, f32[1024,1408]{1,0:T(8,128)} %fusion.29, bf16[1024,2048]{1,0:T(8,128)(2,1)S(1)} %copy-done.20, bf16[2048,1408]{1,0:T(8,128)(2,1)} %param.27), kind=kOutput, calls=%fused_computation.13 | convolution fusion | flops 5927206912 | bytes 30146560 | tf_op jit(solution)/shard_map/dot_general | solution.py:1157
  280.7 10.9 %convolution_convert_fusion.1 = bf16[1024,2048]{1,0:T(8,128)(2,1)S(1)} fusion(bf16[1024,1408]{1,0:T(8,128)(2,1)S(1)} %get-tuple-element.97.refs_8_, bf16[1408,2048]{1,0:T(8,128)(2,1)} %param.28), kind=kOutput, calls=%fused_computation.41 | convolution fusion | flops 5907677184 | bytes 12845056 | tf_op jit(solution)/shard_map/dot_general | solution.py:1157
  291.6 2.7 fusion.26
  294.3 8.9 %fusion.31 = f32[1024,2048]{1,0:T(8,128)} fusion(bf16[1024,1408]{1,0:T(8,128)(2,1)S(1)} %get-tuple-element.98.refs_4_, bf16[2048,1408]{1,0:T(8,128)(2,1)S(1)} %bitcast.93), kind=kOutput, calls=%fused_computation.79 | convolution fusion | flops 5905580032 | bytes 17039360 | tf_op jit(solution)/shard_map/re,de->rd/dot_general | solution.py:1165
  303.2 10.6 %add_convert_fusion.1 = bf16[1024,2048]{1,0:T(8,128)(2,1)} fusion(f32[1024,2048]{1,0:T(8,128)} %fusion.31, bf16[1024,1408]{1,0:T(8,128)(2,1)S(1)} %get-tuple-element.99.refs_6_, bf16[2048,1408]{1,0:T(8,128)(2,1)S(1)} %bitcast.97), kind=kOutput, calls=%fused_computation.7 | convolution fusion | flops 5909774336 | bytes 21233664 | tf_op jit(solution)/shard_map/re,de->rd/dot_general | solution.py:1165
  313.8 23.8 %all-gather.8.cloned.1.call-done.refs_1_ = bf16[1024,2048]{1,0:T(8,128)(2,1)} async-done(((bf16[256,2048]{1,0:T(8,128)(2,1)}), bf16[1024,2048]{1,0:T(8,128)(2,1)}) %all-gather.8.cloned.1.call-update) | async-done | bytes 4194320 | tf_op jit(solution)/shard_map/all_gather | solution.py:1218
  338.1 12.0 %fusion.33 = f32[1024,1408]{1,0:T(8,128)} fusion(bf16[1024,2048]{1,0:T(8,128)(2,1)} %all-gather.8.cloned.1.call-done.refs_1_, bf16[2048,1408]{1,0:T(8,128)(2,1)} %param.26), kind=kOutput, calls=%fused_computation.81 | convolution fusion | flops 5905580032 | bytes 15728640 | tf_op jit(solution)/shard_map/dot_general | solution.py:1157
  350.2 14.3 %multiply_convert_fusion = (bf16[1024,1408]{1,0:T(8,128)(2,1)}, bf16[1024,1408]{1,0:T(8,128)(2,1)S(1)}, bf16[1024,1408]{1,0:T(8,128)(2,1)S(1)}) fusion(f32[1024,1408]{1,0:T(8,128)} %fusion.33, f32[1024,1408]{1,0:T(8,128)} %fusion.32, bf16[1024,2048]{1,0:T(8,128)(2,1)S(1)} %copy-done.21, bf16[2048,1408]{1,0:T(8,128)(2,1)} %param.27), kind=kOutput, calls=%fused_computation.8 | convolution fusion | flops 5927206912 | bytes 30146560 | tf_op jit(solution)/shard_map/dot_general | solution.py:1157
  364.5 8.9 %fusion.34 = f32[1024,2048]{1,0:T(8,128)} fusion(bf16[1024,1408]{1,0:T(8,128)(2,1)S(1)} %get-tuple-element.95.refs_5_, bf16[2048,1408]{1,0:T(8,128)(2,1)S(1)} %bitcast.95), kind=kOutput, calls=%fused_computation.82 | convolution fusion | flops 5905580032 | bytes 17039360 | tf_op jit(solution)/shard_map/re,de->rd/dot_general | solution.py:1165
  373.5 12.2 %add_convert_fusion = bf16[1024,2048]{1,0:T(8,128)(2,1)} fusion(f32[1024,2048]{1,0:T(8,128)} %fusion.34, bf16[1024,1408]{1,0:T(8,128)(2,1)S(1)} %get-tuple-element.96.refs_7_, bf16[2048,1408]{1,0:T(8,128)(2,1)} %param.27), kind=kOutput, calls=%fused_computation.6 | convolution fusion | flops 5909774336 | bytes 21233664 | tf_op jit(solution)/shard_map/re,de->rd/dot_general | solution.py:1165
  386.0 98.6 %ffn_grads.1 = (f32[256,1408]{1,0:T(8,128)}, f32[256,1408]{1,0:T(8,128)}, f32[1408,256]{1,0:T(8,128)}) custom-call(bf16[1024,2048]{1,0:T(8,128)(2,1)} %all-gather.6.cloned.1.call-done.refs_0_, bf16[1024,2048]{1,0:T(8,128)(2,1)} %all-gather.8.cloned.1.call-done.refs_1_, bf16[1024,2048]{1,0:T(8,128)(2,1)} %bitcast.78, bf16[1024,2048]{1,0:T(8,128)(2,1)} %bitcast.76, ...), custom_call_target="tpu_custom_call" | custom-call | tf_op jit(solution)/shard_map/ffn_grads/pallas_call | solution.py:1123
  484.6 10.8 %convolution_convert_fusion = bf16[1024,2048]{1,0:T(8,128)(2,1)} fusion(bf16[1024,1408]{1,0:T(8,128)(2,1)S(1)} %copy-done.25, bf16[1408,2048]{1,0:T(8,128)(2,1)} %param.28), kind=kOutput, calls=%fused_computation.40 | convolution fusion | flops 5907677184 | bytes 12845056 | tf_op jit(solution)/shard_map/dot_general | solution.py:1157
  495.6 4.2 fusion.8
  499.9 0.6 copy-done.7
  500.7 3.2 fusion.24.branch_ref.refs_19_
  503.9 15.3 %mixer_core_back.1 = (bf16[512,2048]{1,0:T(8,128)(2,1)}, f32[16,128,128]{2,1,0:T(8,128)}, f32[1,128]{1,0:T(1,128)}) custom-call(bf16[512,2048]{1,0:T(8,128)(2,1)} %get-tuple-element.52.out_add_ref, bf16[512,2048]{1,0:T(8,128)(2,1)} %get-tuple-element.53.out_map_ref, f32[16,128,128]{2,1,0:T(8,128)} %copy-done.1, f32[1,128]{1,0:T(1,128)} %bitcast.90, ...), custom_call_target="tpu_custom_call" | custom-call | tf_op jit(solution)/shard_map/mixer_core_back/pallas_call | solution.py:253
  519.3 1.2 copy-done.5
  520.5 34.6 %carry_backward.1.refs_12_ = f32[16,128,128]{2,1,0:T(8,128)S(1)} custom-call(bf16[16,128,128]{2,1,0:T(8,128)(2,1)S(1)} %copy-done.3, f32[16,128,128]{2,1,0:T(8,128)S(1)} %copy-done.5), custom_call_target="tpu_custom_call" | custom-call | tf_op jit(solution)/shard_map/carry_backward/pallas_call | solution.py:499
  555.1 1.0 copy-done.4
  556.1 0.7 reduce-scatter.14.cloned.1.call-update
  557.4 0.7 reduce.3
  558.2 217.5 %fused_backward.1 = (f32[4,64,2048]{2,1,0:T(8,128)}, f32[512,2048]{1,0:T(8,128)}, f32[3,4,2048]{2,1,0:T(4,128)}, f32[512,16]{1,0:T(8,128)}) custom-call(s32[512,128]{1,0:T(8,128)} %broadcast_in_dim.21.since_ref.refs_0_, f32[512,16]{1,0:T(8,128)} %fusion.28.beta_ref.refs_1_, bf16[512,2048]{1,0:T(8,128)(2,1)} %copy-done.17, bf16[512,2048]{1,0:T(8,128)(2,1)} %copy-done.19, ...), custom_call_target="tpu_custom_call" | custom-call | tf_op jit(solution)/shard_map/fused_backward/pallas_call | solution.py:907
  775.8 1.6 reshape.129
  777.4 2.8 fusion.19
  780.1 6.3 fusion.18
  786.5 1.9 concatenate.11.small_ref
  788.4 13.5 %reduce_small.1 = f32[32,256]{1,0:T(8,128)S(1)} custom-call(f32[32,2048]{1,0:T(8,128)S(1)} %concatenate.11.small_ref), custom_call_target="tpu_custom_call" | custom-call | tf_op jit(solution)/shard_map/reduce_small/pallas_call | solution.py:596
  802.0 0.6 reshape.132
  802.6 0.6 dynamic-slice_bitcast_fusion.2
  803.2 0.6 dynamic-slice_bitcast_fusion.1
  803.8 0.7 dynamic-slice_bitcast_fusion
  804.5 3.0 slice_bitcast_fusion
  807.7 8.7 %fusion.15 = (bf16[512,2048]{1,0:T(8,128)(2,1)}, bf16[512,2048]{1,0:T(8,128)(2,1)}) fusion(bf16[512,2048]{1,0:T(8,128)(2,1)S(1)} %copy-done.10, f32[512]{0:T(512)S(1)} %broadcast_multiply_fusion, f32[512]{0:T(512)S(1)} %copy-done.41, f32[2048]{0:T(1024)S(1)} %copy-done.35, f32[512]{0:T(512)S(1)} %copy-done.39, f32[512,2048]{1,0:T(8,128)} %get-tuple-element.82, ...), kind=kLoop, calls=%fused_computation.33 | loop fusion | flops 29360128 | bytes 25194496 | tf_op jit(solution)/shard_map/convert_element_type | solution.py:1307
  816.4 1.1 copy.47
  817.5 1.1 copy.48
  818.6 1.1 copy.49
  (147 shorter events, 4.1 us)
Async XLA Ops:
  7.2 30.7 %copy-start = (bf16[2048,16]{0,1:T(8,128)(2,1)S(1)}, bf16[2048,16]{0,1:T(8,128)(2,1)}, u32[]{:S(2)}) copy-start(bf16[2048,16]{0,1:T(8,128)(2,1)} %param.21) | copy-start | bytes 196612
  7.2 4.0 copy-start.9
  7.2 4.0 copy-start.34
  7.2 163.9 %all-gather.4.cloned.1.call-start = ((), (), s32[]{:S(2)}) async-start(), calls=%async_computation.5 | async-start | bytes 10485760 | tf_op jit(solution)/shard_map/all_gather | solution.py:1218
  8.0 248.2 %all-gather.6.cloned.1.call-start = ((), (), s32[]{:S(2)}) async-start(), calls=%async_computation.6 | async-start | bytes 5242880 | tf_op jit(solution)/shard_map/all_gather | solution.py:1218
  11.2 9.9 %slice-start.2 = ((s8[8388608]{0:T(1024)(128)(4,1)}), s8[4194304]{0:T(1024)(128)(4,1)S(1)}, s32[]{:S(2)}) async-start(s8[8388608]{0:T(1024)(128)(4,1)} %bitcast.81), calls=%async_computation.15 | async-start | bytes 8388608
  11.8 14.1 %copy-start.11 = (bf16[512,2048]{1,0:T(8,128)(2,1)}, bf16[512,2048]{1,0:T(8,128)(2,1)S(1)}, u32[]{:S(2)}) copy-start(bf16[512,2048]{1,0:T(8,128)(2,1)S(1)} %fusion.11.refs_18_) | copy-start | bytes 6291460
  11.8 9.3 %slice-start.3 = ((s8[8388608]{0:T(1024)(128)(4,1)}), s8[4194304]{0:T(1024)(128)(4,1)S(1)}, s32[]{:S(2)}) async-start(s8[8388608]{0:T(1024)(128)(4,1)} %bitcast.81), calls=%async_computation.16 | async-start | bytes 8388608
  11.8 14.1 %slice-start = ((s8[8388608]{0:T(1024)(128)(4,1)}), s8[4194304]{0:T(1024)(128)(4,1)S(1)}, s32[]{:S(2)}) async-start(s8[8388608]{0:T(1024)(128)(4,1)} %bitcast.79), calls=%async_computation.13 | async-start | bytes 8388608
  21.1 4.9 copy-start.17
  21.1 4.9 slice-start.1
  26.0 4.8 copy-start.18
  26.0 11.7 %copy-start.42 = (s32[1,4]{1,0:T(1,128)S(1)}, s32[1,4]{1,0:T(1,128)}, u32[]{:S(2)}) copy-start(s32[1,4]{1,0:T(1,128)} %param.16) | copy-start | bytes 52
  30.8 1.4 copy-start.19
  32.1 9.8 %collective-permute-start = (bf16[3,8,2048]{2,1,0:T(8,128)(2,1)S(1)}, bf16[3,8,2048]{2,1,0:T(8,128)(2,1)S(1)}, u32[]{:S(2)}, u32[]{:S(2)}) collective-permute-start(bf16[3,8,2048]{2,1,0:T(8,128)(2,1)S(1)} %pad_maximum_fusion.1), channel_id=1, source_target_pairs={{0,1},{1,2},{2,3},{4,5},{5,6},{6,7},{8,9},{9,10},{10,11},{12,13},{... | collective-permute-start | bytes 294920 | tf_op jit(solution)/shard_map/ppermute | solution.py:1153
  41.9 0.8 copy-start.31
  94.8 28.3 %copy-start.2 = (bf16[16,128,128]{2,1,0:T(8,128)(2,1)}, bf16[16,128,128]{2,1,0:T(8,128)(2,1)S(1)}, u32[]{:S(2)}) copy-start(bf16[16,128,128]{2,1,0:T(8,128)(2,1)S(1)} %slice.97.map_ref) | copy-start | bytes 1572868
  123.1 1.0 copy-start.1
  131.7 9.8 %copy-start.32 = (f32[2048]{0:T(1024)S(1)}, f32[2048]{0:T(1024)}, u32[]{:S(2)}) copy-start(f32[2048]{0:T(1024)} %param.25) | copy-start | bytes 24580
  139.4 2.0 copy-start.6
  140.1 1.4 copy-start.36
  172.6 165.1 %all-gather.8.cloned.1.call-start = ((), (), s32[]{:S(2)}) async-start(), calls=%async_computation.7 | async-start | bytes 5242880 | tf_op jit(solution)/shard_map/all_gather | solution.py:1218
  172.8 16.9 %slice-start.10 = ((s8[5767168]{0:T(1024)(128)(4,1)}), s8[4194304]{0:T(1024)(128)(4,1)S(1)}, s32[]{:S(2)}) async-start(s8[5767168]{0:T(1024)(128)(4,1)} %bitcast.98), calls=%async_computation.23 | async-start | bytes 8388608
  176.8 12.9 %copy-start.14 = (bf16[4,256,2048]{2,1,0:T(8,128)(2,1)}, bf16[4,256,2048]{2,1,0:T(8,128)(2,1)S(1)}, u32[]{:S(2)}) copy-start(bf16[4,256,2048]{2,1,0:T(8,128)(2,1)S(1)} %get-tuple-element.101) | copy-start | bytes 12582916
  176.8 12.9 %copy-start.13 = (bf16[4,256,2048]{2,1,0:T(8,128)(2,1)}, bf16[4,256,2048]{2,1,0:T(8,128)(2,1)S(1)}, u32[]{:S(2)}) copy-start(bf16[4,256,2048]{2,1,0:T(8,128)(2,1)S(1)} %get-tuple-element.100) | copy-start | bytes 12582916
  176.8 12.9 %slice-start.11 = ((s8[5767168]{0:T(1024)(128)(4,1)}), s8[1572864]{0:T(1024)(128)(4,1)S(1)}, s32[]{:S(2)}) async-start(s8[5767168]{0:T(1024)(128)(4,1)} %bitcast.98), calls=%async_computation.24 | async-start | bytes 3145728
  198.3 297.2 %reduce-scatter.6.cloned.1.call-start = ((), (), s32[]{:S(2)}) async-start(), calls=%async_computation.8 | async-start | bytes 5242880 | tf_op jit(solution)/shard_map/reduce_scatter | solution.py:1221
  256.2 11.8 %copy-start.20 = (bf16[1024,2048]{1,0:T(8,128)(2,1)S(1)}, bf16[1024,2048]{1,0:T(8,128)(2,1)}, u32[]{:S(2)}) copy-start(bf16[1024,2048]{1,0:T(8,128)(2,1)} %all-gather.6.cloned.1.call-done.refs_0_) | copy-start | bytes 12582916
  256.2 38.1 %slice-start.4 = ((s8[5767168]{0:T(1024)(128)(4,1)}), s8[4194304]{0:T(1024)(128)(4,1)S(1)}, s32[]{:S(2)}) async-start(s8[5767168]{0:T(1024)(128)(4,1)} %bitcast.92), calls=%async_computation.17 | async-start | bytes 8388608
  268.0 26.3 %slice-start.5 = ((s8[5767168]{0:T(1024)(128)(4,1)}), s8[1572864]{0:T(1024)(128)(4,1)S(1)}, s32[]{:S(2)}) async-start(s8[5767168]{0:T(1024)(128)(4,1)} %bitcast.92), calls=%async_computation.18 | async-start | bytes 3145728
  280.7 10.9 %copy-start.22 = (bf16[1024,1408]{1,0:T(8,128)(2,1)}, bf16[1024,1408]{1,0:T(8,128)(2,1)S(1)}, u32[]{:S(2)}) copy-start(bf16[1024,1408]{1,0:T(8,128)(2,1)S(1)} %get-tuple-element.97.refs_8_) | copy-start | bytes 8650756
  280.7 13.6 %copy-start.23 = (bf16[1024,1408]{1,0:T(8,128)(2,1)}, bf16[1024,1408]{1,0:T(8,128)(2,1)S(1)}, u32[]{:S(2)}) copy-start(bf16[1024,1408]{1,0:T(8,128)(2,1)S(1)} %get-tuple-element.98.refs_4_) | copy-start | bytes 8650756
  280.7 22.5 %copy-start.24 = (bf16[1024,1408]{1,0:T(8,128)(2,1)}, bf16[1024,1408]{1,0:T(8,128)(2,1)S(1)}, u32[]{:S(2)}) copy-start(bf16[1024,1408]{1,0:T(8,128)(2,1)S(1)} %get-tuple-element.99.refs_6_) | copy-start | bytes 8650756
  291.6 11.6 %slice-start.8 = ((s8[5767168]{0:T(1024)(128)(4,1)}), s8[4194304]{0:T(1024)(128)(4,1)S(1)}, s32[]{:S(2)}) async-start(s8[5767168]{0:T(1024)(128)(4,1)} %bitcast.96), calls=%async_computation.21 | async-start | bytes 8388608
  294.3 8.9 %slice-start.9 = ((s8[5767168]{0:T(1024)(128)(4,1)}), s8[1572864]{0:T(1024)(128)(4,1)S(1)}, s32[]{:S(2)}) async-start(s8[5767168]{0:T(1024)(128)(4,1)} %bitcast.96), calls=%async_computation.22 | async-start | bytes 3145728
  337.7 157.8 %reduce-scatter.8.cloned.1.call-start = ((), (), s32[]{:S(2)}) async-start(), calls=%async_computation.9 | async-start | bytes 5242880 | tf_op jit(solution)/shard_map/reduce_scatter | solution.py:1221
  338.1 12.0 %copy-start.21 = (bf16[1024,2048]{1,0:T(8,128)(2,1)S(1)}, bf16[1024,2048]{1,0:T(8,128)(2,1)}, u32[]{:S(2)}) copy-start(bf16[1024,2048]{1,0:T(8,128)(2,1)} %all-gather.8.cloned.1.call-done.refs_1_) | copy-start | bytes 12582916
  338.1 26.4 %slice-start.6 = ((s8[5767168]{0:T(1024)(128)(4,1)}), s8[4194304]{0:T(1024)(128)(4,1)S(1)}, s32[]{:S(2)}) async-start(s8[5767168]{0:T(1024)(128)(4,1)} %bitcast.94), calls=%async_computation.19 | async-start | bytes 8388608
  350.2 14.3 %slice-start.7 = ((s8[5767168]{0:T(1024)(128)(4,1)}), s8[1572864]{0:T(1024)(128)(4,1)S(1)}, s32[]{:S(2)}) async-start(s8[5767168]{0:T(1024)(128)(4,1)} %bitcast.94), calls=%async_computation.20 | async-start | bytes 3145728
  364.5 9.0 %copy-start.26 = (bf16[1024,1408]{1,0:T(8,128)(2,1)}, bf16[1024,1408]{1,0:T(8,128)(2,1)S(1)}, u32[]{:S(2)}) copy-start(bf16[1024,1408]{1,0:T(8,128)(2,1)S(1)} %get-tuple-element.95.refs_5_) | copy-start | bytes 8650756
  364.5 9.0 %copy-start.27 = (bf16[1024,1408]{1,0:T(8,128)(2,1)}, bf16[1024,1408]{1,0:T(8,128)(2,1)S(1)}, u32[]{:S(2)}) copy-start(bf16[1024,1408]{1,0:T(8,128)(2,1)S(1)} %get-tuple-element.96.refs_7_) | copy-start | bytes 8650756
  385.7 418.7 %reduce-scatter.10.cloned.1.call-start = ((), (), s32[]{:S(2)}) async-start(), calls=%async_computation.10 | async-start | bytes 2621440 | tf_op jit(solution)/shard_map/reduce_scatter | solution.py:1221
  385.9 98.6 %copy-start.25 = (bf16[1024,1408]{1,0:T(8,128)(2,1)S(1)}, bf16[1024,1408]{1,0:T(8,128)(2,1)}, u32[]{:S(2)}) copy-start(bf16[1024,1408]{1,0:T(8,128)(2,1)} %get-tuple-element.94.refs_9_) | copy-start | bytes 8650756
  484.6 10.9 %copy-start.33 = (f32[2048]{0:T(1024)S(1)}, f32[2048]{0:T(1024)}, u32[]{:S(2)}) copy-start(f32[2048]{0:T(1024)} %param.25) | copy-start | bytes 24580
  484.6 10.9 %copy-start.37 = (f32[512]{0:T(512)S(1)}, f32[512]{0:T(512)}, u32[]{:S(2)}) copy-start(f32[512]{0:T(512)} %copy-done.36) | copy-start | bytes 6148
  495.4 4.4 copy-start.12
  495.4 4.4 copy-start.15
  495.4 4.4 copy-start.40
  495.5 309.0 %reduce-scatter.12.cloned.1.call-start = ((), (), s32[]{:S(2)}) async-start(), calls=%async_computation.11 | async-start | bytes 2621440 | tf_op jit(solution)/shard_map/reduce_scatter | solution.py:1221
  495.6 4.9 copy-start.7
  495.6 5.2 copy-start.16
  503.9 15.3 %copy-start.3 = (bf16[16,128,128]{2,1,0:T(8,128)(2,1)S(1)}, bf16[16,128,128]{2,1,0:T(8,128)(2,1)}, u32[]{:S(2)}) copy-start(bf16[16,128,128]{2,1,0:T(8,128)(2,1)} %copy-done.2) | copy-start | bytes 1572868
  519.2 1.2 copy-start.5
  520.5 36.9 %copy-start.43 = (f32[1,128]{1,0:T(1,128)S(1)}, f32[1,128]{1,0:T(1,128)}, u32[]{:S(2)}) copy-start(f32[1,128]{1,0:T(1,128)} %get-tuple-element.85) | copy-start | bytes 1540
  555.1 1.0 copy-start.4
  556.1 248.4 %reduce-scatter.14.cloned.1.call-start = ((), (), s32[]{:S(2)}) async-start(), calls=%async_computation.12 | async-start | bytes 5242880 | tf_op jit(solution)/shard_map/reduce_scatter | solution.py:1221
  558.2 221.9 %copy-start.35 = (f32[2048]{0:T(1024)S(1)}, f32[2048]{0:T(1024)}, u32[]{:S(2)}) copy-start(f32[2048]{0:T(1024)} %param.17) | copy-start | bytes 24580
  558.2 221.9 %copy-start.39 = (f32[512]{0:T(512)S(1)}, f32[512]{0:T(512)}, u32[]{:S(2)}) copy-start(f32[512]{0:T(512)} %copy-done.38) | copy-start | bytes 6148
  780.1 27.4 %copy-start.10 = (bf16[512,2048]{1,0:T(8,128)(2,1)S(1)}, bf16[512,2048]{1,0:T(8,128)(2,1)}, u32[]{:S(2)}) copy-start(bf16[512,2048]{1,0:T(8,128)(2,1)} %param.15) | copy-start | bytes 6291460
  786.5 21.0 %copy-start.41 = (f32[512]{0:T(512)S(1)}, f32[512]{0:T(512)}, u32[]{:S(2)}) copy-start(f32[512]{0:T(512)} %get-tuple-element.114) | copy-start | bytes 6148
  804.5 3.2 copy-start.8
  807.7 8.7 %copy-start.30 = (f32[256,1408]{1,0:T(8,128)S(1)}, f32[256,1408]{1,0:T(8,128)}, u32[]{:S(2)}) copy-start(f32[256,1408]{1,0:T(8,128)} %get-tuple-element.148) | copy-start | bytes 4325380
  807.7 9.8 %copy-start.29 = (f32[256,1408]{1,0:T(8,128)S(1)}, f32[256,1408]{1,0:T(8,128)}, u32[]{:S(2)}) copy-start(f32[256,1408]{1,0:T(8,128)} %get-tuple-element.149) | copy-start | bytes 4325380
  816.4 2.2 copy-start.28
  (1 other events, 0.6 us)
Sparse Core Ops, SparseCore 0:
  9.6 161.4 all-gather.3
  173.2 82.8 all-gather.5
  258.3 79.2 all-gather.7
  339.8 75.2 reduce-scatter.5
  417.4 77.2 reduce-scatter.7
  496.8 55.4 reduce-scatter.9
  556.2 43.5 reduce-scatter.11
  602.1 116.3 reduce-scatter.13

commit v10 on v9

--- a/solution.py
+++ b/solution.py
@@ -614,7 +614,7 @@
 
 
 RING = 3
-HELD = 5
+HELD = 6
 LAG = 2
 
 
@@ -848,9 +848,9 @@
         def _():
             third(at - LAG - 1)
 
-        @pl.when(at >= LAG + 2)
+        @pl.when(at >= LAG + 3)
         def _():
-            fourth(at - LAG - 2)
+            fourth(at - LAG - 3)
 
     stages(step)
 
@@ -863,7 +863,7 @@
             stages(at)
             return 0
 
-        lax.fori_loop(units + 1, units + LAG + 2, one, 0)
+        lax.fori_loop(units + 1, units + LAG + 3, one, 0)
         save.wait()
         grad_copy(units - 2).wait()
         grad_copy(units - 1).wait()
@@ -890,9 +890,10 @@
         return jnp.maximum(step - 1, 0)
 
     def whole(shape):
-        return pl.BlockSpec(shape, lambda h: (0,) * len(shape))
+        return pl.BlockSpec(shape, lambda h: (0,) * len(shape), pipeline_mode=pl.Buffered(1))
 
     wide = pl.BlockSpec((tokens, cols), lambda h: (0, now(h)))
+    wide_once = pl.BlockSpec((tokens, cols), lambda h: (0, now(h)), pipeline_mode=pl.Buffered(1))
 
     def lanes(first, second):
         return pl.BlockSpec((first, second, cols), lambda h: (0, 0, now(h)))
@@ -901,19 +902,21 @@
         return pl.BlockSpec((HEADS_STEP,) + tail, lambda h: (now(h),) + (0,) * len(tail))
 
     weight = pl.BlockSpec((width, cols), lambda h: (0, before(h)), pipeline_mode=pl.Buffered(1))
-    mixed_spec = pl.BlockSpec((tokens, cols), lambda h: (0, before(h)))
+    mixed_spec = pl.BlockSpec((tokens, cols), lambda h: (0, before(h)), pipeline_mode=pl.Buffered(1))
     parts = 4
     anywhere = pl.BlockSpec(memory_space=pl.ANY)
     return pl.pallas_call(
         fused_kernel,
         grid=(units + 1,),
         in_specs=[
-            whole(since.shape), whole(beta_logit.shape), wide, wide, wide, lanes(3, PAD), lanes(3, CONV),
+            whole(since.shape), whole(beta_logit.shape), wide_once, wide_once, wide_once, lanes(3, PAD), lanes(3, CONV),
             wide, wide, each(blocks, BLOCK, BLOCK), each(blocks, BLOCK, 2 * BLOCK),
             each(BLOCK, BLOCK), each(BLOCK, BLOCK), wide,
             weight, weight, weight, mixed_spec, anywhere, anywhere,
         ],
-        out_specs=[anywhere, anywhere, lanes(3, CONV), whole(beta_logit.shape)],
+        out_specs=[
+            anywhere, anywhere, lanes(3, CONV), pl.BlockSpec(beta_logit.shape, lambda h: (0, 0)),
+        ],
         out_shape=[
             jax.ShapeDtypeStruct((parts, share, width), F32),
             jax.ShapeDtypeStruct((tokens, width), F32),
@@ -940,7 +943,7 @@
             dma((units, depth - 1, parts)), dma((units, depth - 1, parts)),
         ],
         compiler_params=pltpu.CompilerParams(
-            collective_id=5, has_side_effects=True, vmem_limit_bytes=62 * 1024 * 1024
+            collective_id=5, has_side_effects=True, vmem_limit_bytes=125 * 512 * 1024
         ),
         name="fused_backward",
     )(

time: 833 us -> 833 us (level)
  no operation moved by 1% of the time
where the time goes in v10:
time: 833 us; the launch traced here: 827 us
  Pallas kernels  465 us (56%)
  matrix products  173 us (21%)
  waiting for transfers between devices  113 us (14%)
  local copies, waits for them, and re-layouts  32.5 us (4%)
  other arithmetic  21.3 us (3%)
  between operations  15.2 us (2%)
    pallas_call x1, Pallas kernels, fused_backward(): pl.pallas_call(fused_kernel, grid=(units + 1,), in_specs=[whole(since.sha...  216 us
    all_gather x3, waiting for transfers between devices, gather(): return lax.all_gather(rows, 'narrow', axis=0, tiled=True)  111 us
    dot_general x11, matrix products, matmul(): return jnp.dot(left, right, preferred_element_type=F32)  102 us
    pallas_call x1, Pallas kernels, ffn_grads(): pl.pallas_call(ffn_grads_kernel, in_specs=[pl.BlockSpec(memory_space=pl.A...  98.6 us
    pallas_call x2, Pallas kernels, carry_chain(): pl.pallas_call(functools.partial(chain_kernel, axis, forward), in_specs=[...  61.3 us
    pallas_call x1, Pallas kernels, mixer_forward(): pl.pallas_call(forward_kernel, grid=(heads // HEADS_STEP,), in_specs=[who...  50.7 us
    dot_general x4, matrix products, dot_nt(): return jnp.einsum('re,de->rd', left, right, preferred_element_type=F32)  40.7 us
    dot_general x2, matrix products, local(): d_act = jnp.einsum('rd,fd->rf', cot[at], w_down, preferred_element_type=F32)  21.4 us
  transfers between devices with their start and end apart: 9, of which 4 were waited for; matrix products, arithmetic and copies ran while one was open for 25% of the time, Pallas kernels for 56%

profile of v10, /device:TPU:0, one launch (start us, length us, event | category | flops | bytes accessed | tf_op | source)
XLA Modules:
  0.0 827.5 jit_solution(12394701757650548401)
XLA Ops:
  7.3 0.7 all-gather.4.cloned.1.call-update
  8.0 2.1 fusion.9
  10.1 0.6 multiply_multiply_fusion
  10.7 0.6 copy-done.38
  11.8 9.2 %convolution_convert_fusion.4.query_ref.refs_2_ = bf16[512,2048]{1,0:T(8,128)(2,1)S(1)} fusion(bf16[512,2048]{1,0:T(8,128)(2,1)S(1)} %fusion.11.refs_18_, bf16[2048,2048]{1,0:T(8,128)(2,1)} %refs_14_.1), kind=kOutput, calls=%fused_computation.44 | convolution fusion | flops 4296015872 | bytes 12582912 | tf_op jit(solution)/shard_map/dot_general | solution.py:1160
  21.1 4.8 convolution_convert_fusion.2.value_ref.refs_4_
  26.0 4.8 convolution_convert_fusion.3.key_ref.refs_3_
  30.8 1.3 copy-done.19
  32.1 5.5 collective-permute-start
  37.9 3.0 fusion.28.beta_ref.refs_1_
  40.9 1.0 collective-permute-done.halo_ref.refs_5_
  41.9 0.8 broadcast_in_dim.21.since_ref.refs_0_
  42.8 50.7 %mixer_forward.1 = (bf16[512,2048]{1,0:T(8,128)(2,1)}, bf16[512,2048]{1,0:T(8,128)(2,1)}, bf16[512,2048]{1,0:T(8,128)(2,1)}, bf16[512,2048]{1,0:T(8,128)(2,1)}, ...) custom-call(s32[512,128]{1,0:T(8,128)} %broadcast_in_dim.21.since_ref.refs_0_, ...), custom_call_target="tpu_custom_call" | custom-call | tf_op jit(solution)/shard_map/mixer_forward/pallas_call | solution.py:180
  93.5 1.3 slice.97.map_ref
  94.8 1.5 slice.65.add_ref
  96.4 26.7 %carry_forward.1.entry_ref.refs_11_ = f32[16,128,128]{2,1,0:T(8,128)S(1)} custom-call(bf16[16,128,128]{2,1,0:T(8,128)(2,1)S(1)} %slice.97.map_ref, f32[16,128,128]{2,1,0:T(8,128)S(1)} %slice.65.add_ref), custom_call_target="tpu_custom_call" | custom-call | tf_op jit(solution)/shard_map/carry_forward/pallas_call | solution.py:499
  123.1 1.0 copy-done.1
  124.1 7.6 mixer_join.1.refs_17_
  131.7 7.8 multiply_reduce_fusion
  139.4 0.6 multiply_multiply_fusion.1
  140.1 1.4 copy-done.6
  141.9 29.2 %all-gather.4.cloned.1.call-done = bf16[2048,2048]{1,0:T(8,128)(2,1)} async-done(((bf16[512,2048]{1,0:T(8,128)(2,1)}), bf16[2048,2048]{1,0:T(8,128)(2,1)}) %all-gather.4.cloned.1.call-update) | async-done | bytes 8388624 | tf_op jit(solution)/shard_map/all_gather | solution.py:1221
  171.1 1.4 fusion.27
  172.8 4.0 fusion.25
  176.8 12.9 %fusion.29 = f32[1024,1408]{1,0:T(8,128)} fusion(bf16[1024,2048]{1,0:T(8,128)(2,1)S(1)} %bitcast.77, bf16[1408,2048]{1,0:T(8,128)(2,1)} %param.28), kind=kOutput, calls=%fused_computation.77 | convolution fusion | flops 5905580032 | bytes 15728640 | tf_op jit(solution)/shard_map/rd,fd->rf/dot_general | solution.py:1255
  189.8 8.5 %fusion.32 = f32[1024,1408]{1,0:T(8,128)} fusion(bf16[1024,2048]{1,0:T(8,128)(2,1)S(1)} %bitcast.75, bf16[1408,2048]{1,0:T(8,128)(2,1)S(1)} %bitcast.99), kind=kOutput, calls=%fused_computation.80 | convolution fusion | flops 5905580032 | bytes 15728640 | tf_op jit(solution)/shard_map/rd,fd->rf/dot_general | solution.py:1255
  198.5 57.6 %all-gather.6.cloned.1.call-done.refs_0_ = bf16[1024,2048]{1,0:T(8,128)(2,1)} async-done(((bf16[256,2048]{1,0:T(8,128)(2,1)}), bf16[1024,2048]{1,0:T(8,128)(2,1)}) %all-gather.6.cloned.1.call-update) | async-done | bytes 4194320 | tf_op jit(solution)/shard_map/all_gather | solution.py:1221
  256.2 11.8 %fusion.30 = f32[1024,1408]{1,0:T(8,128)} fusion(bf16[1024,2048]{1,0:T(8,128)(2,1)} %all-gather.6.cloned.1.call-done.refs_0_, bf16[2048,1408]{1,0:T(8,128)(2,1)} %param.26), kind=kOutput, calls=%fused_computation.78 | convolution fusion | flops 5905580032 | bytes 15728640 | tf_op jit(solution)/shard_map/dot_general | solution.py:1160
  268.0 12.7 %multiply_convert_fusion.3 = (bf16[1024,1408]{1,0:T(8,128)(2,1)S(1)}, bf16[1024,1408]{1,0:T(8,128)(2,1)S(1)}, bf16[1024,1408]{1,0:T(8,128)(2,1)S(1)}) fusion(f32[1024,1408]{1,0:T(8,128)} %fusion.30, f32[1024,1408]{1,0:T(8,128)} %fusion.29, bf16[1024,2048]{1,0:T(8,128)(2,1)S(1)} %copy-done.20, bf16[2048,1408]{1,0:T(8,128)(2,1)} %param.27), kind=kOutput, calls=%fused_computation.13 | convolution fusion | flops 5927206912 | bytes 30146560 | tf_op jit(solution)/shard_map/dot_general | solution.py:1160
  280.7 10.9 %convolution_convert_fusion.1 = bf16[1024,2048]{1,0:T(8,128)(2,1)S(1)} fusion(bf16[1024,1408]{1,0:T(8,128)(2,1)S(1)} %get-tuple-element.97.refs_8_, bf16[1408,2048]{1,0:T(8,128)(2,1)} %param.28), kind=kOutput, calls=%fused_computation.41 | convolution fusion | flops 5907677184 | bytes 12845056 | tf_op jit(solution)/shard_map/dot_general | solution.py:1160
  291.6 2.7 fusion.26
  294.3 8.9 %fusion.31 = f32[1024,2048]{1,0:T(8,128)} fusion(bf16[1024,1408]{1,0:T(8,128)(2,1)S(1)} %get-tuple-element.98.refs_4_, bf16[2048,1408]{1,0:T(8,128)(2,1)S(1)} %bitcast.93), kind=kOutput, calls=%fused_computation.79 | convolution fusion | flops 5905580032 | bytes 17039360 | tf_op jit(solution)/shard_map/re,de->rd/dot_general | solution.py:1168
  303.2 10.6 %add_convert_fusion.1 = bf16[1024,2048]{1,0:T(8,128)(2,1)} fusion(f32[1024,2048]{1,0:T(8,128)} %fusion.31, bf16[1024,1408]{1,0:T(8,128)(2,1)S(1)} %get-tuple-element.99.refs_6_, bf16[2048,1408]{1,0:T(8,128)(2,1)S(1)} %bitcast.97), kind=kOutput, calls=%fused_computation.7 | convolution fusion | flops 5909774336 | bytes 21233664 | tf_op jit(solution)/shard_map/re,de->rd/dot_general | solution.py:1168
  313.8 23.8 %all-gather.8.cloned.1.call-done.refs_1_ = bf16[1024,2048]{1,0:T(8,128)(2,1)} async-done(((bf16[256,2048]{1,0:T(8,128)(2,1)}), bf16[1024,2048]{1,0:T(8,128)(2,1)}) %all-gather.8.cloned.1.call-update) | async-done | bytes 4194320 | tf_op jit(solution)/shard_map/all_gather | solution.py:1221
  338.1 12.0 %fusion.33 = f32[1024,1408]{1,0:T(8,128)} fusion(bf16[1024,2048]{1,0:T(8,128)(2,1)} %all-gather.8.cloned.1.call-done.refs_1_, bf16[2048,1408]{1,0:T(8,128)(2,1)} %param.26), kind=kOutput, calls=%fused_computation.81 | convolution fusion | flops 5905580032 | bytes 15728640 | tf_op jit(solution)/shard_map/dot_general | solution.py:1160
  350.2 14.3 %multiply_convert_fusion = (bf16[1024,1408]{1,0:T(8,128)(2,1)}, bf16[1024,1408]{1,0:T(8,128)(2,1)S(1)}, bf16[1024,1408]{1,0:T(8,128)(2,1)S(1)}) fusion(f32[1024,1408]{1,0:T(8,128)} %fusion.33, f32[1024,1408]{1,0:T(8,128)} %fusion.32, bf16[1024,2048]{1,0:T(8,128)(2,1)S(1)} %copy-done.21, bf16[2048,1408]{1,0:T(8,128)(2,1)} %param.27), kind=kOutput, calls=%fused_computation.8 | convolution fusion | flops 5927206912 | bytes 30146560 | tf_op jit(solution)/shard_map/dot_general | solution.py:1160
  364.5 8.9 %fusion.34 = f32[1024,2048]{1,0:T(8,128)} fusion(bf16[1024,1408]{1,0:T(8,128)(2,1)S(1)} %get-tuple-element.95.refs_5_, bf16[2048,1408]{1,0:T(8,128)(2,1)S(1)} %bitcast.95), kind=kOutput, calls=%fused_computation.82 | convolution fusion | flops 5905580032 | bytes 17039360 | tf_op jit(solution)/shard_map/re,de->rd/dot_general | solution.py:1168
  373.5 12.2 %add_convert_fusion = bf16[1024,2048]{1,0:T(8,128)(2,1)} fusion(f32[1024,2048]{1,0:T(8,128)} %fusion.34, bf16[1024,1408]{1,0:T(8,128)(2,1)S(1)} %get-tuple-element.96.refs_7_, bf16[2048,1408]{1,0:T(8,128)(2,1)} %param.27), kind=kOutput, calls=%fused_computation.6 | convolution fusion | flops 5909774336 | bytes 21233664 | tf_op jit(solution)/shard_map/re,de->rd/dot_general | solution.py:1168
  386.0 98.6 %ffn_grads.1 = (f32[256,1408]{1,0:T(8,128)}, f32[256,1408]{1,0:T(8,128)}, f32[1408,256]{1,0:T(8,128)}) custom-call(bf16[1024,2048]{1,0:T(8,128)(2,1)} %all-gather.6.cloned.1.call-done.refs_0_, bf16[1024,2048]{1,0:T(8,128)(2,1)} %all-gather.8.cloned.1.call-done.refs_1_, bf16[1024,2048]{1,0:T(8,128)(2,1)} %bitcast.78, bf16[1024,2048]{1,0:T(8,128)(2,1)} %bitcast.76, ...), custom_call_target="tpu_custom_call" | custom-call | tf_op jit(solution)/shard_map/ffn_grads/pallas_call | solution.py:1126
  484.6 10.8 %convolution_convert_fusion = bf16[1024,2048]{1,0:T(8,128)(2,1)} fusion(bf16[1024,1408]{1,0:T(8,128)(2,1)S(1)} %copy-done.25, bf16[1408,2048]{1,0:T(8,128)(2,1)} %param.28), kind=kOutput, calls=%fused_computation.40 | convolution fusion | flops 5907677184 | bytes 12845056 | tf_op jit(solution)/shard_map/dot_general | solution.py:1160
  495.6 4.2 fusion.8
  499.9 0.6 copy-done.7
  500.7 3.2 fusion.24.branch_ref.refs_19_
  503.9 15.3 %mixer_core_back.1 = (bf16[512,2048]{1,0:T(8,128)(2,1)}, f32[16,128,128]{2,1,0:T(8,128)}, f32[1,128]{1,0:T(1,128)}) custom-call(bf16[512,2048]{1,0:T(8,128)(2,1)} %get-tuple-element.52.out_add_ref, bf16[512,2048]{1,0:T(8,128)(2,1)} %get-tuple-element.53.out_map_ref, f32[16,128,128]{2,1,0:T(8,128)} %copy-done.1, f32[1,128]{1,0:T(1,128)} %bitcast.90, ...), custom_call_target="tpu_custom_call" | custom-call | tf_op jit(solution)/shard_map/mixer_core_back/pallas_call | solution.py:253
  519.3 1.2 copy-done.5
  520.5 34.6 %carry_backward.1.refs_12_ = f32[16,128,128]{2,1,0:T(8,128)S(1)} custom-call(bf16[16,128,128]{2,1,0:T(8,128)(2,1)S(1)} %copy-done.3, f32[16,128,128]{2,1,0:T(8,128)S(1)} %copy-done.5), custom_call_target="tpu_custom_call" | custom-call | tf_op jit(solution)/shard_map/carry_backward/pallas_call | solution.py:499
  555.1 1.0 copy-done.4
  556.1 0.7 reduce-scatter.14.cloned.1.call-update
  557.4 0.7 reduce.3
  558.2 215.6 %fused_backward.1 = (f32[4,64,2048]{2,1,0:T(8,128)}, f32[512,2048]{1,0:T(8,128)}, f32[3,4,2048]{2,1,0:T(4,128)}, f32[512,16]{1,0:T(8,128)}) custom-call(s32[512,128]{1,0:T(8,128)} %broadcast_in_dim.21.since_ref.refs_0_, f32[512,16]{1,0:T(8,128)} %fusion.28.beta_ref.refs_1_, bf16[512,2048]{1,0:T(8,128)(2,1)} %copy-done.17, bf16[512,2048]{1,0:T(8,128)(2,1)} %copy-done.19, ...), custom_call_target="tpu_custom_call" | custom-call | tf_op jit(solution)/shard_map/fused_backward/pallas_call | solution.py:908
  773.9 1.6 reshape.129
  775.5 2.8 fusion.19
  778.2 6.4 fusion.18
  784.6 1.9 concatenate.11.small_ref
  786.5 16.1 %reduce_small.1 = f32[32,256]{1,0:T(8,128)S(1)} custom-call(f32[32,2048]{1,0:T(8,128)S(1)} %concatenate.11.small_ref), custom_call_target="tpu_custom_call" | custom-call | tf_op jit(solution)/shard_map/reduce_small/pallas_call | solution.py:596
  802.7 0.6 reshape.132
  803.3 0.6 dynamic-slice_bitcast_fusion.2
  803.9 0.6 dynamic-slice_bitcast_fusion.1
  804.4 0.7 dynamic-slice_bitcast_fusion
  805.2 3.0 slice_bitcast_fusion
  808.4 8.7 %fusion.15 = (bf16[512,2048]{1,0:T(8,128)(2,1)}, bf16[512,2048]{1,0:T(8,128)(2,1)}) fusion(bf16[512,2048]{1,0:T(8,128)(2,1)S(1)} %copy-done.10, f32[512]{0:T(512)S(1)} %broadcast_multiply_fusion, f32[512]{0:T(512)S(1)} %copy-done.41, f32[2048]{0:T(1024)S(1)} %copy-done.35, f32[512]{0:T(512)S(1)} %copy-done.39, f32[512,2048]{1,0:T(8,128)} %get-tuple-element.82, ...), kind=kLoop, calls=%fused_computation.33 | loop fusion | flops 29360128 | bytes 25194496 | tf_op jit(solution)/shard_map/convert_element_type | solution.py:1310
  817.0 1.1 copy.47
  818.1 1.1 copy.48
  819.2 1.1 copy.49
  (147 shorter events, 4.1 us)
Async XLA Ops:
  7.2 30.7 %copy-start = (bf16[2048,16]{0,1:T(8,128)(2,1)S(1)}, bf16[2048,16]{0,1:T(8,128)(2,1)}, u32[]{:S(2)}) copy-start(bf16[2048,16]{0,1:T(8,128)(2,1)} %param.21) | copy-start | bytes 196612
  7.2 4.0 copy-start.9
  7.2 4.0 copy-start.34
  7.2 163.9 %all-gather.4.cloned.1.call-start = ((), (), s32[]{:S(2)}) async-start(), calls=%async_computation.5 | async-start | bytes 10485760 | tf_op jit(solution)/shard_map/all_gather | solution.py:1221
  8.0 248.2 %all-gather.6.cloned.1.call-start = ((), (), s32[]{:S(2)}) async-start(), calls=%async_computation.6 | async-start | bytes 5242880 | tf_op jit(solution)/shard_map/all_gather | solution.py:1221
  11.2 9.9 %slice-start.2 = ((s8[8388608]{0:T(1024)(128)(4,1)}), s8[4194304]{0:T(1024)(128)(4,1)S(1)}, s32[]{:S(2)}) async-start(s8[8388608]{0:T(1024)(128)(4,1)} %bitcast.81), calls=%async_computation.15 | async-start | bytes 8388608
  11.8 14.1 %copy-start.11 = (bf16[512,2048]{1,0:T(8,128)(2,1)}, bf16[512,2048]{1,0:T(8,128)(2,1)S(1)}, u32[]{:S(2)}) copy-start(bf16[512,2048]{1,0:T(8,128)(2,1)S(1)} %fusion.11.refs_18_) | copy-start | bytes 6291460
  11.8 9.3 %slice-start.3 = ((s8[8388608]{0:T(1024)(128)(4,1)}), s8[4194304]{0:T(1024)(128)(4,1)S(1)}, s32[]{:S(2)}) async-start(s8[8388608]{0:T(1024)(128)(4,1)} %bitcast.81), calls=%async_computation.16 | async-start | bytes 8388608
  11.8 14.1 %slice-start = ((s8[8388608]{0:T(1024)(128)(4,1)}), s8[4194304]{0:T(1024)(128)(4,1)S(1)}, s32[]{:S(2)}) async-start(s8[8388608]{0:T(1024)(128)(4,1)} %bitcast.79), calls=%async_computation.13 | async-start | bytes 8388608
  21.1 4.9 copy-start.17
  21.1 4.9 slice-start.1
  26.0 4.8 copy-start.18
  26.0 11.7 %copy-start.42 = (s32[1,4]{1,0:T(1,128)S(1)}, s32[1,4]{1,0:T(1,128)}, u32[]{:S(2)}) copy-start(s32[1,4]{1,0:T(1,128)} %param.16) | copy-start | bytes 52
  30.8 1.4 copy-start.19
  32.1 9.8 %collective-permute-start = (bf16[3,8,2048]{2,1,0:T(8,128)(2,1)S(1)}, bf16[3,8,2048]{2,1,0:T(8,128)(2,1)S(1)}, u32[]{:S(2)}, u32[]{:S(2)}) collective-permute-start(bf16[3,8,2048]{2,1,0:T(8,128)(2,1)S(1)} %pad_maximum_fusion.1), channel_id=1, source_target_pairs={{0,1},{1,2},{2,3},{4,5},{5,6},{6,7},{8,9},{9,10},{10,11},{12,13},{... | collective-permute-start | bytes 294920 | tf_op jit(solution)/shard_map/ppermute | solution.py:1156
  41.9 0.8 copy-start.31
  94.8 28.3 %copy-start.2 = (bf16[16,128,128]{2,1,0:T(8,128)(2,1)}, bf16[16,128,128]{2,1,0:T(8,128)(2,1)S(1)}, u32[]{:S(2)}) copy-start(bf16[16,128,128]{2,1,0:T(8,128)(2,1)S(1)} %slice.97.map_ref) | copy-start | bytes 1572868
  123.1 1.0 copy-start.1
  131.7 9.8 %copy-start.32 = (f32[2048]{0:T(1024)S(1)}, f32[2048]{0:T(1024)}, u32[]{:S(2)}) copy-start(f32[2048]{0:T(1024)} %param.25) | copy-start | bytes 24580
  139.4 2.0 copy-start.6
  140.1 1.4 copy-start.36
  172.6 165.1 %all-gather.8.cloned.1.call-start = ((), (), s32[]{:S(2)}) async-start(), calls=%async_computation.7 | async-start | bytes 5242880 | tf_op jit(solution)/shard_map/all_gather | solution.py:1221
  172.8 16.9 %slice-start.10 = ((s8[5767168]{0:T(1024)(128)(4,1)}), s8[4194304]{0:T(1024)(128)(4,1)S(1)}, s32[]{:S(2)}) async-start(s8[5767168]{0:T(1024)(128)(4,1)} %bitcast.98), calls=%async_computation.23 | async-start | bytes 8388608
  176.8 12.9 %copy-start.14 = (bf16[4,256,2048]{2,1,0:T(8,128)(2,1)}, bf16[4,256,2048]{2,1,0:T(8,128)(2,1)S(1)}, u32[]{:S(2)}) copy-start(bf16[4,256,2048]{2,1,0:T(8,128)(2,1)S(1)} %get-tuple-element.101) | copy-start | bytes 12582916
  176.8 12.9 %copy-start.13 = (bf16[4,256,2048]{2,1,0:T(8,128)(2,1)}, bf16[4,256,2048]{2,1,0:T(8,128)(2,1)S(1)}, u32[]{:S(2)}) copy-start(bf16[4,256,2048]{2,1,0:T(8,128)(2,1)S(1)} %get-tuple-element.100) | copy-start | bytes 12582916
  176.8 12.9 %slice-start.11 = ((s8[5767168]{0:T(1024)(128)(4,1)}), s8[1572864]{0:T(1024)(128)(4,1)S(1)}, s32[]{:S(2)}) async-start(s8[5767168]{0:T(1024)(128)(4,1)} %bitcast.98), calls=%async_computation.24 | async-start | bytes 3145728
  198.3 297.2 %reduce-scatter.6.cloned.1.call-start = ((), (), s32[]{:S(2)}) async-start(), calls=%async_computation.8 | async-start | bytes 5242880 | tf_op jit(solution)/shard_map/reduce_scatter | solution.py:1224
  256.2 11.8 %copy-start.20 = (bf16[1024,2048]{1,0:T(8,128)(2,1)S(1)}, bf16[1024,2048]{1,0:T(8,128)(2,1)}, u32[]{:S(2)}) copy-start(bf16[1024,2048]{1,0:T(8,128)(2,1)} %all-gather.6.cloned.1.call-done.refs_0_) | copy-start | bytes 12582916
  256.2 38.1 %slice-start.4 = ((s8[5767168]{0:T(1024)(128)(4,1)}), s8[4194304]{0:T(1024)(128)(4,1)S(1)}, s32[]{:S(2)}) async-start(s8[5767168]{0:T(1024)(128)(4,1)} %bitcast.92), calls=%async_computation.17 | async-start | bytes 8388608
  268.0 26.3 %slice-start.5 = ((s8[5767168]{0:T(1024)(128)(4,1)}), s8[1572864]{0:T(1024)(128)(4,1)S(1)}, s32[]{:S(2)}) async-start(s8[5767168]{0:T(1024)(128)(4,1)} %bitcast.92), calls=%async_computation.18 | async-start | bytes 3145728
  280.7 10.9 %copy-start.22 = (bf16[1024,1408]{1,0:T(8,128)(2,1)}, bf16[1024,1408]{1,0:T(8,128)(2,1)S(1)}, u32[]{:S(2)}) copy-start(bf16[1024,1408]{1,0:T(8,128)(2,1)S(1)} %get-tuple-element.97.refs_8_) | copy-start | bytes 8650756
  280.7 13.6 %copy-start.23 = (bf16[1024,1408]{1,0:T(8,128)(2,1)}, bf16[1024,1408]{1,0:T(8,128)(2,1)S(1)}, u32[]{:S(2)}) copy-start(bf16[1024,1408]{1,0:T(8,128)(2,1)S(1)} %get-tuple-element.98.refs_4_) | copy-start | bytes 8650756
  280.7 22.5 %copy-start.24 = (bf16[1024,1408]{1,0:T(8,128)(2,1)}, bf16[1024,1408]{1,0:T(8,128)(2,1)S(1)}, u32[]{:S(2)}) copy-start(bf16[1024,1408]{1,0:T(8,128)(2,1)S(1)} %get-tuple-element.99.refs_6_) | copy-start | bytes 8650756
  291.6 11.6 %slice-start.8 = ((s8[5767168]{0:T(1024)(128)(4,1)}), s8[4194304]{0:T(1024)(128)(4,1)S(1)}, s32[]{:S(2)}) async-start(s8[5767168]{0:T(1024)(128)(4,1)} %bitcast.96), calls=%async_computation.21 | async-start | bytes 8388608
  294.3 8.9 %slice-start.9 = ((s8[5767168]{0:T(1024)(128)(4,1)}), s8[1572864]{0:T(1024)(128)(4,1)S(1)}, s32[]{:S(2)}) async-start(s8[5767168]{0:T(1024)(128)(4,1)} %bitcast.96), calls=%async_computation.22 | async-start | bytes 3145728
  337.7 157.8 %reduce-scatter.8.cloned.1.call-start = ((), (), s32[]{:S(2)}) async-start(), calls=%async_computation.9 | async-start | bytes 5242880 | tf_op jit(solution)/shard_map/reduce_scatter | solution.py:1224
  338.1 12.0 %copy-start.21 = (bf16[1024,2048]{1,0:T(8,128)(2,1)S(1)}, bf16[1024,2048]{1,0:T(8,128)(2,1)}, u32[]{:S(2)}) copy-start(bf16[1024,2048]{1,0:T(8,128)(2,1)} %all-gather.8.cloned.1.call-done.refs_1_) | copy-start | bytes 12582916
  338.1 26.4 %slice-start.6 = ((s8[5767168]{0:T(1024)(128)(4,1)}), s8[4194304]{0:T(1024)(128)(4,1)S(1)}, s32[]{:S(2)}) async-start(s8[5767168]{0:T(1024)(128)(4,1)} %bitcast.94), calls=%async_computation.19 | async-start | bytes 8388608
  350.2 14.3 %slice-start.7 = ((s8[5767168]{0:T(1024)(128)(4,1)}), s8[1572864]{0:T(1024)(128)(4,1)S(1)}, s32[]{:S(2)}) async-start(s8[5767168]{0:T(1024)(128)(4,1)} %bitcast.94), calls=%async_computation.20 | async-start | bytes 3145728
  364.5 9.0 %copy-start.26 = (bf16[1024,1408]{1,0:T(8,128)(2,1)}, bf16[1024,1408]{1,0:T(8,128)(2,1)S(1)}, u32[]{:S(2)}) copy-start(bf16[1024,1408]{1,0:T(8,128)(2,1)S(1)} %get-tuple-element.95.refs_5_) | copy-start | bytes 8650756
  364.5 9.0 %copy-start.27 = (bf16[1024,1408]{1,0:T(8,128)(2,1)}, bf16[1024,1408]{1,0:T(8,128)(2,1)S(1)}, u32[]{:S(2)}) copy-start(bf16[1024,1408]{1,0:T(8,128)(2,1)S(1)} %get-tuple-element.96.refs_7_) | copy-start | bytes 8650756
  385.7 419.4 %reduce-scatter.10.cloned.1.call-start = ((), (), s32[]{:S(2)}) async-start(), calls=%async_computation.10 | async-start | bytes 2621440 | tf_op jit(solution)/shard_map/reduce_scatter | solution.py:1224
  385.9 98.6 %copy-start.25 = (bf16[1024,1408]{1,0:T(8,128)(2,1)S(1)}, bf16[1024,1408]{1,0:T(8,128)(2,1)}, u32[]{:S(2)}) copy-start(bf16[1024,1408]{1,0:T(8,128)(2,1)} %get-tuple-element.94.refs_9_) | copy-start | bytes 8650756
  484.6 10.9 %copy-start.33 = (f32[2048]{0:T(1024)S(1)}, f32[2048]{0:T(1024)}, u32[]{:S(2)}) copy-start(f32[2048]{0:T(1024)} %param.25) | copy-start | bytes 24580
  484.6 10.9 %copy-start.37 = (f32[512]{0:T(512)S(1)}, f32[512]{0:T(512)}, u32[]{:S(2)}) copy-start(f32[512]{0:T(512)} %copy-done.36) | copy-start | bytes 6148
  495.4 4.4 copy-start.12
  495.4 4.4 copy-start.15
  495.4 4.4 copy-start.40
  495.5 309.6 %reduce-scatter.12.cloned.1.call-start = ((), (), s32[]{:S(2)}) async-start(), calls=%async_computation.11 | async-start | bytes 2621440 | tf_op jit(solution)/shard_map/reduce_scatter | solution.py:1224
  495.6 4.9 copy-start.7
  495.6 5.2 copy-start.16
  503.9 15.3 %copy-start.3 = (bf16[16,128,128]{2,1,0:T(8,128)(2,1)S(1)}, bf16[16,128,128]{2,1,0:T(8,128)(2,1)}, u32[]{:S(2)}) copy-start(bf16[16,128,128]{2,1,0:T(8,128)(2,1)} %copy-done.2) | copy-start | bytes 1572868
  519.2 1.2 copy-start.5
  520.5 36.9 %copy-start.43 = (f32[1,128]{1,0:T(1,128)S(1)}, f32[1,128]{1,0:T(1,128)}, u32[]{:S(2)}) copy-start(f32[1,128]{1,0:T(1,128)} %get-tuple-element.85) | copy-start | bytes 1540
  555.1 1.0 copy-start.4
  556.1 249.0 %reduce-scatter.14.cloned.1.call-start = ((), (), s32[]{:S(2)}) async-start(), calls=%async_computation.12 | async-start | bytes 5242880 | tf_op jit(solution)/shard_map/reduce_scatter | solution.py:1224
  558.2 220.0 %copy-start.35 = (f32[2048]{0:T(1024)S(1)}, f32[2048]{0:T(1024)}, u32[]{:S(2)}) copy-start(f32[2048]{0:T(1024)} %param.17) | copy-start | bytes 24580
  558.2 220.0 %copy-start.39 = (f32[512]{0:T(512)S(1)}, f32[512]{0:T(512)}, u32[]{:S(2)}) copy-start(f32[512]{0:T(512)} %copy-done.38) | copy-start | bytes 6148
  778.2 30.0 %copy-start.10 = (bf16[512,2048]{1,0:T(8,128)(2,1)S(1)}, bf16[512,2048]{1,0:T(8,128)(2,1)}, u32[]{:S(2)}) copy-start(bf16[512,2048]{1,0:T(8,128)(2,1)} %param.15) | copy-start | bytes 6291460
  784.6 23.6 %copy-start.41 = (f32[512]{0:T(512)S(1)}, f32[512]{0:T(512)}, u32[]{:S(2)}) copy-start(f32[512]{0:T(512)} %get-tuple-element.114) | copy-start | bytes 6148
  805.1 3.2 copy-start.8
  808.4 8.7 %copy-start.30 = (f32[256,1408]{1,0:T(8,128)S(1)}, f32[256,1408]{1,0:T(8,128)}, u32[]{:S(2)}) copy-start(f32[256,1408]{1,0:T(8,128)} %get-tuple-element.148) | copy-start | bytes 4325380
  808.4 9.8 %copy-start.29 = (f32[256,1408]{1,0:T(8,128)S(1)}, f32[256,1408]{1,0:T(8,128)}, u32[]{:S(2)}) copy-start(f32[256,1408]{1,0:T(8,128)} %get-tuple-element.149) | copy-start | bytes 4325380
  817.0 2.2 copy-start.28
  (1 other events, 0.6 us)
Sparse Core Ops, SparseCore 0:
  9.6 161.4 all-gather.3
  173.2 82.8 all-gather.5
  258.3 79.2 all-gather.7
  339.8 75.2 reduce-scatter.5
  417.4 77.2 reduce-scatter.7
  496.8 55.4 reduce-scatter.9
  556.2 43.2 reduce-scatter.11
  601.8 127.2 reduce-scatter.13
